TPU v7x, 32 devices: a whole 2x2x4 slice. The times are simulated.
32 devices in a mesh: rows: 8 (over z, y), grp: 4 (over x, core).
Axes of the slice: x: 2, y: 2, z: 4, core: 2. Of those that a mesh axis runs over, the one named last changes fastest.
Arguments:
- slab: bfloat16 [18432, 4096], P(('rows', 'grp')), may hold values from -6 to 6
- sketch: bfloat16 [4096, 128], replicated, may hold values from -0.09375 to 0.09375
Outputs:
- basis: float32 [18432, 128], P(('rows', 'grp'))
- projected: bfloat16 [4096, 128], P(('rows', 'grp'))
All inputs are finite; a program needn't handle non-finite values.
Results may differ from a plain program's by a relative error of at most 0.0035.
Values sent between devices are 32-bit elements; how exact they have to be, the bound alone decides.
No kernel may reach another device: no remote copies, remote signals or barrier semaphores. Data moves between devices by JAX's collectives and lax.ppermute only.
A program may use at most 64 MiB of HBM per device.

v0:
```python
import jax
import jax.numpy as jnp
from jax import lax
from jax.sharding import PartitionSpec as P


def right_solve(matrix, gram):
    lower = jnp.linalg.cholesky(gram)
    return lax.linalg.triangular_solve(lower, matrix, left_side=False, lower=True, transpose_a=True)


def local_gram(matrix):
    return jnp.dot(
        matrix.T, matrix, precision=lax.Precision.HIGHEST, preferred_element_type=jnp.float32
    )


def orthonormal(matrix):
    gram = lax.psum(local_gram(matrix), ("rows", "grp"))
    result = right_solve(matrix, gram)
    return result


def local(slab, sketch):
    rows_loc, width = slab.shape
    devices_all = lax.axis_size(("rows", "grp"))
    total_rows = rows_loc * devices_all
    own_rows = width // devices_all
    first = jnp.dot(slab, sketch, preferred_element_type=jnp.float32)
    basis_one = orthonormal(first)
    low_one = basis_one.astype(jnp.bfloat16)
    whole = lax.psum(
        lax.dot_general(
            slab, low_one, (((0,), (0,)), ((), ())), preferred_element_type=jnp.float32
        ),
        ("rows", "grp"),
    )
    final = lax.dynamic_slice_in_dim(whole, lax.axis_index(("rows", "grp")) * own_rows, own_rows, 0)
    basis = basis_one * jnp.sqrt(jnp.float32(total_rows))
    projected = (final * jnp.sqrt(jnp.float32(width) / jnp.float32(total_rows))).astype(
        jnp.bfloat16
    )
    return (basis, projected)


def solution(mesh):
    return jax.shard_map(
        local,
        mesh=mesh,
        in_specs=(P(("rows", "grp"), None), P()),
        out_specs=(P(("rows", "grp"), None), P(("rows", "grp"), None)),
        check_vma=False,
    )
```

profile of v0, /device:TPU:0, one launch (start us, length us, event | category | flops | bytes accessed | tf_op | source)
XLA Modules:
  0.0 308.1 jit_solution(16606027451929187750)
XLA Ops:
  7.2 0.0 copy-start
  7.2 0.0 all-reduce.3.cloned.1.call-start
  7.2 1.2 copy-done
  8.4 3.7 %fusion.5 = f32[576,128]{1,0:T(8,128)S(1)} fusion(bf16[576,4096]{1,0:T(8,128)(2,1)} %param.2, bf16[4096,128]{1,0:T(8,128)(2,1)S(1)} %copy-done), kind=kOutput, calls=%fused_computation.14 | convolution fusion | flops 603979776 | bytes 6062080 | tf_op jit(solution)/shard_map/dot_general | solution.py:29
  12.1 1.3 fusion.6
  13.4 0.0 all-reduce.3.cloned.1.call-update
  13.5 0.0 all-reduce.5.cloned.1.call-start
  13.5 120.9 %all-reduce.3.cloned.1.call-done = f32[128,128]{0,1:T(8,128)} async-done(((f32[128,128]{0,1:T(8,128)}), f32[128,128]{0,1:T(8,128)}) %all-reduce.3.cloned.1.call-update) | async-done | bytes 65552 | tf_op jit(solution)/shard_map/psum | solution.py:19
  134.5 0.9 copy.5
  135.4 0.9 fusion.4
  136.2 11.7 %cholesky.16 = f32[128,128]{1,0:T(8,128)S(1)} custom-call(f32[128,128]{1,0:T(8,128)S(1)} %fusion.4), custom_call_target="Cholesky" | custom-call | tf_op jit(solution)/shard_map/jit(cholesky)/cholesky | solution.py:8
  148.0 0.6 compare_reduce_fusion
  148.6 0.7 fusion.1
  149.3 9.8 %custom-call.6 = f32[1,128,128]{1,2,0:T(8,128)S(1)} custom-call(f32[1,128,128]{2,1,0:T(8,128)S(1)} %fusion.1), custom_call_target="InvertDiagBlocksLowerTriangular" | custom-call | tf_op jit(solution)/shard_map/triangular_solve | solution.py:9
  159.1 1.1 broadcast_multiply_fusion
  160.2 4.6 %convolution_bitcast_fusion = f32[4096,128]{0,1:T(8,128)} fusion(bf16[576,4096]{1,0:T(8,128)(2,1)} %param.2, bf16[576,128]{1,0:T(8,128)(2,1)S(1)} %get-tuple-element.5), kind=kOutput, calls=%fused_computation | convolution fusion | flops 603979776 | bytes 6963200 | tf_op jit(solution)/shard_map/dot_general | solution.py:33
  164.9 0.0 all-reduce.5.cloned.1.call-update
  164.9 134.8 %all-reduce.5.cloned.1.call-done = f32[4096,128]{0,1:T(8,128)} async-done(((f32[4096,128]{0,1:T(8,128)}), f32[4096,128]{0,1:T(8,128)}) %all-reduce.5.cloned.1.call-update) | async-done | bytes 2097168 | tf_op jit(solution)/shard_map/psum | solution.py:32
  299.7 0.8 multiply_convert_fusion
  300.5 0.7 copy.6
  (1 shorter events, 0.0 us)
Async XLA Ops:
  7.2 1.2 copy-start
  7.2 127.3 %all-reduce.3.cloned.1.call-start = ((), (), s32[]{:S(2)}) async-start(), calls=%async_computation | async-start | bytes 131072 | tf_op jit(solution)/shard_map/psum | solution.py:19
  13.5 286.2 %all-reduce.5.cloned.1.call-start = ((), (), s32[]{:S(2)}) async-start(), calls=%async_computation.1 | async-start | bytes 4194304 | tf_op jit(solution)/shard_map/psum | solution.py:32
Sparse Core Ops, SparseCore 0:
  14.2 120.2 all-reduce.2
  165.0 134.5 all-reduce.4
where the time goes:
time: 308 us
  waiting for transfers between devices  256 us (83%)
  other arithmetic  24.6 us (8%)
  between operations  14.1 us (5%)
  matrix products  10.8 us (4%)
    psum x1, waiting for transfers between devices, local(): lax.psum(lax.dot_general(slab, low_one, (((0,), (0,)), ((), ())), preferr...  135 us
    psum x1, waiting for transfers between devices, orthonormal(): gram = lax.psum(local_gram(matrix), ('rows', 'grp'))  121 us
    another operation x3, other arithmetic, right_solve(): lower = jnp.linalg.cholesky(gram)  12.4 us
    another operation x2, other arithmetic, right_solve(): lax.linalg.triangular_solve(lower, matrix, left_side=False, lower=True, t...  10.5 us
  transfers between devices with their start and end apart: 2, of which 2 were waited for; matrix products, arithmetic and copies ran while one was open for 0% of the time, Pallas kernels for 0%

commit v1 on v0

v1 whole, which is shorter than its diff:
```python
import functools

import jax
import jax.numpy as jnp
from jax import lax
from jax.experimental import pallas as pl
from jax.experimental.pallas import tpu as pltpu
from jax.sharding import PartitionSpec as P

AXES = ("rows", "grp")
HIGHEST = lax.Precision.HIGHEST
LANES = 128
VMEM_LIMIT = 40 * 1024 * 1024


def sketch_kernel(slab_ref, sketch_ref, first_ref, split_ref, gram_ref, acc_ref):
    step = pl.program_id(0)
    part = jnp.dot(slab_ref[...], sketch_ref[...], preferred_element_type=jnp.float32)

    @pl.when(step == 0)
    def _():
        acc_ref[...] = part

    @pl.when(step > 0)
    def _():
        acc_ref[...] += part

    @pl.when(step == pl.num_programs(0) - 1)
    def _():
        first = acc_ref[...]
        first_ref[...] = first
        gram_ref[...] = lax.dot_general(
            first, first, (((0,), (0,)), ((), ())),
            precision=HIGHEST, preferred_element_type=jnp.float32,
        )
        high = first.astype(jnp.bfloat16)
        low = (first - high.astype(jnp.float32)).astype(jnp.bfloat16)
        split_ref[...] = jnp.concatenate([high.T, low.T], axis=0)


def sketch_call(slab, sketch):
    rows, width = slab.shape
    rank = sketch.shape[1]
    block = 512
    return pl.pallas_call(
        sketch_kernel,
        grid=(width // block,),
        in_specs=[
            pl.BlockSpec((rows, block), lambda k: (0, k)),
            pl.BlockSpec((block, rank), lambda k: (k, 0)),
        ],
        out_specs=[
            pl.BlockSpec((rows, rank), lambda k: (0, 0)),
            pl.BlockSpec((2 * rank, rows), lambda k: (0, 0)),
            pl.BlockSpec((rank, rank), lambda k: (0, 0)),
        ],
        out_shape=[
            jax.ShapeDtypeStruct((rows, rank), jnp.float32),
            jax.ShapeDtypeStruct((2 * rank, rows), jnp.bfloat16),
            jax.ShapeDtypeStruct((rank, rank), jnp.float32),
        ],
        scratch_shapes=[pltpu.VMEM((rows, rank), jnp.float32)],
        compiler_params=pltpu.CompilerParams(vmem_limit_bytes=VMEM_LIMIT),
        cost_estimate=pl.CostEstimate(
            flops=2 * rows * width * rank, bytes_accessed=rows * width * 2, transcendentals=0
        ),
        name="sketch_rows",
    )(slab, sketch)


def project_kernel(me_ref, split_ref, slab_ref, keep_ref, send_ref, block_ref):
    rank = keep_ref.shape[0] * keep_ref.shape[4]
    half = rank // 2
    both = jnp.dot(split_ref[...], slab_ref[...], preferred_element_type=jnp.float32)
    block_ref[...] = both[:rank] + both[rank:]
    low = lax.rem(me_ref[0], 4)
    for x in range(2):
        for core, out in ((0, keep_ref), (1, send_ref)):
            at = pl.multiple_of(lax.bitwise_xor(low, 2 * x + core) * LANES, LANES)
            out[0, x, 0, 0] = block_ref[:half, pl.ds(at, LANES)]
            out[1, x, 0, 0] = block_ref[half:, pl.ds(at, LANES)]


def project_call(owner, split, slab):
    rows, width = slab.shape
    rank = split.shape[0] // 2
    block = 4 * LANES
    steps = width // block
    out_block = pl.BlockSpec((2, 2, 1, 1, rank // 2, LANES), lambda q, me: (0, 0, q % 2, q // 2, 0, 0))
    out_shape = jax.ShapeDtypeStruct((2, 2, 2, steps // 2, rank // 2, LANES), jnp.float32)
    return pl.pallas_call(
        project_kernel,
        grid_spec=pltpu.PrefetchScalarGridSpec(
            num_scalar_prefetch=1,
            grid=(steps,),
            in_specs=[
                pl.BlockSpec((2 * rank, rows), lambda q, me: (0, 0)),
                pl.BlockSpec((rows, block), lambda q, me: (0, lax.bitwise_xor(me[0] // 4, q))),
            ],
            out_specs=[out_block, out_block],
            scratch_shapes=[pltpu.VMEM((rank, block), jnp.float32)],
        ),
        out_shape=[out_shape, out_shape],
        compiler_params=pltpu.CompilerParams(vmem_limit_bytes=VMEM_LIMIT),
        cost_estimate=pl.CostEstimate(
            flops=4 * rows * width * rank, bytes_accessed=rows * width * 2, transcendentals=0
        ),
        name="project_rows",
    )(owner, split, slab)


def lane(block, at):
    return jnp.broadcast_to(block[:, at : at + 1], block.shape)


def sublane(block, at):
    return jnp.broadcast_to(block[at : at + 1, :], block.shape)


def inverse_factor(gram_ref, inverse_ref):
    size = gram_ref.shape[0]
    blocks = size // 8
    left = [gram_ref[8 * i : 8 * i + 8, :] for i in range(blocks)]
    row_at = lax.broadcasted_iota(jnp.int32, (8, size), 0)
    lane_at = lax.broadcasted_iota(jnp.int32, (8, size), 1)
    right = [jnp.where(lane_at == row_at + 8 * i, 1.0, 0.0).astype(jnp.float32) for i in range(blocks)]
    for p in range(blocks):
        column = [lane(left[p], 8 * p + k) for k in range(8)]
        entry = {(r, c): sublane(column[c], r) for c in range(8) for r in range(c, 8)}
        scale, lower = [], {}
        for k in range(8):
            scale.append(lax.rsqrt(entry[k, k]))
            for r in range(k + 1, 8):
                lower[r, k] = entry[r, k] * scale[k]
            for c in range(k + 1, 8):
                for r in range(c, 8):
                    entry[r, c] = entry[r, c] - lower[r, k] * lower[c, k]
        tops, sides = [], []
        for k in range(8):
            top, side = sublane(left[p], k), sublane(right[p], k)
            for j in range(k):
                top = top - lower[k, j] * tops[j]
                side = side - lower[k, j] * sides[j]
            tops.append(top * scale[k])
            sides.append(side * scale[k])
        result = sides[0]
        for k in range(1, 8):
            result = jnp.where(row_at == k, sides[k], result)
        inverse_ref[8 * p : 8 * p + 8, :] = result
        for i in range(p + 1, blocks):
            weights = []
            for k in range(8):
                weight = lane(left[i], 8 * p + k)
                for j in range(k):
                    weight = weight - lower[k, j] * weights[j]
                weights.append(weight * scale[k])
            for k in range(8):
                left[i] = left[i] - weights[k] * tops[k]
                right[i] = right[i] - weights[k] * sides[k]


def basis_kernel(factor, gram_ref, first_ref, inverse_ref, basis_ref):
    inverse_factor(gram_ref, inverse_ref)
    one = lax.dot_general(
        first_ref[...], inverse_ref[...], (((1,), (1,)), ((), ())),
        precision=HIGHEST, preferred_element_type=jnp.float32,
    )
    basis_ref[...] = one * factor


def basis_call(gram, first, total_rows):
    rows, rank = first.shape
    return pl.pallas_call(
        functools.partial(basis_kernel, float(total_rows) ** 0.5),
        out_shape=[
            jax.ShapeDtypeStruct((rank, rank), jnp.float32),
            jax.ShapeDtypeStruct((rows, rank), jnp.float32),
        ],
        compiler_params=pltpu.CompilerParams(vmem_limit_bytes=VMEM_LIMIT),
        cost_estimate=pl.CostEstimate(
            flops=4000000000, bytes_accessed=rows * rank * 8, transcendentals=rank
        ),
        name="basis_rows",
    )(gram, first)


def final_kernel(factor, inverse_ref, sums_ref, out_ref):
    result = jnp.dot(
        inverse_ref[...], sums_ref[...], precision=HIGHEST, preferred_element_type=jnp.float32
    )
    out_ref[...] = (result.T * factor).astype(out_ref.dtype)


def final_call(inverse, sums, factor):
    rank, own = sums.shape
    return pl.pallas_call(
        functools.partial(final_kernel, factor),
        out_shape=jax.ShapeDtypeStruct((own, rank), jnp.bfloat16),
        compiler_params=pltpu.CompilerParams(vmem_limit_bytes=VMEM_LIMIT),
        name="final_rows",
    )(inverse, sums)


def local(slab, sketch):
    rows_loc, width = slab.shape
    devices_all = lax.axis_size(AXES)
    own = width // devices_all
    bits = devices_all.bit_length() - 1
    low_bits = bits - ((width // LANES).bit_length() - 1)
    total_rows = rows_loc * devices_all
    me = lax.axis_index(AXES)

    def swap(array, bit):
        pairs = [(i, i ^ (1 << bit)) for i in range(devices_all)]
        return lax.ppermute(array, AXES, pairs)

    first, split, gram = sketch_call(slab, sketch)
    owner = lax.shift_right_logical(me, low_bits).astype(jnp.int32).reshape(1)
    keep, send = project_call(owner, split, slab)

    for bit in range(bits):
        gram = gram + swap(gram, bit)
    inverse, basis = basis_call(gram, first, total_rows)

    got = swap(send, low_bits)
    got_a = swap(keep[0, 1] + got[0, 1], low_bits + 1)
    got_b = swap(keep[1, :, 1] + got[1, :, 1], low_bits + 2)
    part_a = keep[0, 0] + got[0, 0]
    part_b = keep[1, :, 0] + got[1, :, 0]
    got_a2 = swap(part_a[1] + got_a[1], low_bits + 2)
    got_b2 = swap(part_b[1] + got_b[1], low_bits + 1)
    sums = jnp.concatenate(
        [part_a[0] + got_a[0] + got_a2, part_b[0] + got_b[0] + got_b2], axis=1
    )
    bit = low_bits + 3
    sums = sums.reshape(sums.shape[0] // 2, 2, *sums.shape[1:])
    sums = sums[:, 0] + swap(sums[:, 1], bit)
    sums = sums[0] + swap(sums[1], bit + 1)
    for bit in reversed(range(low_bits)):
        half = sums.shape[1] // 2
        mine = lax.rem(lax.shift_right_logical(me, bit), 2) == 1
        left, right = sums[:, :half], sums[:, half:]
        sums = jnp.where(mine, right, left) + swap(jnp.where(mine, left, right), bit)
    projected = final_call(inverse, sums, (float(width) / float(total_rows)) ** 0.5)
    return (basis, projected)


def solution(mesh):
    return jax.shard_map(
        local,
        mesh=mesh,
        in_specs=(P(AXES, None), P()),
        out_specs=(P(AXES, None), P(AXES, None)),
        check_vma=False,
    )
```

time: 308 us -> 53.9 us (0.17)
  waiting for transfers between devices: 256 us -> 16.7 us
  other arithmetic: 24.6 us -> 0.29 us
  starting transfers between devices: 0.08 us -> 17.7 us
  Pallas kernels: 0 us -> 14.6 us
  between operations: 14.1 us -> 0.75 us
  matrix products: 10.8 us -> 0 us
    psum x2 -> x0, waiting for transfers between devices: 256 us -> none  [the longest x1 135 us: local(): lax.psum(lax.dot_general(slab, low_one, (((0,), (0,)), ((), ())), preferr...]
    another operation x5 -> x0, other arithmetic: 22.9 us -> none  [the longest x3 12.4 us: right_solve(): lower = jnp.linalg.cholesky(gram)]
    ppermute x0 -> x12, starting transfers between devices: none -> 17.7 us  [swap(): return lax.ppermute(array, AXES, pairs)]
    ppermute x0 -> x12, waiting for transfers between devices: none -> 16.7 us  [swap(): return lax.ppermute(array, AXES, pairs)]
    pallas_call x0 -> x4, Pallas kernels: none -> 14.6 us  [the longest x1 5.63 us: basis_call(): pl.pallas_call(functools.partial(basis_kernel, float(total_rows) ** 0.5),...]
    dot_general x3 -> x0, matrix products: 9.7 us -> none  [the longest x1 4.65 us: local(): lax.dot_general(slab, low_one, (((0,), (0,)), ((), ())), preferred_elemen...]
  transfers between devices with their start and end apart: 2 -> 12, of which waited for: 2 -> 7; matrix products, arithmetic and copies ran while one was open for 0% -> 1% of each run, Pallas kernels for 0% -> 10%
where the time goes in v1:
time: 53.9 us; the launch traced here: 53.7 us
  starting transfers between devices  17.7 us (33%)
  waiting for transfers between devices  16.7 us (31%)
  Pallas kernels  14.6 us (27%)
  local copies, waits for them, and re-layouts  3.57 us (7%)
  between operations  0.75 us (1%)
    ppermute x12, starting transfers between devices, swap(): return lax.ppermute(array, AXES, pairs)  17.7 us
    ppermute x12, waiting for transfers between devices, swap(): return lax.ppermute(array, AXES, pairs)  16.7 us
    pallas_call x1, Pallas kernels, basis_call(): pl.pallas_call(functools.partial(basis_kernel, float(total_rows) ** 0.5),...  5.63 us
    pallas_call x1, Pallas kernels, project_call(): pl.pallas_call(project_kernel, grid_spec=pltpu.PrefetchScalarGridSpec(num...  4.42 us
    pallas_call x1, Pallas kernels, sketch_call(): pl.pallas_call(sketch_kernel, grid=(width // block,), in_specs=[pl.BlockS...  3.66 us
    unnamed x4, local copies, waits for them, and re-layouts  3.55 us
  transfers between devices with their start and end apart: 12, of which 7 were waited for; matrix products, arithmetic and copies ran while one was open for 1% of the time, Pallas kernels for 10%

profile of v1, /device:TPU:0, one launch (start us, length us, event | category | flops | bytes accessed | tf_op | source)
XLA Modules:
  0.0 53.7 jit_solution(6021133488218729825)
XLA Ops:
  0.6 2.3 %copy-done = bf16[576,4096]{1,0:T(8,128)(2,1)S(1)} copy-done((bf16[576,4096]{1,0:T(8,128)(2,1)S(1)}, bf16[576,4096]{1,0:T(8,128)(2,1)}, u32[]{:S(2)}) %copy-start) | copy-done | bytes 4718616
  3.0 1.2 %copy-done.1 = bf16[4096,128]{1,0:T(8,128)(2,1)S(1)} copy-done((bf16[4096,128]{1,0:T(8,128)(2,1)S(1)}, bf16[4096,128]{1,0:T(8,128)(2,1)}, u32[]{:S(2)}) %copy-start.1) | copy-done | bytes 1048600
  4.2 3.7 %sketch_rows.1 = (f32[576,128]{1,0:T(8,128)S(1)}, bf16[256,576]{1,0:T(8,128)(2,1)S(1)}, f32[128,128]{1,0:T(8,128)S(1)}) custom-call(bf16[576,4096]{1,0:T(8,128)(2,1)S(1)} %copy-done, bf16[4096,128]{1,0:T(8,128)(2,1)S(1)} %copy-done.1), custom_call_target="tpu_custom_call" | custom-call | flops 603979776 | bytes 4718592 | tf_op jit(solution)/shard_map/sketch_rows/pallas_call | solution.py:45
  7.9 4.4 %project_rows.1 = (f32[2,2,2,4,64,128]{5,4,3,2,1,0:T(8,128)S(1)}, f32[2,2,2,4,64,128]{5,4,3,2,1,0:T(8,128)S(1)}) custom-call(s32[1]{0:T(128)} %bitcast.me_ref, bf16[256,576]{1,0:T(8,128)(2,1)S(1)} %get-tuple-element.13.split_ref, bf16[576,4096]{1,0:T(8,128)(2,1)S(1)} %copy-done), custom_call_target="tpu_custom_call" | custom-call | flops 1207959552 | bytes 4718592 | tf_op jit(solution)/shard_map/project_rows/pallas_call | solution.py:91
  12.3 0.6 %collective-permute-start.5 = (f32[2,2,2,4,64,128]{5,4,3,2,1,0:T(8,128)S(1)}, f32[2,2,2,4,64,128]{5,4,3,2,1,0:T(8,128)S(1)}, u32[]{:S(2)}, u32[]{:S(2)}) collective-permute-start(f32[2,2,2,4,64,128]{5,4,3,2,1,0:T(8,128)S(1)} %get-tuple-element.15), channel_id=1, source_target_pairs={{0,1},{1,0},{2,3},{3,2},{4,5},{5,4},{6,7},{7,6},{8,9},{9,8},{10,11... | collective-permute-start | bytes 3145736 | tf_op jit(solution)/shard_map/ppermute | solution.py:215
  12.9 2.3 %collective-permute-done = f32[128,128]{1,0:T(8,128)S(1)} collective-permute-done((f32[128,128]{1,0:T(8,128)S(1)}, f32[128,128]{1,0:T(8,128)S(1)}, u32[]{:S(2)}, u32[]{:S(2)}) %collective-permute-start) | collective-permute-done | bytes 65568 | tf_op jit(solution)/shard_map/ppermute | solution.py:215
  15.2 2.9 %collective-permute-start.1 = (f32[128,128]{1,0:T(8,128)S(1)}, f32[128,128]{1,0:T(8,128)S(1)}, u32[]{:S(2)}, u32[]{:S(2)}) collective-permute-start(f32[128,128]{1,0:T(8,128)S(1)} %add.74), channel_id=1, source_target_pairs={{0,2},{1,3},{2,0},{3,1},{4,6},{5,7},{6,4},{7,5},{8,10},{9,11},{10,... | collective-permute-start | bytes 196616 | tf_op jit(solution)/shard_map/ppermute | solution.py:215
  18.2 2.4 %collective-permute-done.1 = f32[128,128]{1,0:T(8,128)S(1)} collective-permute-done((f32[128,128]{1,0:T(8,128)S(1)}, f32[128,128]{1,0:T(8,128)S(1)}, u32[]{:S(2)}, u32[]{:S(2)}) %collective-permute-start.1) | collective-permute-done | bytes 65568 | tf_op jit(solution)/shard_map/ppermute | solution.py:215
  20.6 1.9 %collective-permute-start.2 = (f32[128,128]{1,0:T(8,128)S(1)}, f32[128,128]{1,0:T(8,128)S(1)}, u32[]{:S(2)}, u32[]{:S(2)}) collective-permute-start(f32[128,128]{1,0:T(8,128)S(1)} %add.75), channel_id=1, source_target_pairs={{0,4},{1,5},{2,6},{3,7},{4,0},{5,1},{6,2},{7,3},{8,12},{9,13},{10,... | collective-permute-start | bytes 196616 | tf_op jit(solution)/shard_map/ppermute | solution.py:215
  22.6 0.2 collective-permute-start.8
  22.8 2.0 %collective-permute-start.6 = (f32[2,4,64,128]{3,2,1,0:T(8,128)S(1)}, f32[2,4,64,128]{3,2,1,0:T(8,128)S(1)}, u32[]{:S(2)}, u32[]{:S(2)}) collective-permute-start(f32[2,4,64,128]{3,2,1,0:T(8,128)S(1)} %get-tuple-element.17), channel_id=1, source_target_pairs={{0,2},{1,3},{2,0},{3,1},{4,6},{5,7},{6,4},{7,5},{8,10},{9,11},{10,... | collective-permute-start | bytes 786440 | tf_op jit(solution)/shard_map/ppermute | solution.py:215
  24.8 0.8 %collective-permute-done.2 = f32[128,128]{1,0:T(8,128)S(1)} collective-permute-done((f32[128,128]{1,0:T(8,128)S(1)}, f32[128,128]{1,0:T(8,128)S(1)}, u32[]{:S(2)}, u32[]{:S(2)}) %collective-permute-start.2) | collective-permute-done | bytes 65568 | tf_op jit(solution)/shard_map/ppermute | solution.py:215
  25.6 2.0 %collective-permute-start.3 = (f32[128,128]{1,0:T(8,128)S(1)}, f32[128,128]{1,0:T(8,128)S(1)}, u32[]{:S(2)}, u32[]{:S(2)}) collective-permute-start(f32[128,128]{1,0:T(8,128)S(1)} %add.76), channel_id=1, source_target_pairs={{0,8},{1,9},{2,10},{3,11},{4,12},{5,13},{6,14},{7,15},{8,0},{9,1},... | collective-permute-start | bytes 196616 | tf_op jit(solution)/shard_map/ppermute | solution.py:215
  27.6 2.7 %collective-permute-done.8 = f32[2,4,64,128]{3,2,1,0:T(8,128)S(1)} collective-permute-done((f32[2,4,64,128]{3,2,1,0:T(8,128)S(1)}, f32[2,4,64,128]{3,2,1,0:T(8,128)S(1)}, u32[]{:S(2)}, u32[]{:S(2)}) %collective-permute-start.8) | collective-permute-done | bytes 262176 | tf_op jit(solution)/shard_map/ppermute | solution.py:215
  30.3 1.6 %collective-permute-start.9 = (f32[4,64,128]{2,1,0:T(8,128)S(1)}, f32[4,64,128]{2,1,0:T(8,128)S(1)}, u32[]{:S(2)}, u32[]{:S(2)}) collective-permute-start(f32[4,64,128]{2,1,0:T(8,128)S(1)} %fusion.3), channel_id=1, source_target_pairs={{0,2},{1,3},{2,0},{3,1},{4,6},{5,7},{6,4},{7,5},{8,10},{9,11},{10,... | collective-permute-start | bytes 393224 | tf_op jit(solution)/shard_map/ppermute | solution.py:215
  31.9 0.9 %collective-permute-start.7 = (f32[4,64,128]{2,1,0:T(8,128)S(1)}, f32[4,64,128]{2,1,0:T(8,128)S(1)}, u32[]{:S(2)}, u32[]{:S(2)}) collective-permute-start(f32[4,64,128]{2,1,0:T(8,128)S(1)} %fusion.6), channel_id=1, source_target_pairs={{0,4},{1,5},{2,6},{3,7},{4,0},{5,1},{6,2},{7,3},{8,12},{9,13},{10,... | collective-permute-start | bytes 393224 | tf_op jit(solution)/shard_map/ppermute | solution.py:215
  32.8 2.5 %collective-permute-done.9 = f32[4,64,128]{2,1,0:T(8,128)S(1)} collective-permute-done((f32[4,64,128]{2,1,0:T(8,128)S(1)}, f32[4,64,128]{2,1,0:T(8,128)S(1)}, u32[]{:S(2)}, u32[]{:S(2)}) %collective-permute-start.9) | collective-permute-done | bytes 131104 | tf_op jit(solution)/shard_map/ppermute | solution.py:215
  35.3 1.6 %collective-permute-done.7 = f32[4,64,128]{2,1,0:T(8,128)S(1)} collective-permute-done((f32[4,64,128]{2,1,0:T(8,128)S(1)}, f32[4,64,128]{2,1,0:T(8,128)S(1)}, u32[]{:S(2)}, u32[]{:S(2)}) %collective-permute-start.7) | collective-permute-done | bytes 131104 | tf_op jit(solution)/shard_map/ppermute | solution.py:215
  37.0 1.6 %collective-permute-start.10 = (f32[2,128,128]{2,1,0:T(8,128)S(1)}, f32[2,128,128]{2,1,0:T(8,128)S(1)}, u32[]{:S(2)}, u32[]{:S(2)}) collective-permute-start(f32[2,128,128]{2,1,0:T(8,128)S(1)} %slice_bitcast_fusion), channel_id=1, source_target_pairs={{0,8},{1,9},{2,10},{3,11},{4,12},{5,13},{6,14},{7,15},{8,0},{9,1},... | collective-permute-start | bytes 393224 | tf_op jit(solution)/shard_map/ppermute | solution.py:215
  38.6 2.6 %collective-permute-start.4 = (f32[128,128]{1,0:T(8,128)S(1)}, f32[128,128]{1,0:T(8,128)S(1)}, u32[]{:S(2)}, u32[]{:S(2)}) collective-permute-start(f32[128,128]{1,0:T(8,128)S(1)} %add.77), channel_id=1, source_target_pairs={{0,16},{1,17},{2,18},{3,19},{4,20},{5,21},{6,22},{7,23},{8,24},{9,... | collective-permute-start | bytes 196616 | tf_op jit(solution)/shard_map/ppermute | solution.py:215
  41.3 4.5 %collective-permute-done.4 = f32[128,128]{1,0:T(8,128)S(1)} collective-permute-done((f32[128,128]{1,0:T(8,128)S(1)}, f32[128,128]{1,0:T(8,128)S(1)}, u32[]{:S(2)}, u32[]{:S(2)}) %collective-permute-start.4) | collective-permute-done | bytes 65568 | tf_op jit(solution)/shard_map/ppermute | solution.py:215
  45.8 1.3 %collective-permute-start.11 = (f32[128,128]{1,0:T(8,128)S(1)}, f32[128,128]{1,0:T(8,128)S(1)}, u32[]{:S(2)}, u32[]{:S(2)}) collective-permute-start(f32[128,128]{1,0:T(8,128)S(1)} %slice_bitcast_fusion.6), channel_id=1, source_target_pairs={{0,16},{1,17},{2,18},{3,19},{4,20},{5,21},{6,22},{7,23},{8,24},{9,... | collective-permute-start | bytes 196616 | tf_op jit(solution)/shard_map/ppermute | solution.py:215
  47.1 5.6 %basis_rows.1 = (f32[128,128]{1,0:T(8,128)S(1)}, f32[576,128]{1,0:T(8,128)}) custom-call(f32[128,128]{1,0:T(8,128)S(1)} %add.78.gram_ref, f32[576,128]{1,0:T(8,128)S(1)} %get-tuple-element.10.first_ref), custom_call_target="tpu_custom_call" | custom-call | flops 4000000000 | bytes 589824 | tf_op jit(solution)/shard_map/basis_rows/pallas_call | solution.py:173
  52.8 0.9 %final_rows.1 = bf16[128,128]{1,0:T(8,128)(2,1)} custom-call(f32[128,128]{1,0:T(8,128)S(1)} %get-tuple-element.12.inverse_ref, f32[128,128]{1,0:T(8,128)S(1)} %fusion.9.sums_ref), custom_call_target="tpu_custom_call" | custom-call | tf_op jit(solution)/shard_map/final_rows/pallas_call | solution.py:196
  (24 shorter events, 0.4 us)
Async XLA Ops:
  0.6 2.3 %copy-start = (bf16[576,4096]{1,0:T(8,128)(2,1)S(1)}, bf16[576,4096]{1,0:T(8,128)(2,1)}, u32[]{:S(2)}) copy-start(bf16[576,4096]{1,0:T(8,128)(2,1)} %slab_ref.3) | copy-start | bytes 14155780
  3.0 1.2 %copy-start.1 = (bf16[4096,128]{1,0:T(8,128)(2,1)S(1)}, bf16[4096,128]{1,0:T(8,128)(2,1)}, u32[]{:S(2)}) copy-start(bf16[4096,128]{1,0:T(8,128)(2,1)} %sketch_ref.1) | copy-start | bytes 3145732
  12.3 10.2 %collective-permute-start.5 = (f32[2,2,2,4,64,128]{5,4,3,2,1,0:T(8,128)S(1)}, f32[2,2,2,4,64,128]{5,4,3,2,1,0:T(8,128)S(1)}, u32[]{:S(2)}, u32[]{:S(2)}) collective-permute-start(f32[2,2,2,4,64,128]{5,4,3,2,1,0:T(8,128)S(1)} %get-tuple-element.15), channel_id=1, source_target_pairs={{0,1},{1,0},{2,3},{3,2},{4,5},{5,4},{6,7},{7,6},{8,9},{9,8},{10,11... | collective-permute-start | bytes 3145736 | tf_op jit(solution)/shard_map/ppermute | solution.py:215
  12.9 2.4 %collective-permute-start = (f32[128,128]{1,0:T(8,128)S(1)}, f32[128,128]{1,0:T(8,128)S(1)}, u32[]{:S(2)}, u32[]{:S(2)}) collective-permute-start(f32[128,128]{1,0:T(8,128)S(1)} %get-tuple-element.9), channel_id=1, source_target_pairs={{0,1},{1,0},{2,3},{3,2},{4,5},{5,4},{6,7},{7,6},{8,9},{9,8},{10,11... | collective-permute-start | bytes 196616 | tf_op jit(solution)/shard_map/ppermute | solution.py:215
  15.2 5.3 %collective-permute-start.1 = (f32[128,128]{1,0:T(8,128)S(1)}, f32[128,128]{1,0:T(8,128)S(1)}, u32[]{:S(2)}, u32[]{:S(2)}) collective-permute-start(f32[128,128]{1,0:T(8,128)S(1)} %add.74), channel_id=1, source_target_pairs={{0,2},{1,3},{2,0},{3,1},{4,6},{5,7},{6,4},{7,5},{8,10},{9,11},{10,... | collective-permute-start | bytes 196616 | tf_op jit(solution)/shard_map/ppermute | solution.py:215
  20.6 5.0 %collective-permute-start.2 = (f32[128,128]{1,0:T(8,128)S(1)}, f32[128,128]{1,0:T(8,128)S(1)}, u32[]{:S(2)}, u32[]{:S(2)}) collective-permute-start(f32[128,128]{1,0:T(8,128)S(1)} %add.75), channel_id=1, source_target_pairs={{0,4},{1,5},{2,6},{3,7},{4,0},{5,1},{6,2},{7,3},{8,12},{9,13},{10,... | collective-permute-start | bytes 196616 | tf_op jit(solution)/shard_map/ppermute | solution.py:215
  22.6 7.7 %collective-permute-start.8 = (f32[2,4,64,128]{3,2,1,0:T(8,128)S(1)}, f32[2,4,64,128]{3,2,1,0:T(8,128)S(1)}, u32[]{:S(2)}, u32[]{:S(2)}) collective-permute-start(f32[2,4,64,128]{3,2,1,0:T(8,128)S(1)} %get-tuple-element.19), channel_id=1, source_target_pairs={{0,4},{1,5},{2,6},{3,7},{4,0},{5,1},{6,2},{7,3},{8,12},{9,13},{10,... | collective-permute-start | bytes 786440 | tf_op jit(solution)/shard_map/ppermute | solution.py:215
  22.8 9.0 %collective-permute-start.6 = (f32[2,4,64,128]{3,2,1,0:T(8,128)S(1)}, f32[2,4,64,128]{3,2,1,0:T(8,128)S(1)}, u32[]{:S(2)}, u32[]{:S(2)}) collective-permute-start(f32[2,4,64,128]{3,2,1,0:T(8,128)S(1)} %get-tuple-element.17), channel_id=1, source_target_pairs={{0,2},{1,3},{2,0},{3,1},{4,6},{5,7},{6,4},{7,5},{8,10},{9,11},{10,... | collective-permute-start | bytes 786440 | tf_op jit(solution)/shard_map/ppermute | solution.py:215
  25.6 13.0 %collective-permute-start.3 = (f32[128,128]{1,0:T(8,128)S(1)}, f32[128,128]{1,0:T(8,128)S(1)}, u32[]{:S(2)}, u32[]{:S(2)}) collective-permute-start(f32[128,128]{1,0:T(8,128)S(1)} %add.76), channel_id=1, source_target_pairs={{0,8},{1,9},{2,10},{3,11},{4,12},{5,13},{6,14},{7,15},{8,0},{9,1},... | collective-permute-start | bytes 196616 | tf_op jit(solution)/shard_map/ppermute | solution.py:215
  30.3 5.0 %collective-permute-start.9 = (f32[4,64,128]{2,1,0:T(8,128)S(1)}, f32[4,64,128]{2,1,0:T(8,128)S(1)}, u32[]{:S(2)}, u32[]{:S(2)}) collective-permute-start(f32[4,64,128]{2,1,0:T(8,128)S(1)} %fusion.3), channel_id=1, source_target_pairs={{0,2},{1,3},{2,0},{3,1},{4,6},{5,7},{6,4},{7,5},{8,10},{9,11},{10,... | collective-permute-start | bytes 393224 | tf_op jit(solution)/shard_map/ppermute | solution.py:215
  31.9 5.0 %collective-permute-start.7 = (f32[4,64,128]{2,1,0:T(8,128)S(1)}, f32[4,64,128]{2,1,0:T(8,128)S(1)}, u32[]{:S(2)}, u32[]{:S(2)}) collective-permute-start(f32[4,64,128]{2,1,0:T(8,128)S(1)} %fusion.6), channel_id=1, source_target_pairs={{0,4},{1,5},{2,6},{3,7},{4,0},{5,1},{6,2},{7,3},{8,12},{9,13},{10,... | collective-permute-start | bytes 393224 | tf_op jit(solution)/shard_map/ppermute | solution.py:215
  37.0 8.8 %collective-permute-start.10 = (f32[2,128,128]{2,1,0:T(8,128)S(1)}, f32[2,128,128]{2,1,0:T(8,128)S(1)}, u32[]{:S(2)}, u32[]{:S(2)}) collective-permute-start(f32[2,128,128]{2,1,0:T(8,128)S(1)} %slice_bitcast_fusion), channel_id=1, source_target_pairs={{0,8},{1,9},{2,10},{3,11},{4,12},{5,13},{6,14},{7,15},{8,0},{9,1},... | collective-permute-start | bytes 393224 | tf_op jit(solution)/shard_map/ppermute | solution.py:215
  38.6 7.1 %collective-permute-start.4 = (f32[128,128]{1,0:T(8,128)S(1)}, f32[128,128]{1,0:T(8,128)S(1)}, u32[]{:S(2)}, u32[]{:S(2)}) collective-permute-start(f32[128,128]{1,0:T(8,128)S(1)} %add.77), channel_id=1, source_target_pairs={{0,16},{1,17},{2,18},{3,19},{4,20},{5,21},{6,22},{7,23},{8,24},{9,... | collective-permute-start | bytes 196616 | tf_op jit(solution)/shard_map/ppermute | solution.py:215
  45.8 7.0 %collective-permute-start.11 = (f32[128,128]{1,0:T(8,128)S(1)}, f32[128,128]{1,0:T(8,128)S(1)}, u32[]{:S(2)}, u32[]{:S(2)}) collective-permute-start(f32[128,128]{1,0:T(8,128)S(1)} %slice_bitcast_fusion.6), channel_id=1, source_target_pairs={{0,16},{1,17},{2,18},{3,19},{4,20},{5,21},{6,22},{7,23},{8,24},{9,... | collective-permute-start | bytes 196616 | tf_op jit(solution)/shard_map/ppermute | solution.py:215

commit v2 on v1

--- a/solution.py
+++ b/solution.py
@@ -11,102 +11,91 @@
 HIGHEST = lax.Precision.HIGHEST
 LANES = 128
 VMEM_LIMIT = 40 * 1024 * 1024
-
-
-def sketch_kernel(slab_ref, sketch_ref, first_ref, split_ref, gram_ref, acc_ref):
-    step = pl.program_id(0)
-    part = jnp.dot(slab_ref[...], sketch_ref[...], preferred_element_type=jnp.float32)
-
-    @pl.when(step == 0)
-    def _():
-        acc_ref[...] = part
-
-    @pl.when(step > 0)
-    def _():
-        acc_ref[...] += part
-
-    @pl.when(step == pl.num_programs(0) - 1)
-    def _():
-        first = acc_ref[...]
-        first_ref[...] = first
-        gram_ref[...] = lax.dot_general(
-            first, first, (((0,), (0,)), ((), ())),
-            precision=HIGHEST, preferred_element_type=jnp.float32,
-        )
-        high = first.astype(jnp.bfloat16)
-        low = (first - high.astype(jnp.float32)).astype(jnp.bfloat16)
-        split_ref[...] = jnp.concatenate([high.T, low.T], axis=0)
-
-
-def sketch_call(slab, sketch):
+ROWS_VMEM = 40 * 1024 * 1024
+GRAM_BITS = 5
+
+
+CHUNKS = 4
+
+
+def rows_kernel(
+    me_ref, slab_hbm, sketch_hbm, first_ref, gram_ref, keep_ref, send_ref,
+    slab_ref, sketch_ref, split_ref, slab_sem, sketch_sem,
+):
+    rows, width = slab_ref.shape
+    rank = sketch_ref.shape[1]
+    step = width // CHUNKS
+    copies = []
+    for k in range(CHUNKS):
+        at = pl.ds(k * step, step)
+        copies.append((
+            pltpu.make_async_copy(sketch_hbm.at[at, :], sketch_ref.at[at, :], sketch_sem.at[k]),
+            pltpu.make_async_copy(slab_hbm.at[:, at], slab_ref.at[:, at], slab_sem.at[k]),
+        ))
+    for pair in copies:
+        for copy in pair:
+            copy.start()
+    for k in range(CHUNKS):
+        for copy in copies[k]:
+            copy.wait()
+        at = pl.ds(k * step, step)
+        part = jnp.dot(slab_ref[:, at], sketch_ref[at, :], preferred_element_type=jnp.float32)
+        if k == 0:
+            first_ref[...] = part
+        else:
+            first_ref[...] += part
+    first = first_ref[...]
+    turned = first.T
+    high = turned.astype(jnp.bfloat16)
+    split_ref[:rank] = high
+    split_ref[rank:] = (turned - high.astype(jnp.float32)).astype(jnp.bfloat16)
+    gram_ref[...] = jnp.dot(turned, first, precision=HIGHEST, preferred_element_type=jnp.float32)
+    odd = lax.rem(me_ref[0], 2) == 1
+    for q in range(width // (2 * LANES)):
+        at = pl.ds(q * 2 * LANES, 2 * LANES)
+        both = jnp.dot(split_ref[...], slab_ref[:, at], preferred_element_type=jnp.float32)
+        sums = both[:rank] + both[rank:]
+        even_part, odd_part = sums[:, :LANES], sums[:, LANES:]
+        keep_ref[q % 4, q // 4] = jnp.where(odd, odd_part, even_part)
+        send_ref[q % 4, q // 4] = jnp.where(odd, even_part, odd_part)
+
+
+def rows_call(owner, slab, sketch):
     rows, width = slab.shape
     rank = sketch.shape[1]
-    block = 512
+    blocks = (4, width // (8 * LANES), rank, LANES)
+    vmem = pl.BlockSpec(memory_space=pltpu.VMEM)
     return pl.pallas_call(
-        sketch_kernel,
-        grid=(width // block,),
+        rows_kernel,
         in_specs=[
-            pl.BlockSpec((rows, block), lambda k: (0, k)),
-            pl.BlockSpec((block, rank), lambda k: (k, 0)),
-        ],
-        out_specs=[
-            pl.BlockSpec((rows, rank), lambda k: (0, 0)),
-            pl.BlockSpec((2 * rank, rows), lambda k: (0, 0)),
-            pl.BlockSpec((rank, rank), lambda k: (0, 0)),
-        ],
+            pl.BlockSpec(memory_space=pltpu.SMEM),
+            pl.BlockSpec(memory_space=pltpu.HBM),
+            pl.BlockSpec(memory_space=pltpu.HBM),
+        ],
+        out_specs=[vmem] * 4,
         out_shape=[
             jax.ShapeDtypeStruct((rows, rank), jnp.float32),
-            jax.ShapeDtypeStruct((2 * rank, rows), jnp.bfloat16),
             jax.ShapeDtypeStruct((rank, rank), jnp.float32),
-        ],
-        scratch_shapes=[pltpu.VMEM((rows, rank), jnp.float32)],
-        compiler_params=pltpu.CompilerParams(vmem_limit_bytes=VMEM_LIMIT),
+            jax.ShapeDtypeStruct(blocks, jnp.float32),
+            jax.ShapeDtypeStruct(blocks, jnp.float32),
+        ],
+        scratch_shapes=[
+            pltpu.VMEM((rows, width), jnp.bfloat16),
+            pltpu.VMEM((width, rank), jnp.bfloat16),
+            pltpu.VMEM((2 * rank, rows), jnp.bfloat16),
+            pltpu.SemaphoreType.DMA((CHUNKS,)),
+            pltpu.SemaphoreType.DMA((CHUNKS,)),
+        ],
+        compiler_params=pltpu.CompilerParams(vmem_limit_bytes=ROWS_VMEM),
         cost_estimate=pl.CostEstimate(
-            flops=2 * rows * width * rank, bytes_accessed=rows * width * 2, transcendentals=0
-        ),
-        name="sketch_rows",
-    )(slab, sketch)
-
-
-def project_kernel(me_ref, split_ref, slab_ref, keep_ref, send_ref, block_ref):
-    rank = keep_ref.shape[0] * keep_ref.shape[4]
-    half = rank // 2
-    both = jnp.dot(split_ref[...], slab_ref[...], preferred_element_type=jnp.float32)
-    block_ref[...] = both[:rank] + both[rank:]
-    low = lax.rem(me_ref[0], 4)
-    for x in range(2):
-        for core, out in ((0, keep_ref), (1, send_ref)):
-            at = pl.multiple_of(lax.bitwise_xor(low, 2 * x + core) * LANES, LANES)
-            out[0, x, 0, 0] = block_ref[:half, pl.ds(at, LANES)]
-            out[1, x, 0, 0] = block_ref[half:, pl.ds(at, LANES)]
-
-
-def project_call(owner, split, slab):
-    rows, width = slab.shape
-    rank = split.shape[0] // 2
-    block = 4 * LANES
-    steps = width // block
-    out_block = pl.BlockSpec((2, 2, 1, 1, rank // 2, LANES), lambda q, me: (0, 0, q % 2, q // 2, 0, 0))
-    out_shape = jax.ShapeDtypeStruct((2, 2, 2, steps // 2, rank // 2, LANES), jnp.float32)
-    return pl.pallas_call(
-        project_kernel,
-        grid_spec=pltpu.PrefetchScalarGridSpec(
-            num_scalar_prefetch=1,
-            grid=(steps,),
-            in_specs=[
-                pl.BlockSpec((2 * rank, rows), lambda q, me: (0, 0)),
-                pl.BlockSpec((rows, block), lambda q, me: (0, lax.bitwise_xor(me[0] // 4, q))),
-            ],
-            out_specs=[out_block, out_block],
-            scratch_shapes=[pltpu.VMEM((rank, block), jnp.float32)],
-        ),
-        out_shape=[out_shape, out_shape],
-        compiler_params=pltpu.CompilerParams(vmem_limit_bytes=VMEM_LIMIT),
-        cost_estimate=pl.CostEstimate(
-            flops=4 * rows * width * rank, bytes_accessed=rows * width * 2, transcendentals=0
+            flops=6 * rows * width * rank, bytes_accessed=rows * width * 2, transcendentals=0
         ),
         name="project_rows",
-    )(owner, split, slab)
+    )(
+        owner,
+        pltpu.with_memory_space_constraint(slab, pltpu.HBM),
+        pltpu.with_memory_space_constraint(sketch, pltpu.HBM),
+    )
 
 
 def lane(block, at):
@@ -214,28 +203,30 @@
         pairs = [(i, i ^ (1 << bit)) for i in range(devices_all)]
         return lax.ppermute(array, AXES, pairs)
 
-    first, split, gram = sketch_call(slab, sketch)
+    def spread(array, shift, count):
+        mask = ((1 << count) - 1) << shift
+        groups = [
+            [base | (i << shift) for i in range(1 << count)]
+            for base in range(devices_all) if base & mask == 0
+        ]
+        return lax.all_to_all(
+            array, AXES, split_axis=0, concat_axis=0, axis_index_groups=groups, tiled=True
+        )
+
     owner = lax.shift_right_logical(me, low_bits).astype(jnp.int32).reshape(1)
-    keep, send = project_call(owner, split, slab)
-
-    for bit in range(bits):
-        gram = gram + swap(gram, bit)
+    first, gram, keep, send = rows_call(owner, slab, sketch)
+    rank = first.shape[1]
+
+    parts = 1 << GRAM_BITS
+    share = spread(gram, 0, GRAM_BITS).reshape(parts, rank // parts, rank).sum(axis=0)
+    for bit in range(GRAM_BITS, bits):
+        share = share + swap(share, bit)
+    gram = spread(jnp.tile(share, (parts, 1)), 0, GRAM_BITS)
     inverse, basis = basis_call(gram, first, total_rows)
 
-    got = swap(send, low_bits)
-    got_a = swap(keep[0, 1] + got[0, 1], low_bits + 1)
-    got_b = swap(keep[1, :, 1] + got[1, :, 1], low_bits + 2)
-    part_a = keep[0, 0] + got[0, 0]
-    part_b = keep[1, :, 0] + got[1, :, 0]
-    got_a2 = swap(part_a[1] + got_a[1], low_bits + 2)
-    got_b2 = swap(part_b[1] + got_b[1], low_bits + 1)
-    sums = jnp.concatenate(
-        [part_a[0] + got_a[0] + got_a2, part_b[0] + got_b[0] + got_b2], axis=1
-    )
-    bit = low_bits + 3
-    sums = sums.reshape(sums.shape[0] // 2, 2, *sums.shape[1:])
-    sums = sums[:, 0] + swap(sums[:, 1], bit)
-    sums = sums[0] + swap(sums[1], bit + 1)
+    kept = keep + swap(send, low_bits)
+    kept = spread(kept, low_bits + 1, 2).sum(axis=0)
+    sums = spread(kept, low_bits + 3, 2).sum(axis=0)
     for bit in reversed(range(low_bits)):
         half = sums.shape[1] // 2
         mine = lax.rem(lax.shift_right_logical(me, bit), 2) == 1

time: 53.9 us -> 65.3 us (1.21)
  waiting for transfers between devices: 16.7 us -> 30.9 us
  local copies, waits for them, and re-layouts: 3.57 us -> 0.64 us
  other arithmetic: 0.29 us -> 1.9 us
  Pallas kernels: 14.6 us -> 13.8 us
  starting transfers between devices: 17.7 us -> 17 us
    all_to_all x0 -> x4, waiting for transfers between devices: none -> 30.9 us  [spread(): lax.all_to_all(array, AXES, split_axis=0, concat_axis=0, axis_index_group...]
    ppermute x12 -> x1, starting transfers between devices: 17.7 us -> 0.52 us  [swap(): return lax.ppermute(array, AXES, pairs)]
    ppermute x12 -> x1, waiting for transfers between devices: 16.7 us -> 0.01 us  [swap(): return lax.ppermute(array, AXES, pairs)]
    all_to_all x0 -> x4, starting transfers between devices: none -> 16.4 us  [spread(): lax.all_to_all(array, AXES, split_axis=0, concat_axis=0, axis_index_group...]
    unnamed x4 -> x0, local copies, waits for them, and re-layouts: 3.55 us -> none
    reduce_sum x0 -> x3, other arithmetic: none -> 0.82 us  [the longest x1 0.76 us: local(): kept = spread(kept, low_bits + 1, 2).sum(axis=0)]
    add x13 -> x1, other arithmetic: 0.27 us -> 1.08 us  [local(): kept = keep + swap(send, low_bits)]
    pallas_call x2 -> x1, Pallas kernels: 8.08 us -> 7.32 us  [rows_call(): pl.pallas_call(rows_kernel, in_specs=[pl.BlockSpec(memory_space=pltpu.SME...]
  transfers between devices with their start and end apart: 12 -> 5, of which waited for: 7 -> 4; matrix products, arithmetic and copies ran while one was open for 1% -> 3% of each run, Pallas kernels for 10% -> 9%
where the time goes in v2:
time: 65.3 us; the launch traced here: 64.9 us
  waiting for transfers between devices  30.9 us (47%)
  starting transfers between devices  17 us (26%)
  Pallas kernels  13.8 us (21%)
  other arithmetic  1.9 us (3%)
  between operations  0.69 us (1%)
    all_to_all x4, waiting for transfers between devices, spread(): lax.all_to_all(array, AXES, split_axis=0, concat_axis=0, axis_index_group...  30.9 us
    all_to_all x4, starting transfers between devices, spread(): lax.all_to_all(array, AXES, split_axis=0, concat_axis=0, axis_index_group...  16.4 us
    pallas_call x1, Pallas kernels, rows_call(): pl.pallas_call(rows_kernel, in_specs=[pl.BlockSpec(memory_space=pltpu.SME...  7.32 us
    pallas_call x1, Pallas kernels, basis_call(): pl.pallas_call(functools.partial(basis_kernel, float(total_rows) ** 0.5),...  5.62 us
  transfers between devices with their start and end apart: 5, of which 4 were waited for; matrix products, arithmetic and copies ran while one was open for 3% of the time, Pallas kernels for 9%

profile of v2, /device:TPU:0, one launch (start us, length us, event | category | flops | bytes accessed | tf_op | source)
XLA Modules:
  0.0 64.9 jit_solution(6166413069194622562)
XLA Ops:
  0.6 7.3 %project_rows.1 = (f32[576,128]{1,0:T(8,128)S(1)}, f32[128,128]{1,0:T(8,128)}, f32[4,4,128,128]{3,2,1,0:T(8,128)S(1)}, f32[4,4,128,128]{3,2,1,0:T(8,128)S(1)}) custom-call(s32[1]{0:T(128)} %bitcast.me_ref, bf16[576,4096]{1,0:T(8,128)(2,1)} %slab_hbm.1, bf16[4096,128]{1,0:T(8,128)(2,1)} %sketch_hbm.1), custom_call_target="tpu_custom_call" | custom-call | flops 1811939328 | bytes 4718592 | tf_op jit(solution)/shard_map/project_rows/pallas_call | solution.py:68
  8.0 0.5 collective-permute-start
  8.5 7.0 %all-to-all-start = ((f32[32,4,128]{2,1,0:T(4,128)}), f32[32,4,128]{2,1,0:T(4,128)S(1)}, u32[]{:S(2)}, u32[]{:S(2)}) async-start(f32[32,4,128]{2,1,0:T(4,128)} %bitcast.1), calls=%async_computation | async-start | bytes 131072 | tf_op jit(solution)/shard_map/all_to_all | solution.py:212
  15.4 0.0 collective-permute-done
  15.5 1.1 %add.7 = f32[4,4,128,128]{3,2,1,0:T(8,128)} add(f32[4,4,128,128]{3,2,1,0:T(8,128)S(1)} %get-tuple-element.12, f32[4,4,128,128]{3,2,1,0:T(8,128)S(1)} %collective-permute-done) | non-fusion elementwise | flops 262144 | bytes 3145728 | tf_op jit(solution)/shard_map/add | solution.py:227
  16.5 6.3 %all-to-all-done = f32[32,4,128]{2,1,0:T(4,128)S(1)} async-done(((f32[32,4,128]{2,1,0:T(4,128)}), f32[32,4,128]{2,1,0:T(4,128)S(1)}, u32[]{:S(2)}, u32[]{:S(2)}) %all-to-all-start) | async-done | bytes 65568 | tf_op jit(solution)/shard_map/all_to_all | solution.py:212
  22.9 3.5 %all-to-all-start.2 = ((f32[4,4,128,128]{3,2,1,0:T(8,128)}), f32[4,4,128,128]{3,2,1,0:T(8,128)S(1)}, u32[]{:S(2)}, u32[]{:S(2)}) async-start(f32[4,4,128,128]{3,2,1,0:T(8,128)} %add.7), calls=%async_computation.2 | async-start | bytes 2097152 | tf_op jit(solution)/shard_map/all_to_all | solution.py:212
  26.4 14.1 %all-to-all-done.2 = f32[4,4,128,128]{3,2,1,0:T(8,128)S(1)} async-done(((f32[4,4,128,128]{3,2,1,0:T(8,128)}), f32[4,4,128,128]{3,2,1,0:T(8,128)S(1)}, u32[]{:S(2)}, u32[]{:S(2)}) %all-to-all-start.2) | async-done | bytes 1048608 | tf_op jit(solution)/shard_map/all_to_all | solution.py:212
  40.5 0.6 tile.2
  41.2 2.6 %all-to-all-start.1 = ((f32[32,4,128]{2,1,0:T(4,128)}), f32[32,4,128]{2,1,0:T(4,128)S(1)}, u32[]{:S(2)}, u32[]{:S(2)}) async-start(f32[32,4,128]{2,1,0:T(4,128)} %tile.2), calls=%async_computation.1 | async-start | bytes 131072 | tf_op jit(solution)/shard_map/all_to_all | solution.py:212
  43.8 0.8 %reduce_sum.28 = f32[4,128,128]{2,1,0:T(8,128)} reduce(f32[4,4,128,128]{3,2,1,0:T(8,128)S(1)} %all-to-all-done.2, f32[]{:T(128)} %constant.14.clone.1), dimensions={0}, to_apply=%region_1.0 | reduce | flops 196608 | bytes 1310724 | tf_op jit(solution)/shard_map/reduce_sum | solution.py:228
  44.5 6.7 %all-to-all-done.1 = f32[32,4,128]{2,1,0:T(4,128)S(1)} async-done(((f32[32,4,128]{2,1,0:T(4,128)}), f32[32,4,128]{2,1,0:T(4,128)S(1)}, u32[]{:S(2)}, u32[]{:S(2)}) %all-to-all-start.1) | async-done | bytes 65568 | tf_op jit(solution)/shard_map/all_to_all | solution.py:212
  51.2 3.4 %all-to-all-start.3 = ((f32[4,128,128]{2,1,0:T(8,128)}), f32[4,128,128]{2,1,0:T(8,128)S(1)}, u32[]{:S(2)}, u32[]{:S(2)}) async-start(f32[4,128,128]{2,1,0:T(8,128)} %reduce_sum.28), calls=%async_computation.3 | async-start | bytes 524288 | tf_op jit(solution)/shard_map/all_to_all | solution.py:212
  54.6 5.6 %basis_rows.1 = (f32[128,128]{1,0:T(8,128)S(1)}, f32[576,128]{1,0:T(8,128)}) custom-call(f32[128,128]{1,0:T(8,128)S(1)} %bitcast.3, f32[576,128]{1,0:T(8,128)S(1)} %get-tuple-element.9.first_ref), custom_call_target="tpu_custom_call" | custom-call | flops 4000000000 | bytes 589824 | tf_op jit(solution)/shard_map/basis_rows/pallas_call | solution.py:162
  60.2 3.8 %all-to-all-done.3 = f32[4,128,128]{2,1,0:T(8,128)S(1)} async-done(((f32[4,128,128]{2,1,0:T(8,128)}), f32[4,128,128]{2,1,0:T(8,128)S(1)}, u32[]{:S(2)}, u32[]{:S(2)}) %all-to-all-start.3) | async-done | bytes 262176 | tf_op jit(solution)/shard_map/all_to_all | solution.py:212
  64.0 0.9 %final_rows.1 = bf16[128,128]{1,0:T(8,128)(2,1)} custom-call(f32[128,128]{1,0:T(8,128)S(1)} %get-tuple-element.11.inverse_ref, f32[128,128]{1,0:T(8,128)S(1)} %reduce_sum.29.sums_ref), custom_call_target="tpu_custom_call" | custom-call | tf_op jit(solution)/shard_map/final_rows/pallas_call | solution.py:185
  (2 shorter events, 0.1 us)
Async XLA Ops:
  8.0 7.5 %collective-permute-start = (f32[4,4,128,128]{3,2,1,0:T(8,128)S(1)}, f32[4,4,128,128]{3,2,1,0:T(8,128)S(1)}, u32[]{:S(2)}, u32[]{:S(2)}) collective-permute-start(f32[4,4,128,128]{3,2,1,0:T(8,128)S(1)} %get-tuple-element.13), channel_id=1, source_target_pairs={{0,1},{1,0},{2,3},{3,2},{4,5},{5,4},{6,7},{7,6},{8,9},{9,8},{10,11... | collective-permute-start | bytes 3145736 | tf_op jit(solution)/shard_map/ppermute | solution.py:204
  8.5 14.4 %all-to-all-start = ((f32[32,4,128]{2,1,0:T(4,128)}), f32[32,4,128]{2,1,0:T(4,128)S(1)}, u32[]{:S(2)}, u32[]{:S(2)}) async-start(f32[32,4,128]{2,1,0:T(4,128)} %bitcast.1), calls=%async_computation | async-start | bytes 131072 | tf_op jit(solution)/shard_map/all_to_all | solution.py:212
  22.9 17.7 %all-to-all-start.2 = ((f32[4,4,128,128]{3,2,1,0:T(8,128)}), f32[4,4,128,128]{3,2,1,0:T(8,128)S(1)}, u32[]{:S(2)}, u32[]{:S(2)}) async-start(f32[4,4,128,128]{3,2,1,0:T(8,128)} %add.7), calls=%async_computation.2 | async-start | bytes 2097152 | tf_op jit(solution)/shard_map/all_to_all | solution.py:212
  41.2 10.0 %all-to-all-start.1 = ((f32[32,4,128]{2,1,0:T(4,128)}), f32[32,4,128]{2,1,0:T(4,128)S(1)}, u32[]{:S(2)}, u32[]{:S(2)}) async-start(f32[32,4,128]{2,1,0:T(4,128)} %tile.2), calls=%async_computation.1 | async-start | bytes 131072 | tf_op jit(solution)/shard_map/all_to_all | solution.py:212
  51.2 12.8 %all-to-all-start.3 = ((f32[4,128,128]{2,1,0:T(8,128)}), f32[4,128,128]{2,1,0:T(8,128)S(1)}, u32[]{:S(2)}, u32[]{:S(2)}) async-start(f32[4,128,128]{2,1,0:T(8,128)} %reduce_sum.28), calls=%async_computation.3 | async-start | bytes 524288 | tf_op jit(solution)/shard_map/all_to_all | solution.py:212

commit v3 on v2

--- a/solution.py
+++ b/solution.py
@@ -11,19 +11,15 @@
 HIGHEST = lax.Precision.HIGHEST
 LANES = 128
 VMEM_LIMIT = 40 * 1024 * 1024
-ROWS_VMEM = 40 * 1024 * 1024
-GRAM_BITS = 5
 
 
 CHUNKS = 4
 
 
-def rows_kernel(
-    me_ref, slab_hbm, sketch_hbm, first_ref, gram_ref, keep_ref, send_ref,
-    slab_ref, sketch_ref, split_ref, slab_sem, sketch_sem,
+def sketch_kernel(
+    slab_hbm, sketch_hbm, slab_ref, first_ref, split_ref, gram_ref, sketch_ref, slab_sem, sketch_sem
 ):
-    rows, width = slab_ref.shape
-    rank = sketch_ref.shape[1]
+    width, rank = sketch_ref.shape
     step = width // CHUNKS
     copies = []
     for k in range(CHUNKS):
@@ -46,56 +42,84 @@
             first_ref[...] += part
     first = first_ref[...]
     turned = first.T
+    gram_ref[...] = jnp.dot(turned, first, precision=HIGHEST, preferred_element_type=jnp.float32)
     high = turned.astype(jnp.bfloat16)
     split_ref[:rank] = high
     split_ref[rank:] = (turned - high.astype(jnp.float32)).astype(jnp.bfloat16)
-    gram_ref[...] = jnp.dot(turned, first, precision=HIGHEST, preferred_element_type=jnp.float32)
-    odd = lax.rem(me_ref[0], 2) == 1
-    for q in range(width // (2 * LANES)):
-        at = pl.ds(q * 2 * LANES, 2 * LANES)
-        both = jnp.dot(split_ref[...], slab_ref[:, at], preferred_element_type=jnp.float32)
-        sums = both[:rank] + both[rank:]
-        even_part, odd_part = sums[:, :LANES], sums[:, LANES:]
-        keep_ref[q % 4, q // 4] = jnp.where(odd, odd_part, even_part)
-        send_ref[q % 4, q // 4] = jnp.where(odd, even_part, odd_part)
-
-
-def rows_call(owner, slab, sketch):
+
+
+def sketch_call(slab, sketch):
     rows, width = slab.shape
     rank = sketch.shape[1]
-    blocks = (4, width // (8 * LANES), rank, LANES)
-    vmem = pl.BlockSpec(memory_space=pltpu.VMEM)
-    return pl.pallas_call(
-        rows_kernel,
-        in_specs=[
-            pl.BlockSpec(memory_space=pltpu.SMEM),
-            pl.BlockSpec(memory_space=pltpu.HBM),
-            pl.BlockSpec(memory_space=pltpu.HBM),
-        ],
-        out_specs=[vmem] * 4,
+    return pl.pallas_call(
+        sketch_kernel,
+        in_specs=[pl.BlockSpec(memory_space=pltpu.HBM)] * 2,
+        out_specs=[pl.BlockSpec(memory_space=pltpu.VMEM)] * 4,
         out_shape=[
+            jax.ShapeDtypeStruct((rows, width), jnp.bfloat16),
             jax.ShapeDtypeStruct((rows, rank), jnp.float32),
+            jax.ShapeDtypeStruct((2 * rank, rows), jnp.bfloat16),
             jax.ShapeDtypeStruct((rank, rank), jnp.float32),
-            jax.ShapeDtypeStruct(blocks, jnp.float32),
-            jax.ShapeDtypeStruct(blocks, jnp.float32),
         ],
         scratch_shapes=[
-            pltpu.VMEM((rows, width), jnp.bfloat16),
             pltpu.VMEM((width, rank), jnp.bfloat16),
-            pltpu.VMEM((2 * rank, rows), jnp.bfloat16),
             pltpu.SemaphoreType.DMA((CHUNKS,)),
             pltpu.SemaphoreType.DMA((CHUNKS,)),
         ],
-        compiler_params=pltpu.CompilerParams(vmem_limit_bytes=ROWS_VMEM),
+        compiler_params=pltpu.CompilerParams(vmem_limit_bytes=VMEM_LIMIT),
         cost_estimate=pl.CostEstimate(
-            flops=6 * rows * width * rank, bytes_accessed=rows * width * 2, transcendentals=0
+            flops=2 * rows * width * rank, bytes_accessed=rows * width * 2, transcendentals=0
         ),
-        name="project_rows",
+        name="sketch_rows",
     )(
-        owner,
         pltpu.with_memory_space_constraint(slab, pltpu.HBM),
         pltpu.with_memory_space_constraint(sketch, pltpu.HBM),
     )
+
+
+def project_kernel(sibling, owner_ref, split_ref, slab_ref, out_ref):
+    rank = out_ref.shape[1]
+    owner = owner_ref[0]
+    core = lax.bitwise_and(owner, 1)
+    wanted = lax.bitwise_xor(core, sibling)
+    mine = lax.shift_right_logical(owner, 1)
+
+    def columns(q):
+        at = pl.multiple_of((2 * q + wanted) * LANES, LANES)
+        return slab_ref[:, pl.ds(at, LANES)]
+
+    def place(q):
+        away = lax.bitwise_xor(mine, q)
+        bit = [lax.bitwise_and(lax.shift_right_logical(away, i), 1) for i in range(4)]
+        straight = 8 * bit[0] + 4 * bit[1] + 2 * bit[2] + bit[3]
+        turned = 8 * bit[1] + 4 * bit[0] + 2 * bit[3] + bit[2]
+        return jnp.where(wanted == 0, straight, turned)
+
+    for q in range(0, out_ref.shape[0], 2):
+        both = jnp.dot(
+            split_ref[...], jnp.concatenate([columns(q), columns(q + 1)], axis=1),
+            preferred_element_type=jnp.float32,
+        )
+        sums = both[:rank] + both[rank:]
+        out_ref[place(q)] = sums[:, :LANES]
+        out_ref[place(q + 1)] = sums[:, LANES:]
+
+
+def project_call(owner, split, slab, sibling):
+    rows, width = slab.shape
+    rank = split.shape[0] // 2
+    vmem = pl.BlockSpec(memory_space=pltpu.VMEM)
+    return pl.pallas_call(
+        functools.partial(project_kernel, sibling),
+        in_specs=[pl.BlockSpec(memory_space=pltpu.SMEM), vmem, vmem],
+        out_specs=vmem,
+        out_shape=jax.ShapeDtypeStruct((width // (2 * LANES), rank, LANES), jnp.float32),
+        compiler_params=pltpu.CompilerParams(vmem_limit_bytes=VMEM_LIMIT),
+        cost_estimate=pl.CostEstimate(
+            flops=2 * rows * width * rank, bytes_accessed=rows * width, transcendentals=0
+        ),
+        name="project_sibling" if sibling else "project_own",
+    )(owner, split, slab)
 
 
 def lane(block, at):
@@ -203,30 +227,28 @@
         pairs = [(i, i ^ (1 << bit)) for i in range(devices_all)]
         return lax.ppermute(array, AXES, pairs)
 
-    def spread(array, shift, count):
-        mask = ((1 << count) - 1) << shift
-        groups = [
-            [base | (i << shift) for i in range(1 << count)]
-            for base in range(devices_all) if base & mask == 0
-        ]
-        return lax.all_to_all(
-            array, AXES, split_axis=0, concat_axis=0, axis_index_groups=groups, tiled=True
-        )
+    def exchange(array, bit, other):
+        pairs = [(i, i ^ (1 << (other if (i >> low_bits) & 1 else bit))) for i in range(devices_all)]
+        return lax.ppermute(array, AXES, pairs)
+
+    core, x, y, z, zz = range(low_bits, low_bits + 5)
+    rounds = [(core, core), (x, y), (y, x), (z, zz), (zz, z)]
 
     owner = lax.shift_right_logical(me, low_bits).astype(jnp.int32).reshape(1)
-    first, gram, keep, send = rows_call(owner, slab, sketch)
-    rank = first.shape[1]
-
-    parts = 1 << GRAM_BITS
-    share = spread(gram, 0, GRAM_BITS).reshape(parts, rank // parts, rank).sum(axis=0)
-    for bit in range(GRAM_BITS, bits):
-        share = share + swap(share, bit)
-    gram = spread(jnp.tile(share, (parts, 1)), 0, GRAM_BITS)
+    slab_near, first, split, gram = sketch_call(slab, sketch)
+    gram = gram + exchange(gram, *rounds[0])
+    got = exchange(project_call(owner, split, slab_near, 1), *rounds[0])
+    sums = project_call(owner, split, slab_near, 0)
+    for pair in rounds[1:]:
+        gram = gram + exchange(gram, *pair)
+        sums = sums + got
+        half = sums.shape[0] // 2
+        got = exchange(sums[half:], *pair)
+        sums = sums[:half]
+    sums = (sums + got)[0]
+    for bit in range(low_bits):
+        gram = gram + swap(gram, bit)
     inverse, basis = basis_call(gram, first, total_rows)
-
-    kept = keep + swap(send, low_bits)
-    kept = spread(kept, low_bits + 1, 2).sum(axis=0)
-    sums = spread(kept, low_bits + 3, 2).sum(axis=0)
     for bit in reversed(range(low_bits)):
         half = sums.shape[1] // 2
         mine = lax.rem(lax.shift_right_logical(me, bit), 2) == 1

time: 65.3 us -> 51.1 us (0.78)
  waiting for transfers between devices: 30.9 us -> 20.8 us
  other arithmetic: 1.9 us -> 0.34 us
  starting transfers between devices: 17 us -> 15.6 us
    all_to_all x4 -> x0, waiting for transfers between devices: 30.9 us -> none  [spread(): lax.all_to_all(array, AXES, split_axis=0, concat_axis=0, axis_index_group...]
    ppermute x1 -> x10, waiting for transfers between devices: 0.01 us -> 20.8 us  [exchange(): return lax.ppermute(array, AXES, pairs)]
    all_to_all x4 -> x0, starting transfers between devices: 16.4 us -> none  [spread(): lax.all_to_all(array, AXES, split_axis=0, concat_axis=0, axis_index_group...]
    ppermute x1 -> x10, starting transfers between devices: 0.52 us -> 15.6 us  [exchange(): return lax.ppermute(array, AXES, pairs)]
    reduce_sum x3 -> x0, other arithmetic: 0.82 us -> none  [the longest x1 0.76 us: local(): kept = spread(kept, low_bits + 1, 2).sum(axis=0)]
    add x1 -> x9, other arithmetic: 1.08 us -> 0.33 us  [the longest x4 0.28 us: local(): sums = sums + got]
    pallas_call x1 -> x3, Pallas kernels: 7.32 us -> 6.86 us  [the longest x1 4.58 us: sketch_call(): pl.pallas_call(sketch_kernel, in_specs=[pl.BlockSpec(memory_space=pltpu.H...]
  transfers between devices with their start and end apart: 5 -> 10, of which waited for: 4 -> 7; matrix products, arithmetic and copies ran while one was open for 3% -> 0% of each run, Pallas kernels for 9% -> 13%
where the time goes in v3:
time: 51.1 us; the launch traced here: 51 us
  waiting for transfers between devices  20.8 us (41%)
  starting transfers between devices  15.6 us (31%)
  Pallas kernels  13.4 us (26%)
  between operations  0.75 us (1%)
    ppermute x10, waiting for transfers between devices, exchange(): return lax.ppermute(array, AXES, pairs)  20.8 us
    ppermute x10, starting transfers between devices, exchange(): return lax.ppermute(array, AXES, pairs)  15.6 us
    pallas_call x1, Pallas kernels, basis_call(): pl.pallas_call(functools.partial(basis_kernel, float(total_rows) ** 0.5),...  5.62 us
    pallas_call x1, Pallas kernels, sketch_call(): pl.pallas_call(sketch_kernel, in_specs=[pl.BlockSpec(memory_space=pltpu.H...  4.58 us
    pallas_call x2, Pallas kernels, project_call(): pl.pallas_call(functools.partial(project_kernel, sibling), in_specs=[pl.B...  2.28 us
  transfers between devices with their start and end apart: 10, of which 7 were waited for; matrix products, arithmetic and copies ran while one was open for 0% of the time, Pallas kernels for 13%

profile of v3, /device:TPU:0, one launch (start us, length us, event | category | flops | bytes accessed | tf_op | source)
XLA Modules:
  0.0 51.0 jit_solution(10924314830960498006)
XLA Ops:
  0.6 4.6 %sketch_rows.1 = (bf16[576,4096]{1,0:T(8,128)(2,1)S(1)}, f32[576,128]{1,0:T(8,128)S(1)}, bf16[256,576]{1,0:T(8,128)(2,1)S(1)}, f32[128,128]{1,0:T(8,128)S(1)}) custom-call(bf16[576,4096]{1,0:T(8,128)(2,1)} %slab_hbm.1, bf16[4096,128]{1,0:T(8,128)(2,1)} %sketch_hbm.1), custom_call_target="tpu_custom_call" | custom-call | flops 603979776 | bytes 4718592 | tf_op jit(solution)/shard_map/sketch_rows/pallas_call | solution.py:54
  5.2 1.1 %project_sibling.1 = f32[16,128,128]{2,1,0:T(8,128)S(1)} custom-call(s32[1]{0:T(128)} %bitcast.owner_ref, bf16[256,576]{1,0:T(8,128)(2,1)S(1)} %get-tuple-element.12.split_ref, bf16[576,4096]{1,0:T(8,128)(2,1)S(1)} %get-tuple-element.13.slab_ref), custom_call_target="tpu_custom_call" | custom-call | flops 603979776 | bytes 2359296 | tf_op jit(solution)/shard_map/project_sibling/pallas_call | solution.py:112
  6.4 0.5 %collective-permute-start.5 = (f32[16,128,128]{2,1,0:T(8,128)S(1)}, f32[16,128,128]{2,1,0:T(8,128)S(1)}, u32[]{:S(2)}, u32[]{:S(2)}) collective-permute-start(f32[16,128,128]{2,1,0:T(8,128)S(1)} %project_sibling.1), channel_id=1, source_target_pairs={{0,1},{1,0},{2,3},{3,2},{4,5},{5,4},{6,7},{7,6},{8,9},{9,8},{10,11... | collective-permute-start | bytes 3145736 | tf_op jit(solution)/shard_map/ppermute | solution.py:232
  6.9 1.1 %project_own.1 = f32[16,128,128]{2,1,0:T(8,128)S(1)} custom-call(s32[1]{0:T(128)} %bitcast.owner_ref, bf16[256,576]{1,0:T(8,128)(2,1)S(1)} %get-tuple-element.12.split_ref, bf16[576,4096]{1,0:T(8,128)(2,1)S(1)} %get-tuple-element.13.slab_ref), custom_call_target="tpu_custom_call" | custom-call | flops 603979776 | bytes 2359296 | tf_op jit(solution)/shard_map/project_own/pallas_call | solution.py:112
  8.0 1.1 %collective-permute-done.5 = f32[16,128,128]{2,1,0:T(8,128)S(1)} collective-permute-done((f32[16,128,128]{2,1,0:T(8,128)S(1)}, f32[16,128,128]{2,1,0:T(8,128)S(1)}, u32[]{:S(2)}, u32[]{:S(2)}) %collective-permute-start.5) | collective-permute-done | bytes 1048608 | tf_op jit(solution)/shard_map/ppermute | solution.py:232
  9.2 0.1 add.39
  9.4 2.9 %collective-permute-start.6 = (f32[8,128,128]{2,1,0:T(8,128)S(1)}, f32[8,128,128]{2,1,0:T(8,128)S(1)}, u32[]{:S(2)}, u32[]{:S(2)}) collective-permute-start(f32[8,128,128]{2,1,0:T(8,128)S(1)} %slice.33), channel_id=1, source_target_pairs={{0,2},{1,5},{2,0},{3,7},{4,6},{5,1},{6,4},{7,3},{8,10},{9,13},{10,... | collective-permute-start | bytes 1572872 | tf_op jit(solution)/shard_map/ppermute | solution.py:232
  12.3 7.2 %collective-permute-done.6 = f32[8,128,128]{2,1,0:T(8,128)S(1)} collective-permute-done((f32[8,128,128]{2,1,0:T(8,128)S(1)}, f32[8,128,128]{2,1,0:T(8,128)S(1)}, u32[]{:S(2)}, u32[]{:S(2)}) %collective-permute-start.6) | collective-permute-done | bytes 524320 | tf_op jit(solution)/shard_map/ppermute | solution.py:232
  19.5 0.1 slice_add_fusion
  19.6 2.1 %collective-permute-start.7 = (f32[4,128,128]{2,1,0:T(8,128)S(1)}, f32[4,128,128]{2,1,0:T(8,128)S(1)}, u32[]{:S(2)}, u32[]{:S(2)}) collective-permute-start(f32[4,128,128]{2,1,0:T(8,128)S(1)} %slice.35), channel_id=1, source_target_pairs={{0,4},{1,3},{2,6},{3,1},{4,0},{5,7},{6,2},{7,5},{8,12},{9,11},{10,... | collective-permute-start | bytes 786440 | tf_op jit(solution)/shard_map/ppermute | solution.py:232
  21.7 1.3 %collective-permute-done = f32[128,128]{1,0:T(8,128)S(1)} collective-permute-done((f32[128,128]{1,0:T(8,128)S(1)}, f32[128,128]{1,0:T(8,128)S(1)}, u32[]{:S(2)}, u32[]{:S(2)}) %collective-permute-start) | collective-permute-done | bytes 65568 | tf_op jit(solution)/shard_map/ppermute | solution.py:232
  23.0 1.6 %collective-permute-start.1 = (f32[128,128]{1,0:T(8,128)S(1)}, f32[128,128]{1,0:T(8,128)S(1)}, u32[]{:S(2)}, u32[]{:S(2)}) collective-permute-start(f32[128,128]{1,0:T(8,128)S(1)} %add.33), channel_id=1, source_target_pairs={{0,2},{1,5},{2,0},{3,7},{4,6},{5,1},{6,4},{7,3},{8,10},{9,13},{10,... | collective-permute-start | bytes 196616 | tf_op jit(solution)/shard_map/ppermute | solution.py:232
  24.5 2.8 %collective-permute-done.1 = f32[128,128]{1,0:T(8,128)S(1)} collective-permute-done((f32[128,128]{1,0:T(8,128)S(1)}, f32[128,128]{1,0:T(8,128)S(1)}, u32[]{:S(2)}, u32[]{:S(2)}) %collective-permute-start.1) | collective-permute-done | bytes 65568 | tf_op jit(solution)/shard_map/ppermute | solution.py:232
  27.3 0.2 collective-permute-start.2
  27.5 4.1 %collective-permute-done.2 = f32[128,128]{1,0:T(8,128)S(1)} collective-permute-done((f32[128,128]{1,0:T(8,128)S(1)}, f32[128,128]{1,0:T(8,128)S(1)}, u32[]{:S(2)}, u32[]{:S(2)}) %collective-permute-start.2) | collective-permute-done | bytes 65568 | tf_op jit(solution)/shard_map/ppermute | solution.py:232
  31.6 1.7 %collective-permute-start.3 = (f32[128,128]{1,0:T(8,128)S(1)}, f32[128,128]{1,0:T(8,128)S(1)}, u32[]{:S(2)}, u32[]{:S(2)}) collective-permute-start(f32[128,128]{1,0:T(8,128)S(1)} %add.35), channel_id=1, source_target_pairs={{0,8},{1,17},{2,10},{3,19},{4,12},{5,21},{6,14},{7,23},{8,0},{9,25... | collective-permute-start | bytes 196616 | tf_op jit(solution)/shard_map/ppermute | solution.py:232
  33.3 0.0 collective-permute-done.7
  33.4 0.5 collective-permute-start.8
  33.9 2.1 %collective-permute-done.3 = f32[128,128]{1,0:T(8,128)S(1)} collective-permute-done((f32[128,128]{1,0:T(8,128)S(1)}, f32[128,128]{1,0:T(8,128)S(1)}, u32[]{:S(2)}, u32[]{:S(2)}) %collective-permute-start.3) | collective-permute-done | bytes 65568 | tf_op jit(solution)/shard_map/ppermute | solution.py:232
  36.0 3.1 %collective-permute-start.4 = (f32[128,128]{1,0:T(8,128)S(1)}, f32[128,128]{1,0:T(8,128)S(1)}, u32[]{:S(2)}, u32[]{:S(2)}) collective-permute-start(f32[128,128]{1,0:T(8,128)S(1)} %add.36), channel_id=1, source_target_pairs={{0,16},{1,9},{2,18},{3,11},{4,20},{5,13},{6,22},{7,15},{8,24},{9,1... | collective-permute-start | bytes 196616 | tf_op jit(solution)/shard_map/ppermute | solution.py:232
  39.1 2.2 %collective-permute-done.4 = f32[128,128]{1,0:T(8,128)S(1)} collective-permute-done((f32[128,128]{1,0:T(8,128)S(1)}, f32[128,128]{1,0:T(8,128)S(1)}, u32[]{:S(2)}, u32[]{:S(2)}) %collective-permute-start.4) | collective-permute-done | bytes 65568 | tf_op jit(solution)/shard_map/ppermute | solution.py:232
  41.4 3.1 %collective-permute-start.9 = (f32[1,128,128]{2,1,0:T(8,128)S(1)}, f32[1,128,128]{2,1,0:T(8,128)S(1)}, u32[]{:S(2)}, u32[]{:S(2)}) collective-permute-start(f32[1,128,128]{2,1,0:T(8,128)S(1)} %slice.39), channel_id=1, source_target_pairs={{0,16},{1,9},{2,18},{3,11},{4,20},{5,13},{6,22},{7,15},{8,24},{9,1... | collective-permute-start | bytes 196616 | tf_op jit(solution)/shard_map/ppermute | solution.py:232
  44.5 5.6 %basis_rows.1 = (f32[128,128]{1,0:T(8,128)S(1)}, f32[576,128]{1,0:T(8,128)}) custom-call(f32[128,128]{1,0:T(8,128)S(1)} %add.37.gram_ref, f32[576,128]{1,0:T(8,128)S(1)} %get-tuple-element.9.first_ref), custom_call_target="tpu_custom_call" | custom-call | flops 4000000000 | bytes 589824 | tf_op jit(solution)/shard_map/basis_rows/pallas_call | solution.py:186
  50.1 0.9 %final_rows.1 = bf16[128,128]{1,0:T(8,128)(2,1)} custom-call(f32[128,128]{1,0:T(8,128)S(1)} %get-tuple-element.11.inverse_ref, f32[128,128]{1,0:T(8,128)S(1)} %fusion.sums_ref), custom_call_target="tpu_custom_call" | custom-call | tf_op jit(solution)/shard_map/final_rows/pallas_call | solution.py:209
  (15 shorter events, 0.2 us)
Async XLA Ops:
  6.4 2.8 %collective-permute-start.5 = (f32[16,128,128]{2,1,0:T(8,128)S(1)}, f32[16,128,128]{2,1,0:T(8,128)S(1)}, u32[]{:S(2)}, u32[]{:S(2)}) collective-permute-start(f32[16,128,128]{2,1,0:T(8,128)S(1)} %project_sibling.1), channel_id=1, source_target_pairs={{0,1},{1,0},{2,3},{3,2},{4,5},{5,4},{6,7},{7,6},{8,9},{9,8},{10,11... | collective-permute-start | bytes 3145736 | tf_op jit(solution)/shard_map/ppermute | solution.py:232
  9.4 10.1 %collective-permute-start.6 = (f32[8,128,128]{2,1,0:T(8,128)S(1)}, f32[8,128,128]{2,1,0:T(8,128)S(1)}, u32[]{:S(2)}, u32[]{:S(2)}) collective-permute-start(f32[8,128,128]{2,1,0:T(8,128)S(1)} %slice.33), channel_id=1, source_target_pairs={{0,2},{1,5},{2,0},{3,7},{4,6},{5,1},{6,4},{7,3},{8,10},{9,13},{10,... | collective-permute-start | bytes 1572872 | tf_op jit(solution)/shard_map/ppermute | solution.py:232
  19.6 13.7 %collective-permute-start.7 = (f32[4,128,128]{2,1,0:T(8,128)S(1)}, f32[4,128,128]{2,1,0:T(8,128)S(1)}, u32[]{:S(2)}, u32[]{:S(2)}) collective-permute-start(f32[4,128,128]{2,1,0:T(8,128)S(1)} %slice.35), channel_id=1, source_target_pairs={{0,4},{1,3},{2,6},{3,1},{4,0},{5,7},{6,2},{7,5},{8,12},{9,11},{10,... | collective-permute-start | bytes 786440 | tf_op jit(solution)/shard_map/ppermute | solution.py:232
  21.7 1.3 %collective-permute-start = (f32[128,128]{1,0:T(8,128)S(1)}, f32[128,128]{1,0:T(8,128)S(1)}, u32[]{:S(2)}, u32[]{:S(2)}) collective-permute-start(f32[128,128]{1,0:T(8,128)S(1)} %get-tuple-element.8), channel_id=1, source_target_pairs={{0,1},{1,0},{2,3},{3,2},{4,5},{5,4},{6,7},{7,6},{8,9},{9,8},{10,11... | collective-permute-start | bytes 196616 | tf_op jit(solution)/shard_map/ppermute | solution.py:232
  23.0 4.3 %collective-permute-start.1 = (f32[128,128]{1,0:T(8,128)S(1)}, f32[128,128]{1,0:T(8,128)S(1)}, u32[]{:S(2)}, u32[]{:S(2)}) collective-permute-start(f32[128,128]{1,0:T(8,128)S(1)} %add.33), channel_id=1, source_target_pairs={{0,2},{1,5},{2,0},{3,7},{4,6},{5,1},{6,4},{7,3},{8,10},{9,13},{10,... | collective-permute-start | bytes 196616 | tf_op jit(solution)/shard_map/ppermute | solution.py:232
  27.3 4.3 %collective-permute-start.2 = (f32[128,128]{1,0:T(8,128)S(1)}, f32[128,128]{1,0:T(8,128)S(1)}, u32[]{:S(2)}, u32[]{:S(2)}) collective-permute-start(f32[128,128]{1,0:T(8,128)S(1)} %add.34), channel_id=1, source_target_pairs={{0,4},{1,3},{2,6},{3,1},{4,0},{5,7},{6,2},{7,5},{8,12},{9,11},{10,... | collective-permute-start | bytes 196616 | tf_op jit(solution)/shard_map/ppermute | solution.py:232
  31.6 4.3 %collective-permute-start.3 = (f32[128,128]{1,0:T(8,128)S(1)}, f32[128,128]{1,0:T(8,128)S(1)}, u32[]{:S(2)}, u32[]{:S(2)}) collective-permute-start(f32[128,128]{1,0:T(8,128)S(1)} %add.35), channel_id=1, source_target_pairs={{0,8},{1,17},{2,10},{3,19},{4,12},{5,21},{6,14},{7,23},{8,0},{9,25... | collective-permute-start | bytes 196616 | tf_op jit(solution)/shard_map/ppermute | solution.py:232
  33.4 8.0 %collective-permute-start.8 = (f32[2,128,128]{2,1,0:T(8,128)S(1)}, f32[2,128,128]{2,1,0:T(8,128)S(1)}, u32[]{:S(2)}, u32[]{:S(2)}) collective-permute-start(f32[2,128,128]{2,1,0:T(8,128)S(1)} %slice.37), channel_id=1, source_target_pairs={{0,8},{1,17},{2,10},{3,19},{4,12},{5,21},{6,14},{7,23},{8,0},{9,25... | collective-permute-start | bytes 393224 | tf_op jit(solution)/shard_map/ppermute | solution.py:232
  36.0 5.3 %collective-permute-start.4 = (f32[128,128]{1,0:T(8,128)S(1)}, f32[128,128]{1,0:T(8,128)S(1)}, u32[]{:S(2)}, u32[]{:S(2)}) collective-permute-start(f32[128,128]{1,0:T(8,128)S(1)} %add.36), channel_id=1, source_target_pairs={{0,16},{1,9},{2,18},{3,11},{4,20},{5,13},{6,22},{7,15},{8,24},{9,1... | collective-permute-start | bytes 196616 | tf_op jit(solution)/shard_map/ppermute | solution.py:232
  41.4 8.7 %collective-permute-start.9 = (f32[1,128,128]{2,1,0:T(8,128)S(1)}, f32[1,128,128]{2,1,0:T(8,128)S(1)}, u32[]{:S(2)}, u32[]{:S(2)}) collective-permute-start(f32[1,128,128]{2,1,0:T(8,128)S(1)} %slice.39), channel_id=1, source_target_pairs={{0,16},{1,9},{2,18},{3,11},{4,20},{5,13},{6,22},{7,15},{8,24},{9,1... | collective-permute-start | bytes 196616 | tf_op jit(solution)/shard_map/ppermute | solution.py:232

commit v4 on v3

--- a/solution.py
+++ b/solution.py
@@ -172,8 +172,25 @@
                 right[i] = right[i] - weights[k] * sides[k]
 
 
-def basis_kernel(factor, gram_ref, first_ref, inverse_ref, basis_ref):
+def factor_kernel(gram_ref, inverse_ref):
     inverse_factor(gram_ref, inverse_ref)
+
+
+def factor_call(gram):
+    return pl.pallas_call(
+        factor_kernel,
+        in_specs=[pl.BlockSpec(memory_space=pltpu.VMEM)],
+        out_specs=pl.BlockSpec(memory_space=pltpu.VMEM),
+        out_shape=jax.ShapeDtypeStruct(gram.shape, jnp.float32),
+        compiler_params=pltpu.CompilerParams(vmem_limit_bytes=VMEM_LIMIT),
+        cost_estimate=pl.CostEstimate(
+            flops=4000000000, bytes_accessed=gram.size * 8, transcendentals=gram.shape[0]
+        ),
+        name="factor",
+    )(gram)
+
+
+def basis_kernel(factor, inverse_ref, first_ref, basis_ref):
     one = lax.dot_general(
         first_ref[...], inverse_ref[...], (((1,), (1,)), ((), ())),
         precision=HIGHEST, preferred_element_type=jnp.float32,
@@ -181,20 +198,19 @@
     basis_ref[...] = one * factor
 
 
-def basis_call(gram, first, total_rows):
+def basis_call(inverse, first, total_rows):
     rows, rank = first.shape
+    vmem = pl.BlockSpec(memory_space=pltpu.VMEM)
     return pl.pallas_call(
         functools.partial(basis_kernel, float(total_rows) ** 0.5),
-        out_shape=[
-            jax.ShapeDtypeStruct((rank, rank), jnp.float32),
-            jax.ShapeDtypeStruct((rows, rank), jnp.float32),
-        ],
-        compiler_params=pltpu.CompilerParams(vmem_limit_bytes=VMEM_LIMIT),
-        cost_estimate=pl.CostEstimate(
-            flops=4000000000, bytes_accessed=rows * rank * 8, transcendentals=rank
+        in_specs=[vmem, vmem],
+        out_shape=jax.ShapeDtypeStruct((rows, rank), jnp.float32),
+        compiler_params=pltpu.CompilerParams(vmem_limit_bytes=VMEM_LIMIT),
+        cost_estimate=pl.CostEstimate(
+            flops=12 * rows * rank * rank, bytes_accessed=rows * rank * 8, transcendentals=0
         ),
         name="basis_rows",
-    )(gram, first)
+    )(inverse, first)
 
 
 def final_kernel(factor, inverse_ref, sums_ref, out_ref):
@@ -232,23 +248,36 @@
         return lax.ppermute(array, AXES, pairs)
 
     core, x, y, z, zz = range(low_bits, low_bits + 5)
-    rounds = [(core, core), (x, y), (y, x), (z, zz), (zz, z)]
+    tie = lax.optimization_barrier
 
     owner = lax.shift_right_logical(me, low_bits).astype(jnp.int32).reshape(1)
     slab_near, first, split, gram = sketch_call(slab, sketch)
-    gram = gram + exchange(gram, *rounds[0])
-    got = exchange(project_call(owner, split, slab_near, 1), *rounds[0])
-    sums = project_call(owner, split, slab_near, 0)
-    for pair in rounds[1:]:
-        gram = gram + exchange(gram, *pair)
-        sums = sums + got
-        half = sums.shape[0] // 2
-        got = exchange(sums[half:], *pair)
-        sums = sums[:half]
-    sums = (sums + got)[0]
+    gram = gram + exchange(gram, core, core)
+    send = project_call(owner, split, slab_near, 1)
+    send, split, gram = tie((send, split, gram))
+    got = exchange(send, core, core)
+    gram = gram + exchange(gram, z, zz)
+    got, gram = tie((got, gram))
+    sums = project_call(owner, split, slab_near, 0) + got
+    got = exchange(sums[8:], x, y)
+    gram = gram + exchange(gram, zz, z)
+    got, gram = tie((got, gram))
+    gram = gram + exchange(gram, x, y)
+    sums = sums[:8] + got
+    got = exchange(sums[4:], y, x)
+    gram = gram + exchange(gram, y, x)
     for bit in range(low_bits):
         gram = gram + swap(gram, bit)
-    inverse, basis = basis_call(gram, first, total_rows)
+    got, gram = tie((got, gram))
+    sums = sums[:4] + got
+    got = exchange(sums[2:], z, zz)
+    sums, gram = tie((sums, gram))
+    inverse = factor_call(gram)
+    got, inverse = tie((got, inverse))
+    sums = sums[:2] + got
+    kept, moved, inverse = tie((sums[0], sums[1], inverse))
+    sums = kept + exchange(moved, zz, z)
+    basis = basis_call(inverse, first, total_rows)
     for bit in reversed(range(low_bits)):
         half = sums.shape[1] // 2
         mine = lax.rem(lax.shift_right_logical(me, bit), 2) == 1

time: 51.1 us -> 50.6 us (level)
  local copies, waits for them, and re-layouts: 0.07 us -> 4.53 us
  waiting for transfers between devices: 20.8 us -> 17 us
  starting transfers between devices: 15.6 us -> 14.9 us
    pallas_call x1, Pallas kernels: 5.62 us -> 1.12 us  [basis_call(): pl.pallas_call(functools.partial(basis_kernel, float(total_rows) ** 0.5),...]
    unnamed x0 -> x4, local copies, waits for them, and re-layouts: none -> 4.46 us
    pallas_call x0 -> x1, Pallas kernels: none -> 4.02 us  [factor_call(): pl.pallas_call(factor_kernel, in_specs=[pl.BlockSpec(memory_space=pltpu.V...]
    ppermute x10, waiting for transfers between devices: 20.8 us -> 17 us  [exchange(): return lax.ppermute(array, AXES, pairs)]
    ppermute x10, starting transfers between devices: 15.6 us -> 14.9 us  [exchange(): return lax.ppermute(array, AXES, pairs)]
  transfers between devices with their start and end apart: 10 -> 10, of which waited for: 7 -> 6; matrix products, arithmetic and copies ran while one was open for 0% -> 0% of each run, Pallas kernels for 13% -> 15%
where the time goes in v4:
time: 50.6 us; the launch traced here: 50.5 us
  waiting for transfers between devices  17 us (34%)
  starting transfers between devices  14.9 us (29%)
  Pallas kernels  12.9 us (25%)
  local copies, waits for them, and re-layouts  4.53 us (9%)
  between operations  0.8 us (2%)
    ppermute x10, waiting for transfers between devices, exchange(): return lax.ppermute(array, AXES, pairs)  17 us
    ppermute x10, starting transfers between devices, exchange(): return lax.ppermute(array, AXES, pairs)  14.9 us
    pallas_call x1, Pallas kernels, sketch_call(): pl.pallas_call(sketch_kernel, in_specs=[pl.BlockSpec(memory_space=pltpu.H...  4.56 us
    unnamed x4, local copies, waits for them, and re-layouts  4.46 us
    pallas_call x1, Pallas kernels, factor_call(): pl.pallas_call(factor_kernel, in_specs=[pl.BlockSpec(memory_space=pltpu.V...  4.02 us
    pallas_call x2, Pallas kernels, project_call(): pl.pallas_call(functools.partial(project_kernel, sibling), in_specs=[pl.B...  2.29 us
    pallas_call x1, Pallas kernels, basis_call(): pl.pallas_call(functools.partial(basis_kernel, float(total_rows) ** 0.5),...  1.12 us
  transfers between devices with their start and end apart: 10, of which 6 were waited for; matrix products, arithmetic and copies ran while one was open for 0% of the time, Pallas kernels for 15%

profile of v4, /device:TPU:0, one launch (start us, length us, event | category | flops | bytes accessed | tf_op | source)
XLA Modules:
  0.0 50.5 jit_solution(1932377133096025569)
XLA Ops:
  0.6 4.6 %sketch_rows.1 = (bf16[576,4096]{1,0:T(8,128)(2,1)S(1)}, f32[576,128]{1,0:T(8,128)S(1)}, bf16[256,576]{1,0:T(8,128)(2,1)S(1)}, f32[128,128]{1,0:T(8,128)S(1)}) custom-call(bf16[576,4096]{1,0:T(8,128)(2,1)} %slab_hbm.1, bf16[4096,128]{1,0:T(8,128)(2,1)} %sketch_hbm.1), custom_call_target="tpu_custom_call" | custom-call | flops 603979776 | bytes 4718592 | tf_op jit(solution)/shard_map/sketch_rows/pallas_call | solution.py:54
  5.2 2.1 %copy-done = bf16[576,4096]{1,0:T(8,128)(2,1)} copy-done((bf16[576,4096]{1,0:T(8,128)(2,1)}, bf16[576,4096]{1,0:T(8,128)(2,1)S(1)}, u32[]{:S(2)}) %copy-start) | copy-done | bytes 4718616
  7.3 0.5 collective-permute-start
  7.8 2.3 %copy-done.1 = bf16[576,4096]{1,0:T(8,128)(2,1)S(1)} copy-done((bf16[576,4096]{1,0:T(8,128)(2,1)S(1)}, bf16[576,4096]{1,0:T(8,128)(2,1)}, u32[]{:S(2)}) %copy-start.1) | copy-done | bytes 4718616
  10.1 1.1 %project_sibling.1 = f32[16,128,128]{2,1,0:T(8,128)S(1)} custom-call(s32[1]{0:T(128)} %bitcast.owner_ref, bf16[256,576]{1,0:T(8,128)(2,1)S(1)} %get-tuple-element.25.split_ref, bf16[576,4096]{1,0:T(8,128)(2,1)S(1)} %copy-done.1), custom_call_target="tpu_custom_call" | custom-call | flops 603979776 | bytes 2359296 | tf_op jit(solution)/shard_map/project_sibling/pallas_call | solution.py:112
  11.3 0.1 collective-permute-start.1
  11.4 3.0 %collective-permute-start.2 = (f32[128,128]{1,0:T(8,128)S(1)}, f32[128,128]{1,0:T(8,128)S(1)}, u32[]{:S(2)}, u32[]{:S(2)}) collective-permute-start(f32[128,128]{1,0:T(8,128)S(1)} %add.34), channel_id=1, source_target_pairs={{0,8},{1,17},{2,10},{3,19},{4,12},{5,21},{6,14},{7,23},{8,0},{9,25... | collective-permute-start | bytes 196616 | tf_op jit(solution)/shard_map/ppermute | solution.py:248
  14.5 1.2 %project_own.1 = f32[16,128,128]{2,1,0:T(8,128)S(1)} custom-call(s32[1]{0:T(128)} %bitcast.owner_ref, bf16[256,576]{1,0:T(8,128)(2,1)S(1)} %get-tuple-element.25.split_ref, bf16[576,4096]{1,0:T(8,128)(2,1)S(1)} %copy-done.1), custom_call_target="tpu_custom_call" | custom-call | flops 603979776 | bytes 2359296 | tf_op jit(solution)/shard_map/project_own/pallas_call | solution.py:112
  15.6 1.8 %collective-permute-done.2 = f32[128,128]{1,0:T(8,128)S(1)} collective-permute-done((f32[128,128]{1,0:T(8,128)S(1)}, f32[128,128]{1,0:T(8,128)S(1)}, u32[]{:S(2)}, u32[]{:S(2)}) %collective-permute-start.2) | collective-permute-done | bytes 65568 | tf_op jit(solution)/shard_map/ppermute | solution.py:248
  17.4 0.1 add.36
  17.6 2.0 %collective-permute-start.3 = (f32[8,128,128]{2,1,0:T(8,128)S(1)}, f32[8,128,128]{2,1,0:T(8,128)S(1)}, u32[]{:S(2)}, u32[]{:S(2)}) collective-permute-start(f32[8,128,128]{2,1,0:T(8,128)S(1)} %slice.33), channel_id=1, source_target_pairs={{0,2},{1,5},{2,0},{3,7},{4,6},{5,1},{6,4},{7,3},{8,10},{9,13},{10,... | collective-permute-start | bytes 1572872 | tf_op jit(solution)/shard_map/ppermute | solution.py:248
  19.6 1.9 %collective-permute-start.4 = (f32[128,128]{1,0:T(8,128)S(1)}, f32[128,128]{1,0:T(8,128)S(1)}, u32[]{:S(2)}, u32[]{:S(2)}) collective-permute-start(f32[128,128]{1,0:T(8,128)S(1)} %add.35), channel_id=1, source_target_pairs={{0,16},{1,9},{2,18},{3,11},{4,20},{5,13},{6,22},{7,15},{8,24},{9,1... | collective-permute-start | bytes 196616 | tf_op jit(solution)/shard_map/ppermute | solution.py:248
  21.5 3.3 %collective-permute-done.4 = f32[128,128]{1,0:T(8,128)S(1)} collective-permute-done((f32[128,128]{1,0:T(8,128)S(1)}, f32[128,128]{1,0:T(8,128)S(1)}, u32[]{:S(2)}, u32[]{:S(2)}) %collective-permute-start.4) | collective-permute-done | bytes 65568 | tf_op jit(solution)/shard_map/ppermute | solution.py:248
  24.8 2.1 %collective-permute-done.3 = f32[8,128,128]{2,1,0:T(8,128)S(1)} collective-permute-done((f32[8,128,128]{2,1,0:T(8,128)S(1)}, f32[8,128,128]{2,1,0:T(8,128)S(1)}, u32[]{:S(2)}, u32[]{:S(2)}) %collective-permute-start.3) | collective-permute-done | bytes 524320 | tf_op jit(solution)/shard_map/ppermute | solution.py:248
  27.0 2.0 %collective-permute-start.5 = (f32[4,128,128]{2,1,0:T(8,128)S(1)}, f32[4,128,128]{2,1,0:T(8,128)S(1)}, u32[]{:S(2)}, u32[]{:S(2)}) collective-permute-start(f32[4,128,128]{2,1,0:T(8,128)S(1)} %slice.35), channel_id=1, source_target_pairs={{0,4},{1,3},{2,6},{3,1},{4,0},{5,7},{6,2},{7,5},{8,12},{9,11},{10,... | collective-permute-start | bytes 786440 | tf_op jit(solution)/shard_map/ppermute | solution.py:248
  29.0 1.5 %collective-permute-start.6 = (f32[128,128]{1,0:T(8,128)S(1)}, f32[128,128]{1,0:T(8,128)S(1)}, u32[]{:S(2)}, u32[]{:S(2)}) collective-permute-start(f32[128,128]{1,0:T(8,128)S(1)} %add.37), channel_id=1, source_target_pairs={{0,2},{1,5},{2,0},{3,7},{4,6},{5,1},{6,4},{7,3},{8,10},{9,13},{10,... | collective-permute-start | bytes 196616 | tf_op jit(solution)/shard_map/ppermute | solution.py:248
  30.5 3.2 %collective-permute-done.6 = f32[128,128]{1,0:T(8,128)S(1)} collective-permute-done((f32[128,128]{1,0:T(8,128)S(1)}, f32[128,128]{1,0:T(8,128)S(1)}, u32[]{:S(2)}, u32[]{:S(2)}) %collective-permute-start.6) | collective-permute-done | bytes 65568 | tf_op jit(solution)/shard_map/ppermute | solution.py:248
  33.8 4.3 %collective-permute-done.7 = f32[128,128]{1,0:T(8,128)S(1)} collective-permute-done((f32[128,128]{1,0:T(8,128)S(1)}, f32[128,128]{1,0:T(8,128)S(1)}, u32[]{:S(2)}, u32[]{:S(2)}) %collective-permute-start.7) | collective-permute-done | bytes 65568 | tf_op jit(solution)/shard_map/ppermute | solution.py:248
  38.1 1.4 %collective-permute-start.8 = (f32[2,128,128]{2,1,0:T(8,128)S(1)}, f32[2,128,128]{2,1,0:T(8,128)S(1)}, u32[]{:S(2)}, u32[]{:S(2)}) collective-permute-start(f32[2,128,128]{2,1,0:T(8,128)S(1)} %slice.36), channel_id=1, source_target_pairs={{0,8},{1,17},{2,10},{3,19},{4,12},{5,21},{6,14},{7,23},{8,0},{9,25... | collective-permute-start | bytes 393224 | tf_op jit(solution)/shard_map/ppermute | solution.py:248
  39.6 4.0 %factor.1.inverse_ref = f32[128,128]{1,0:T(8,128)S(1)} custom-call(f32[128,128]{1,0:T(8,128)S(1)} %add.40.gram_ref), custom_call_target="tpu_custom_call" | custom-call | flops 4000000000 | bytes 131072 | tf_op jit(solution)/shard_map/factor/pallas_call | solution.py:180
  43.6 2.4 %collective-permute-start.9 = (f32[128,128]{1,0:T(8,128)S(1)}, f32[128,128]{1,0:T(8,128)S(1)}, u32[]{:S(2)}, u32[]{:S(2)}) collective-permute-start(f32[128,128]{1,0:T(8,128)S(1)} %get-tuple-element.41), channel_id=1, source_target_pairs={{0,16},{1,9},{2,18},{3,11},{4,20},{5,13},{6,22},{7,15},{8,24},{9,1... | collective-permute-start | bytes 196616 | tf_op jit(solution)/shard_map/ppermute | solution.py:248
  46.1 1.1 %basis_rows.1 = f32[576,128]{1,0:T(8,128)} custom-call(f32[128,128]{1,0:T(8,128)S(1)} %factor.1.inverse_ref, f32[576,128]{1,0:T(8,128)S(1)} %get-tuple-element.39.first_ref), custom_call_target="tpu_custom_call" | custom-call | flops 113246208 | bytes 589824 | tf_op jit(solution)/shard_map/basis_rows/pallas_call | solution.py:204
  47.2 2.4 %collective-permute-done.9 = f32[128,128]{1,0:T(8,128)S(1)} collective-permute-done((f32[128,128]{1,0:T(8,128)S(1)}, f32[128,128]{1,0:T(8,128)S(1)}, u32[]{:S(2)}, u32[]{:S(2)}) %collective-permute-start.9) | collective-permute-done | bytes 65568 | tf_op jit(solution)/shard_map/ppermute | solution.py:248
  49.6 0.9 %final_rows.1 = bf16[128,128]{1,0:T(8,128)(2,1)} custom-call(f32[128,128]{1,0:T(8,128)S(1)} %factor.1.inverse_ref, f32[128,128]{1,0:T(8,128)S(1)} %add.43.sums_ref), custom_call_target="tpu_custom_call" | custom-call | tf_op jit(solution)/shard_map/final_rows/pallas_call | solution.py:225
  (20 shorter events, 0.3 us)
Async XLA Ops:
  5.2 2.1 %copy-start = (bf16[576,4096]{1,0:T(8,128)(2,1)}, bf16[576,4096]{1,0:T(8,128)(2,1)S(1)}, u32[]{:S(2)}) copy-start(bf16[576,4096]{1,0:T(8,128)(2,1)S(1)} %get-tuple-element.23.slab_ref) | copy-start | bytes 14155780
  7.3 3.9 %collective-permute-start = (f32[128,128]{1,0:T(8,128)S(1)}, f32[128,128]{1,0:T(8,128)S(1)}, u32[]{:S(2)}, u32[]{:S(2)}) collective-permute-start(f32[128,128]{1,0:T(8,128)S(1)} %get-tuple-element.24), channel_id=1, source_target_pairs={{0,1},{1,0},{2,3},{3,2},{4,5},{5,4},{6,7},{7,6},{8,9},{9,8},{10,11... | collective-permute-start | bytes 196616 | tf_op jit(solution)/shard_map/ppermute | solution.py:248
  7.8 2.3 %copy-start.1 = (bf16[576,4096]{1,0:T(8,128)(2,1)S(1)}, bf16[576,4096]{1,0:T(8,128)(2,1)}, u32[]{:S(2)}) copy-start(bf16[576,4096]{1,0:T(8,128)(2,1)} %copy-done) | copy-start | bytes 14155780
  11.3 6.1 %collective-permute-start.1 = (f32[16,128,128]{2,1,0:T(8,128)S(1)}, f32[16,128,128]{2,1,0:T(8,128)S(1)}, u32[]{:S(2)}, u32[]{:S(2)}) collective-permute-start(f32[16,128,128]{2,1,0:T(8,128)S(1)} %project_sibling.1), channel_id=1, source_target_pairs={{0,1},{1,0},{2,3},{3,2},{4,5},{5,4},{6,7},{7,6},{8,9},{9,8},{10,11... | collective-permute-start | bytes 3145736 | tf_op jit(solution)/shard_map/ppermute | solution.py:248
  11.4 6.0 %collective-permute-start.2 = (f32[128,128]{1,0:T(8,128)S(1)}, f32[128,128]{1,0:T(8,128)S(1)}, u32[]{:S(2)}, u32[]{:S(2)}) collective-permute-start(f32[128,128]{1,0:T(8,128)S(1)} %add.34), channel_id=1, source_target_pairs={{0,8},{1,17},{2,10},{3,19},{4,12},{5,21},{6,14},{7,23},{8,0},{9,25... | collective-permute-start | bytes 196616 | tf_op jit(solution)/shard_map/ppermute | solution.py:248
  17.6 9.2 %collective-permute-start.3 = (f32[8,128,128]{2,1,0:T(8,128)S(1)}, f32[8,128,128]{2,1,0:T(8,128)S(1)}, u32[]{:S(2)}, u32[]{:S(2)}) collective-permute-start(f32[8,128,128]{2,1,0:T(8,128)S(1)} %slice.33), channel_id=1, source_target_pairs={{0,2},{1,5},{2,0},{3,7},{4,6},{5,1},{6,4},{7,3},{8,10},{9,13},{10,... | collective-permute-start | bytes 1572872 | tf_op jit(solution)/shard_map/ppermute | solution.py:248
  19.6 5.2 %collective-permute-start.4 = (f32[128,128]{1,0:T(8,128)S(1)}, f32[128,128]{1,0:T(8,128)S(1)}, u32[]{:S(2)}, u32[]{:S(2)}) collective-permute-start(f32[128,128]{1,0:T(8,128)S(1)} %add.35), channel_id=1, source_target_pairs={{0,16},{1,9},{2,18},{3,11},{4,20},{5,13},{6,22},{7,15},{8,24},{9,1... | collective-permute-start | bytes 196616 | tf_op jit(solution)/shard_map/ppermute | solution.py:248
  27.0 11.1 %collective-permute-start.5 = (f32[4,128,128]{2,1,0:T(8,128)S(1)}, f32[4,128,128]{2,1,0:T(8,128)S(1)}, u32[]{:S(2)}, u32[]{:S(2)}) collective-permute-start(f32[4,128,128]{2,1,0:T(8,128)S(1)} %slice.35), channel_id=1, source_target_pairs={{0,4},{1,3},{2,6},{3,1},{4,0},{5,7},{6,2},{7,5},{8,12},{9,11},{10,... | collective-permute-start | bytes 786440 | tf_op jit(solution)/shard_map/ppermute | solution.py:248
  29.0 4.7 %collective-permute-start.6 = (f32[128,128]{1,0:T(8,128)S(1)}, f32[128,128]{1,0:T(8,128)S(1)}, u32[]{:S(2)}, u32[]{:S(2)}) collective-permute-start(f32[128,128]{1,0:T(8,128)S(1)} %add.37), channel_id=1, source_target_pairs={{0,2},{1,5},{2,0},{3,7},{4,6},{5,1},{6,4},{7,3},{8,10},{9,13},{10,... | collective-permute-start | bytes 196616 | tf_op jit(solution)/shard_map/ppermute | solution.py:248
  33.7 4.3 %collective-permute-start.7 = (f32[128,128]{1,0:T(8,128)S(1)}, f32[128,128]{1,0:T(8,128)S(1)}, u32[]{:S(2)}, u32[]{:S(2)}) collective-permute-start(f32[128,128]{1,0:T(8,128)S(1)} %add.39), channel_id=1, source_target_pairs={{0,4},{1,3},{2,6},{3,1},{4,0},{5,7},{6,2},{7,5},{8,12},{9,11},{10,... | collective-permute-start | bytes 196616 | tf_op jit(solution)/shard_map/ppermute | solution.py:248
  38.1 5.5 %collective-permute-start.8 = (f32[2,128,128]{2,1,0:T(8,128)S(1)}, f32[2,128,128]{2,1,0:T(8,128)S(1)}, u32[]{:S(2)}, u32[]{:S(2)}) collective-permute-start(f32[2,128,128]{2,1,0:T(8,128)S(1)} %slice.36), channel_id=1, source_target_pairs={{0,8},{1,17},{2,10},{3,19},{4,12},{5,21},{6,14},{7,23},{8,0},{9,25... | collective-permute-start | bytes 393224 | tf_op jit(solution)/shard_map/ppermute | solution.py:248
  43.6 5.9 %collective-permute-start.9 = (f32[128,128]{1,0:T(8,128)S(1)}, f32[128,128]{1,0:T(8,128)S(1)}, u32[]{:S(2)}, u32[]{:S(2)}) collective-permute-start(f32[128,128]{1,0:T(8,128)S(1)} %get-tuple-element.41), channel_id=1, source_target_pairs={{0,16},{1,9},{2,18},{3,11},{4,20},{5,13},{6,22},{7,15},{8,24},{9,1... | collective-permute-start | bytes 196616 | tf_op jit(solution)/shard_map/ppermute | solution.py:248

commit v5 on v4

--- a/solution.py
+++ b/solution.py
@@ -10,7 +10,7 @@
 AXES = ("rows", "grp")
 HIGHEST = lax.Precision.HIGHEST
 LANES = 128
-VMEM_LIMIT = 40 * 1024 * 1024
+VMEM_LIMIT = 24 * 1024 * 1024
 
 
 CHUNKS = 4
@@ -56,10 +56,10 @@
         in_specs=[pl.BlockSpec(memory_space=pltpu.HBM)] * 2,
         out_specs=[pl.BlockSpec(memory_space=pltpu.VMEM)] * 4,
         out_shape=[
-            jax.ShapeDtypeStruct((rows, width), jnp.bfloat16),
-            jax.ShapeDtypeStruct((rows, rank), jnp.float32),
-            jax.ShapeDtypeStruct((2 * rank, rows), jnp.bfloat16),
-            jax.ShapeDtypeStruct((rank, rank), jnp.float32),
+            pltpu.VMEM((rows, width), jnp.bfloat16),
+            pltpu.VMEM((rows, rank), jnp.float32),
+            pltpu.VMEM((2 * rank, rows), jnp.bfloat16),
+            pltpu.VMEM((rank, rank), jnp.float32),
         ],
         scratch_shapes=[
             pltpu.VMEM((width, rank), jnp.bfloat16),
@@ -119,7 +119,7 @@
             flops=2 * rows * width * rank, bytes_accessed=rows * width, transcendentals=0
         ),
         name="project_sibling" if sibling else "project_own",
-    )(owner, split, slab)
+    )(owner, split, pltpu.with_memory_space_constraint(slab, pltpu.VMEM))
 
 
 def lane(block, at):
@@ -252,17 +252,16 @@
 
     owner = lax.shift_right_logical(me, low_bits).astype(jnp.int32).reshape(1)
     slab_near, first, split, gram = sketch_call(slab, sketch)
-    gram = gram + exchange(gram, core, core)
+    gram = gram + exchange(gram, z, zz)
     send = project_call(owner, split, slab_near, 1)
-    send, split, gram = tie((send, split, gram))
+    send, gram = tie((send, gram))
     got = exchange(send, core, core)
-    gram = gram + exchange(gram, z, zz)
-    got, gram = tie((got, gram))
+    gram = gram + exchange(gram, zz, z)
     sums = project_call(owner, split, slab_near, 0) + got
     got = exchange(sums[8:], x, y)
-    gram = gram + exchange(gram, zz, z)
+    gram = gram + exchange(gram, core, core)
+    gram = gram + exchange(gram, x, y)
     got, gram = tie((got, gram))
-    gram = gram + exchange(gram, x, y)
     sums = sums[:8] + got
     got = exchange(sums[4:], y, x)
     gram = gram + exchange(gram, y, x)

time: 50.6 us -> 48.8 us (0.964)
  waiting for transfers between devices: 17 us -> 15.2 us
    ppermute x10, waiting for transfers between devices: 17 us -> 15.2 us  [exchange(): return lax.ppermute(array, AXES, pairs)]
where the time goes in v5:
time: 48.8 us; the launch traced here: 48.6 us
  waiting for transfers between devices  15.2 us (31%)
  starting transfers between devices  14.9 us (31%)
  Pallas kernels  12.9 us (26%)
  local copies, waits for them, and re-layouts  4.53 us (9%)
  between operations  0.8 us (2%)
    ppermute x10, waiting for transfers between devices, exchange(): return lax.ppermute(array, AXES, pairs)  15.2 us
    ppermute x10, starting transfers between devices, exchange(): return lax.ppermute(array, AXES, pairs)  14.9 us
    pallas_call x1, Pallas kernels, sketch_call(): pl.pallas_call(sketch_kernel, in_specs=[pl.BlockSpec(memory_space=pltpu.H...  4.56 us
    unnamed x4, local copies, waits for them, and re-layouts  4.46 us
    pallas_call x1, Pallas kernels, factor_call(): pl.pallas_call(factor_kernel, in_specs=[pl.BlockSpec(memory_space=pltpu.V...  4.02 us
    pallas_call x2, Pallas kernels, project_call(): pl.pallas_call(functools.partial(project_kernel, sibling), in_specs=[pl.B...  2.29 us
    pallas_call x1, Pallas kernels, basis_call(): pl.pallas_call(functools.partial(basis_kernel, float(total_rows) ** 0.5),...  1.11 us
  transfers between devices with their start and end apart: 10, of which 6 were waited for; matrix products, arithmetic and copies ran while one was open for 0% of the time, Pallas kernels for 15%

profile of v5, /device:TPU:0, one launch (start us, length us, event | category | flops | bytes accessed | tf_op | source)
XLA Modules:
  0.0 48.6 jit_solution(6896178085244401870)
XLA Ops:
  0.6 4.6 %sketch_rows.1 = (bf16[576,4096]{1,0:T(8,128)(2,1)S(1)}, f32[576,128]{1,0:T(8,128)S(1)}, bf16[256,576]{1,0:T(8,128)(2,1)S(1)}, f32[128,128]{1,0:T(8,128)S(1)}) custom-call(bf16[576,4096]{1,0:T(8,128)(2,1)} %slab_hbm.1, bf16[4096,128]{1,0:T(8,128)(2,1)} %sketch_hbm.1), custom_call_target="tpu_custom_call" | custom-call | flops 603979776 | bytes 4718592 | tf_op jit(solution)/shard_map/sketch_rows/pallas_call | solution.py:54
  5.2 2.1 %copy-done = bf16[576,4096]{1,0:T(8,128)(2,1)} copy-done((bf16[576,4096]{1,0:T(8,128)(2,1)}, bf16[576,4096]{1,0:T(8,128)(2,1)S(1)}, u32[]{:S(2)}) %copy-start) | copy-done | bytes 4718616
  7.3 3.0 %collective-permute-start = (f32[128,128]{1,0:T(8,128)S(1)}, f32[128,128]{1,0:T(8,128)S(1)}, u32[]{:S(2)}, u32[]{:S(2)}) collective-permute-start(f32[128,128]{1,0:T(8,128)S(1)} %get-tuple-element.21), channel_id=1, source_target_pairs={{0,8},{1,17},{2,10},{3,19},{4,12},{5,21},{6,14},{7,23},{8,0},{9,25... | collective-permute-start | bytes 196616 | tf_op jit(solution)/shard_map/ppermute | solution.py:248
  10.4 2.3 %copy-done.1 = bf16[576,4096]{1,0:T(8,128)(2,1)S(1)} copy-done((bf16[576,4096]{1,0:T(8,128)(2,1)S(1)}, bf16[576,4096]{1,0:T(8,128)(2,1)}, u32[]{:S(2)}) %copy-start.1) | copy-done | bytes 4718616
  12.7 1.1 %project_sibling.1 = f32[16,128,128]{2,1,0:T(8,128)S(1)} custom-call(s32[1]{0:T(128)} %bitcast.owner_ref, bf16[256,576]{1,0:T(8,128)(2,1)S(1)} %get-tuple-element.19.split_ref, bf16[576,4096]{1,0:T(8,128)(2,1)S(1)} %copy-done.1), custom_call_target="tpu_custom_call" | custom-call | flops 603979776 | bytes 2359296 | tf_op jit(solution)/shard_map/project_sibling/pallas_call | solution.py:112
  13.9 0.6 %collective-permute-start.1 = (f32[16,128,128]{2,1,0:T(8,128)S(1)}, f32[16,128,128]{2,1,0:T(8,128)S(1)}, u32[]{:S(2)}, u32[]{:S(2)}) collective-permute-start(f32[16,128,128]{2,1,0:T(8,128)S(1)} %project_sibling.1), channel_id=1, source_target_pairs={{0,1},{1,0},{2,3},{3,2},{4,5},{5,4},{6,7},{7,6},{8,9},{9,8},{10,11... | collective-permute-start | bytes 3145736 | tf_op jit(solution)/shard_map/ppermute | solution.py:248
  14.5 1.2 %project_own.1 = f32[16,128,128]{2,1,0:T(8,128)S(1)} custom-call(s32[1]{0:T(128)} %bitcast.owner_ref, bf16[256,576]{1,0:T(8,128)(2,1)S(1)} %get-tuple-element.19.split_ref, bf16[576,4096]{1,0:T(8,128)(2,1)S(1)} %copy-done.1), custom_call_target="tpu_custom_call" | custom-call | flops 603979776 | bytes 2359296 | tf_op jit(solution)/shard_map/project_own/pallas_call | solution.py:112
  15.7 1.1 %collective-permute-done.1 = f32[16,128,128]{2,1,0:T(8,128)S(1)} collective-permute-done((f32[16,128,128]{2,1,0:T(8,128)S(1)}, f32[16,128,128]{2,1,0:T(8,128)S(1)}, u32[]{:S(2)}, u32[]{:S(2)}) %collective-permute-start.1) | collective-permute-done | bytes 1048608 | tf_op jit(solution)/shard_map/ppermute | solution.py:248
  16.8 0.1 add.35
  17.0 1.6 %collective-permute-start.2 = (f32[8,128,128]{2,1,0:T(8,128)S(1)}, f32[8,128,128]{2,1,0:T(8,128)S(1)}, u32[]{:S(2)}, u32[]{:S(2)}) collective-permute-start(f32[8,128,128]{2,1,0:T(8,128)S(1)} %slice.33), channel_id=1, source_target_pairs={{0,2},{1,5},{2,0},{3,7},{4,6},{5,1},{6,4},{7,3},{8,10},{9,13},{10,... | collective-permute-start | bytes 1572872 | tf_op jit(solution)/shard_map/ppermute | solution.py:248
  18.5 2.4 %collective-permute-start.3 = (f32[128,128]{1,0:T(8,128)S(1)}, f32[128,128]{1,0:T(8,128)S(1)}, u32[]{:S(2)}, u32[]{:S(2)}) collective-permute-start(f32[128,128]{1,0:T(8,128)S(1)} %add.34), channel_id=1, source_target_pairs={{0,16},{1,9},{2,18},{3,11},{4,20},{5,13},{6,22},{7,15},{8,24},{9,1... | collective-permute-start | bytes 196616 | tf_op jit(solution)/shard_map/ppermute | solution.py:248
  20.9 2.8 %collective-permute-done.3 = f32[128,128]{1,0:T(8,128)S(1)} collective-permute-done((f32[128,128]{1,0:T(8,128)S(1)}, f32[128,128]{1,0:T(8,128)S(1)}, u32[]{:S(2)}, u32[]{:S(2)}) %collective-permute-start.3) | collective-permute-done | bytes 65568 | tf_op jit(solution)/shard_map/ppermute | solution.py:248
  23.8 1.2 %collective-permute-done.4 = f32[128,128]{1,0:T(8,128)S(1)} collective-permute-done((f32[128,128]{1,0:T(8,128)S(1)}, f32[128,128]{1,0:T(8,128)S(1)}, u32[]{:S(2)}, u32[]{:S(2)}) %collective-permute-start.4) | collective-permute-done | bytes 65568 | tf_op jit(solution)/shard_map/ppermute | solution.py:248
  25.1 0.6 %collective-permute-start.5 = (f32[128,128]{1,0:T(8,128)S(1)}, f32[128,128]{1,0:T(8,128)S(1)}, u32[]{:S(2)}, u32[]{:S(2)}) collective-permute-start(f32[128,128]{1,0:T(8,128)S(1)} %add.37), channel_id=1, source_target_pairs={{0,2},{1,5},{2,0},{3,7},{4,6},{5,1},{6,4},{7,3},{8,10},{9,13},{10,... | collective-permute-start | bytes 196616 | tf_op jit(solution)/shard_map/ppermute | solution.py:248
  25.6 3.7 %collective-permute-done.5 = f32[128,128]{1,0:T(8,128)S(1)} collective-permute-done((f32[128,128]{1,0:T(8,128)S(1)}, f32[128,128]{1,0:T(8,128)S(1)}, u32[]{:S(2)}, u32[]{:S(2)}) %collective-permute-start.5) | collective-permute-done | bytes 65568 | tf_op jit(solution)/shard_map/ppermute | solution.py:248
  29.5 1.6 %collective-permute-start.6 = (f32[4,128,128]{2,1,0:T(8,128)S(1)}, f32[4,128,128]{2,1,0:T(8,128)S(1)}, u32[]{:S(2)}, u32[]{:S(2)}) collective-permute-start(f32[4,128,128]{2,1,0:T(8,128)S(1)} %slice.35), channel_id=1, source_target_pairs={{0,4},{1,3},{2,6},{3,1},{4,0},{5,7},{6,2},{7,5},{8,12},{9,11},{10,... | collective-permute-start | bytes 786440 | tf_op jit(solution)/shard_map/ppermute | solution.py:248
  31.1 0.5 %collective-permute-start.7 = (f32[128,128]{1,0:T(8,128)S(1)}, f32[128,128]{1,0:T(8,128)S(1)}, u32[]{:S(2)}, u32[]{:S(2)}) collective-permute-start(f32[128,128]{1,0:T(8,128)S(1)} %add.38), channel_id=1, source_target_pairs={{0,4},{1,3},{2,6},{3,1},{4,0},{5,7},{6,2},{7,5},{8,12},{9,11},{10,... | collective-permute-start | bytes 196616 | tf_op jit(solution)/shard_map/ppermute | solution.py:248
  31.6 5.0 %collective-permute-done.7 = f32[128,128]{1,0:T(8,128)S(1)} collective-permute-done((f32[128,128]{1,0:T(8,128)S(1)}, f32[128,128]{1,0:T(8,128)S(1)}, u32[]{:S(2)}, u32[]{:S(2)}) %collective-permute-start.7) | collective-permute-done | bytes 65568 | tf_op jit(solution)/shard_map/ppermute | solution.py:248
  36.7 1.6 %collective-permute-start.8 = (f32[2,128,128]{2,1,0:T(8,128)S(1)}, f32[2,128,128]{2,1,0:T(8,128)S(1)}, u32[]{:S(2)}, u32[]{:S(2)}) collective-permute-start(f32[2,128,128]{2,1,0:T(8,128)S(1)} %slice.36), channel_id=1, source_target_pairs={{0,8},{1,17},{2,10},{3,19},{4,12},{5,21},{6,14},{7,23},{8,0},{9,25... | collective-permute-start | bytes 393224 | tf_op jit(solution)/shard_map/ppermute | solution.py:248
  38.4 4.0 %factor.1.inverse_ref = f32[128,128]{1,0:T(8,128)S(1)} custom-call(f32[128,128]{1,0:T(8,128)S(1)} %add.40.gram_ref), custom_call_target="tpu_custom_call" | custom-call | flops 4000000000 | bytes 131072 | tf_op jit(solution)/shard_map/factor/pallas_call | solution.py:180
  42.4 2.9 %collective-permute-start.9 = (f32[128,128]{1,0:T(8,128)S(1)}, f32[128,128]{1,0:T(8,128)S(1)}, u32[]{:S(2)}, u32[]{:S(2)}) collective-permute-start(f32[128,128]{1,0:T(8,128)S(1)} %get-tuple-element.35), channel_id=1, source_target_pairs={{0,16},{1,9},{2,18},{3,11},{4,20},{5,13},{6,22},{7,15},{8,24},{9,1... | collective-permute-start | bytes 196616 | tf_op jit(solution)/shard_map/ppermute | solution.py:248
  45.4 1.1 %basis_rows.1 = f32[576,128]{1,0:T(8,128)} custom-call(f32[128,128]{1,0:T(8,128)S(1)} %factor.1.inverse_ref, f32[576,128]{1,0:T(8,128)S(1)} %get-tuple-element.33.first_ref), custom_call_target="tpu_custom_call" | custom-call | flops 113246208 | bytes 589824 | tf_op jit(solution)/shard_map/basis_rows/pallas_call | solution.py:204
  46.5 1.2 %collective-permute-done.9 = f32[128,128]{1,0:T(8,128)S(1)} collective-permute-done((f32[128,128]{1,0:T(8,128)S(1)}, f32[128,128]{1,0:T(8,128)S(1)}, u32[]{:S(2)}, u32[]{:S(2)}) %collective-permute-start.9) | collective-permute-done | bytes 65568 | tf_op jit(solution)/shard_map/ppermute | solution.py:248
  47.7 0.9 %final_rows.1 = bf16[128,128]{1,0:T(8,128)(2,1)} custom-call(f32[128,128]{1,0:T(8,128)S(1)} %factor.1.inverse_ref, f32[128,128]{1,0:T(8,128)S(1)} %add.43.sums_ref), custom_call_target="tpu_custom_call" | custom-call | tf_op jit(solution)/shard_map/final_rows/pallas_call | solution.py:225
  (20 shorter events, 0.3 us)
Async XLA Ops:
  5.2 2.1 %copy-start = (bf16[576,4096]{1,0:T(8,128)(2,1)}, bf16[576,4096]{1,0:T(8,128)(2,1)S(1)}, u32[]{:S(2)}) copy-start(bf16[576,4096]{1,0:T(8,128)(2,1)S(1)} %get-tuple-element.20.slab_ref) | copy-start | bytes 14155780
  7.3 6.5 %collective-permute-start = (f32[128,128]{1,0:T(8,128)S(1)}, f32[128,128]{1,0:T(8,128)S(1)}, u32[]{:S(2)}, u32[]{:S(2)}) collective-permute-start(f32[128,128]{1,0:T(8,128)S(1)} %get-tuple-element.21), channel_id=1, source_target_pairs={{0,8},{1,17},{2,10},{3,19},{4,12},{5,21},{6,14},{7,23},{8,0},{9,25... | collective-permute-start | bytes 196616 | tf_op jit(solution)/shard_map/ppermute | solution.py:248
  10.4 2.3 %copy-start.1 = (bf16[576,4096]{1,0:T(8,128)(2,1)S(1)}, bf16[576,4096]{1,0:T(8,128)(2,1)}, u32[]{:S(2)}) copy-start(bf16[576,4096]{1,0:T(8,128)(2,1)} %copy-done) | copy-start | bytes 14155780
  13.9 2.9 %collective-permute-start.1 = (f32[16,128,128]{2,1,0:T(8,128)S(1)}, f32[16,128,128]{2,1,0:T(8,128)S(1)}, u32[]{:S(2)}, u32[]{:S(2)}) collective-permute-start(f32[16,128,128]{2,1,0:T(8,128)S(1)} %project_sibling.1), channel_id=1, source_target_pairs={{0,1},{1,0},{2,3},{3,2},{4,5},{5,4},{6,7},{7,6},{8,9},{9,8},{10,11... | collective-permute-start | bytes 3145736 | tf_op jit(solution)/shard_map/ppermute | solution.py:248
  17.0 12.4 %collective-permute-start.2 = (f32[8,128,128]{2,1,0:T(8,128)S(1)}, f32[8,128,128]{2,1,0:T(8,128)S(1)}, u32[]{:S(2)}, u32[]{:S(2)}) collective-permute-start(f32[8,128,128]{2,1,0:T(8,128)S(1)} %slice.33), channel_id=1, source_target_pairs={{0,2},{1,5},{2,0},{3,7},{4,6},{5,1},{6,4},{7,3},{8,10},{9,13},{10,... | collective-permute-start | bytes 1572872 | tf_op jit(solution)/shard_map/ppermute | solution.py:248
  18.5 5.2 %collective-permute-start.3 = (f32[128,128]{1,0:T(8,128)S(1)}, f32[128,128]{1,0:T(8,128)S(1)}, u32[]{:S(2)}, u32[]{:S(2)}) collective-permute-start(f32[128,128]{1,0:T(8,128)S(1)} %add.34), channel_id=1, source_target_pairs={{0,16},{1,9},{2,18},{3,11},{4,20},{5,13},{6,22},{7,15},{8,24},{9,1... | collective-permute-start | bytes 196616 | tf_op jit(solution)/shard_map/ppermute | solution.py:248
  23.7 1.3 %collective-permute-start.4 = (f32[128,128]{1,0:T(8,128)S(1)}, f32[128,128]{1,0:T(8,128)S(1)}, u32[]{:S(2)}, u32[]{:S(2)}) collective-permute-start(f32[128,128]{1,0:T(8,128)S(1)} %add.36), channel_id=1, source_target_pairs={{0,1},{1,0},{2,3},{3,2},{4,5},{5,4},{6,7},{7,6},{8,9},{9,8},{10,11... | collective-permute-start | bytes 196616 | tf_op jit(solution)/shard_map/ppermute | solution.py:248
  25.1 4.3 %collective-permute-start.5 = (f32[128,128]{1,0:T(8,128)S(1)}, f32[128,128]{1,0:T(8,128)S(1)}, u32[]{:S(2)}, u32[]{:S(2)}) collective-permute-start(f32[128,128]{1,0:T(8,128)S(1)} %add.37), channel_id=1, source_target_pairs={{0,2},{1,5},{2,0},{3,7},{4,6},{5,1},{6,4},{7,3},{8,10},{9,13},{10,... | collective-permute-start | bytes 196616 | tf_op jit(solution)/shard_map/ppermute | solution.py:248
  29.5 7.2 %collective-permute-start.6 = (f32[4,128,128]{2,1,0:T(8,128)S(1)}, f32[4,128,128]{2,1,0:T(8,128)S(1)}, u32[]{:S(2)}, u32[]{:S(2)}) collective-permute-start(f32[4,128,128]{2,1,0:T(8,128)S(1)} %slice.35), channel_id=1, source_target_pairs={{0,4},{1,3},{2,6},{3,1},{4,0},{5,7},{6,2},{7,5},{8,12},{9,11},{10,... | collective-permute-start | bytes 786440 | tf_op jit(solution)/shard_map/ppermute | solution.py:248
  31.1 5.6 %collective-permute-start.7 = (f32[128,128]{1,0:T(8,128)S(1)}, f32[128,128]{1,0:T(8,128)S(1)}, u32[]{:S(2)}, u32[]{:S(2)}) collective-permute-start(f32[128,128]{1,0:T(8,128)S(1)} %add.38), channel_id=1, source_target_pairs={{0,4},{1,3},{2,6},{3,1},{4,0},{5,7},{6,2},{7,5},{8,12},{9,11},{10,... | collective-permute-start | bytes 196616 | tf_op jit(solution)/shard_map/ppermute | solution.py:248
  36.7 5.7 %collective-permute-start.8 = (f32[2,128,128]{2,1,0:T(8,128)S(1)}, f32[2,128,128]{2,1,0:T(8,128)S(1)}, u32[]{:S(2)}, u32[]{:S(2)}) collective-permute-start(f32[2,128,128]{2,1,0:T(8,128)S(1)} %slice.36), channel_id=1, source_target_pairs={{0,8},{1,17},{2,10},{3,19},{4,12},{5,21},{6,14},{7,23},{8,0},{9,25... | collective-permute-start | bytes 393224 | tf_op jit(solution)/shard_map/ppermute | solution.py:248
  42.4 5.2 %collective-permute-start.9 = (f32[128,128]{1,0:T(8,128)S(1)}, f32[128,128]{1,0:T(8,128)S(1)}, u32[]{:S(2)}, u32[]{:S(2)}) collective-permute-start(f32[128,128]{1,0:T(8,128)S(1)} %get-tuple-element.35), channel_id=1, source_target_pairs={{0,16},{1,9},{2,18},{3,11},{4,20},{5,13},{6,22},{7,15},{8,24},{9,1... | collective-permute-start | bytes 196616 | tf_op jit(solution)/shard_map/ppermute | solution.py:248

commit v6 on v5

--- a/solution.py
+++ b/solution.py
@@ -11,82 +11,11 @@
 HIGHEST = lax.Precision.HIGHEST
 LANES = 128
 VMEM_LIMIT = 24 * 1024 * 1024
-
-
-CHUNKS = 4
-
-
-def sketch_kernel(
-    slab_hbm, sketch_hbm, slab_ref, first_ref, split_ref, gram_ref, sketch_ref, slab_sem, sketch_sem
-):
-    width, rank = sketch_ref.shape
-    step = width // CHUNKS
-    copies = []
-    for k in range(CHUNKS):
-        at = pl.ds(k * step, step)
-        copies.append((
-            pltpu.make_async_copy(sketch_hbm.at[at, :], sketch_ref.at[at, :], sketch_sem.at[k]),
-            pltpu.make_async_copy(slab_hbm.at[:, at], slab_ref.at[:, at], slab_sem.at[k]),
-        ))
-    for pair in copies:
-        for copy in pair:
-            copy.start()
-    for k in range(CHUNKS):
-        for copy in copies[k]:
-            copy.wait()
-        at = pl.ds(k * step, step)
-        part = jnp.dot(slab_ref[:, at], sketch_ref[at, :], preferred_element_type=jnp.float32)
-        if k == 0:
-            first_ref[...] = part
-        else:
-            first_ref[...] += part
-    first = first_ref[...]
-    turned = first.T
-    gram_ref[...] = jnp.dot(turned, first, precision=HIGHEST, preferred_element_type=jnp.float32)
-    high = turned.astype(jnp.bfloat16)
-    split_ref[:rank] = high
-    split_ref[rank:] = (turned - high.astype(jnp.float32)).astype(jnp.bfloat16)
-
-
-def sketch_call(slab, sketch):
-    rows, width = slab.shape
-    rank = sketch.shape[1]
-    return pl.pallas_call(
-        sketch_kernel,
-        in_specs=[pl.BlockSpec(memory_space=pltpu.HBM)] * 2,
-        out_specs=[pl.BlockSpec(memory_space=pltpu.VMEM)] * 4,
-        out_shape=[
-            pltpu.VMEM((rows, width), jnp.bfloat16),
-            pltpu.VMEM((rows, rank), jnp.float32),
-            pltpu.VMEM((2 * rank, rows), jnp.bfloat16),
-            pltpu.VMEM((rank, rank), jnp.float32),
-        ],
-        scratch_shapes=[
-            pltpu.VMEM((width, rank), jnp.bfloat16),
-            pltpu.SemaphoreType.DMA((CHUNKS,)),
-            pltpu.SemaphoreType.DMA((CHUNKS,)),
-        ],
-        compiler_params=pltpu.CompilerParams(vmem_limit_bytes=VMEM_LIMIT),
-        cost_estimate=pl.CostEstimate(
-            flops=2 * rows * width * rank, bytes_accessed=rows * width * 2, transcendentals=0
-        ),
-        name="sketch_rows",
-    )(
-        pltpu.with_memory_space_constraint(slab, pltpu.HBM),
-        pltpu.with_memory_space_constraint(sketch, pltpu.HBM),
-    )
-
-
-def project_kernel(sibling, owner_ref, split_ref, slab_ref, out_ref):
+AHEAD = 2
+
+
+def project(out_ref, split_ref, columns, mine, wanted):
     rank = out_ref.shape[1]
-    owner = owner_ref[0]
-    core = lax.bitwise_and(owner, 1)
-    wanted = lax.bitwise_xor(core, sibling)
-    mine = lax.shift_right_logical(owner, 1)
-
-    def columns(q):
-        at = pl.multiple_of((2 * q + wanted) * LANES, LANES)
-        return slab_ref[:, pl.ds(at, LANES)]
 
     def place(q):
         away = lax.bitwise_xor(mine, q)
@@ -105,21 +34,130 @@
         out_ref[place(q + 1)] = sums[:, LANES:]
 
 
-def project_call(owner, split, slab, sibling):
+def rows_kernel(
+    owner_ref, slab_hbm, sketch_hbm, first_ref, gram_ref, split_ref, send_ref,
+    slab_ref, sketch_ref, slab_sem, sketch_sem,
+):
+    rows, width = slab_ref.shape
+    rank = sketch_ref.shape[1]
+    starts = list(range(0, rows, LANES))
+    copies = [
+        pltpu.make_async_copy(
+            slab_hbm.at[pl.ds(r, min(LANES, rows - r)), :],
+            slab_ref.at[pl.ds(r, min(LANES, rows - r)), :],
+            slab_sem.at[k],
+        )
+        for k, r in enumerate(starts)
+    ]
+    sketch_copy = pltpu.make_async_copy(sketch_hbm, sketch_ref, sketch_sem)
+    sketch_copy.start()
+    for copy in copies[:AHEAD]:
+        copy.start()
+    sketch_copy.wait()
+    for k, r in enumerate(starts):
+        copies[k].wait()
+        if k + AHEAD < len(starts):
+            copies[k + AHEAD].start()
+        at = pl.ds(r, min(LANES, rows - r))
+        first = jnp.dot(slab_ref[at, :], sketch_ref[...], preferred_element_type=jnp.float32)
+        first_ref[at, :] = first
+        turned = first.T
+        high = turned.astype(jnp.bfloat16)
+        split_ref[:rank, at] = high
+        split_ref[rank:, at] = (turned - high.astype(jnp.float32)).astype(jnp.bfloat16)
+        gram = jnp.dot(turned, first, precision=HIGHEST, preferred_element_type=jnp.float32)
+        if k == 0:
+            gram_ref[...] = gram
+        else:
+            gram_ref[...] += gram
+
+    owner = owner_ref[0]
+    other = 1 - lax.bitwise_and(owner, 1)
+
+    def columns(q):
+        return slab_ref[:, pl.ds(pl.multiple_of((2 * q + other) * LANES, LANES), LANES)]
+
+    project(send_ref, split_ref, columns, lax.shift_right_logical(owner, 1), other)
+
+
+def own_kernel(owner_ref, split_ref, slab_hbm, keep_ref, slab_ref, sems):
+    owner = owner_ref[0]
+    core = lax.bitwise_and(owner, 1)
+    copies = []
+    for q in range(keep_ref.shape[0]):
+        at = pl.multiple_of((2 * q + core) * LANES, LANES)
+        copies.append(
+            pltpu.make_async_copy(slab_hbm.at[:, pl.ds(at, LANES)], slab_ref.at[q], sems.at[q])
+        )
+    for copy in copies:
+        copy.start()
+
+    def columns(q):
+        copies[q].wait()
+        return slab_ref[q]
+
+    project(keep_ref, split_ref, columns, lax.shift_right_logical(owner, 1), core)
+
+
+def own_call(owner, split, slab):
     rows, width = slab.shape
     rank = split.shape[0] // 2
     vmem = pl.BlockSpec(memory_space=pltpu.VMEM)
-    return pl.pallas_call(
-        functools.partial(project_kernel, sibling),
-        in_specs=[pl.BlockSpec(memory_space=pltpu.SMEM), vmem, vmem],
+    chunks = width // (2 * LANES)
+    return pl.pallas_call(
+        own_kernel,
+        in_specs=[
+            pl.BlockSpec(memory_space=pltpu.SMEM), vmem, pl.BlockSpec(memory_space=pltpu.HBM)
+        ],
         out_specs=vmem,
-        out_shape=jax.ShapeDtypeStruct((width // (2 * LANES), rank, LANES), jnp.float32),
+        out_shape=jax.ShapeDtypeStruct((chunks, rank, LANES), jnp.float32),
+        scratch_shapes=[
+            pltpu.VMEM((chunks, rows, LANES), jnp.bfloat16),
+            pltpu.SemaphoreType.DMA((chunks,)),
+        ],
         compiler_params=pltpu.CompilerParams(vmem_limit_bytes=VMEM_LIMIT),
         cost_estimate=pl.CostEstimate(
             flops=2 * rows * width * rank, bytes_accessed=rows * width, transcendentals=0
         ),
-        name="project_sibling" if sibling else "project_own",
-    )(owner, split, pltpu.with_memory_space_constraint(slab, pltpu.VMEM))
+        name="project_own",
+    )(owner, split, pltpu.with_memory_space_constraint(slab, pltpu.HBM))
+
+
+def rows_call(owner, slab, sketch):
+    rows, width = slab.shape
+    rank = sketch.shape[1]
+    vmem = pl.BlockSpec(memory_space=pltpu.VMEM)
+    chunks = (width // (2 * LANES), rank, LANES)
+    return pl.pallas_call(
+        rows_kernel,
+        in_specs=[
+            pl.BlockSpec(memory_space=pltpu.SMEM),
+            pl.BlockSpec(memory_space=pltpu.HBM),
+            pl.BlockSpec(memory_space=pltpu.HBM),
+        ],
+        out_specs=[vmem] * 4,
+        out_shape=[
+            jax.ShapeDtypeStruct((rows, rank), jnp.float32),
+            jax.ShapeDtypeStruct((rank, rank), jnp.float32),
+            jax.ShapeDtypeStruct((2 * rank, rows), jnp.bfloat16),
+            jax.ShapeDtypeStruct(chunks, jnp.float32),
+        ],
+        scratch_shapes=[
+            pltpu.VMEM((rows, width), jnp.bfloat16),
+            pltpu.VMEM((width, rank), jnp.bfloat16),
+            pltpu.SemaphoreType.DMA((-(-rows // LANES),)),
+            pltpu.SemaphoreType.DMA,
+        ],
+        compiler_params=pltpu.CompilerParams(vmem_limit_bytes=VMEM_LIMIT),
+        cost_estimate=pl.CostEstimate(
+            flops=4 * rows * width * rank, bytes_accessed=rows * width * 2, transcendentals=0
+        ),
+        name="sketch_rows",
+    )(
+        owner,
+        pltpu.with_memory_space_constraint(slab, pltpu.HBM),
+        pltpu.with_memory_space_constraint(sketch, pltpu.HBM),
+    )
 
 
 def lane(block, at):
@@ -224,6 +262,7 @@
     rank, own = sums.shape
     return pl.pallas_call(
         functools.partial(final_kernel, factor),
+        in_specs=[pl.BlockSpec(memory_space=pltpu.VMEM)] * 2,
         out_shape=jax.ShapeDtypeStruct((own, rank), jnp.bfloat16),
         compiler_params=pltpu.CompilerParams(vmem_limit_bytes=VMEM_LIMIT),
         name="final_rows",
@@ -251,25 +290,24 @@
     tie = lax.optimization_barrier
 
     owner = lax.shift_right_logical(me, low_bits).astype(jnp.int32).reshape(1)
-    slab_near, first, split, gram = sketch_call(slab, sketch)
-    gram = gram + exchange(gram, z, zz)
-    send = project_call(owner, split, slab_near, 1)
-    send, gram = tie((send, gram))
+    first, gram, split, send = rows_call(owner, slab, sketch)
     got = exchange(send, core, core)
-    gram = gram + exchange(gram, zz, z)
-    sums = project_call(owner, split, slab_near, 0) + got
-    got = exchange(sums[8:], x, y)
     gram = gram + exchange(gram, core, core)
+    split, gram = tie((split, gram))
     gram = gram + exchange(gram, x, y)
     got, gram = tie((got, gram))
+    sums = own_call(owner, split, slab) + got
+    got = exchange(sums[8:], x, y)
+    gram = gram + exchange(gram, z, zz)
+    gram = gram + exchange(gram, zz, z)
+    got, gram = tie((got, gram))
     sums = sums[:8] + got
-    got = exchange(sums[4:], y, x)
-    gram = gram + exchange(gram, y, x)
+    got = exchange(jnp.concatenate([sums[4:], gram[None]]), y, x)
+    gram = gram + got[4]
+    sums = sums[:4] + got[:4]
+    got = exchange(sums[2:], z, zz)
     for bit in range(low_bits):
         gram = gram + swap(gram, bit)
-    got, gram = tie((got, gram))
-    sums = sums[:4] + got
-    got = exchange(sums[2:], z, zz)
     sums, gram = tie((sums, gram))
     inverse = factor_call(gram)
     got, inverse = tie((got, inverse))

time: 48.8 us -> 47.1 us (0.965)
  local copies, waits for them, and re-layouts: 4.53 us -> 0.08 us
  Pallas kernels: 12.9 us -> 15.9 us
    unnamed x4 -> x0, local copies, waits for them, and re-layouts: 4.46 us -> none
    pallas_call x4 -> x3, Pallas kernels: 7.76 us -> 10.8 us  [the longest x1 5.64 us: rows_call(): pl.pallas_call(rows_kernel, in_specs=[pl.BlockSpec(memory_space=pltpu.SME...]
    ppermute x10 -> x9, starting transfers between devices: 14.9 us -> 14.6 us  [exchange(): return lax.ppermute(array, AXES, pairs)]
    ppermute x10 -> x9, waiting for transfers between devices: 15.2 us -> 15.3 us  [exchange(): return lax.ppermute(array, AXES, pairs)]
  transfers between devices with their start and end apart: 10 -> 9, of which waited for: 6 -> 5; matrix products, arithmetic and copies ran while one was open for 0% -> 0% of each run, Pallas kernels for 15% -> 20%
where the time goes in v6:
time: 47.1 us; the launch traced here: 47 us
  Pallas kernels  15.9 us (34%)
  waiting for transfers between devices  15.3 us (32%)
  starting transfers between devices  14.6 us (31%)
  between operations  0.79 us (2%)
    ppermute x9, waiting for transfers between devices, exchange(): return lax.ppermute(array, AXES, pairs)  15.3 us
    ppermute x9, starting transfers between devices, exchange(): return lax.ppermute(array, AXES, pairs)  14.6 us
    pallas_call x1, Pallas kernels, rows_call(): pl.pallas_call(rows_kernel, in_specs=[pl.BlockSpec(memory_space=pltpu.SME...  5.64 us
    pallas_call x1, Pallas kernels, own_call(): pl.pallas_call(own_kernel, in_specs=[pl.BlockSpec(memory_space=pltpu.SMEM...  4.27 us
    pallas_call x1, Pallas kernels, factor_call(): pl.pallas_call(factor_kernel, in_specs=[pl.BlockSpec(memory_space=pltpu.V...  4.02 us
    pallas_call x1, Pallas kernels, basis_call(): pl.pallas_call(functools.partial(basis_kernel, float(total_rows) ** 0.5),...  1.11 us
  transfers between devices with their start and end apart: 9, of which 5 were waited for; matrix products, arithmetic and copies ran while one was open for 0% of the time, Pallas kernels for 20%

profile of v6, /device:TPU:0, one launch (start us, length us, event | category | flops | bytes accessed | tf_op | source)
XLA Modules:
  0.0 47.0 jit_solution(18022668807204862382)
XLA Ops:
  0.6 5.6 %sketch_rows.1 = (f32[576,128]{1,0:T(8,128)S(1)}, f32[128,128]{1,0:T(8,128)S(1)}, bf16[256,576]{1,0:T(8,128)(2,1)S(1)}, f32[16,128,128]{2,1,0:T(8,128)S(1)}) custom-call(s32[1]{0:T(128)} %bitcast.owner_ref, bf16[576,4096]{1,0:T(8,128)(2,1)} %slab_hbm.3, bf16[4096,128]{1,0:T(8,128)(2,1)} %sketch_hbm.1), custom_call_target="tpu_custom_call" | custom-call | flops 1207959552 | bytes 4718592 | tf_op jit(solution)/shard_map/sketch_rows/pallas_call | solution.py:131
  6.3 0.5 %collective-permute-start.1 = (f32[16,128,128]{2,1,0:T(8,128)S(1)}, f32[16,128,128]{2,1,0:T(8,128)S(1)}, u32[]{:S(2)}, u32[]{:S(2)}) collective-permute-start(f32[16,128,128]{2,1,0:T(8,128)S(1)} %get-tuple-element.22), channel_id=1, source_target_pairs={{0,1},{1,0},{2,3},{3,2},{4,5},{5,4},{6,7},{7,6},{8,9},{9,8},{10,11... | collective-permute-start | bytes 3145736 | tf_op jit(solution)/shard_map/ppermute | solution.py:287
  6.8 0.1 collective-permute-start
  6.9 2.3 %collective-permute-done = f32[128,128]{1,0:T(8,128)S(1)} collective-permute-done((f32[128,128]{1,0:T(8,128)S(1)}, f32[128,128]{1,0:T(8,128)S(1)}, u32[]{:S(2)}, u32[]{:S(2)}) %collective-permute-start) | collective-permute-done | bytes 65568 | tf_op jit(solution)/shard_map/ppermute | solution.py:287
  9.2 2.9 %collective-permute-start.2 = (f32[128,128]{1,0:T(8,128)S(1)}, f32[128,128]{1,0:T(8,128)S(1)}, u32[]{:S(2)}, u32[]{:S(2)}) collective-permute-start(f32[128,128]{1,0:T(8,128)S(1)} %add.34), channel_id=1, source_target_pairs={{0,2},{1,5},{2,0},{3,7},{4,6},{5,1},{6,4},{7,3},{8,10},{9,13},{10,... | collective-permute-start | bytes 196616 | tf_op jit(solution)/shard_map/ppermute | solution.py:287
  12.1 4.3 %project_own.1 = f32[16,128,128]{2,1,0:T(8,128)S(1)} custom-call(s32[1]{0:T(128)} %bitcast.owner_ref, bf16[256,576]{1,0:T(8,128)(2,1)S(1)} %get-tuple-element.21.split_ref, bf16[576,4096]{1,0:T(8,128)(2,1)} %slab_hbm.3), custom_call_target="tpu_custom_call" | custom-call | flops 603979776 | bytes 2359296 | tf_op jit(solution)/shard_map/project_own/pallas_call | solution.py:107
  16.4 0.0 collective-permute-done.2
  16.4 0.0 collective-permute-done.1
  16.4 0.1 add.36
  16.6 0.1 collective-permute-start.3
  16.7 2.1 %collective-permute-start.4 = (f32[128,128]{1,0:T(8,128)S(1)}, f32[128,128]{1,0:T(8,128)S(1)}, u32[]{:S(2)}, u32[]{:S(2)}) collective-permute-start(f32[128,128]{1,0:T(8,128)S(1)} %add.35), channel_id=1, source_target_pairs={{0,8},{1,17},{2,10},{3,19},{4,12},{5,21},{6,14},{7,23},{8,0},{9,25... | collective-permute-start | bytes 196616 | tf_op jit(solution)/shard_map/ppermute | solution.py:287
  18.8 2.8 %collective-permute-done.4 = f32[128,128]{1,0:T(8,128)S(1)} collective-permute-done((f32[128,128]{1,0:T(8,128)S(1)}, f32[128,128]{1,0:T(8,128)S(1)}, u32[]{:S(2)}, u32[]{:S(2)}) %collective-permute-start.4) | collective-permute-done | bytes 65568 | tf_op jit(solution)/shard_map/ppermute | solution.py:287
  21.6 2.5 %collective-permute-start.5 = (f32[128,128]{1,0:T(8,128)S(1)}, f32[128,128]{1,0:T(8,128)S(1)}, u32[]{:S(2)}, u32[]{:S(2)}) collective-permute-start(f32[128,128]{1,0:T(8,128)S(1)} %add.37), channel_id=1, source_target_pairs={{0,16},{1,9},{2,18},{3,11},{4,20},{5,13},{6,22},{7,15},{8,24},{9,1... | collective-permute-start | bytes 196616 | tf_op jit(solution)/shard_map/ppermute | solution.py:287
  24.1 2.7 %collective-permute-done.5 = f32[128,128]{1,0:T(8,128)S(1)} collective-permute-done((f32[128,128]{1,0:T(8,128)S(1)}, f32[128,128]{1,0:T(8,128)S(1)}, u32[]{:S(2)}, u32[]{:S(2)}) %collective-permute-start.5) | collective-permute-done | bytes 65568 | tf_op jit(solution)/shard_map/ppermute | solution.py:287
  26.9 0.1 slice_add_fusion
  27.0 1.6 %collective-permute-start.6 = (f32[5,128,128]{2,1,0:T(8,128)S(1)}, f32[5,128,128]{2,1,0:T(8,128)S(1)}, u32[]{:S(2)}, u32[]{:S(2)}) collective-permute-start(f32[5,128,128]{2,1,0:T(8,128)S(1)} %pad_maximum_fusion), channel_id=1, source_target_pairs={{0,4},{1,3},{2,6},{3,1},{4,0},{5,7},{6,2},{7,5},{8,12},{9,11},{10,... | collective-permute-start | bytes 983048 | tf_op jit(solution)/shard_map/ppermute | solution.py:287
  28.7 5.5 %collective-permute-done.6 = f32[5,128,128]{2,1,0:T(8,128)S(1)} collective-permute-done((f32[5,128,128]{2,1,0:T(8,128)S(1)}, f32[5,128,128]{2,1,0:T(8,128)S(1)}, u32[]{:S(2)}, u32[]{:S(2)}) %collective-permute-start.6) | collective-permute-done | bytes 327712 | tf_op jit(solution)/shard_map/ppermute | solution.py:287
  34.2 1.8 %collective-permute-start.7 = (f32[2,128,128]{2,1,0:T(8,128)S(1)}, f32[2,128,128]{2,1,0:T(8,128)S(1)}, u32[]{:S(2)}, u32[]{:S(2)}) collective-permute-start(f32[2,128,128]{2,1,0:T(8,128)S(1)} %slice.46), channel_id=1, source_target_pairs={{0,8},{1,17},{2,10},{3,19},{4,12},{5,21},{6,14},{7,23},{8,0},{9,25... | collective-permute-start | bytes 393224 | tf_op jit(solution)/shard_map/ppermute | solution.py:287
  36.0 4.0 %factor.1.inverse_ref = f32[128,128]{1,0:T(8,128)S(1)} custom-call(f32[128,128]{1,0:T(8,128)S(1)} %fusion.gram_ref), custom_call_target="tpu_custom_call" | custom-call | flops 4000000000 | bytes 131072 | tf_op jit(solution)/shard_map/factor/pallas_call | solution.py:218
  40.1 0.0 collective-permute-done.7
  40.1 2.9 %collective-permute-start.8 = (f32[128,128]{1,0:T(8,128)S(1)}, f32[128,128]{1,0:T(8,128)S(1)}, u32[]{:S(2)}, u32[]{:S(2)}) collective-permute-start(f32[128,128]{1,0:T(8,128)S(1)} %get-tuple-element.35), channel_id=1, source_target_pairs={{0,16},{1,9},{2,18},{3,11},{4,20},{5,13},{6,22},{7,15},{8,24},{9,1... | collective-permute-start | bytes 196616 | tf_op jit(solution)/shard_map/ppermute | solution.py:287
  43.0 1.1 %basis_rows.1 = f32[576,128]{1,0:T(8,128)} custom-call(f32[128,128]{1,0:T(8,128)S(1)} %factor.1.inverse_ref, f32[576,128]{1,0:T(8,128)S(1)} %get-tuple-element.33.first_ref), custom_call_target="tpu_custom_call" | custom-call | flops 113246208 | bytes 589824 | tf_op jit(solution)/shard_map/basis_rows/pallas_call | solution.py:242
  44.1 1.9 %collective-permute-done.8 = f32[128,128]{1,0:T(8,128)S(1)} collective-permute-done((f32[128,128]{1,0:T(8,128)S(1)}, f32[128,128]{1,0:T(8,128)S(1)}, u32[]{:S(2)}, u32[]{:S(2)}) %collective-permute-start.8) | collective-permute-done | bytes 65568 | tf_op jit(solution)/shard_map/ppermute | solution.py:287
  46.1 0.9 %final_rows.1 = bf16[128,128]{1,0:T(8,128)(2,1)} custom-call(f32[128,128]{1,0:T(8,128)S(1)} %factor.1.inverse_ref, f32[128,128]{1,0:T(8,128)S(1)} %add.43.sums_ref), custom_call_target="tpu_custom_call" | custom-call | tf_op jit(solution)/shard_map/final_rows/pallas_call | solution.py:263
  (14 shorter events, 0.2 us)
Async XLA Ops:
  6.3 10.1 %collective-permute-start.1 = (f32[16,128,128]{2,1,0:T(8,128)S(1)}, f32[16,128,128]{2,1,0:T(8,128)S(1)}, u32[]{:S(2)}, u32[]{:S(2)}) collective-permute-start(f32[16,128,128]{2,1,0:T(8,128)S(1)} %get-tuple-element.22), channel_id=1, source_target_pairs={{0,1},{1,0},{2,3},{3,2},{4,5},{5,4},{6,7},{7,6},{8,9},{9,8},{10,11... | collective-permute-start | bytes 3145736 | tf_op jit(solution)/shard_map/ppermute | solution.py:287
  6.8 2.4 %collective-permute-start = (f32[128,128]{1,0:T(8,128)S(1)}, f32[128,128]{1,0:T(8,128)S(1)}, u32[]{:S(2)}, u32[]{:S(2)}) collective-permute-start(f32[128,128]{1,0:T(8,128)S(1)} %get-tuple-element.20), channel_id=1, source_target_pairs={{0,1},{1,0},{2,3},{3,2},{4,5},{5,4},{6,7},{7,6},{8,9},{9,8},{10,11... | collective-permute-start | bytes 196616 | tf_op jit(solution)/shard_map/ppermute | solution.py:287
  9.2 7.2 %collective-permute-start.2 = (f32[128,128]{1,0:T(8,128)S(1)}, f32[128,128]{1,0:T(8,128)S(1)}, u32[]{:S(2)}, u32[]{:S(2)}) collective-permute-start(f32[128,128]{1,0:T(8,128)S(1)} %add.34), channel_id=1, source_target_pairs={{0,2},{1,5},{2,0},{3,7},{4,6},{5,1},{6,4},{7,3},{8,10},{9,13},{10,... | collective-permute-start | bytes 196616 | tf_op jit(solution)/shard_map/ppermute | solution.py:287
  16.6 10.3 %collective-permute-start.3 = (f32[8,128,128]{2,1,0:T(8,128)S(1)}, f32[8,128,128]{2,1,0:T(8,128)S(1)}, u32[]{:S(2)}, u32[]{:S(2)}) collective-permute-start(f32[8,128,128]{2,1,0:T(8,128)S(1)} %slice.41), channel_id=1, source_target_pairs={{0,2},{1,5},{2,0},{3,7},{4,6},{5,1},{6,4},{7,3},{8,10},{9,13},{10,... | collective-permute-start | bytes 1572872 | tf_op jit(solution)/shard_map/ppermute | solution.py:287
  16.7 4.9 %collective-permute-start.4 = (f32[128,128]{1,0:T(8,128)S(1)}, f32[128,128]{1,0:T(8,128)S(1)}, u32[]{:S(2)}, u32[]{:S(2)}) collective-permute-start(f32[128,128]{1,0:T(8,128)S(1)} %add.35), channel_id=1, source_target_pairs={{0,8},{1,17},{2,10},{3,19},{4,12},{5,21},{6,14},{7,23},{8,0},{9,25... | collective-permute-start | bytes 196616 | tf_op jit(solution)/shard_map/ppermute | solution.py:287
  21.6 5.2 %collective-permute-start.5 = (f32[128,128]{1,0:T(8,128)S(1)}, f32[128,128]{1,0:T(8,128)S(1)}, u32[]{:S(2)}, u32[]{:S(2)}) collective-permute-start(f32[128,128]{1,0:T(8,128)S(1)} %add.37), channel_id=1, source_target_pairs={{0,16},{1,9},{2,18},{3,11},{4,20},{5,13},{6,22},{7,15},{8,24},{9,1... | collective-permute-start | bytes 196616 | tf_op jit(solution)/shard_map/ppermute | solution.py:287
  27.0 7.1 %collective-permute-start.6 = (f32[5,128,128]{2,1,0:T(8,128)S(1)}, f32[5,128,128]{2,1,0:T(8,128)S(1)}, u32[]{:S(2)}, u32[]{:S(2)}) collective-permute-start(f32[5,128,128]{2,1,0:T(8,128)S(1)} %pad_maximum_fusion), channel_id=1, source_target_pairs={{0,4},{1,3},{2,6},{3,1},{4,0},{5,7},{6,2},{7,5},{8,12},{9,11},{10,... | collective-permute-start | bytes 983048 | tf_op jit(solution)/shard_map/ppermute | solution.py:287
  34.2 5.8 %collective-permute-start.7 = (f32[2,128,128]{2,1,0:T(8,128)S(1)}, f32[2,128,128]{2,1,0:T(8,128)S(1)}, u32[]{:S(2)}, u32[]{:S(2)}) collective-permute-start(f32[2,128,128]{2,1,0:T(8,128)S(1)} %slice.46), channel_id=1, source_target_pairs={{0,8},{1,17},{2,10},{3,19},{4,12},{5,21},{6,14},{7,23},{8,0},{9,25... | collective-permute-start | bytes 393224 | tf_op jit(solution)/shard_map/ppermute | solution.py:287
  40.1 5.9 %collective-permute-start.8 = (f32[128,128]{1,0:T(8,128)S(1)}, f32[128,128]{1,0:T(8,128)S(1)}, u32[]{:S(2)}, u32[]{:S(2)}) collective-permute-start(f32[128,128]{1,0:T(8,128)S(1)} %get-tuple-element.35), channel_id=1, source_target_pairs={{0,16},{1,9},{2,18},{3,11},{4,20},{5,13},{6,22},{7,15},{8,24},{9,1... | collective-permute-start | bytes 196616 | tf_op jit(solution)/shard_map/ppermute | solution.py:287

commit v7 on v6

v7 whole, which is shorter than its diff:
```python
import functools

import jax
import jax.numpy as jnp
from jax import lax
from jax.experimental import pallas as pl
from jax.experimental.pallas import tpu as pltpu
from jax.sharding import PartitionSpec as P

AXES = ("rows", "grp")
HIGHEST = lax.Precision.HIGHEST
LANES = 128
VMEM_LIMIT = 24 * 1024 * 1024
AHEAD = 2


def rows_kernel(
    owner_ref, slab_hbm, sketch_hbm, first_ref, gram_ref, send_ref, keep_ref,
    slab_ref, sketch_ref, split_ref, slab_sem, sketch_sem,
):
    rows, width = slab_ref.shape
    rank = sketch_ref.shape[1]
    starts = list(range(0, rows, LANES))
    copies = [
        pltpu.make_async_copy(
            slab_hbm.at[pl.ds(r, min(LANES, rows - r)), :],
            slab_ref.at[pl.ds(r, min(LANES, rows - r)), :],
            slab_sem.at[k],
        )
        for k, r in enumerate(starts)
    ]
    sketch_copy = pltpu.make_async_copy(sketch_hbm, sketch_ref, sketch_sem)
    sketch_copy.start()
    for copy in copies[:AHEAD]:
        copy.start()
    sketch_copy.wait()
    for k, r in enumerate(starts):
        copies[k].wait()
        if k + AHEAD < len(starts):
            copies[k + AHEAD].start()
        at = pl.ds(r, min(LANES, rows - r))
        first = jnp.dot(slab_ref[at, :], sketch_ref[...], preferred_element_type=jnp.float32)
        first_ref[at, :] = first
        turned = first.T
        high = turned.astype(jnp.bfloat16)
        split_ref[:rank, at] = high
        split_ref[rank:, at] = (turned - high.astype(jnp.float32)).astype(jnp.bfloat16)
        gram = jnp.dot(turned, first, precision=HIGHEST, preferred_element_type=jnp.float32)
        if k == 0:
            gram_ref[...] = gram
        else:
            gram_ref[...] += gram

    owner = owner_ref[0]
    core = lax.bitwise_and(owner, 1)
    mine = lax.shift_right_logical(owner, 1)

    def project(out_ref, wanted):
        def columns(q):
            at = pl.multiple_of((2 * q + wanted) * LANES, LANES)
            return slab_ref[:, pl.ds(at, LANES)]

        def place(q):
            away = lax.bitwise_xor(mine, q)
            bit = [lax.bitwise_and(lax.shift_right_logical(away, i), 1) for i in range(4)]
            straight = 8 * bit[0] + 4 * bit[1]
            turned = 8 * bit[1] + 4 * bit[0]
            return jnp.where(wanted == 0, straight, turned) + 2 * bit[3] + bit[2]

        for q in range(0, out_ref.shape[0], 2):
            both = jnp.dot(
                split_ref[...], jnp.concatenate([columns(q), columns(q + 1)], axis=1),
                preferred_element_type=jnp.float32,
            )
            sums = both[:rank] + both[rank:]
            out_ref[place(q)] = sums[:, :LANES]
            out_ref[place(q + 1)] = sums[:, LANES:]

    project(send_ref, 1 - core)
    project(keep_ref, core)


def rows_call(owner, slab, sketch):
    rows, width = slab.shape
    rank = sketch.shape[1]
    vmem = pl.BlockSpec(memory_space=pltpu.VMEM)
    chunks = (width // (2 * LANES), rank, LANES)
    return pl.pallas_call(
        rows_kernel,
        in_specs=[
            pl.BlockSpec(memory_space=pltpu.SMEM),
            pl.BlockSpec(memory_space=pltpu.HBM),
            pl.BlockSpec(memory_space=pltpu.HBM),
        ],
        out_specs=[vmem] * 4,
        out_shape=[
            jax.ShapeDtypeStruct((rows, rank), jnp.float32),
            jax.ShapeDtypeStruct((rank, rank), jnp.float32),
            jax.ShapeDtypeStruct(chunks, jnp.float32),
            jax.ShapeDtypeStruct(chunks, jnp.float32),
        ],
        scratch_shapes=[
            pltpu.VMEM((rows, width), jnp.bfloat16),
            pltpu.VMEM((width, rank), jnp.bfloat16),
            pltpu.VMEM((2 * rank, rows), jnp.bfloat16),
            pltpu.SemaphoreType.DMA((-(-rows // LANES),)),
            pltpu.SemaphoreType.DMA,
        ],
        compiler_params=pltpu.CompilerParams(vmem_limit_bytes=VMEM_LIMIT),
        cost_estimate=pl.CostEstimate(
            flops=6 * rows * width * rank, bytes_accessed=rows * width * 2, transcendentals=0
        ),
        name="project_rows",
    )(
        owner,
        pltpu.with_memory_space_constraint(slab, pltpu.HBM),
        pltpu.with_memory_space_constraint(sketch, pltpu.HBM),
    )


def lane(block, at):
    return jnp.broadcast_to(block[:, at : at + 1], block.shape)


def sublane(block, at):
    return jnp.broadcast_to(block[at : at + 1, :], block.shape)


def inverse_factor(gram_ref, inverse_ref):
    size = gram_ref.shape[0]
    blocks = size // 8
    left = [gram_ref[8 * i : 8 * i + 8, :] for i in range(blocks)]
    row_at = lax.broadcasted_iota(jnp.int32, (8, size), 0)
    lane_at = lax.broadcasted_iota(jnp.int32, (8, size), 1)
    right = [jnp.where(lane_at == row_at + 8 * i, 1.0, 0.0).astype(jnp.float32) for i in range(blocks)]
    for p in range(blocks):
        column = [lane(left[p], 8 * p + k) for k in range(8)]
        entry = {(r, c): sublane(column[c], r) for c in range(8) for r in range(c, 8)}
        scale, lower = [], {}
        for k in range(8):
            scale.append(lax.rsqrt(entry[k, k]))
            for r in range(k + 1, 8):
                lower[r, k] = entry[r, k] * scale[k]
            for c in range(k + 1, 8):
                for r in range(c, 8):
                    entry[r, c] = entry[r, c] - lower[r, k] * lower[c, k]
        tops, sides = [], []
        for k in range(8):
            top, side = sublane(left[p], k), sublane(right[p], k)
            for j in range(k):
                top = top - lower[k, j] * tops[j]
                side = side - lower[k, j] * sides[j]
            tops.append(top * scale[k])
            sides.append(side * scale[k])
        result = sides[0]
        for k in range(1, 8):
            result = jnp.where(row_at == k, sides[k], result)
        inverse_ref[8 * p : 8 * p + 8, :] = result
        for i in range(p + 1, blocks):
            weights = []
            for k in range(8):
                weight = lane(left[i], 8 * p + k)
                for j in range(k):
                    weight = weight - lower[k, j] * weights[j]
                weights.append(weight * scale[k])
            for k in range(8):
                left[i] = left[i] - weights[k] * tops[k]
                right[i] = right[i] - weights[k] * sides[k]


def factor_kernel(gram_ref, inverse_ref):
    inverse_factor(gram_ref, inverse_ref)


def factor_call(gram):
    return pl.pallas_call(
        factor_kernel,
        in_specs=[pl.BlockSpec(memory_space=pltpu.VMEM)],
        out_specs=pl.BlockSpec(memory_space=pltpu.VMEM),
        out_shape=jax.ShapeDtypeStruct(gram.shape, jnp.float32),
        compiler_params=pltpu.CompilerParams(vmem_limit_bytes=VMEM_LIMIT),
        cost_estimate=pl.CostEstimate(
            flops=4000000000, bytes_accessed=gram.size * 8, transcendentals=gram.shape[0]
        ),
        name="factor",
    )(gram)


def finish_kernel(basis_factor, factor, inverse_ref, first_ref, sums_ref, *refs):
    basis_ref, out_ref = refs[-2:]
    inverse = inverse_ref[...]
    one = lax.dot_general(
        first_ref[...], inverse, (((1,), (1,)), ((), ())),
        precision=HIGHEST, preferred_element_type=jnp.float32,
    )
    basis_ref[...] = one * basis_factor
    sums = sums_ref[...]
    for got_ref in refs[:-2]:
        sums = sums + got_ref[...]
    result = jnp.dot(inverse, sums, precision=HIGHEST, preferred_element_type=jnp.float32)
    out_ref[...] = (result.T * factor).astype(out_ref.dtype)


def finish_call(inverse, first, total_rows, factor, sums):
    rows, rank = first.shape
    own = sums[0].shape[1]
    return pl.pallas_call(
        functools.partial(finish_kernel, float(total_rows) ** 0.5, factor),
        in_specs=[pl.BlockSpec(memory_space=pltpu.VMEM)] * (2 + len(sums)),
        out_shape=[
            jax.ShapeDtypeStruct((rows, rank), jnp.float32),
            jax.ShapeDtypeStruct((own, rank), jnp.bfloat16),
        ],
        compiler_params=pltpu.CompilerParams(vmem_limit_bytes=VMEM_LIMIT),
        cost_estimate=pl.CostEstimate(
            flops=12 * rows * rank * rank, bytes_accessed=rows * rank * 8, transcendentals=0
        ),
        name="finish",
    )(inverse, first, *sums)


def local(slab, sketch):
    rows_loc, width = slab.shape
    devices_all = lax.axis_size(AXES)
    own = width // devices_all
    bits = devices_all.bit_length() - 1
    low_bits = bits - ((width // LANES).bit_length() - 1)
    total_rows = rows_loc * devices_all
    me = lax.axis_index(AXES)

    core, x, y, z, zz = [1 << bit for bit in range(low_bits, low_bits + 5)]
    tie = lax.optimization_barrier

    def exchange(array, away, away_odd=None):
        odd = away if away_odd is None else away_odd
        pairs = [(i, i ^ (odd if i & core else away)) for i in range(devices_all)]
        return lax.ppermute(array, AXES, pairs)

    owner = lax.shift_right_logical(me, low_bits).astype(jnp.int32).reshape(1)
    first, gram, send, keep = rows_call(owner, slab, sketch)
    got, gram = tie((exchange(send, core), gram + exchange(gram, core)))
    sums = keep + got
    got = exchange(sums[8:], x, y)
    over_z = [exchange(gram, away) for away in (z | zz, zz, z)]
    gram = (gram + over_z[2]) + (over_z[1] + over_z[0])
    got, gram = tie((got, gram))
    sums = sums[:8] + got
    got = exchange(jnp.concatenate([sums[4:], gram[None]]), y, x)
    sums = sums[:4] + got[:4]
    gram = gram + got[4]
    gram = gram + exchange(gram, x, y)
    over_z = [exchange(sums[i], away) for i, away in ((3, z | zz), (2, zz), (1, z))]
    for bit in range(low_bits):
        gram = gram + exchange(gram, 1 << bit)
    sums, gram = tie((sums, gram))
    inverse = factor_call(gram)
    sums = [sums[0], *over_z]
    if low_bits > 0:
        sums = sum(sums)
        for bit in reversed(range(low_bits)):
            half = sums.shape[1] // 2
            mine = lax.rem(lax.shift_right_logical(me, bit), 2) == 1
            left, right = sums[:, :half], sums[:, half:]
            sums = jnp.where(mine, right, left) + exchange(jnp.where(mine, left, right), 1 << bit)
        sums = [sums]
    factor = (float(width) / float(total_rows)) ** 0.5
    return tuple(finish_call(inverse, first, total_rows, factor, sums))


def solution(mesh):
    return jax.shard_map(
        local,
        mesh=mesh,
        in_specs=(P(AXES, None), P()),
        out_specs=(P(AXES, None), P(AXES, None)),
        check_vma=False,
    )
```

time: 47.1 us -> 41.7 us (0.89)
  Pallas kernels: 15.9 us -> 11.7 us
  waiting for transfers between devices: 15.3 us -> 13.7 us
  starting transfers between devices: 14.6 us -> 15.1 us
    pallas_call x3 -> x1, Pallas kernels: 6.29 us -> 1.17 us  [finish_call(): pl.pallas_call(functools.partial(finish_kernel, float(total_rows) ** 0.5,...]
    ppermute x9 -> x11, waiting for transfers between devices: 15.3 us -> 13.7 us  [exchange(): return lax.ppermute(array, AXES, pairs)]
    pallas_call x1, Pallas kernels: 5.64 us -> 6.47 us  [rows_call(): pl.pallas_call(rows_kernel, in_specs=[pl.BlockSpec(memory_space=pltpu.SME...]
    ppermute x9 -> x11, starting transfers between devices: 14.6 us -> 15.1 us  [exchange(): return lax.ppermute(array, AXES, pairs)]
  transfers between devices with their start and end apart: 9 -> 11, of which waited for: 5 -> 5; matrix products, arithmetic and copies ran while one was open for 0% -> 0% of each run, Pallas kernels for 20% -> 10%
where the time goes in v7:
time: 41.7 us; the launch traced here: 41.5 us
  starting transfers between devices  15.1 us (36%)
  waiting for transfers between devices  13.7 us (33%)
  Pallas kernels  11.7 us (28%)
  between operations  0.75 us (2%)
    ppermute x11, starting transfers between devices, exchange(): return lax.ppermute(array, AXES, pairs)  15.1 us
    ppermute x11, waiting for transfers between devices, exchange(): return lax.ppermute(array, AXES, pairs)  13.7 us
    pallas_call x1, Pallas kernels, rows_call(): pl.pallas_call(rows_kernel, in_specs=[pl.BlockSpec(memory_space=pltpu.SME...  6.47 us
    pallas_call x1, Pallas kernels, factor_call(): pl.pallas_call(factor_kernel, in_specs=[pl.BlockSpec(memory_space=pltpu.V...  4.02 us
    pallas_call x1, Pallas kernels, finish_call(): pl.pallas_call(functools.partial(finish_kernel, float(total_rows) ** 0.5,...  1.17 us
  transfers between devices with their start and end apart: 11, of which 5 were waited for; matrix products, arithmetic and copies ran while one was open for 0% of the time, Pallas kernels for 10%

profile of v7, /device:TPU:0, one launch (start us, length us, event | category | flops | bytes accessed | tf_op | source)
XLA Modules:
  0.0 41.5 jit_solution(8751480616377319584)
XLA Ops:
  0.6 6.5 %project_rows.1 = (f32[576,128]{1,0:T(8,128)S(1)}, f32[128,128]{1,0:T(8,128)S(1)}, f32[16,128,128]{2,1,0:T(8,128)S(1)}, f32[16,128,128]{2,1,0:T(8,128)S(1)}) custom-call(s32[1]{0:T(128)} %bitcast.owner_ref, bf16[576,4096]{1,0:T(8,128)(2,1)} %slab_hbm.1, bf16[4096,128]{1,0:T(8,128)(2,1)} %sketch_hbm.1), custom_call_target="tpu_custom_call" | custom-call | flops 1811939328 | bytes 4718592 | tf_op jit(solution)/shard_map/project_rows/pallas_call | solution.py:88
  7.1 0.5 %collective-permute-start = (f32[16,128,128]{2,1,0:T(8,128)S(1)}, f32[16,128,128]{2,1,0:T(8,128)S(1)}, u32[]{:S(2)}, u32[]{:S(2)}) collective-permute-start(f32[16,128,128]{2,1,0:T(8,128)S(1)} %get-tuple-element.13), channel_id=1, source_target_pairs={{0,1},{1,0},{2,3},{3,2},{4,5},{5,4},{6,7},{7,6},{8,9},{9,8},{10,11... | collective-permute-start | bytes 3145736 | tf_op jit(solution)/shard_map/ppermute | solution.py:237
  7.6 0.1 collective-permute-start.1
  7.7 2.3 %collective-permute-done.1 = f32[128,128]{1,0:T(8,128)S(1)} collective-permute-done((f32[128,128]{1,0:T(8,128)S(1)}, f32[128,128]{1,0:T(8,128)S(1)}, u32[]{:S(2)}, u32[]{:S(2)}) %collective-permute-start.1) | collective-permute-done | bytes 65568 | tf_op jit(solution)/shard_map/ppermute | solution.py:237
  10.0 0.0 collective-permute-done
  10.0 0.1 add.32
  10.2 2.9 %collective-permute-start.2 = (f32[8,128,128]{2,1,0:T(8,128)S(1)}, f32[8,128,128]{2,1,0:T(8,128)S(1)}, u32[]{:S(2)}, u32[]{:S(2)}) collective-permute-start(f32[8,128,128]{2,1,0:T(8,128)S(1)} %slice.41), channel_id=1, source_target_pairs={{0,2},{1,5},{2,0},{3,7},{4,6},{5,1},{6,4},{7,3},{8,10},{9,13},{10,... | collective-permute-start | bytes 1572872 | tf_op jit(solution)/shard_map/ppermute | solution.py:237
  13.1 3.6 %collective-permute-start.5 = (f32[128,128]{1,0:T(8,128)S(1)}, f32[128,128]{1,0:T(8,128)S(1)}, u32[]{:S(2)}, u32[]{:S(2)}) collective-permute-start(f32[128,128]{1,0:T(8,128)S(1)} %add.31), channel_id=1, source_target_pairs={{0,24},{1,25},{2,26},{3,27},{4,28},{5,29},{6,30},{7,31},{8,16},{9,... | collective-permute-start | bytes 196616 | tf_op jit(solution)/shard_map/ppermute | solution.py:237
  16.7 0.0 collective-permute-start.4
  16.8 0.8 %collective-permute-start.3 = (f32[128,128]{1,0:T(8,128)S(1)}, f32[128,128]{1,0:T(8,128)S(1)}, u32[]{:S(2)}, u32[]{:S(2)}) collective-permute-start(f32[128,128]{1,0:T(8,128)S(1)} %add.31), channel_id=1, source_target_pairs={{0,8},{1,9},{2,10},{3,11},{4,12},{5,13},{6,14},{7,15},{8,0},{9,1},... | collective-permute-start | bytes 196616 | tf_op jit(solution)/shard_map/ppermute | solution.py:237
  17.5 2.1 %collective-permute-done.5 = f32[128,128]{1,0:T(8,128)S(1)} collective-permute-done((f32[128,128]{1,0:T(8,128)S(1)}, f32[128,128]{1,0:T(8,128)S(1)}, u32[]{:S(2)}, u32[]{:S(2)}) %collective-permute-start.5) | collective-permute-done | bytes 65568 | tf_op jit(solution)/shard_map/ppermute | solution.py:237
  19.6 2.8 %collective-permute-done.4 = f32[128,128]{1,0:T(8,128)S(1)} collective-permute-done((f32[128,128]{1,0:T(8,128)S(1)}, f32[128,128]{1,0:T(8,128)S(1)}, u32[]{:S(2)}, u32[]{:S(2)}) %collective-permute-start.4) | collective-permute-done | bytes 65568 | tf_op jit(solution)/shard_map/ppermute | solution.py:237
  22.4 0.0 collective-permute-done.3
  22.4 0.0 collective-permute-done.2
  22.4 0.1 slice_add_fusion
  22.6 1.3 %collective-permute-start.6 = (f32[5,128,128]{2,1,0:T(8,128)S(1)}, f32[5,128,128]{2,1,0:T(8,128)S(1)}, u32[]{:S(2)}, u32[]{:S(2)}) collective-permute-start(f32[5,128,128]{2,1,0:T(8,128)S(1)} %pad_maximum_fusion), channel_id=1, source_target_pairs={{0,4},{1,3},{2,6},{3,1},{4,0},{5,7},{6,2},{7,5},{8,12},{9,11},{10,... | collective-permute-start | bytes 983048 | tf_op jit(solution)/shard_map/ppermute | solution.py:237
  23.9 5.8 %collective-permute-done.6 = f32[5,128,128]{2,1,0:T(8,128)S(1)} collective-permute-done((f32[5,128,128]{2,1,0:T(8,128)S(1)}, f32[5,128,128]{2,1,0:T(8,128)S(1)}, u32[]{:S(2)}, u32[]{:S(2)}) %collective-permute-start.6) | collective-permute-done | bytes 327712 | tf_op jit(solution)/shard_map/ppermute | solution.py:237
  29.7 1.4 %collective-permute-start.7 = (f32[128,128]{1,0:T(8,128)S(1)}, f32[128,128]{1,0:T(8,128)S(1)}, u32[]{:S(2)}, u32[]{:S(2)}) collective-permute-start(f32[128,128]{1,0:T(8,128)S(1)} %fusion), channel_id=1, source_target_pairs={{0,2},{1,5},{2,0},{3,7},{4,6},{5,1},{6,4},{7,3},{8,10},{9,13},{10,... | collective-permute-start | bytes 196616 | tf_op jit(solution)/shard_map/ppermute | solution.py:237
  31.2 1.3 %collective-permute-start.10 = (f32[128,128]{1,0:T(8,128)S(1)}, f32[128,128]{1,0:T(8,128)S(1)}, u32[]{:S(2)}, u32[]{:S(2)}) collective-permute-start(f32[128,128]{1,0:T(8,128)S(1)} %get-tuple-element.22), channel_id=1, source_target_pairs={{0,8},{1,9},{2,10},{3,11},{4,12},{5,13},{6,14},{7,15},{8,0},{9,1},... | collective-permute-start | bytes 196616 | tf_op jit(solution)/shard_map/ppermute | solution.py:237
  32.5 1.8 %collective-permute-start.9 = (f32[128,128]{1,0:T(8,128)S(1)}, f32[128,128]{1,0:T(8,128)S(1)}, u32[]{:S(2)}, u32[]{:S(2)}) collective-permute-start(f32[128,128]{1,0:T(8,128)S(1)} %get-tuple-element.23), channel_id=1, source_target_pairs={{0,16},{1,17},{2,18},{3,19},{4,20},{5,21},{6,22},{7,23},{8,24},{9,... | collective-permute-start | bytes 196616 | tf_op jit(solution)/shard_map/ppermute | solution.py:237
  34.3 1.3 %collective-permute-start.8 = (f32[128,128]{1,0:T(8,128)S(1)}, f32[128,128]{1,0:T(8,128)S(1)}, u32[]{:S(2)}, u32[]{:S(2)}) collective-permute-start(f32[128,128]{1,0:T(8,128)S(1)} %get-tuple-element.24), channel_id=1, source_target_pairs={{0,24},{1,25},{2,26},{3,27},{4,28},{5,29},{6,30},{7,31},{8,16},{9,... | collective-permute-start | bytes 196616 | tf_op jit(solution)/shard_map/ppermute | solution.py:237
  35.7 4.0 %factor.1.inverse_ref = f32[128,128]{1,0:T(8,128)S(1)} custom-call(f32[128,128]{1,0:T(8,128)S(1)} %add.39.gram_ref), custom_call_target="tpu_custom_call" | custom-call | flops 4000000000 | bytes 131072 | tf_op jit(solution)/shard_map/factor/pallas_call | solution.py:176
  39.7 0.6 %collective-permute-done.8.refs_0_ = f32[128,128]{1,0:T(8,128)S(1)} collective-permute-done((f32[128,128]{1,0:T(8,128)S(1)}, f32[128,128]{1,0:T(8,128)S(1)}, u32[]{:S(2)}, u32[]{:S(2)}) %collective-permute-start.8) | collective-permute-done | bytes 65568 | tf_op jit(solution)/shard_map/ppermute | solution.py:237
  40.4 1.2 %finish.1 = (f32[576,128]{1,0:T(8,128)}, bf16[128,128]{1,0:T(8,128)(2,1)}) custom-call(f32[128,128]{1,0:T(8,128)S(1)} %factor.1.inverse_ref, f32[576,128]{1,0:T(8,128)S(1)} %get-tuple-element.20.first_ref, f32[128,128]{1,0:T(8,128)S(1)} %slice_bitcast_fusion.4.sums_ref, f32[128,128]{1,0:T(8,128)S(1)} %collective-permute-done.8.refs_0_, ...), custom_call_target="tpu_custom_call" | custom-call | flops 113246208 | bytes 589824 | tf_op jit(solution)/shard_map/finish/pallas_call | solution.py:207
  (13 shorter events, 0.2 us)
Async XLA Ops:
  7.1 2.9 %collective-permute-start = (f32[16,128,128]{2,1,0:T(8,128)S(1)}, f32[16,128,128]{2,1,0:T(8,128)S(1)}, u32[]{:S(2)}, u32[]{:S(2)}) collective-permute-start(f32[16,128,128]{2,1,0:T(8,128)S(1)} %get-tuple-element.13), channel_id=1, source_target_pairs={{0,1},{1,0},{2,3},{3,2},{4,5},{5,4},{6,7},{7,6},{8,9},{9,8},{10,11... | collective-permute-start | bytes 3145736 | tf_op jit(solution)/shard_map/ppermute | solution.py:237
  7.6 2.4 %collective-permute-start.1 = (f32[128,128]{1,0:T(8,128)S(1)}, f32[128,128]{1,0:T(8,128)S(1)}, u32[]{:S(2)}, u32[]{:S(2)}) collective-permute-start(f32[128,128]{1,0:T(8,128)S(1)} %get-tuple-element.14), channel_id=1, source_target_pairs={{0,1},{1,0},{2,3},{3,2},{4,5},{5,4},{6,7},{7,6},{8,9},{9,8},{10,11... | collective-permute-start | bytes 196616 | tf_op jit(solution)/shard_map/ppermute | solution.py:237
  10.2 12.2 %collective-permute-start.2 = (f32[8,128,128]{2,1,0:T(8,128)S(1)}, f32[8,128,128]{2,1,0:T(8,128)S(1)}, u32[]{:S(2)}, u32[]{:S(2)}) collective-permute-start(f32[8,128,128]{2,1,0:T(8,128)S(1)} %slice.41), channel_id=1, source_target_pairs={{0,2},{1,5},{2,0},{3,7},{4,6},{5,1},{6,4},{7,3},{8,10},{9,13},{10,... | collective-permute-start | bytes 1572872 | tf_op jit(solution)/shard_map/ppermute | solution.py:237
  13.1 6.5 %collective-permute-start.5 = (f32[128,128]{1,0:T(8,128)S(1)}, f32[128,128]{1,0:T(8,128)S(1)}, u32[]{:S(2)}, u32[]{:S(2)}) collective-permute-start(f32[128,128]{1,0:T(8,128)S(1)} %add.31), channel_id=1, source_target_pairs={{0,24},{1,25},{2,26},{3,27},{4,28},{5,29},{6,30},{7,31},{8,16},{9,... | collective-permute-start | bytes 196616 | tf_op jit(solution)/shard_map/ppermute | solution.py:237
  16.7 5.7 %collective-permute-start.4 = (f32[128,128]{1,0:T(8,128)S(1)}, f32[128,128]{1,0:T(8,128)S(1)}, u32[]{:S(2)}, u32[]{:S(2)}) collective-permute-start(f32[128,128]{1,0:T(8,128)S(1)} %add.31), channel_id=1, source_target_pairs={{0,16},{1,17},{2,18},{3,19},{4,20},{5,21},{6,22},{7,23},{8,24},{9,... | collective-permute-start | bytes 196616 | tf_op jit(solution)/shard_map/ppermute | solution.py:237
  16.8 5.7 %collective-permute-start.3 = (f32[128,128]{1,0:T(8,128)S(1)}, f32[128,128]{1,0:T(8,128)S(1)}, u32[]{:S(2)}, u32[]{:S(2)}) collective-permute-start(f32[128,128]{1,0:T(8,128)S(1)} %add.31), channel_id=1, source_target_pairs={{0,8},{1,9},{2,10},{3,11},{4,12},{5,13},{6,14},{7,15},{8,0},{9,1},... | collective-permute-start | bytes 196616 | tf_op jit(solution)/shard_map/ppermute | solution.py:237
  22.6 7.1 %collective-permute-start.6 = (f32[5,128,128]{2,1,0:T(8,128)S(1)}, f32[5,128,128]{2,1,0:T(8,128)S(1)}, u32[]{:S(2)}, u32[]{:S(2)}) collective-permute-start(f32[5,128,128]{2,1,0:T(8,128)S(1)} %pad_maximum_fusion), channel_id=1, source_target_pairs={{0,4},{1,3},{2,6},{3,1},{4,0},{5,7},{6,2},{7,5},{8,12},{9,11},{10,... | collective-permute-start | bytes 983048 | tf_op jit(solution)/shard_map/ppermute | solution.py:237
  29.7 5.9 %collective-permute-start.7 = (f32[128,128]{1,0:T(8,128)S(1)}, f32[128,128]{1,0:T(8,128)S(1)}, u32[]{:S(2)}, u32[]{:S(2)}) collective-permute-start(f32[128,128]{1,0:T(8,128)S(1)} %fusion), channel_id=1, source_target_pairs={{0,2},{1,5},{2,0},{3,7},{4,6},{5,1},{6,4},{7,3},{8,10},{9,13},{10,... | collective-permute-start | bytes 196616 | tf_op jit(solution)/shard_map/ppermute | solution.py:237
  31.2 8.5 %collective-permute-start.10 = (f32[128,128]{1,0:T(8,128)S(1)}, f32[128,128]{1,0:T(8,128)S(1)}, u32[]{:S(2)}, u32[]{:S(2)}) collective-permute-start(f32[128,128]{1,0:T(8,128)S(1)} %get-tuple-element.22), channel_id=1, source_target_pairs={{0,8},{1,9},{2,10},{3,11},{4,12},{5,13},{6,14},{7,15},{8,0},{9,1},... | collective-permute-start | bytes 196616 | tf_op jit(solution)/shard_map/ppermute | solution.py:237
  32.5 7.2 %collective-permute-start.9 = (f32[128,128]{1,0:T(8,128)S(1)}, f32[128,128]{1,0:T(8,128)S(1)}, u32[]{:S(2)}, u32[]{:S(2)}) collective-permute-start(f32[128,128]{1,0:T(8,128)S(1)} %get-tuple-element.23), channel_id=1, source_target_pairs={{0,16},{1,17},{2,18},{3,19},{4,20},{5,21},{6,22},{7,23},{8,24},{9,... | collective-permute-start | bytes 196616 | tf_op jit(solution)/shard_map/ppermute | solution.py:237
  34.3 6.1 %collective-permute-start.8 = (f32[128,128]{1,0:T(8,128)S(1)}, f32[128,128]{1,0:T(8,128)S(1)}, u32[]{:S(2)}, u32[]{:S(2)}) collective-permute-start(f32[128,128]{1,0:T(8,128)S(1)} %get-tuple-element.24), channel_id=1, source_target_pairs={{0,24},{1,25},{2,26},{3,27},{4,28},{5,29},{6,30},{7,31},{8,16},{9,... | collective-permute-start | bytes 196616 | tf_op jit(solution)/shard_map/ppermute | solution.py:237

commit v8 on v7

--- a/solution.py
+++ b/solution.py
@@ -11,12 +11,63 @@
 HIGHEST = lax.Precision.HIGHEST
 LANES = 128
 VMEM_LIMIT = 24 * 1024 * 1024
-AHEAD = 2
+AHEAD = 5
+
+
+def project(out_ref, split_ref, slab_ref, owner, sibling):
+    rank = out_ref.shape[1]
+    wanted = lax.bitwise_xor(lax.bitwise_and(owner, 1), sibling)
+    mine = lax.shift_right_logical(owner, 1)
+
+    def columns(q):
+        at = pl.multiple_of((2 * q + wanted) * LANES, LANES)
+        return slab_ref[:, pl.ds(at, LANES)]
+
+    def place(q):
+        away = lax.bitwise_xor(mine, q)
+        bit = [lax.bitwise_and(lax.shift_right_logical(away, i), 1) for i in range(4)]
+        straight = 8 * bit[0] + 4 * bit[1]
+        turned = 8 * bit[1] + 4 * bit[0]
+        return jnp.where(wanted == 0, straight, turned) + 2 * bit[3] + bit[2]
+
+    for q in range(0, out_ref.shape[0], 2):
+        both = jnp.dot(
+            split_ref[...], jnp.concatenate([columns(q), columns(q + 1)], axis=1),
+            preferred_element_type=jnp.float32,
+        )
+        sums = both[:rank] + both[rank:]
+        out_ref[place(q)] = sums[:, :LANES]
+        out_ref[place(q + 1)] = sums[:, LANES:]
+
+
+def pack(gram):
+    half = gram.shape[0] // 2
+    top, bottom = gram[:half], gram[half:]
+    row = lax.broadcasted_iota(jnp.int32, top.shape, 0)
+    column = lax.broadcasted_iota(jnp.int32, top.shape, 1)
+    body = jnp.where(column - half < row, jnp.where(column < half, bottom, pltpu.roll(top, half, 1)), bottom)
+    diagonal = jnp.sum(jnp.where(row == column, top, 0.0), axis=0, keepdims=True)
+    tail = jnp.where(row[:8] == 0, jnp.broadcast_to(diagonal, (8, diagonal.shape[1])), 0.0)
+    return jnp.concatenate([body, tail], axis=0)
+
+
+def unpack(packed):
+    half = packed.shape[0] - 8
+    body = packed[:half]
+    row = lax.broadcasted_iota(jnp.int32, body.shape, 0)
+    column = lax.broadcasted_iota(jnp.int32, body.shape, 1)
+    diagonal = jnp.broadcast_to(packed[half : half + 1], body.shape)
+    top = jnp.where(column < row, pltpu.roll(body, half, 1), jnp.where(column == row, diagonal, 0.0))
+    bottom = jnp.where(column - half < row, jnp.where(column < half, body, 0.0), body)
+    parts = jnp.concatenate([top, bottom], axis=0)
+    row = lax.broadcasted_iota(jnp.int32, parts.shape, 0)
+    column = lax.broadcasted_iota(jnp.int32, parts.shape, 1)
+    return parts + jnp.where(row == column, 0.0, parts.T)
 
 
 def rows_kernel(
-    owner_ref, slab_hbm, sketch_hbm, first_ref, gram_ref, send_ref, keep_ref,
-    slab_ref, sketch_ref, split_ref, slab_sem, sketch_sem,
+    owner_ref, slab_hbm, sketch_hbm, slab_ref, first_ref, gram_ref, split_ref, send_ref,
+    sketch_ref, sum_ref, slab_sem, sketch_sem,
 ):
     rows, width = slab_ref.shape
     rank = sketch_ref.shape[1]
@@ -47,37 +98,33 @@
         split_ref[rank:, at] = (turned - high.astype(jnp.float32)).astype(jnp.bfloat16)
         gram = jnp.dot(turned, first, precision=HIGHEST, preferred_element_type=jnp.float32)
         if k == 0:
-            gram_ref[...] = gram
+            sum_ref[...] = gram
         else:
-            gram_ref[...] += gram
-
-    owner = owner_ref[0]
-    core = lax.bitwise_and(owner, 1)
-    mine = lax.shift_right_logical(owner, 1)
-
-    def project(out_ref, wanted):
-        def columns(q):
-            at = pl.multiple_of((2 * q + wanted) * LANES, LANES)
-            return slab_ref[:, pl.ds(at, LANES)]
-
-        def place(q):
-            away = lax.bitwise_xor(mine, q)
-            bit = [lax.bitwise_and(lax.shift_right_logical(away, i), 1) for i in range(4)]
-            straight = 8 * bit[0] + 4 * bit[1]
-            turned = 8 * bit[1] + 4 * bit[0]
-            return jnp.where(wanted == 0, straight, turned) + 2 * bit[3] + bit[2]
-
-        for q in range(0, out_ref.shape[0], 2):
-            both = jnp.dot(
-                split_ref[...], jnp.concatenate([columns(q), columns(q + 1)], axis=1),
-                preferred_element_type=jnp.float32,
-            )
-            sums = both[:rank] + both[rank:]
-            out_ref[place(q)] = sums[:, :LANES]
-            out_ref[place(q + 1)] = sums[:, LANES:]
-
-    project(send_ref, 1 - core)
-    project(keep_ref, core)
+            sum_ref[...] += gram
+    gram_ref[...] = pack(sum_ref[...])
+
+    project(send_ref, split_ref, slab_ref, owner_ref[0], 1)
+
+
+def own_kernel(owner_ref, split_ref, slab_ref, keep_ref):
+    project(keep_ref, split_ref, slab_ref, owner_ref[0], 0)
+
+
+def own_call(owner, split, slab):
+    rows, width = slab.shape
+    rank = split.shape[0] // 2
+    vmem = pl.BlockSpec(memory_space=pltpu.VMEM)
+    return pl.pallas_call(
+        own_kernel,
+        in_specs=[pl.BlockSpec(memory_space=pltpu.SMEM), vmem, vmem],
+        out_specs=vmem,
+        out_shape=jax.ShapeDtypeStruct((width // (2 * LANES), rank, LANES), jnp.float32),
+        compiler_params=pltpu.CompilerParams(vmem_limit_bytes=VMEM_LIMIT),
+        cost_estimate=pl.CostEstimate(
+            flops=2 * rows * width * rank, bytes_accessed=rows * width, transcendentals=0
+        ),
+        name="project_own",
+    )(owner, split, slab)
 
 
 def rows_call(owner, slab, sketch):
@@ -92,25 +139,25 @@
             pl.BlockSpec(memory_space=pltpu.HBM),
             pl.BlockSpec(memory_space=pltpu.HBM),
         ],
-        out_specs=[vmem] * 4,
+        out_specs=[vmem] * 5,
         out_shape=[
+            jax.ShapeDtypeStruct((rows, width), jnp.bfloat16),
             jax.ShapeDtypeStruct((rows, rank), jnp.float32),
-            jax.ShapeDtypeStruct((rank, rank), jnp.float32),
-            jax.ShapeDtypeStruct(chunks, jnp.float32),
+            jax.ShapeDtypeStruct((rank // 2 + 8, rank), jnp.float32),
+            jax.ShapeDtypeStruct((2 * rank, rows), jnp.bfloat16),
             jax.ShapeDtypeStruct(chunks, jnp.float32),
         ],
         scratch_shapes=[
-            pltpu.VMEM((rows, width), jnp.bfloat16),
             pltpu.VMEM((width, rank), jnp.bfloat16),
-            pltpu.VMEM((2 * rank, rows), jnp.bfloat16),
+            pltpu.VMEM((rank, rank), jnp.float32),
             pltpu.SemaphoreType.DMA((-(-rows // LANES),)),
             pltpu.SemaphoreType.DMA,
         ],
         compiler_params=pltpu.CompilerParams(vmem_limit_bytes=VMEM_LIMIT),
         cost_estimate=pl.CostEstimate(
-            flops=6 * rows * width * rank, bytes_accessed=rows * width * 2, transcendentals=0
+            flops=4 * rows * width * rank, bytes_accessed=rows * width * 2, transcendentals=0
         ),
-        name="project_rows",
+        name="sketch_rows",
     )(
         owner,
         pltpu.with_memory_space_constraint(slab, pltpu.HBM),
@@ -126,10 +173,10 @@
     return jnp.broadcast_to(block[at : at + 1, :], block.shape)
 
 
-def inverse_factor(gram_ref, inverse_ref):
-    size = gram_ref.shape[0]
+def inverse_factor(gram, inverse_ref):
+    size = gram.shape[0]
     blocks = size // 8
-    left = [gram_ref[8 * i : 8 * i + 8, :] for i in range(blocks)]
+    left = [gram[8 * i : 8 * i + 8, :] for i in range(blocks)]
     row_at = lax.broadcasted_iota(jnp.int32, (8, size), 0)
     lane_at = lax.broadcasted_iota(jnp.int32, (8, size), 1)
     right = [jnp.where(lane_at == row_at + 8 * i, 1.0, 0.0).astype(jnp.float32) for i in range(blocks)]
@@ -169,7 +216,7 @@
 
 
 def factor_kernel(gram_ref, inverse_ref):
-    inverse_factor(gram_ref, inverse_ref)
+    inverse_factor(unpack(gram_ref[...]), inverse_ref)
 
 
 def factor_call(gram):
@@ -177,7 +224,7 @@
         factor_kernel,
         in_specs=[pl.BlockSpec(memory_space=pltpu.VMEM)],
         out_specs=pl.BlockSpec(memory_space=pltpu.VMEM),
-        out_shape=jax.ShapeDtypeStruct(gram.shape, jnp.float32),
+        out_shape=jax.ShapeDtypeStruct((gram.shape[1], gram.shape[1]), jnp.float32),
         compiler_params=pltpu.CompilerParams(vmem_limit_bytes=VMEM_LIMIT),
         cost_estimate=pl.CostEstimate(
             flops=4000000000, bytes_accessed=gram.size * 8, transcendentals=gram.shape[0]
@@ -237,18 +284,21 @@
         return lax.ppermute(array, AXES, pairs)
 
     owner = lax.shift_right_logical(me, low_bits).astype(jnp.int32).reshape(1)
-    first, gram, send, keep = rows_call(owner, slab, sketch)
-    got, gram = tie((exchange(send, core), gram + exchange(gram, core)))
+    near, first, gram, split, send = rows_call(owner, slab, sketch)
+    got = exchange(send, core)
+    keep = own_call(owner, split, near)
+    got, gram = tie((got, gram + exchange(gram, core)))
     sums = keep + got
     got = exchange(sums[8:], x, y)
     over_z = [exchange(gram, away) for away in (z | zz, zz, z)]
     gram = (gram + over_z[2]) + (over_z[1] + over_z[0])
     got, gram = tie((got, gram))
     sums = sums[:8] + got
-    got = exchange(jnp.concatenate([sums[4:], gram[None]]), y, x)
-    sums = sums[:4] + got[:4]
-    gram = gram + got[4]
+    got = exchange(sums[4:], y, x)
     gram = gram + exchange(gram, x, y)
+    got, gram = tie((got, gram))
+    sums = sums[:4] + got
+    gram = gram + exchange(gram, y, x)
     over_z = [exchange(sums[i], away) for i, away in ((3, z | zz), (2, zz), (1, z))]
     for bit in range(low_bits):
         gram = gram + exchange(gram, 1 << bit)

time: 41.7 us -> 40.6 us (0.974)
  waiting for transfers between devices: 13.7 us -> 10.1 us
  Pallas kernels: 11.7 us -> 13 us
  starting transfers between devices: 15.1 us -> 16.2 us
    ppermute x11 -> x12, waiting for transfers between devices: 13.7 us -> 10.1 us  [exchange(): return lax.ppermute(array, AXES, pairs)]
    ppermute x11 -> x12, starting transfers between devices: 15.1 us -> 16.2 us  [exchange(): return lax.ppermute(array, AXES, pairs)]
    pallas_call x0 -> x1, Pallas kernels: none -> 1.14 us  [own_call(): pl.pallas_call(own_kernel, in_specs=[pl.BlockSpec(memory_space=pltpu.SMEM...]
  transfers between devices with their start and end apart: 11 -> 12, of which waited for: 5 -> 6; matrix products, arithmetic and copies ran while one was open for 0% -> 0% of each run, Pallas kernels for 10% -> 13%
where the time goes in v8:
time: 40.6 us; the launch traced here: 40.5 us
  starting transfers between devices  16.2 us (40%)
  Pallas kernels  13 us (32%)
  waiting for transfers between devices  10.1 us (25%)
  between operations  0.74 us (2%)
    ppermute x12, starting transfers between devices, exchange(): return lax.ppermute(array, AXES, pairs)  16.2 us
    ppermute x12, waiting for transfers between devices, exchange(): return lax.ppermute(array, AXES, pairs)  10.1 us
    pallas_call x1, Pallas kernels, rows_call(): pl.pallas_call(rows_kernel, in_specs=[pl.BlockSpec(memory_space=pltpu.SME...  6.52 us
    pallas_call x1, Pallas kernels, factor_call(): pl.pallas_call(factor_kernel, in_specs=[pl.BlockSpec(memory_space=pltpu.V...  4.21 us
    pallas_call x1, Pallas kernels, finish_call(): pl.pallas_call(functools.partial(finish_kernel, float(total_rows) ** 0.5,...  1.17 us
    pallas_call x1, Pallas kernels, own_call(): pl.pallas_call(own_kernel, in_specs=[pl.BlockSpec(memory_space=pltpu.SMEM...  1.14 us
  transfers between devices with their start and end apart: 12, of which 6 were waited for; matrix products, arithmetic and copies ran while one was open for 0% of the time, Pallas kernels for 13%

profile of v8, /device:TPU:0, one launch (start us, length us, event | category | flops | bytes accessed | tf_op | source)
XLA Modules:
  0.0 40.5 jit_solution(15136065656210664036)
XLA Ops:
  0.6 6.5 %sketch_rows.1 = (bf16[576,4096]{1,0:T(8,128)(2,1)S(1)}, f32[576,128]{1,0:T(8,128)S(1)}, f32[72,128]{1,0:T(8,128)S(1)}, bf16[256,576]{1,0:T(8,128)(2,1)S(1)}, f32[16,128,128]{2,1,0:T(8,128)S(1)}) custom-call(s32[1]{0:T(128)} %bitcast.owner_ref, bf16[576,4096]{1,0:T(8,128)(2,1)} %slab_hbm.1, bf16[4096,128]{1,0:T(8,128)(2,1)} %sketch_hbm.1), custom_call_target="tpu_custom_call" | custom-call | flops 1207959552 | bytes 4718592 | tf_op jit(solution)/shard_map/sketch_rows/pallas_call | solution.py:135
  7.2 0.5 %collective-permute-start = (f32[16,128,128]{2,1,0:T(8,128)S(1)}, f32[16,128,128]{2,1,0:T(8,128)S(1)}, u32[]{:S(2)}, u32[]{:S(2)}) collective-permute-start(f32[16,128,128]{2,1,0:T(8,128)S(1)} %get-tuple-element.17), channel_id=1, source_target_pairs={{0,1},{1,0},{2,3},{3,2},{4,5},{5,4},{6,7},{7,6},{8,9},{9,8},{10,11... | collective-permute-start | bytes 3145736 | tf_op jit(solution)/shard_map/ppermute | solution.py:284
  7.7 0.1 collective-permute-start.1
  7.8 1.1 %project_own.1 = f32[16,128,128]{2,1,0:T(8,128)S(1)} custom-call(s32[1]{0:T(128)} %bitcast.owner_ref, bf16[256,576]{1,0:T(8,128)(2,1)S(1)} %get-tuple-element.15.split_ref, bf16[576,4096]{1,0:T(8,128)(2,1)S(1)} %get-tuple-element.16.slab_ref), custom_call_target="tpu_custom_call" | custom-call | flops 603979776 | bytes 2359296 | tf_op jit(solution)/shard_map/project_own/pallas_call | solution.py:117
  8.9 1.1 %collective-permute-done.1 = f32[72,128]{1,0:T(8,128)S(1)} collective-permute-done((f32[72,128]{1,0:T(8,128)S(1)}, f32[72,128]{1,0:T(8,128)S(1)}, u32[]{:S(2)}, u32[]{:S(2)}) %collective-permute-start.1) | collective-permute-done | bytes 36896 | tf_op jit(solution)/shard_map/ppermute | solution.py:284
  10.0 0.1 add.32
  10.2 2.9 %collective-permute-start.2 = (f32[8,128,128]{2,1,0:T(8,128)S(1)}, f32[8,128,128]{2,1,0:T(8,128)S(1)}, u32[]{:S(2)}, u32[]{:S(2)}) collective-permute-start(f32[8,128,128]{2,1,0:T(8,128)S(1)} %slice.33), channel_id=1, source_target_pairs={{0,2},{1,5},{2,0},{3,7},{4,6},{5,1},{6,4},{7,3},{8,10},{9,13},{10,... | collective-permute-start | bytes 1572872 | tf_op jit(solution)/shard_map/ppermute | solution.py:284
  13.1 3.6 %collective-permute-start.5 = (f32[72,128]{1,0:T(8,128)S(1)}, f32[72,128]{1,0:T(8,128)S(1)}, u32[]{:S(2)}, u32[]{:S(2)}) collective-permute-start(f32[72,128]{1,0:T(8,128)S(1)} %add.31), channel_id=1, source_target_pairs={{0,24},{1,25},{2,26},{3,27},{4,28},{5,29},{6,30},{7,31},{8,16},{9,... | collective-permute-start | bytes 110600 | tf_op jit(solution)/shard_map/ppermute | solution.py:284
  16.8 0.0 collective-permute-start.4
  16.8 0.8 %collective-permute-start.3 = (f32[72,128]{1,0:T(8,128)S(1)}, f32[72,128]{1,0:T(8,128)S(1)}, u32[]{:S(2)}, u32[]{:S(2)}) collective-permute-start(f32[72,128]{1,0:T(8,128)S(1)} %add.31), channel_id=1, source_target_pairs={{0,8},{1,9},{2,10},{3,11},{4,12},{5,13},{6,14},{7,15},{8,0},{9,1},... | collective-permute-start | bytes 110600 | tf_op jit(solution)/shard_map/ppermute | solution.py:284
  17.5 1.4 %collective-permute-done.5 = f32[72,128]{1,0:T(8,128)S(1)} collective-permute-done((f32[72,128]{1,0:T(8,128)S(1)}, f32[72,128]{1,0:T(8,128)S(1)}, u32[]{:S(2)}, u32[]{:S(2)}) %collective-permute-start.5) | collective-permute-done | bytes 36896 | tf_op jit(solution)/shard_map/ppermute | solution.py:284
  19.0 2.6 %collective-permute-done.4 = f32[72,128]{1,0:T(8,128)S(1)} collective-permute-done((f32[72,128]{1,0:T(8,128)S(1)}, f32[72,128]{1,0:T(8,128)S(1)}, u32[]{:S(2)}, u32[]{:S(2)}) %collective-permute-start.4) | collective-permute-done | bytes 36896 | tf_op jit(solution)/shard_map/ppermute | solution.py:284
  21.6 0.1 slice_add_fusion
  21.8 1.6 %collective-permute-start.6 = (f32[4,128,128]{2,1,0:T(8,128)S(1)}, f32[4,128,128]{2,1,0:T(8,128)S(1)}, u32[]{:S(2)}, u32[]{:S(2)}) collective-permute-start(f32[4,128,128]{2,1,0:T(8,128)S(1)} %slice.35), channel_id=1, source_target_pairs={{0,4},{1,3},{2,6},{3,1},{4,0},{5,7},{6,2},{7,5},{8,12},{9,11},{10,... | collective-permute-start | bytes 786440 | tf_op jit(solution)/shard_map/ppermute | solution.py:284
  23.3 0.7 %collective-permute-start.7 = (f32[72,128]{1,0:T(8,128)S(1)}, f32[72,128]{1,0:T(8,128)S(1)}, u32[]{:S(2)}, u32[]{:S(2)}) collective-permute-start(f32[72,128]{1,0:T(8,128)S(1)} %add_add_fusion), channel_id=1, source_target_pairs={{0,2},{1,5},{2,0},{3,7},{4,6},{5,1},{6,4},{7,3},{8,10},{9,13},{10,... | collective-permute-start | bytes 110600 | tf_op jit(solution)/shard_map/ppermute | solution.py:284
  24.0 3.3 %collective-permute-done.7 = f32[72,128]{1,0:T(8,128)S(1)} collective-permute-done((f32[72,128]{1,0:T(8,128)S(1)}, f32[72,128]{1,0:T(8,128)S(1)}, u32[]{:S(2)}, u32[]{:S(2)}) %collective-permute-start.7) | collective-permute-done | bytes 36896 | tf_op jit(solution)/shard_map/ppermute | solution.py:284
  27.3 0.9 %collective-permute-done.6 = f32[4,128,128]{2,1,0:T(8,128)S(1)} collective-permute-done((f32[4,128,128]{2,1,0:T(8,128)S(1)}, f32[4,128,128]{2,1,0:T(8,128)S(1)}, u32[]{:S(2)}, u32[]{:S(2)}) %collective-permute-start.6) | collective-permute-done | bytes 262176 | tf_op jit(solution)/shard_map/ppermute | solution.py:284
  28.2 1.6 %collective-permute-start.8 = (f32[72,128]{1,0:T(8,128)S(1)}, f32[72,128]{1,0:T(8,128)S(1)}, u32[]{:S(2)}, u32[]{:S(2)}) collective-permute-start(f32[72,128]{1,0:T(8,128)S(1)} %add.37), channel_id=1, source_target_pairs={{0,4},{1,3},{2,6},{3,1},{4,0},{5,7},{6,2},{7,5},{8,12},{9,11},{10,... | collective-permute-start | bytes 110600 | tf_op jit(solution)/shard_map/ppermute | solution.py:284
  29.8 0.8 %collective-permute-start.11 = (f32[128,128]{1,0:T(8,128)S(1)}, f32[128,128]{1,0:T(8,128)S(1)}, u32[]{:S(2)}, u32[]{:S(2)}) collective-permute-start(f32[128,128]{1,0:T(8,128)S(1)} %get-tuple-element.28), channel_id=1, source_target_pairs={{0,8},{1,9},{2,10},{3,11},{4,12},{5,13},{6,14},{7,15},{8,0},{9,1},... | collective-permute-start | bytes 196616 | tf_op jit(solution)/shard_map/ppermute | solution.py:284
  30.7 2.6 %collective-permute-start.10 = (f32[128,128]{1,0:T(8,128)S(1)}, f32[128,128]{1,0:T(8,128)S(1)}, u32[]{:S(2)}, u32[]{:S(2)}) collective-permute-start(f32[128,128]{1,0:T(8,128)S(1)} %get-tuple-element.29), channel_id=1, source_target_pairs={{0,16},{1,17},{2,18},{3,19},{4,20},{5,21},{6,22},{7,23},{8,24},{9,... | collective-permute-start | bytes 196616 | tf_op jit(solution)/shard_map/ppermute | solution.py:284
  33.3 1.0 %collective-permute-start.9 = (f32[128,128]{1,0:T(8,128)S(1)}, f32[128,128]{1,0:T(8,128)S(1)}, u32[]{:S(2)}, u32[]{:S(2)}) collective-permute-start(f32[128,128]{1,0:T(8,128)S(1)} %get-tuple-element.30), channel_id=1, source_target_pairs={{0,24},{1,25},{2,26},{3,27},{4,28},{5,29},{6,30},{7,31},{8,16},{9,... | collective-permute-start | bytes 196616 | tf_op jit(solution)/shard_map/ppermute | solution.py:284
  34.3 4.2 %factor.1.inverse_ref = f32[128,128]{1,0:T(8,128)S(1)} custom-call(f32[72,128]{1,0:T(8,128)S(1)} %add.39.gram_ref), custom_call_target="tpu_custom_call" | custom-call | flops 4000000000 | bytes 73728 | tf_op jit(solution)/shard_map/factor/pallas_call | solution.py:223
  38.5 0.8 %collective-permute-done.9.refs_0_ = f32[128,128]{1,0:T(8,128)S(1)} collective-permute-done((f32[128,128]{1,0:T(8,128)S(1)}, f32[128,128]{1,0:T(8,128)S(1)}, u32[]{:S(2)}, u32[]{:S(2)}) %collective-permute-start.9) | collective-permute-done | bytes 65568 | tf_op jit(solution)/shard_map/ppermute | solution.py:284
  39.3 1.2 %finish.1 = (f32[576,128]{1,0:T(8,128)}, bf16[128,128]{1,0:T(8,128)(2,1)}) custom-call(f32[128,128]{1,0:T(8,128)S(1)} %factor.1.inverse_ref, f32[576,128]{1,0:T(8,128)S(1)} %get-tuple-element.26.first_ref, f32[128,128]{1,0:T(8,128)S(1)} %slice_bitcast_fusion.3.sums_ref, f32[128,128]{1,0:T(8,128)S(1)} %collective-permute-done.9.refs_0_, ...), custom_call_target="tpu_custom_call" | custom-call | flops 113246208 | bytes 589824 | tf_op jit(solution)/shard_map/finish/pallas_call | solution.py:254
  (15 shorter events, 0.1 us)
Async XLA Ops:
  7.2 2.9 %collective-permute-start = (f32[16,128,128]{2,1,0:T(8,128)S(1)}, f32[16,128,128]{2,1,0:T(8,128)S(1)}, u32[]{:S(2)}, u32[]{:S(2)}) collective-permute-start(f32[16,128,128]{2,1,0:T(8,128)S(1)} %get-tuple-element.17), channel_id=1, source_target_pairs={{0,1},{1,0},{2,3},{3,2},{4,5},{5,4},{6,7},{7,6},{8,9},{9,8},{10,11... | collective-permute-start | bytes 3145736 | tf_op jit(solution)/shard_map/ppermute | solution.py:284
  7.7 2.3 %collective-permute-start.1 = (f32[72,128]{1,0:T(8,128)S(1)}, f32[72,128]{1,0:T(8,128)S(1)}, u32[]{:S(2)}, u32[]{:S(2)}) collective-permute-start(f32[72,128]{1,0:T(8,128)S(1)} %get-tuple-element.18), channel_id=1, source_target_pairs={{0,1},{1,0},{2,3},{3,2},{4,5},{5,4},{6,7},{7,6},{8,9},{9,8},{10,11... | collective-permute-start | bytes 110600 | tf_op jit(solution)/shard_map/ppermute | solution.py:284
  10.2 11.4 %collective-permute-start.2 = (f32[8,128,128]{2,1,0:T(8,128)S(1)}, f32[8,128,128]{2,1,0:T(8,128)S(1)}, u32[]{:S(2)}, u32[]{:S(2)}) collective-permute-start(f32[8,128,128]{2,1,0:T(8,128)S(1)} %slice.33), channel_id=1, source_target_pairs={{0,2},{1,5},{2,0},{3,7},{4,6},{5,1},{6,4},{7,3},{8,10},{9,13},{10,... | collective-permute-start | bytes 1572872 | tf_op jit(solution)/shard_map/ppermute | solution.py:284
  13.1 5.8 %collective-permute-start.5 = (f32[72,128]{1,0:T(8,128)S(1)}, f32[72,128]{1,0:T(8,128)S(1)}, u32[]{:S(2)}, u32[]{:S(2)}) collective-permute-start(f32[72,128]{1,0:T(8,128)S(1)} %add.31), channel_id=1, source_target_pairs={{0,24},{1,25},{2,26},{3,27},{4,28},{5,29},{6,30},{7,31},{8,16},{9,... | collective-permute-start | bytes 110600 | tf_op jit(solution)/shard_map/ppermute | solution.py:284
  16.8 4.9 %collective-permute-start.4 = (f32[72,128]{1,0:T(8,128)S(1)}, f32[72,128]{1,0:T(8,128)S(1)}, u32[]{:S(2)}, u32[]{:S(2)}) collective-permute-start(f32[72,128]{1,0:T(8,128)S(1)} %add.31), channel_id=1, source_target_pairs={{0,16},{1,17},{2,18},{3,19},{4,20},{5,21},{6,22},{7,23},{8,24},{9,... | collective-permute-start | bytes 110600 | tf_op jit(solution)/shard_map/ppermute | solution.py:284
  16.8 4.9 %collective-permute-start.3 = (f32[72,128]{1,0:T(8,128)S(1)}, f32[72,128]{1,0:T(8,128)S(1)}, u32[]{:S(2)}, u32[]{:S(2)}) collective-permute-start(f32[72,128]{1,0:T(8,128)S(1)} %add.31), channel_id=1, source_target_pairs={{0,8},{1,9},{2,10},{3,11},{4,12},{5,13},{6,14},{7,15},{8,0},{9,1},... | collective-permute-start | bytes 110600 | tf_op jit(solution)/shard_map/ppermute | solution.py:284
  21.8 6.4 %collective-permute-start.6 = (f32[4,128,128]{2,1,0:T(8,128)S(1)}, f32[4,128,128]{2,1,0:T(8,128)S(1)}, u32[]{:S(2)}, u32[]{:S(2)}) collective-permute-start(f32[4,128,128]{2,1,0:T(8,128)S(1)} %slice.35), channel_id=1, source_target_pairs={{0,4},{1,3},{2,6},{3,1},{4,0},{5,7},{6,2},{7,5},{8,12},{9,11},{10,... | collective-permute-start | bytes 786440 | tf_op jit(solution)/shard_map/ppermute | solution.py:284
  23.3 4.0 %collective-permute-start.7 = (f32[72,128]{1,0:T(8,128)S(1)}, f32[72,128]{1,0:T(8,128)S(1)}, u32[]{:S(2)}, u32[]{:S(2)}) collective-permute-start(f32[72,128]{1,0:T(8,128)S(1)} %add_add_fusion), channel_id=1, source_target_pairs={{0,2},{1,5},{2,0},{3,7},{4,6},{5,1},{6,4},{7,3},{8,10},{9,13},{10,... | collective-permute-start | bytes 110600 | tf_op jit(solution)/shard_map/ppermute | solution.py:284
  28.2 6.1 %collective-permute-start.8 = (f32[72,128]{1,0:T(8,128)S(1)}, f32[72,128]{1,0:T(8,128)S(1)}, u32[]{:S(2)}, u32[]{:S(2)}) collective-permute-start(f32[72,128]{1,0:T(8,128)S(1)} %add.37), channel_id=1, source_target_pairs={{0,4},{1,3},{2,6},{3,1},{4,0},{5,7},{6,2},{7,5},{8,12},{9,11},{10,... | collective-permute-start | bytes 110600 | tf_op jit(solution)/shard_map/ppermute | solution.py:284
  29.8 8.7 %collective-permute-start.11 = (f32[128,128]{1,0:T(8,128)S(1)}, f32[128,128]{1,0:T(8,128)S(1)}, u32[]{:S(2)}, u32[]{:S(2)}) collective-permute-start(f32[128,128]{1,0:T(8,128)S(1)} %get-tuple-element.28), channel_id=1, source_target_pairs={{0,8},{1,9},{2,10},{3,11},{4,12},{5,13},{6,14},{7,15},{8,0},{9,1},... | collective-permute-start | bytes 196616 | tf_op jit(solution)/shard_map/ppermute | solution.py:284
  30.7 7.9 %collective-permute-start.10 = (f32[128,128]{1,0:T(8,128)S(1)}, f32[128,128]{1,0:T(8,128)S(1)}, u32[]{:S(2)}, u32[]{:S(2)}) collective-permute-start(f32[128,128]{1,0:T(8,128)S(1)} %get-tuple-element.29), channel_id=1, source_target_pairs={{0,16},{1,17},{2,18},{3,19},{4,20},{5,21},{6,22},{7,23},{8,24},{9,... | collective-permute-start | bytes 196616 | tf_op jit(solution)/shard_map/ppermute | solution.py:284
  33.3 6.1 %collective-permute-start.9 = (f32[128,128]{1,0:T(8,128)S(1)}, f32[128,128]{1,0:T(8,128)S(1)}, u32[]{:S(2)}, u32[]{:S(2)}) collective-permute-start(f32[128,128]{1,0:T(8,128)S(1)} %get-tuple-element.30), channel_id=1, source_target_pairs={{0,24},{1,25},{2,26},{3,27},{4,28},{5,29},{6,30},{7,31},{8,16},{9,... | collective-permute-start | bytes 196616 | tf_op jit(solution)/shard_map/ppermute | solution.py:284

commit v9 on v8

--- a/solution.py
+++ b/solution.py
@@ -11,33 +11,29 @@
 HIGHEST = lax.Precision.HIGHEST
 LANES = 128
 VMEM_LIMIT = 24 * 1024 * 1024
-AHEAD = 5
-
-
-def project(out_ref, split_ref, slab_ref, owner, sibling):
+AHEAD = 2
+
+
+def project(out_ref, split_ref, slab_ref, owner, sibling, first_place):
     rank = out_ref.shape[1]
     wanted = lax.bitwise_xor(lax.bitwise_and(owner, 1), sibling)
     mine = lax.shift_right_logical(owner, 1)
 
-    def columns(q):
-        at = pl.multiple_of((2 * q + wanted) * LANES, LANES)
+    def columns(place):
+        one, two = place // 8, place // 4 % 2
+        away = jnp.where(wanted == 0, one + 2 * two, two + 2 * one) + 4 * (place % 4)
+        at = pl.multiple_of((2 * lax.bitwise_xor(mine, away) + wanted) * LANES, LANES)
         return slab_ref[:, pl.ds(at, LANES)]
 
-    def place(q):
-        away = lax.bitwise_xor(mine, q)
-        bit = [lax.bitwise_and(lax.shift_right_logical(away, i), 1) for i in range(4)]
-        straight = 8 * bit[0] + 4 * bit[1]
-        turned = 8 * bit[1] + 4 * bit[0]
-        return jnp.where(wanted == 0, straight, turned) + 2 * bit[3] + bit[2]
-
-    for q in range(0, out_ref.shape[0], 2):
+    for i in range(0, out_ref.shape[0], 2):
+        place = first_place + i
         both = jnp.dot(
-            split_ref[...], jnp.concatenate([columns(q), columns(q + 1)], axis=1),
+            split_ref[...], jnp.concatenate([columns(place), columns(place + 1)], axis=1),
             preferred_element_type=jnp.float32,
         )
         sums = both[:rank] + both[rank:]
-        out_ref[place(q)] = sums[:, :LANES]
-        out_ref[place(q + 1)] = sums[:, LANES:]
+        out_ref[i] = sums[:, :LANES]
+        out_ref[i + 1] = sums[:, LANES:]
 
 
 def pack(gram):
@@ -103,27 +99,29 @@
             sum_ref[...] += gram
     gram_ref[...] = pack(sum_ref[...])
 
-    project(send_ref, split_ref, slab_ref, owner_ref[0], 1)
-
-
-def own_kernel(owner_ref, split_ref, slab_ref, keep_ref):
-    project(keep_ref, split_ref, slab_ref, owner_ref[0], 0)
-
-
-def own_call(owner, split, slab):
+    project(send_ref, split_ref, slab_ref, owner_ref[0], 1, 8)
+
+
+def project_kernel(parts, owner_ref, split_ref, slab_ref, *out_refs):
+    for (sibling, first_place), out_ref in zip(parts, out_refs):
+        project(out_ref, split_ref, slab_ref, owner_ref[0], sibling, first_place)
+
+
+def project_call(owner, split, slab, parts, name):
     rows, width = slab.shape
     rank = split.shape[0] // 2
     vmem = pl.BlockSpec(memory_space=pltpu.VMEM)
+    chunks = jax.ShapeDtypeStruct((width // (4 * LANES), rank, LANES), jnp.float32)
     return pl.pallas_call(
-        own_kernel,
+        functools.partial(project_kernel, parts),
         in_specs=[pl.BlockSpec(memory_space=pltpu.SMEM), vmem, vmem],
-        out_specs=vmem,
-        out_shape=jax.ShapeDtypeStruct((width // (2 * LANES), rank, LANES), jnp.float32),
+        out_specs=[vmem] * len(parts),
+        out_shape=[chunks] * len(parts),
         compiler_params=pltpu.CompilerParams(vmem_limit_bytes=VMEM_LIMIT),
         cost_estimate=pl.CostEstimate(
-            flops=2 * rows * width * rank, bytes_accessed=rows * width, transcendentals=0
+            flops=len(parts) * rows * width * rank, bytes_accessed=rows * width, transcendentals=0
         ),
-        name="project_own",
+        name=name,
     )(owner, split, slab)
 
 
@@ -131,7 +129,7 @@
     rows, width = slab.shape
     rank = sketch.shape[1]
     vmem = pl.BlockSpec(memory_space=pltpu.VMEM)
-    chunks = (width // (2 * LANES), rank, LANES)
+    chunks = (width // (4 * LANES), rank, LANES)
     return pl.pallas_call(
         rows_kernel,
         in_specs=[
@@ -155,7 +153,7 @@
         ],
         compiler_params=pltpu.CompilerParams(vmem_limit_bytes=VMEM_LIMIT),
         cost_estimate=pl.CostEstimate(
-            flops=4 * rows * width * rank, bytes_accessed=rows * width * 2, transcendentals=0
+            flops=3 * rows * width * rank, bytes_accessed=rows * width * 2, transcendentals=0
         ),
         name="sketch_rows",
     )(
@@ -286,14 +284,15 @@
     owner = lax.shift_right_logical(me, low_bits).astype(jnp.int32).reshape(1)
     near, first, gram, split, send = rows_call(owner, slab, sketch)
     got = exchange(send, core)
-    keep = own_call(owner, split, near)
+    keep, = project_call(owner, split, near, ((0, 8),), "project_first")
     got, gram = tie((got, gram + exchange(gram, core)))
-    sums = keep + got
-    got = exchange(sums[8:], x, y)
+    got = exchange(keep + got, x, y)
+    send, sums = project_call(owner, split, near, ((1, 0), (0, 0)), "project_rest")
+    sums = sums + exchange(send, core)
     over_z = [exchange(gram, away) for away in (z | zz, zz, z)]
     gram = (gram + over_z[2]) + (over_z[1] + over_z[0])
     got, gram = tie((got, gram))
-    sums = sums[:8] + got
+    sums = sums + got
     got = exchange(sums[4:], y, x)
     gram = gram + exchange(gram, x, y)
     got, gram = tie((got, gram))

time: 40.6 us -> 40.5 us (level)
  Pallas kernels: 13 us -> 12.4 us
  waiting for transfers between devices: 10.1 us -> 10.7 us
    pallas_call x1, Pallas kernels: 6.52 us -> 5.24 us  [rows_call(): pl.pallas_call(rows_kernel, in_specs=[pl.BlockSpec(memory_space=pltpu.SME...]
    pallas_call x1 -> x2, Pallas kernels: 1.14 us -> 1.77 us  [project_call(): pl.pallas_call(functools.partial(project_kernel, parts), in_specs=[pl.Blo...]
    ppermute x12 -> x13, waiting for transfers between devices: 10.1 us -> 10.7 us  [exchange(): return lax.ppermute(array, AXES, pairs)]
    ppermute x12 -> x13, starting transfers between devices: 16.2 us -> 16.2 us  [exchange(): return lax.ppermute(array, AXES, pairs)]
  transfers between devices with their start and end apart: 12 -> 13, of which waited for: 6 -> 5; matrix products, arithmetic and copies ran while one was open for 0% -> 0% of each run, Pallas kernels for 13% -> 15%
where the time goes in v9:
time: 40.5 us; the launch traced here: 40.3 us
  starting transfers between devices  16.2 us (40%)
  Pallas kernels  12.4 us (31%)
  waiting for transfers between devices  10.7 us (26%)
  between operations  0.75 us (2%)
    ppermute x13, starting transfers between devices, exchange(): return lax.ppermute(array, AXES, pairs)  16.2 us
    ppermute x13, waiting for transfers between devices, exchange(): return lax.ppermute(array, AXES, pairs)  10.7 us
    pallas_call x1, Pallas kernels, rows_call(): pl.pallas_call(rows_kernel, in_specs=[pl.BlockSpec(memory_space=pltpu.SME...  5.24 us
    pallas_call x1, Pallas kernels, factor_call(): pl.pallas_call(factor_kernel, in_specs=[pl.BlockSpec(memory_space=pltpu.V...  4.21 us
    pallas_call x2, Pallas kernels, project_call(): pl.pallas_call(functools.partial(project_kernel, parts), in_specs=[pl.Blo...  1.77 us
    pallas_call x1, Pallas kernels, finish_call(): pl.pallas_call(functools.partial(finish_kernel, float(total_rows) ** 0.5,...  1.17 us
  transfers between devices with their start and end apart: 13, of which 5 were waited for; matrix products, arithmetic and copies ran while one was open for 0% of the time, Pallas kernels for 15%

profile of v9, /device:TPU:0, one launch (start us, length us, event | category | flops | bytes accessed | tf_op | source)
XLA Modules:
  0.0 40.3 jit_solution(1781244607075085688)
XLA Ops:
  0.6 5.2 %sketch_rows.1 = (bf16[576,4096]{1,0:T(8,128)(2,1)S(1)}, f32[576,128]{1,0:T(8,128)S(1)}, f32[72,128]{1,0:T(8,128)S(1)}, bf16[256,576]{1,0:T(8,128)(2,1)S(1)}, f32[8,128,128]{2,1,0:T(8,128)S(1)}) custom-call(s32[1]{0:T(128)} %bitcast.owner_ref, bf16[576,4096]{1,0:T(8,128)(2,1)} %slab_hbm.1, bf16[4096,128]{1,0:T(8,128)(2,1)} %sketch_hbm.1), custom_call_target="tpu_custom_call" | custom-call | flops 905969664 | bytes 4718592 | tf_op jit(solution)/shard_map/sketch_rows/pallas_call | solution.py:133
  5.9 0.5 %collective-permute-start.1 = (f32[8,128,128]{2,1,0:T(8,128)S(1)}, f32[8,128,128]{2,1,0:T(8,128)S(1)}, u32[]{:S(2)}, u32[]{:S(2)}) collective-permute-start(f32[8,128,128]{2,1,0:T(8,128)S(1)} %get-tuple-element.21), channel_id=1, source_target_pairs={{0,1},{1,0},{2,3},{3,2},{4,5},{5,4},{6,7},{7,6},{8,9},{9,8},{10,11... | collective-permute-start | bytes 1572872 | tf_op jit(solution)/shard_map/ppermute | solution.py:282
  6.4 0.1 collective-permute-start.2
  6.5 0.7 %project_first.1 = f32[8,128,128]{2,1,0:T(8,128)S(1)} custom-call(s32[1]{0:T(128)} %bitcast.owner_ref, bf16[256,576]{1,0:T(8,128)(2,1)S(1)} %get-tuple-element.17.split_ref, bf16[576,4096]{1,0:T(8,128)(2,1)S(1)} %get-tuple-element.18.slab_ref), custom_call_target="tpu_custom_call" | custom-call | flops 301989888 | bytes 2359296 | tf_op jit(solution)/shard_map/project_first/pallas_call | solution.py:115
  7.2 0.8 %collective-permute-done.2 = f32[72,128]{1,0:T(8,128)S(1)} collective-permute-done((f32[72,128]{1,0:T(8,128)S(1)}, f32[72,128]{1,0:T(8,128)S(1)}, u32[]{:S(2)}, u32[]{:S(2)}) %collective-permute-start.2) | collective-permute-done | bytes 36896 | tf_op jit(solution)/shard_map/ppermute | solution.py:282
  8.0 0.1 add.36
  8.1 2.9 %collective-permute-start.3 = (f32[8,128,128]{2,1,0:T(8,128)S(1)}, f32[8,128,128]{2,1,0:T(8,128)S(1)}, u32[]{:S(2)}, u32[]{:S(2)}) collective-permute-start(f32[8,128,128]{2,1,0:T(8,128)S(1)} %add.36), channel_id=1, source_target_pairs={{0,2},{1,5},{2,0},{3,7},{4,6},{5,1},{6,4},{7,3},{8,10},{9,13},{10,... | collective-permute-start | bytes 1572872 | tf_op jit(solution)/shard_map/ppermute | solution.py:282
  11.0 1.1 %project_rest.1 = (f32[8,128,128]{2,1,0:T(8,128)S(1)}, f32[8,128,128]{2,1,0:T(8,128)S(1)}) custom-call(s32[1]{0:T(128)} %bitcast.owner_ref, bf16[256,576]{1,0:T(8,128)(2,1)S(1)} %get-tuple-element.17.split_ref, bf16[576,4096]{1,0:T(8,128)(2,1)S(1)} %get-tuple-element.18.slab_ref), custom_call_target="tpu_custom_call" | custom-call | flops 603979776 | bytes 2359296 | tf_op jit(solution)/shard_map/project_rest/pallas_call | solution.py:115
  12.1 0.1 collective-permute-start
  12.2 1.6 %collective-permute-start.4 = (f32[72,128]{1,0:T(8,128)S(1)}, f32[72,128]{1,0:T(8,128)S(1)}, u32[]{:S(2)}, u32[]{:S(2)}) collective-permute-start(f32[72,128]{1,0:T(8,128)S(1)} %add.35), channel_id=1, source_target_pairs={{0,8},{1,9},{2,10},{3,11},{4,12},{5,13},{6,14},{7,15},{8,0},{9,1},... | collective-permute-start | bytes 110600 | tf_op jit(solution)/shard_map/ppermute | solution.py:282
  13.8 2.6 %collective-permute-start.5 = (f32[72,128]{1,0:T(8,128)S(1)}, f32[72,128]{1,0:T(8,128)S(1)}, u32[]{:S(2)}, u32[]{:S(2)}) collective-permute-start(f32[72,128]{1,0:T(8,128)S(1)} %add.35), channel_id=1, source_target_pairs={{0,16},{1,17},{2,18},{3,19},{4,20},{5,21},{6,22},{7,23},{8,24},{9,... | collective-permute-start | bytes 110600 | tf_op jit(solution)/shard_map/ppermute | solution.py:282
  16.4 0.2 collective-permute-start.6
  16.6 2.8 %collective-permute-done.5 = f32[72,128]{1,0:T(8,128)S(1)} collective-permute-done((f32[72,128]{1,0:T(8,128)S(1)}, f32[72,128]{1,0:T(8,128)S(1)}, u32[]{:S(2)}, u32[]{:S(2)}) %collective-permute-start.5) | collective-permute-done | bytes 36896 | tf_op jit(solution)/shard_map/ppermute | solution.py:282
  19.4 2.8 %collective-permute-done.6 = f32[72,128]{1,0:T(8,128)S(1)} collective-permute-done((f32[72,128]{1,0:T(8,128)S(1)}, f32[72,128]{1,0:T(8,128)S(1)}, u32[]{:S(2)}, u32[]{:S(2)}) %collective-permute-start.6) | collective-permute-done | bytes 36896 | tf_op jit(solution)/shard_map/ppermute | solution.py:282
  22.2 0.1 add_add_fusion
  22.3 1.6 %collective-permute-start.7 = (f32[4,128,128]{2,1,0:T(8,128)S(1)}, f32[4,128,128]{2,1,0:T(8,128)S(1)}, u32[]{:S(2)}, u32[]{:S(2)}) collective-permute-start(f32[4,128,128]{2,1,0:T(8,128)S(1)} %slice.25), channel_id=1, source_target_pairs={{0,4},{1,3},{2,6},{3,1},{4,0},{5,7},{6,2},{7,5},{8,12},{9,11},{10,... | collective-permute-start | bytes 786440 | tf_op jit(solution)/shard_map/ppermute | solution.py:282
  23.9 0.6 %collective-permute-start.8 = (f32[72,128]{1,0:T(8,128)S(1)}, f32[72,128]{1,0:T(8,128)S(1)}, u32[]{:S(2)}, u32[]{:S(2)}) collective-permute-start(f32[72,128]{1,0:T(8,128)S(1)} %add_add_fusion.1), channel_id=1, source_target_pairs={{0,2},{1,5},{2,0},{3,7},{4,6},{5,1},{6,4},{7,3},{8,10},{9,13},{10,... | collective-permute-start | bytes 110600 | tf_op jit(solution)/shard_map/ppermute | solution.py:282
  24.5 3.4 %collective-permute-done.8 = f32[72,128]{1,0:T(8,128)S(1)} collective-permute-done((f32[72,128]{1,0:T(8,128)S(1)}, f32[72,128]{1,0:T(8,128)S(1)}, u32[]{:S(2)}, u32[]{:S(2)}) %collective-permute-start.8) | collective-permute-done | bytes 36896 | tf_op jit(solution)/shard_map/ppermute | solution.py:282
  27.9 0.9 %collective-permute-done.7 = f32[4,128,128]{2,1,0:T(8,128)S(1)} collective-permute-done((f32[4,128,128]{2,1,0:T(8,128)S(1)}, f32[4,128,128]{2,1,0:T(8,128)S(1)}, u32[]{:S(2)}, u32[]{:S(2)}) %collective-permute-start.7) | collective-permute-done | bytes 262176 | tf_op jit(solution)/shard_map/ppermute | solution.py:282
  28.8 1.6 %collective-permute-start.9 = (f32[72,128]{1,0:T(8,128)S(1)}, f32[72,128]{1,0:T(8,128)S(1)}, u32[]{:S(2)}, u32[]{:S(2)}) collective-permute-start(f32[72,128]{1,0:T(8,128)S(1)} %add.41), channel_id=1, source_target_pairs={{0,4},{1,3},{2,6},{3,1},{4,0},{5,7},{6,2},{7,5},{8,12},{9,11},{10,... | collective-permute-start | bytes 110600 | tf_op jit(solution)/shard_map/ppermute | solution.py:282
  30.4 0.6 %collective-permute-start.10 = (f32[128,128]{1,0:T(8,128)S(1)}, f32[128,128]{1,0:T(8,128)S(1)}, u32[]{:S(2)}, u32[]{:S(2)}) collective-permute-start(f32[128,128]{1,0:T(8,128)S(1)} %get-tuple-element.34), channel_id=1, source_target_pairs={{0,24},{1,25},{2,26},{3,27},{4,28},{5,29},{6,30},{7,31},{8,16},{9,... | collective-permute-start | bytes 196616 | tf_op jit(solution)/shard_map/ppermute | solution.py:282
  31.0 3.8 %collective-permute-start.12 = (f32[128,128]{1,0:T(8,128)S(1)}, f32[128,128]{1,0:T(8,128)S(1)}, u32[]{:S(2)}, u32[]{:S(2)}) collective-permute-start(f32[128,128]{1,0:T(8,128)S(1)} %get-tuple-element.32), channel_id=1, source_target_pairs={{0,8},{1,9},{2,10},{3,11},{4,12},{5,13},{6,14},{7,15},{8,0},{9,1},... | collective-permute-start | bytes 196616 | tf_op jit(solution)/shard_map/ppermute | solution.py:282
  34.9 4.2 %factor.1.inverse_ref = f32[128,128]{1,0:T(8,128)S(1)} custom-call(f32[72,128]{1,0:T(8,128)S(1)} %add.43.gram_ref), custom_call_target="tpu_custom_call" | custom-call | flops 4000000000 | bytes 73728 | tf_op jit(solution)/shard_map/factor/pallas_call | solution.py:221
  39.1 1.2 %finish.1 = (f32[576,128]{1,0:T(8,128)}, bf16[128,128]{1,0:T(8,128)(2,1)}) custom-call(f32[128,128]{1,0:T(8,128)S(1)} %factor.1.inverse_ref, f32[576,128]{1,0:T(8,128)S(1)} %get-tuple-element.30.first_ref, f32[128,128]{1,0:T(8,128)S(1)} %slice_bitcast_fusion.3.sums_ref, f32[128,128]{1,0:T(8,128)S(1)} %collective-permute-done.10.refs_0_, ...), custom_call_target="tpu_custom_call" | custom-call | flops 113246208 | bytes 589824 | tf_op jit(solution)/shard_map/finish/pallas_call | solution.py:252
  (17 shorter events, 0.1 us)
Async XLA Ops:
  5.9 2.1 %collective-permute-start.1 = (f32[8,128,128]{2,1,0:T(8,128)S(1)}, f32[8,128,128]{2,1,0:T(8,128)S(1)}, u32[]{:S(2)}, u32[]{:S(2)}) collective-permute-start(f32[8,128,128]{2,1,0:T(8,128)S(1)} %get-tuple-element.21), channel_id=1, source_target_pairs={{0,1},{1,0},{2,3},{3,2},{4,5},{5,4},{6,7},{7,6},{8,9},{9,8},{10,11... | collective-permute-start | bytes 1572872 | tf_op jit(solution)/shard_map/ppermute | solution.py:282
  6.4 1.6 %collective-permute-start.2 = (f32[72,128]{1,0:T(8,128)S(1)}, f32[72,128]{1,0:T(8,128)S(1)}, u32[]{:S(2)}, u32[]{:S(2)}) collective-permute-start(f32[72,128]{1,0:T(8,128)S(1)} %get-tuple-element.22), channel_id=1, source_target_pairs={{0,1},{1,0},{2,3},{3,2},{4,5},{5,4},{6,7},{7,6},{8,9},{9,8},{10,11... | collective-permute-start | bytes 110600 | tf_op jit(solution)/shard_map/ppermute | solution.py:282
  8.1 14.1 %collective-permute-start.3 = (f32[8,128,128]{2,1,0:T(8,128)S(1)}, f32[8,128,128]{2,1,0:T(8,128)S(1)}, u32[]{:S(2)}, u32[]{:S(2)}) collective-permute-start(f32[8,128,128]{2,1,0:T(8,128)S(1)} %add.36), channel_id=1, source_target_pairs={{0,2},{1,5},{2,0},{3,7},{4,6},{5,1},{6,4},{7,3},{8,10},{9,13},{10,... | collective-permute-start | bytes 1572872 | tf_op jit(solution)/shard_map/ppermute | solution.py:282
  12.1 10.1 %collective-permute-start = (f32[8,128,128]{2,1,0:T(8,128)S(1)}, f32[8,128,128]{2,1,0:T(8,128)S(1)}, u32[]{:S(2)}, u32[]{:S(2)}) collective-permute-start(f32[8,128,128]{2,1,0:T(8,128)S(1)} %get-tuple-element.20), channel_id=1, source_target_pairs={{0,1},{1,0},{2,3},{3,2},{4,5},{5,4},{6,7},{7,6},{8,9},{9,8},{10,11... | collective-permute-start | bytes 1572872 | tf_op jit(solution)/shard_map/ppermute | solution.py:282
  12.2 4.5 %collective-permute-start.4 = (f32[72,128]{1,0:T(8,128)S(1)}, f32[72,128]{1,0:T(8,128)S(1)}, u32[]{:S(2)}, u32[]{:S(2)}) collective-permute-start(f32[72,128]{1,0:T(8,128)S(1)} %add.35), channel_id=1, source_target_pairs={{0,8},{1,9},{2,10},{3,11},{4,12},{5,13},{6,14},{7,15},{8,0},{9,1},... | collective-permute-start | bytes 110600 | tf_op jit(solution)/shard_map/ppermute | solution.py:282
  13.8 5.6 %collective-permute-start.5 = (f32[72,128]{1,0:T(8,128)S(1)}, f32[72,128]{1,0:T(8,128)S(1)}, u32[]{:S(2)}, u32[]{:S(2)}) collective-permute-start(f32[72,128]{1,0:T(8,128)S(1)} %add.35), channel_id=1, source_target_pairs={{0,16},{1,17},{2,18},{3,19},{4,20},{5,21},{6,22},{7,23},{8,24},{9,... | collective-permute-start | bytes 110600 | tf_op jit(solution)/shard_map/ppermute | solution.py:282
  16.4 5.8 %collective-permute-start.6 = (f32[72,128]{1,0:T(8,128)S(1)}, f32[72,128]{1,0:T(8,128)S(1)}, u32[]{:S(2)}, u32[]{:S(2)}) collective-permute-start(f32[72,128]{1,0:T(8,128)S(1)} %add.35), channel_id=1, source_target_pairs={{0,24},{1,25},{2,26},{3,27},{4,28},{5,29},{6,30},{7,31},{8,16},{9,... | collective-permute-start | bytes 110600 | tf_op jit(solution)/shard_map/ppermute | solution.py:282
  22.3 6.4 %collective-permute-start.7 = (f32[4,128,128]{2,1,0:T(8,128)S(1)}, f32[4,128,128]{2,1,0:T(8,128)S(1)}, u32[]{:S(2)}, u32[]{:S(2)}) collective-permute-start(f32[4,128,128]{2,1,0:T(8,128)S(1)} %slice.25), channel_id=1, source_target_pairs={{0,4},{1,3},{2,6},{3,1},{4,0},{5,7},{6,2},{7,5},{8,12},{9,11},{10,... | collective-permute-start | bytes 786440 | tf_op jit(solution)/shard_map/ppermute | solution.py:282
  23.9 4.0 %collective-permute-start.8 = (f32[72,128]{1,0:T(8,128)S(1)}, f32[72,128]{1,0:T(8,128)S(1)}, u32[]{:S(2)}, u32[]{:S(2)}) collective-permute-start(f32[72,128]{1,0:T(8,128)S(1)} %add_add_fusion.1), channel_id=1, source_target_pairs={{0,2},{1,5},{2,0},{3,7},{4,6},{5,1},{6,4},{7,3},{8,10},{9,13},{10,... | collective-permute-start | bytes 110600 | tf_op jit(solution)/shard_map/ppermute | solution.py:282
  28.8 6.0 %collective-permute-start.9 = (f32[72,128]{1,0:T(8,128)S(1)}, f32[72,128]{1,0:T(8,128)S(1)}, u32[]{:S(2)}, u32[]{:S(2)}) collective-permute-start(f32[72,128]{1,0:T(8,128)S(1)} %add.41), channel_id=1, source_target_pairs={{0,4},{1,3},{2,6},{3,1},{4,0},{5,7},{6,2},{7,5},{8,12},{9,11},{10,... | collective-permute-start | bytes 110600 | tf_op jit(solution)/shard_map/ppermute | solution.py:282
  30.4 8.7 %collective-permute-start.10 = (f32[128,128]{1,0:T(8,128)S(1)}, f32[128,128]{1,0:T(8,128)S(1)}, u32[]{:S(2)}, u32[]{:S(2)}) collective-permute-start(f32[128,128]{1,0:T(8,128)S(1)} %get-tuple-element.34), channel_id=1, source_target_pairs={{0,24},{1,25},{2,26},{3,27},{4,28},{5,29},{6,30},{7,31},{8,16},{9,... | collective-permute-start | bytes 196616 | tf_op jit(solution)/shard_map/ppermute | solution.py:282
  31.0 8.1 %collective-permute-start.11 = (f32[128,128]{1,0:T(8,128)S(1)}, f32[128,128]{1,0:T(8,128)S(1)}, u32[]{:S(2)}, u32[]{:S(2)}) collective-permute-start(f32[128,128]{1,0:T(8,128)S(1)} %get-tuple-element.33), channel_id=1, source_target_pairs={{0,16},{1,17},{2,18},{3,19},{4,20},{5,21},{6,22},{7,23},{8,24},{9,... | collective-permute-start | bytes 196616 | tf_op jit(solution)/shard_map/ppermute | solution.py:282
  31.0 8.1 %collective-permute-start.12 = (f32[128,128]{1,0:T(8,128)S(1)}, f32[128,128]{1,0:T(8,128)S(1)}, u32[]{:S(2)}, u32[]{:S(2)}) collective-permute-start(f32[128,128]{1,0:T(8,128)S(1)} %get-tuple-element.32), channel_id=1, source_target_pairs={{0,8},{1,9},{2,10},{3,11},{4,12},{5,13},{6,14},{7,15},{8,0},{9,1},... | collective-permute-start | bytes 196616 | tf_op jit(solution)/shard_map/ppermute | solution.py:282

commit v10 on v9

--- a/solution.py
+++ b/solution.py
@@ -286,14 +286,15 @@
     got = exchange(send, core)
     keep, = project_call(owner, split, near, ((0, 8),), "project_first")
     got, gram = tie((got, gram + exchange(gram, core)))
-    got = exchange(keep + got, x, y)
+    far, split = tie((keep + got, split))
+    got = exchange(far, x, y)
     send, sums = project_call(owner, split, near, ((1, 0), (0, 0)), "project_rest")
     sums = sums + exchange(send, core)
     over_z = [exchange(gram, away) for away in (z | zz, zz, z)]
+    got, over_z[0] = tie((got, over_z[0]))
+    sums, gram = tie((sums + got, gram))
+    got = exchange(sums[4:], y, x)
     gram = (gram + over_z[2]) + (over_z[1] + over_z[0])
-    got, gram = tie((got, gram))
-    sums = sums + got
-    got = exchange(sums[4:], y, x)
     gram = gram + exchange(gram, x, y)
     got, gram = tie((got, gram))
     sums = sums[:4] + got

time: 40.5 us -> 38.5 us (0.951)
  waiting for transfers between devices: 10.7 us -> 6.9 us
  starting transfers between devices: 16.2 us -> 18.1 us
    ppermute x13, waiting for transfers between devices: 10.7 us -> 6.9 us  [exchange(): return lax.ppermute(array, AXES, pairs)]
    ppermute x13, starting transfers between devices: 16.2 us -> 18.1 us  [exchange(): return lax.ppermute(array, AXES, pairs)]
  transfers between devices with their start and end apart: 13 -> 13, of which waited for: 5 -> 7; matrix products, arithmetic and copies ran while one was open for 0% -> 0% of each run, Pallas kernels for 15% -> 16%
where the time goes in v10:
time: 38.5 us; the launch traced here: 38.4 us
  starting transfers between devices  18.1 us (47%)
  Pallas kernels  12.4 us (32%)
  waiting for transfers between devices  6.9 us (18%)
  between operations  0.74 us (2%)
    ppermute x13, starting transfers between devices, exchange(): return lax.ppermute(array, AXES, pairs)  18.1 us
    ppermute x13, waiting for transfers between devices, exchange(): return lax.ppermute(array, AXES, pairs)  6.9 us
    pallas_call x1, Pallas kernels, rows_call(): pl.pallas_call(rows_kernel, in_specs=[pl.BlockSpec(memory_space=pltpu.SME...  5.24 us
    pallas_call x1, Pallas kernels, factor_call(): pl.pallas_call(factor_kernel, in_specs=[pl.BlockSpec(memory_space=pltpu.V...  4.21 us
    pallas_call x2, Pallas kernels, project_call(): pl.pallas_call(functools.partial(project_kernel, parts), in_specs=[pl.Blo...  1.77 us
    pallas_call x1, Pallas kernels, finish_call(): pl.pallas_call(functools.partial(finish_kernel, float(total_rows) ** 0.5,...  1.17 us
  transfers between devices with their start and end apart: 13, of which 7 were waited for; matrix products, arithmetic and copies ran while one was open for 0% of the time, Pallas kernels for 16%

profile of v10, /device:TPU:0, one launch (start us, length us, event | category | flops | bytes accessed | tf_op | source)
XLA Modules:
  0.0 38.4 jit_solution(15499446903898633313)
XLA Ops:
  0.6 5.2 %sketch_rows.1 = (bf16[576,4096]{1,0:T(8,128)(2,1)S(1)}, f32[576,128]{1,0:T(8,128)S(1)}, f32[72,128]{1,0:T(8,128)S(1)}, bf16[256,576]{1,0:T(8,128)(2,1)S(1)}, f32[8,128,128]{2,1,0:T(8,128)S(1)}) custom-call(s32[1]{0:T(128)} %bitcast.owner_ref, bf16[576,4096]{1,0:T(8,128)(2,1)} %slab_hbm.1, bf16[4096,128]{1,0:T(8,128)(2,1)} %sketch_hbm.1), custom_call_target="tpu_custom_call" | custom-call | flops 905969664 | bytes 4718592 | tf_op jit(solution)/shard_map/sketch_rows/pallas_call | solution.py:133
  5.9 0.5 %collective-permute-start = (f32[8,128,128]{2,1,0:T(8,128)S(1)}, f32[8,128,128]{2,1,0:T(8,128)S(1)}, u32[]{:S(2)}, u32[]{:S(2)}) collective-permute-start(f32[8,128,128]{2,1,0:T(8,128)S(1)} %get-tuple-element.23), channel_id=1, source_target_pairs={{0,1},{1,0},{2,3},{3,2},{4,5},{5,4},{6,7},{7,6},{8,9},{9,8},{10,11... | collective-permute-start | bytes 1572872 | tf_op jit(solution)/shard_map/ppermute | solution.py:282
  6.4 0.1 collective-permute-start.1
  6.5 0.7 %project_first.1 = f32[8,128,128]{2,1,0:T(8,128)S(1)} custom-call(s32[1]{0:T(128)} %bitcast.owner_ref, bf16[256,576]{1,0:T(8,128)(2,1)S(1)} %get-tuple-element.26.split_ref, bf16[576,4096]{1,0:T(8,128)(2,1)S(1)} %get-tuple-element.22.slab_ref), custom_call_target="tpu_custom_call" | custom-call | flops 301989888 | bytes 2359296 | tf_op jit(solution)/shard_map/project_first/pallas_call | solution.py:115
  7.2 0.8 %collective-permute-done.1 = f32[72,128]{1,0:T(8,128)S(1)} collective-permute-done((f32[72,128]{1,0:T(8,128)S(1)}, f32[72,128]{1,0:T(8,128)S(1)}, u32[]{:S(2)}, u32[]{:S(2)}) %collective-permute-start.1) | collective-permute-done | bytes 36896 | tf_op jit(solution)/shard_map/ppermute | solution.py:282
  8.1 2.9 %collective-permute-start.3 = (f32[8,128,128]{2,1,0:T(8,128)S(1)}, f32[8,128,128]{2,1,0:T(8,128)S(1)}, u32[]{:S(2)}, u32[]{:S(2)}) collective-permute-start(f32[8,128,128]{2,1,0:T(8,128)S(1)} %add.35), channel_id=1, source_target_pairs={{0,2},{1,5},{2,0},{3,7},{4,6},{5,1},{6,4},{7,3},{8,10},{9,13},{10,... | collective-permute-start | bytes 1572872 | tf_op jit(solution)/shard_map/ppermute | solution.py:282
  11.0 1.1 %project_rest.1 = (f32[8,128,128]{2,1,0:T(8,128)S(1)}, f32[8,128,128]{2,1,0:T(8,128)S(1)}) custom-call(s32[1]{0:T(128)} %bitcast.owner_ref, bf16[256,576]{1,0:T(8,128)(2,1)S(1)} %get-tuple-element.26.split_ref, bf16[576,4096]{1,0:T(8,128)(2,1)S(1)} %get-tuple-element.22.slab_ref), custom_call_target="tpu_custom_call" | custom-call | flops 603979776 | bytes 2359296 | tf_op jit(solution)/shard_map/project_rest/pallas_call | solution.py:115
  12.2 3.7 %collective-permute-start.4 = (f32[72,128]{1,0:T(8,128)S(1)}, f32[72,128]{1,0:T(8,128)S(1)}, u32[]{:S(2)}, u32[]{:S(2)}) collective-permute-start(f32[72,128]{1,0:T(8,128)S(1)} %add.34), channel_id=1, source_target_pairs={{0,24},{1,25},{2,26},{3,27},{4,28},{5,29},{6,30},{7,31},{8,16},{9,... | collective-permute-start | bytes 110600 | tf_op jit(solution)/shard_map/ppermute | solution.py:282
  15.9 0.8 %collective-permute-start.6 = (f32[72,128]{1,0:T(8,128)S(1)}, f32[72,128]{1,0:T(8,128)S(1)}, u32[]{:S(2)}, u32[]{:S(2)}) collective-permute-start(f32[72,128]{1,0:T(8,128)S(1)} %add.34), channel_id=1, source_target_pairs={{0,8},{1,9},{2,10},{3,11},{4,12},{5,13},{6,14},{7,15},{8,0},{9,1},... | collective-permute-start | bytes 110600 | tf_op jit(solution)/shard_map/ppermute | solution.py:282
  16.6 1.4 %collective-permute-done.4 = f32[72,128]{1,0:T(8,128)S(1)} collective-permute-done((f32[72,128]{1,0:T(8,128)S(1)}, f32[72,128]{1,0:T(8,128)S(1)}, u32[]{:S(2)}, u32[]{:S(2)}) %collective-permute-start.4) | collective-permute-done | bytes 36896 | tf_op jit(solution)/shard_map/ppermute | solution.py:282
  18.0 0.2 collective-permute-done.3
  18.2 0.1 add_add_fusion
  18.3 2.1 %collective-permute-start.5 = (f32[4,128,128]{2,1,0:T(8,128)S(1)}, f32[4,128,128]{2,1,0:T(8,128)S(1)}, u32[]{:S(2)}, u32[]{:S(2)}) collective-permute-start(f32[4,128,128]{2,1,0:T(8,128)S(1)} %slice.19), channel_id=1, source_target_pairs={{0,4},{1,3},{2,6},{3,1},{4,0},{5,7},{6,2},{7,5},{8,12},{9,11},{10,... | collective-permute-start | bytes 786440 | tf_op jit(solution)/shard_map/ppermute | solution.py:282
  20.4 0.3 collective-permute-done.7
  20.7 1.4 %collective-permute-start.8 = (f32[72,128]{1,0:T(8,128)S(1)}, f32[72,128]{1,0:T(8,128)S(1)}, u32[]{:S(2)}, u32[]{:S(2)}) collective-permute-start(f32[72,128]{1,0:T(8,128)S(1)} %add_add_fusion.1), channel_id=1, source_target_pairs={{0,2},{1,5},{2,0},{3,7},{4,6},{5,1},{6,4},{7,3},{8,10},{9,13},{10,... | collective-permute-start | bytes 110600 | tf_op jit(solution)/shard_map/ppermute | solution.py:282
  22.1 2.6 %collective-permute-done.8 = f32[72,128]{1,0:T(8,128)S(1)} collective-permute-done((f32[72,128]{1,0:T(8,128)S(1)}, f32[72,128]{1,0:T(8,128)S(1)}, u32[]{:S(2)}, u32[]{:S(2)}) %collective-permute-start.8) | collective-permute-done | bytes 36896 | tf_op jit(solution)/shard_map/ppermute | solution.py:282
  24.8 0.4 %collective-permute-done.5 = f32[4,128,128]{2,1,0:T(8,128)S(1)} collective-permute-done((f32[4,128,128]{2,1,0:T(8,128)S(1)}, f32[4,128,128]{2,1,0:T(8,128)S(1)}, u32[]{:S(2)}, u32[]{:S(2)}) %collective-permute-start.5) | collective-permute-done | bytes 262176 | tf_op jit(solution)/shard_map/ppermute | solution.py:282
  25.2 2.1 %collective-permute-start.9 = (f32[72,128]{1,0:T(8,128)S(1)}, f32[72,128]{1,0:T(8,128)S(1)}, u32[]{:S(2)}, u32[]{:S(2)}) collective-permute-start(f32[72,128]{1,0:T(8,128)S(1)} %add.41), channel_id=1, source_target_pairs={{0,4},{1,3},{2,6},{3,1},{4,0},{5,7},{6,2},{7,5},{8,12},{9,11},{10,... | collective-permute-start | bytes 110600 | tf_op jit(solution)/shard_map/ppermute | solution.py:282
  27.3 1.2 %collective-permute-start.12 = (f32[128,128]{1,0:T(8,128)S(1)}, f32[128,128]{1,0:T(8,128)S(1)}, u32[]{:S(2)}, u32[]{:S(2)}) collective-permute-start(f32[128,128]{1,0:T(8,128)S(1)} %get-tuple-element.40), channel_id=1, source_target_pairs={{0,8},{1,9},{2,10},{3,11},{4,12},{5,13},{6,14},{7,15},{8,0},{9,1},... | collective-permute-start | bytes 196616 | tf_op jit(solution)/shard_map/ppermute | solution.py:282
  28.6 2.6 %collective-permute-start.11 = (f32[128,128]{1,0:T(8,128)S(1)}, f32[128,128]{1,0:T(8,128)S(1)}, u32[]{:S(2)}, u32[]{:S(2)}) collective-permute-start(f32[128,128]{1,0:T(8,128)S(1)} %get-tuple-element.41), channel_id=1, source_target_pairs={{0,16},{1,17},{2,18},{3,19},{4,20},{5,21},{6,22},{7,23},{8,24},{9,... | collective-permute-start | bytes 196616 | tf_op jit(solution)/shard_map/ppermute | solution.py:282
  31.1 0.6 %collective-permute-start.10 = (f32[128,128]{1,0:T(8,128)S(1)}, f32[128,128]{1,0:T(8,128)S(1)}, u32[]{:S(2)}, u32[]{:S(2)}) collective-permute-start(f32[128,128]{1,0:T(8,128)S(1)} %get-tuple-element.42), channel_id=1, source_target_pairs={{0,24},{1,25},{2,26},{3,27},{4,28},{5,29},{6,30},{7,31},{8,16},{9,... | collective-permute-start | bytes 196616 | tf_op jit(solution)/shard_map/ppermute | solution.py:282
  31.8 4.2 %factor.1.inverse_ref = f32[128,128]{1,0:T(8,128)S(1)} custom-call(f32[72,128]{1,0:T(8,128)S(1)} %add.43.gram_ref), custom_call_target="tpu_custom_call" | custom-call | flops 4000000000 | bytes 73728 | tf_op jit(solution)/shard_map/factor/pallas_call | solution.py:221
  36.0 1.2 %collective-permute-done.10.refs_0_ = f32[128,128]{1,0:T(8,128)S(1)} collective-permute-done((f32[128,128]{1,0:T(8,128)S(1)}, f32[128,128]{1,0:T(8,128)S(1)}, u32[]{:S(2)}, u32[]{:S(2)}) %collective-permute-start.10) | collective-permute-done | bytes 65568 | tf_op jit(solution)/shard_map/ppermute | solution.py:282
  37.2 1.2 %finish.1 = (f32[576,128]{1,0:T(8,128)}, bf16[128,128]{1,0:T(8,128)(2,1)}) custom-call(f32[128,128]{1,0:T(8,128)S(1)} %factor.1.inverse_ref, f32[576,128]{1,0:T(8,128)S(1)} %get-tuple-element.38.first_ref, f32[128,128]{1,0:T(8,128)S(1)} %slice_bitcast_fusion.3.sums_ref, f32[128,128]{1,0:T(8,128)S(1)} %collective-permute-done.10.refs_0_, ...), custom_call_target="tpu_custom_call" | custom-call | flops 113246208 | bytes 589824 | tf_op jit(solution)/shard_map/finish/pallas_call | solution.py:252
  (17 shorter events, 0.3 us)
Async XLA Ops:
  5.9 2.1 %collective-permute-start = (f32[8,128,128]{2,1,0:T(8,128)S(1)}, f32[8,128,128]{2,1,0:T(8,128)S(1)}, u32[]{:S(2)}, u32[]{:S(2)}) collective-permute-start(f32[8,128,128]{2,1,0:T(8,128)S(1)} %get-tuple-element.23), channel_id=1, source_target_pairs={{0,1},{1,0},{2,3},{3,2},{4,5},{5,4},{6,7},{7,6},{8,9},{9,8},{10,11... | collective-permute-start | bytes 1572872 | tf_op jit(solution)/shard_map/ppermute | solution.py:282
  6.4 1.6 %collective-permute-start.1 = (f32[72,128]{1,0:T(8,128)S(1)}, f32[72,128]{1,0:T(8,128)S(1)}, u32[]{:S(2)}, u32[]{:S(2)}) collective-permute-start(f32[72,128]{1,0:T(8,128)S(1)} %get-tuple-element.24), channel_id=1, source_target_pairs={{0,1},{1,0},{2,3},{3,2},{4,5},{5,4},{6,7},{7,6},{8,9},{9,8},{10,11... | collective-permute-start | bytes 110600 | tf_op jit(solution)/shard_map/ppermute | solution.py:282
  8.1 10.1 %collective-permute-start.3 = (f32[8,128,128]{2,1,0:T(8,128)S(1)}, f32[8,128,128]{2,1,0:T(8,128)S(1)}, u32[]{:S(2)}, u32[]{:S(2)}) collective-permute-start(f32[8,128,128]{2,1,0:T(8,128)S(1)} %add.35), channel_id=1, source_target_pairs={{0,2},{1,5},{2,0},{3,7},{4,6},{5,1},{6,4},{7,3},{8,10},{9,13},{10,... | collective-permute-start | bytes 1572872 | tf_op jit(solution)/shard_map/ppermute | solution.py:282
  12.1 6.1 %collective-permute-start.2 = (f32[8,128,128]{2,1,0:T(8,128)S(1)}, f32[8,128,128]{2,1,0:T(8,128)S(1)}, u32[]{:S(2)}, u32[]{:S(2)}) collective-permute-start(f32[8,128,128]{2,1,0:T(8,128)S(1)} %get-tuple-element.28), channel_id=1, source_target_pairs={{0,1},{1,0},{2,3},{3,2},{4,5},{5,4},{6,7},{7,6},{8,9},{9,8},{10,11... | collective-permute-start | bytes 1572872 | tf_op jit(solution)/shard_map/ppermute | solution.py:282
  12.2 5.8 %collective-permute-start.4 = (f32[72,128]{1,0:T(8,128)S(1)}, f32[72,128]{1,0:T(8,128)S(1)}, u32[]{:S(2)}, u32[]{:S(2)}) collective-permute-start(f32[72,128]{1,0:T(8,128)S(1)} %add.34), channel_id=1, source_target_pairs={{0,24},{1,25},{2,26},{3,27},{4,28},{5,29},{6,30},{7,31},{8,16},{9,... | collective-permute-start | bytes 110600 | tf_op jit(solution)/shard_map/ppermute | solution.py:282
  15.8 4.9 %collective-permute-start.7 = (f32[72,128]{1,0:T(8,128)S(1)}, f32[72,128]{1,0:T(8,128)S(1)}, u32[]{:S(2)}, u32[]{:S(2)}) collective-permute-start(f32[72,128]{1,0:T(8,128)S(1)} %add.34), channel_id=1, source_target_pairs={{0,16},{1,17},{2,18},{3,19},{4,20},{5,21},{6,22},{7,23},{8,24},{9,... | collective-permute-start | bytes 110600 | tf_op jit(solution)/shard_map/ppermute | solution.py:282
  15.9 4.9 %collective-permute-start.6 = (f32[72,128]{1,0:T(8,128)S(1)}, f32[72,128]{1,0:T(8,128)S(1)}, u32[]{:S(2)}, u32[]{:S(2)}) collective-permute-start(f32[72,128]{1,0:T(8,128)S(1)} %add.34), channel_id=1, source_target_pairs={{0,8},{1,9},{2,10},{3,11},{4,12},{5,13},{6,14},{7,15},{8,0},{9,1},... | collective-permute-start | bytes 110600 | tf_op jit(solution)/shard_map/ppermute | solution.py:282
  18.3 6.9 %collective-permute-start.5 = (f32[4,128,128]{2,1,0:T(8,128)S(1)}, f32[4,128,128]{2,1,0:T(8,128)S(1)}, u32[]{:S(2)}, u32[]{:S(2)}) collective-permute-start(f32[4,128,128]{2,1,0:T(8,128)S(1)} %slice.19), channel_id=1, source_target_pairs={{0,4},{1,3},{2,6},{3,1},{4,0},{5,7},{6,2},{7,5},{8,12},{9,11},{10,... | collective-permute-start | bytes 786440 | tf_op jit(solution)/shard_map/ppermute | solution.py:282
  20.7 4.0 %collective-permute-start.8 = (f32[72,128]{1,0:T(8,128)S(1)}, f32[72,128]{1,0:T(8,128)S(1)}, u32[]{:S(2)}, u32[]{:S(2)}) collective-permute-start(f32[72,128]{1,0:T(8,128)S(1)} %add_add_fusion.1), channel_id=1, source_target_pairs={{0,2},{1,5},{2,0},{3,7},{4,6},{5,1},{6,4},{7,3},{8,10},{9,13},{10,... | collective-permute-start | bytes 110600 | tf_op jit(solution)/shard_map/ppermute | solution.py:282
  25.2 6.6 %collective-permute-start.9 = (f32[72,128]{1,0:T(8,128)S(1)}, f32[72,128]{1,0:T(8,128)S(1)}, u32[]{:S(2)}, u32[]{:S(2)}) collective-permute-start(f32[72,128]{1,0:T(8,128)S(1)} %add.41), channel_id=1, source_target_pairs={{0,4},{1,3},{2,6},{3,1},{4,0},{5,7},{6,2},{7,5},{8,12},{9,11},{10,... | collective-permute-start | bytes 110600 | tf_op jit(solution)/shard_map/ppermute | solution.py:282
  27.3 8.7 %collective-permute-start.12 = (f32[128,128]{1,0:T(8,128)S(1)}, f32[128,128]{1,0:T(8,128)S(1)}, u32[]{:S(2)}, u32[]{:S(2)}) collective-permute-start(f32[128,128]{1,0:T(8,128)S(1)} %get-tuple-element.40), channel_id=1, source_target_pairs={{0,8},{1,9},{2,10},{3,11},{4,12},{5,13},{6,14},{7,15},{8,0},{9,1},... | collective-permute-start | bytes 196616 | tf_op jit(solution)/shard_map/ppermute | solution.py:282
  28.6 7.5 %collective-permute-start.11 = (f32[128,128]{1,0:T(8,128)S(1)}, f32[128,128]{1,0:T(8,128)S(1)}, u32[]{:S(2)}, u32[]{:S(2)}) collective-permute-start(f32[128,128]{1,0:T(8,128)S(1)} %get-tuple-element.41), channel_id=1, source_target_pairs={{0,16},{1,17},{2,18},{3,19},{4,20},{5,21},{6,22},{7,23},{8,24},{9,... | collective-permute-start | bytes 196616 | tf_op jit(solution)/shard_map/ppermute | solution.py:282
  31.1 6.1 %collective-permute-start.10 = (f32[128,128]{1,0:T(8,128)S(1)}, f32[128,128]{1,0:T(8,128)S(1)}, u32[]{:S(2)}, u32[]{:S(2)}) collective-permute-start(f32[128,128]{1,0:T(8,128)S(1)} %get-tuple-element.42), channel_id=1, source_target_pairs={{0,24},{1,25},{2,26},{3,27},{4,28},{5,29},{6,30},{7,31},{8,16},{9,... | collective-permute-start | bytes 196616 | tf_op jit(solution)/shard_map/ppermute | solution.py:282

commit v11 on v10

--- a/solution.py
+++ b/solution.py
@@ -20,8 +20,10 @@
     mine = lax.shift_right_logical(owner, 1)
 
     def columns(place):
-        one, two = place // 8, place // 4 % 2
-        away = jnp.where(wanted == 0, one + 2 * two, two + 2 * one) + 4 * (place % 4)
+        one, rest = place // 8, place % 8
+        even = one + 2 * (rest // 4) + 4 * (rest % 4)
+        odd = 2 * one + rest % 2 + 4 * (rest // 2)
+        away = jnp.where(wanted == 0, even, odd)
         at = pl.multiple_of((2 * lax.bitwise_xor(mine, away) + wanted) * LANES, LANES)
         return slab_ref[:, pl.ds(at, LANES)]
 
@@ -279,7 +281,7 @@
     def exchange(array, away, away_odd=None):
         odd = away if away_odd is None else away_odd
         pairs = [(i, i ^ (odd if i & core else away)) for i in range(devices_all)]
-        return lax.ppermute(array, AXES, pairs)
+        return lax.ppermute(array, AXES, [(i, j) for i, j in pairs if i != j])
 
     owner = lax.shift_right_logical(me, low_bits).astype(jnp.int32).reshape(1)
     near, first, gram, split, send = rows_call(owner, slab, sketch)
@@ -293,13 +295,19 @@
     over_z = [exchange(gram, away) for away in (z | zz, zz, z)]
     got, over_z[0] = tie((got, over_z[0]))
     sums, gram = tie((sums + got, gram))
-    got = exchange(sums[4:], y, x)
+    got_far = exchange(sums[6:], y, z | zz)
+    got_mid = exchange(sums[4:6], y, zz)
+    got_near = exchange(sums[2:4], 0, z)
     gram = (gram + over_z[2]) + (over_z[1] + over_z[0])
-    gram = gram + exchange(gram, x, y)
-    got, gram = tie((got, gram))
-    sums = sums[:4] + got
-    gram = gram + exchange(gram, y, x)
-    over_z = [exchange(sums[i], away) for i, away in ((3, z | zz), (2, zz), (1, z))]
+    got_gram = exchange(gram, x)
+    upper, gram = tie((sums[2:4] + got_far, gram))
+    over_z = [exchange(upper[1], z | zz, 0), exchange(upper[0], zz, 0)]
+    gram = gram + got_gram
+    got_gram = exchange(gram, y)
+    sums = sums[:2] + got_mid + got_near + jnp.where(lax.bitwise_and(owner[0], 1) == 1, got_far, 0.0)
+    sums, gram = tie((sums, gram))
+    over_z.append(exchange(sums[1], z, x))
+    gram = gram + got_gram
     for bit in range(low_bits):
         gram = gram + exchange(gram, 1 << bit)
     sums, gram = tie((sums, gram))

time: 38.5 us -> 42.8 us (1.11)
  starting transfers between devices: 18.1 us -> 22.8 us
  waiting for transfers between devices: 6.9 us -> 6.33 us
    ppermute x13 -> x15, starting transfers between devices: 18.1 us -> 22.8 us  [exchange(): return lax.ppermute(array, AXES, [(i, j) for i, j in pairs if i != j])]
    ppermute x13 -> x15, waiting for transfers between devices: 6.9 us -> 6.33 us  [exchange(): return lax.ppermute(array, AXES, [(i, j) for i, j in pairs if i != j])]
  transfers between devices with their start and end apart: 13 -> 15, of which waited for: 7 -> 6; matrix products, arithmetic and copies ran while one was open for 0% -> 0% of each run, Pallas kernels for 16% -> 14%
where the time goes in v11:
time: 42.8 us; the launch traced here: 42.6 us
  starting transfers between devices  22.8 us (53%)
  Pallas kernels  12.4 us (29%)
  waiting for transfers between devices  6.33 us (15%)
  between operations  0.81 us (2%)
    ppermute x15, starting transfers between devices, exchange(): return lax.ppermute(array, AXES, [(i, j) for i, j in pairs if i != j])  22.8 us
    ppermute x15, waiting for transfers between devices, exchange(): return lax.ppermute(array, AXES, [(i, j) for i, j in pairs if i != j])  6.33 us
    pallas_call x1, Pallas kernels, rows_call(): pl.pallas_call(rows_kernel, in_specs=[pl.BlockSpec(memory_space=pltpu.SME...  5.23 us
    pallas_call x1, Pallas kernels, factor_call(): pl.pallas_call(factor_kernel, in_specs=[pl.BlockSpec(memory_space=pltpu.V...  4.21 us
    pallas_call x2, Pallas kernels, project_call(): pl.pallas_call(functools.partial(project_kernel, parts), in_specs=[pl.Blo...  1.75 us
    pallas_call x1, Pallas kernels, finish_call(): pl.pallas_call(functools.partial(finish_kernel, float(total_rows) ** 0.5,...  1.17 us
  transfers between devices with their start and end apart: 15, of which 6 were waited for; matrix products, arithmetic and copies ran while one was open for 0% of the time, Pallas kernels for 14%

profile of v11, /device:TPU:0, one launch (start us, length us, event | category | flops | bytes accessed | tf_op | source)
XLA Modules:
  0.0 42.6 jit_solution(16253901566646424525)
XLA Ops:
  0.6 5.2 %sketch_rows.1 = (bf16[576,4096]{1,0:T(8,128)(2,1)S(1)}, f32[576,128]{1,0:T(8,128)S(1)}, f32[72,128]{1,0:T(8,128)S(1)}, bf16[256,576]{1,0:T(8,128)(2,1)S(1)}, f32[8,128,128]{2,1,0:T(8,128)S(1)}) custom-call(s32[1]{0:T(128)} %bitcast.owner_ref, bf16[576,4096]{1,0:T(8,128)(2,1)} %slab_hbm.1, bf16[4096,128]{1,0:T(8,128)(2,1)} %sketch_hbm.1), custom_call_target="tpu_custom_call" | custom-call | flops 905969664 | bytes 4718592 | tf_op jit(solution)/shard_map/sketch_rows/pallas_call | solution.py:135
  5.9 0.5 %collective-permute-start = (f32[8,128,128]{2,1,0:T(8,128)S(1)}, f32[8,128,128]{2,1,0:T(8,128)S(1)}, u32[]{:S(2)}, u32[]{:S(2)}) collective-permute-start(f32[8,128,128]{2,1,0:T(8,128)S(1)} %get-tuple-element.25), channel_id=1, source_target_pairs={{0,1},{1,0},{2,3},{3,2},{4,5},{5,4},{6,7},{7,6},{8,9},{9,8},{10,11... | collective-permute-start | bytes 1572872 | tf_op jit(solution)/shard_map/ppermute | solution.py:284
  6.4 0.1 collective-permute-start.1
  6.5 0.7 %project_first.1 = f32[8,128,128]{2,1,0:T(8,128)S(1)} custom-call(s32[1]{0:T(128)} %bitcast.owner_ref, bf16[256,576]{1,0:T(8,128)(2,1)S(1)} %get-tuple-element.28.split_ref, bf16[576,4096]{1,0:T(8,128)(2,1)S(1)} %get-tuple-element.24.slab_ref), custom_call_target="tpu_custom_call" | custom-call | flops 301989888 | bytes 2359296 | tf_op jit(solution)/shard_map/project_first/pallas_call | solution.py:117
  7.2 0.8 %collective-permute-done.1 = f32[72,128]{1,0:T(8,128)S(1)} collective-permute-done((f32[72,128]{1,0:T(8,128)S(1)}, f32[72,128]{1,0:T(8,128)S(1)}, u32[]{:S(2)}, u32[]{:S(2)}) %collective-permute-start.1) | collective-permute-done | bytes 36896 | tf_op jit(solution)/shard_map/ppermute | solution.py:284
  8.1 2.9 %collective-permute-start.3 = (f32[8,128,128]{2,1,0:T(8,128)S(1)}, f32[8,128,128]{2,1,0:T(8,128)S(1)}, u32[]{:S(2)}, u32[]{:S(2)}) collective-permute-start(f32[8,128,128]{2,1,0:T(8,128)S(1)} %add.44), channel_id=1, source_target_pairs={{0,2},{1,5},{2,0},{3,7},{4,6},{5,1},{6,4},{7,3},{8,10},{9,13},{10,... | collective-permute-start | bytes 1572872 | tf_op jit(solution)/shard_map/ppermute | solution.py:284
  11.0 1.1 %project_rest.1 = (f32[8,128,128]{2,1,0:T(8,128)S(1)}, f32[8,128,128]{2,1,0:T(8,128)S(1)}) custom-call(s32[1]{0:T(128)} %bitcast.owner_ref, bf16[256,576]{1,0:T(8,128)(2,1)S(1)} %get-tuple-element.28.split_ref, bf16[576,4096]{1,0:T(8,128)(2,1)S(1)} %get-tuple-element.24.slab_ref), custom_call_target="tpu_custom_call" | custom-call | flops 603979776 | bytes 2359296 | tf_op jit(solution)/shard_map/project_rest/pallas_call | solution.py:117
  12.2 3.7 %collective-permute-start.4 = (f32[72,128]{1,0:T(8,128)S(1)}, f32[72,128]{1,0:T(8,128)S(1)}, u32[]{:S(2)}, u32[]{:S(2)}) collective-permute-start(f32[72,128]{1,0:T(8,128)S(1)} %add.43), channel_id=1, source_target_pairs={{0,24},{1,25},{2,26},{3,27},{4,28},{5,29},{6,30},{7,31},{8,16},{9,... | collective-permute-start | bytes 110600 | tf_op jit(solution)/shard_map/ppermute | solution.py:284
  15.8 0.8 %collective-permute-start.8 = (f32[72,128]{1,0:T(8,128)S(1)}, f32[72,128]{1,0:T(8,128)S(1)}, u32[]{:S(2)}, u32[]{:S(2)}) collective-permute-start(f32[72,128]{1,0:T(8,128)S(1)} %add.43), channel_id=1, source_target_pairs={{0,8},{1,9},{2,10},{3,11},{4,12},{5,13},{6,14},{7,15},{8,0},{9,1},... | collective-permute-start | bytes 110600 | tf_op jit(solution)/shard_map/ppermute | solution.py:284
  16.6 1.4 %collective-permute-done.4 = f32[72,128]{1,0:T(8,128)S(1)} collective-permute-done((f32[72,128]{1,0:T(8,128)S(1)}, f32[72,128]{1,0:T(8,128)S(1)}, u32[]{:S(2)}, u32[]{:S(2)}) %collective-permute-start.4) | collective-permute-done | bytes 36896 | tf_op jit(solution)/shard_map/ppermute | solution.py:284
  18.0 0.2 collective-permute-done.3
  18.2 0.1 add_add_fusion
  18.3 2.1 %collective-permute-start.5 = (f32[2,128,128]{2,1,0:T(8,128)S(1)}, f32[2,128,128]{2,1,0:T(8,128)S(1)}, u32[]{:S(2)}, u32[]{:S(2)}) collective-permute-start(f32[2,128,128]{2,1,0:T(8,128)S(1)} %get-tuple-element.46), channel_id=1, source_target_pairs={{0,4},{1,17},{2,6},{3,19},{4,0},{5,21},{6,2},{7,23},{8,12},{9,25},... | collective-permute-start | bytes 393224 | tf_op jit(solution)/shard_map/ppermute | solution.py:284
  20.5 0.7 %collective-permute-start.6 = (f32[2,128,128]{2,1,0:T(8,128)S(1)}, f32[2,128,128]{2,1,0:T(8,128)S(1)}, u32[]{:S(2)}, u32[]{:S(2)}) collective-permute-start(f32[2,128,128]{2,1,0:T(8,128)S(1)} %get-tuple-element.48), channel_id=1, source_target_pairs={{1,9},{3,11},{5,13},{7,15},{9,1},{11,3},{13,5},{15,7},{17,25},{19,... | collective-permute-start | bytes 393224 | tf_op jit(solution)/shard_map/ppermute | solution.py:284
  21.2 2.0 %collective-permute-start.10 = (f32[72,128]{1,0:T(8,128)S(1)}, f32[72,128]{1,0:T(8,128)S(1)}, u32[]{:S(2)}, u32[]{:S(2)}) collective-permute-start(f32[72,128]{1,0:T(8,128)S(1)} %add_add_fusion.1), channel_id=1, source_target_pairs={{0,2},{1,3},{2,0},{3,1},{4,6},{5,7},{6,4},{7,5},{8,10},{9,11},{10,... | collective-permute-start | bytes 110600 | tf_op jit(solution)/shard_map/ppermute | solution.py:284
  23.2 0.2 collective-permute-done.5
  23.3 2.0 %collective-permute-done.7 = f32[2,128,128]{2,1,0:T(8,128)S(1)} collective-permute-done((f32[2,128,128]{2,1,0:T(8,128)S(1)}, f32[2,128,128]{2,1,0:T(8,128)S(1)}, u32[]{:S(2)}, u32[]{:S(2)}) %collective-permute-start.7) | collective-permute-done | bytes 131104 | tf_op jit(solution)/shard_map/ppermute | solution.py:284
  25.4 1.7 %collective-permute-start.11 = (f32[72,128]{1,0:T(8,128)S(1)}, f32[72,128]{1,0:T(8,128)S(1)}, u32[]{:S(2)}, u32[]{:S(2)}) collective-permute-start(f32[72,128]{1,0:T(8,128)S(1)} %add.54), channel_id=1, source_target_pairs={{0,4},{1,5},{2,6},{3,7},{4,0},{5,1},{6,2},{7,3},{8,12},{9,13},{10,... | collective-permute-start | bytes 110600 | tf_op jit(solution)/shard_map/ppermute | solution.py:284
  27.2 1.6 %collective-permute-start.14 = (f32[128,128]{1,0:T(8,128)S(1)}, f32[128,128]{1,0:T(8,128)S(1)}, u32[]{:S(2)}, u32[]{:S(2)}) collective-permute-start(f32[128,128]{1,0:T(8,128)S(1)} %slice_bitcast_fusion), channel_id=1, source_target_pairs={{0,8},{1,3},{2,10},{3,1},{4,12},{5,7},{6,14},{7,5},{8,0},{9,11},{1... | collective-permute-start | bytes 196616 | tf_op jit(solution)/shard_map/ppermute | solution.py:284
  28.8 4.7 %collective-permute-start.13 = (f32[128,128]{1,0:T(8,128)S(1)}, f32[128,128]{1,0:T(8,128)S(1)}, u32[]{:S(2)}, u32[]{:S(2)}) collective-permute-start(f32[128,128]{1,0:T(8,128)S(1)} %get-tuple-element.49), channel_id=1, source_target_pairs={{0,16},{2,18},{4,20},{6,22},{8,24},{10,26},{12,28},{14,30},{16,0},... | collective-permute-start | bytes 196616 | tf_op jit(solution)/shard_map/ppermute | solution.py:284
  33.5 1.9 %collective-permute-start.12 = (f32[128,128]{1,0:T(8,128)S(1)}, f32[128,128]{1,0:T(8,128)S(1)}, u32[]{:S(2)}, u32[]{:S(2)}) collective-permute-start(f32[128,128]{1,0:T(8,128)S(1)} %get-tuple-element.50), channel_id=1, source_target_pairs={{0,24},{2,26},{4,28},{6,30},{8,16},{10,18},{12,20},{14,22},{16,8},... | collective-permute-start | bytes 196616 | tf_op jit(solution)/shard_map/ppermute | solution.py:284
  35.4 4.2 %factor.1.inverse_ref = f32[128,128]{1,0:T(8,128)S(1)} custom-call(f32[72,128]{1,0:T(8,128)S(1)} %add.55.gram_ref), custom_call_target="tpu_custom_call" | custom-call | flops 4000000000 | bytes 73728 | tf_op jit(solution)/shard_map/factor/pallas_call | solution.py:223
  39.7 1.8 %collective-permute-done.12.refs_0_ = f32[128,128]{1,0:T(8,128)S(1)} collective-permute-done((f32[128,128]{1,0:T(8,128)S(1)}, f32[128,128]{1,0:T(8,128)S(1)}, u32[]{:S(2)}, u32[]{:S(2)}) %collective-permute-start.12) | collective-permute-done | bytes 65568 | tf_op jit(solution)/shard_map/ppermute | solution.py:284
  41.4 1.2 %finish.1 = (f32[576,128]{1,0:T(8,128)}, bf16[128,128]{1,0:T(8,128)(2,1)}) custom-call(f32[128,128]{1,0:T(8,128)S(1)} %factor.1.inverse_ref, f32[576,128]{1,0:T(8,128)S(1)} %get-tuple-element.41.first_ref, f32[128,128]{1,0:T(8,128)S(1)} %slice_bitcast_fusion.3.sums_ref, f32[128,128]{1,0:T(8,128)S(1)} %collective-permute-done.12.refs_0_, ...), custom_call_target="tpu_custom_call" | custom-call | flops 113246208 | bytes 589824 | tf_op jit(solution)/shard_map/finish/pallas_call | solution.py:254
  (22 shorter events, 0.4 us)
Async XLA Ops:
  5.9 2.1 %collective-permute-start = (f32[8,128,128]{2,1,0:T(8,128)S(1)}, f32[8,128,128]{2,1,0:T(8,128)S(1)}, u32[]{:S(2)}, u32[]{:S(2)}) collective-permute-start(f32[8,128,128]{2,1,0:T(8,128)S(1)} %get-tuple-element.25), channel_id=1, source_target_pairs={{0,1},{1,0},{2,3},{3,2},{4,5},{5,4},{6,7},{7,6},{8,9},{9,8},{10,11... | collective-permute-start | bytes 1572872 | tf_op jit(solution)/shard_map/ppermute | solution.py:284
  6.4 1.6 %collective-permute-start.1 = (f32[72,128]{1,0:T(8,128)S(1)}, f32[72,128]{1,0:T(8,128)S(1)}, u32[]{:S(2)}, u32[]{:S(2)}) collective-permute-start(f32[72,128]{1,0:T(8,128)S(1)} %get-tuple-element.26), channel_id=1, source_target_pairs={{0,1},{1,0},{2,3},{3,2},{4,5},{5,4},{6,7},{7,6},{8,9},{9,8},{10,11... | collective-permute-start | bytes 110600 | tf_op jit(solution)/shard_map/ppermute | solution.py:284
  8.1 10.1 %collective-permute-start.3 = (f32[8,128,128]{2,1,0:T(8,128)S(1)}, f32[8,128,128]{2,1,0:T(8,128)S(1)}, u32[]{:S(2)}, u32[]{:S(2)}) collective-permute-start(f32[8,128,128]{2,1,0:T(8,128)S(1)} %add.44), channel_id=1, source_target_pairs={{0,2},{1,5},{2,0},{3,7},{4,6},{5,1},{6,4},{7,3},{8,10},{9,13},{10,... | collective-permute-start | bytes 1572872 | tf_op jit(solution)/shard_map/ppermute | solution.py:284
  12.1 6.1 %collective-permute-start.2 = (f32[8,128,128]{2,1,0:T(8,128)S(1)}, f32[8,128,128]{2,1,0:T(8,128)S(1)}, u32[]{:S(2)}, u32[]{:S(2)}) collective-permute-start(f32[8,128,128]{2,1,0:T(8,128)S(1)} %get-tuple-element.30), channel_id=1, source_target_pairs={{0,1},{1,0},{2,3},{3,2},{4,5},{5,4},{6,7},{7,6},{8,9},{9,8},{10,11... | collective-permute-start | bytes 1572872 | tf_op jit(solution)/shard_map/ppermute | solution.py:284
  12.2 5.8 %collective-permute-start.4 = (f32[72,128]{1,0:T(8,128)S(1)}, f32[72,128]{1,0:T(8,128)S(1)}, u32[]{:S(2)}, u32[]{:S(2)}) collective-permute-start(f32[72,128]{1,0:T(8,128)S(1)} %add.43), channel_id=1, source_target_pairs={{0,24},{1,25},{2,26},{3,27},{4,28},{5,29},{6,30},{7,31},{8,16},{9,... | collective-permute-start | bytes 110600 | tf_op jit(solution)/shard_map/ppermute | solution.py:284
  15.8 5.3 %collective-permute-start.9 = (f32[72,128]{1,0:T(8,128)S(1)}, f32[72,128]{1,0:T(8,128)S(1)}, u32[]{:S(2)}, u32[]{:S(2)}) collective-permute-start(f32[72,128]{1,0:T(8,128)S(1)} %add.43), channel_id=1, source_target_pairs={{0,16},{1,17},{2,18},{3,19},{4,20},{5,21},{6,22},{7,23},{8,24},{9,... | collective-permute-start | bytes 110600 | tf_op jit(solution)/shard_map/ppermute | solution.py:284
  15.8 5.3 %collective-permute-start.8 = (f32[72,128]{1,0:T(8,128)S(1)}, f32[72,128]{1,0:T(8,128)S(1)}, u32[]{:S(2)}, u32[]{:S(2)}) collective-permute-start(f32[72,128]{1,0:T(8,128)S(1)} %add.43), channel_id=1, source_target_pairs={{0,8},{1,9},{2,10},{3,11},{4,12},{5,13},{6,14},{7,15},{8,0},{9,1},... | collective-permute-start | bytes 110600 | tf_op jit(solution)/shard_map/ppermute | solution.py:284
  18.3 5.0 %collective-permute-start.5 = (f32[2,128,128]{2,1,0:T(8,128)S(1)}, f32[2,128,128]{2,1,0:T(8,128)S(1)}, u32[]{:S(2)}, u32[]{:S(2)}) collective-permute-start(f32[2,128,128]{2,1,0:T(8,128)S(1)} %get-tuple-element.46), channel_id=1, source_target_pairs={{0,4},{1,17},{2,6},{3,19},{4,0},{5,21},{6,2},{7,23},{8,12},{9,25},... | collective-permute-start | bytes 393224 | tf_op jit(solution)/shard_map/ppermute | solution.py:284
  20.4 5.0 %collective-permute-start.7 = (f32[2,128,128]{2,1,0:T(8,128)S(1)}, f32[2,128,128]{2,1,0:T(8,128)S(1)}, u32[]{:S(2)}, u32[]{:S(2)}) collective-permute-start(f32[2,128,128]{2,1,0:T(8,128)S(1)} %get-tuple-element.47), channel_id=1, source_target_pairs={{0,4},{1,25},{2,6},{3,27},{4,0},{5,29},{6,2},{7,31},{8,12},{9,17},... | collective-permute-start | bytes 393224 | tf_op jit(solution)/shard_map/ppermute | solution.py:284
  20.5 4.9 %collective-permute-start.6 = (f32[2,128,128]{2,1,0:T(8,128)S(1)}, f32[2,128,128]{2,1,0:T(8,128)S(1)}, u32[]{:S(2)}, u32[]{:S(2)}) collective-permute-start(f32[2,128,128]{2,1,0:T(8,128)S(1)} %get-tuple-element.48), channel_id=1, source_target_pairs={{1,9},{3,11},{5,13},{7,15},{9,1},{11,3},{13,5},{15,7},{17,25},{19,... | collective-permute-start | bytes 393224 | tf_op jit(solution)/shard_map/ppermute | solution.py:284
  21.2 4.2 %collective-permute-start.10 = (f32[72,128]{1,0:T(8,128)S(1)}, f32[72,128]{1,0:T(8,128)S(1)}, u32[]{:S(2)}, u32[]{:S(2)}) collective-permute-start(f32[72,128]{1,0:T(8,128)S(1)} %add_add_fusion.1), channel_id=1, source_target_pairs={{0,2},{1,3},{2,0},{3,1},{4,6},{5,7},{6,4},{7,5},{8,10},{9,11},{10,... | collective-permute-start | bytes 110600 | tf_op jit(solution)/shard_map/ppermute | solution.py:284
  25.4 10.0 %collective-permute-start.11 = (f32[72,128]{1,0:T(8,128)S(1)}, f32[72,128]{1,0:T(8,128)S(1)}, u32[]{:S(2)}, u32[]{:S(2)}) collective-permute-start(f32[72,128]{1,0:T(8,128)S(1)} %add.54), channel_id=1, source_target_pairs={{0,4},{1,5},{2,6},{3,7},{4,0},{5,1},{6,2},{7,3},{8,12},{9,13},{10,... | collective-permute-start | bytes 110600 | tf_op jit(solution)/shard_map/ppermute | solution.py:284
  27.2 12.5 %collective-permute-start.14 = (f32[128,128]{1,0:T(8,128)S(1)}, f32[128,128]{1,0:T(8,128)S(1)}, u32[]{:S(2)}, u32[]{:S(2)}) collective-permute-start(f32[128,128]{1,0:T(8,128)S(1)} %slice_bitcast_fusion), channel_id=1, source_target_pairs={{0,8},{1,3},{2,10},{3,1},{4,12},{5,7},{6,14},{7,5},{8,0},{9,11},{1... | collective-permute-start | bytes 196616 | tf_op jit(solution)/shard_map/ppermute | solution.py:284
  28.8 10.9 %collective-permute-start.13 = (f32[128,128]{1,0:T(8,128)S(1)}, f32[128,128]{1,0:T(8,128)S(1)}, u32[]{:S(2)}, u32[]{:S(2)}) collective-permute-start(f32[128,128]{1,0:T(8,128)S(1)} %get-tuple-element.49), channel_id=1, source_target_pairs={{0,16},{2,18},{4,20},{6,22},{8,24},{10,26},{12,28},{14,30},{16,0},... | collective-permute-start | bytes 196616 | tf_op jit(solution)/shard_map/ppermute | solution.py:284
  33.5 8.0 %collective-permute-start.12 = (f32[128,128]{1,0:T(8,128)S(1)}, f32[128,128]{1,0:T(8,128)S(1)}, u32[]{:S(2)}, u32[]{:S(2)}) collective-permute-start(f32[128,128]{1,0:T(8,128)S(1)} %get-tuple-element.50), channel_id=1, source_target_pairs={{0,24},{2,26},{4,28},{6,30},{8,16},{10,18},{12,20},{14,22},{16,8},... | collective-permute-start | bytes 196616 | tf_op jit(solution)/shard_map/ppermute | solution.py:284

commit v12 on v10

--- a/solution.py
+++ b/solution.py
@@ -12,6 +12,7 @@
 LANES = 128
 VMEM_LIMIT = 24 * 1024 * 1024
 AHEAD = 2
+ROWS = 256
 
 
 def project(out_ref, split_ref, slab_ref, owner, sibling, first_place):
@@ -67,11 +68,11 @@
 ):
     rows, width = slab_ref.shape
     rank = sketch_ref.shape[1]
-    starts = list(range(0, rows, LANES))
+    starts = list(range(0, rows, ROWS))
     copies = [
         pltpu.make_async_copy(
-            slab_hbm.at[pl.ds(r, min(LANES, rows - r)), :],
-            slab_ref.at[pl.ds(r, min(LANES, rows - r)), :],
+            slab_hbm.at[pl.ds(r, min(ROWS, rows - r)), :],
+            slab_ref.at[pl.ds(r, min(ROWS, rows - r)), :],
             slab_sem.at[k],
         )
         for k, r in enumerate(starts)
@@ -85,7 +86,7 @@
         copies[k].wait()
         if k + AHEAD < len(starts):
             copies[k + AHEAD].start()
-        at = pl.ds(r, min(LANES, rows - r))
+        at = pl.ds(r, min(ROWS, rows - r))
         first = jnp.dot(slab_ref[at, :], sketch_ref[...], preferred_element_type=jnp.float32)
         first_ref[at, :] = first
         turned = first.T
@@ -148,7 +149,7 @@
         scratch_shapes=[
             pltpu.VMEM((width, rank), jnp.bfloat16),
             pltpu.VMEM((rank, rank), jnp.float32),
-            pltpu.SemaphoreType.DMA((-(-rows // LANES),)),
+            pltpu.SemaphoreType.DMA((-(-rows // ROWS),)),
             pltpu.SemaphoreType.DMA,
         ],
         compiler_params=pltpu.CompilerParams(vmem_limit_bytes=VMEM_LIMIT),
@@ -299,7 +300,7 @@
     got, gram = tie((got, gram))
     sums = sums[:4] + got
     gram = gram + exchange(gram, y, x)
-    over_z = [exchange(sums[i], away) for i, away in ((3, z | zz), (2, zz), (1, z))]
+    over_z = [exchange(sums[i], away) for i, away in ((1, z), (2, zz), (3, z | zz))]
     for bit in range(low_bits):
         gram = gram + exchange(gram, 1 << bit)
     sums, gram = tie((sums, gram))

time: 38.5 us -> 37.1 us (0.964)
  waiting for transfers between devices: 6.9 us -> 5.73 us
    ppermute x13, waiting for transfers between devices: 6.9 us -> 5.73 us  [exchange(): return lax.ppermute(array, AXES, pairs)]
  transfers between devices with their start and end apart: 13 -> 13, of which waited for: 7 -> 6; matrix products, arithmetic and copies ran while one was open for 0% -> 0% of each run, Pallas kernels for 16% -> 16%
where the time goes in v12:
time: 37.1 us; the launch traced here: 37 us
  starting transfers between devices  18.1 us (49%)
  Pallas kernels  12.1 us (33%)
  waiting for transfers between devices  5.73 us (15%)
  between operations  0.74 us (2%)
    ppermute x13, starting transfers between devices, exchange(): return lax.ppermute(array, AXES, pairs)  18.1 us
    ppermute x13, waiting for transfers between devices, exchange(): return lax.ppermute(array, AXES, pairs)  5.73 us
    pallas_call x1, Pallas kernels, rows_call(): pl.pallas_call(rows_kernel, in_specs=[pl.BlockSpec(memory_space=pltpu.SME...  4.99 us
    pallas_call x1, Pallas kernels, factor_call(): pl.pallas_call(factor_kernel, in_specs=[pl.BlockSpec(memory_space=pltpu.V...  4.21 us
    pallas_call x2, Pallas kernels, project_call(): pl.pallas_call(functools.partial(project_kernel, parts), in_specs=[pl.Blo...  1.77 us
    pallas_call x1, Pallas kernels, finish_call(): pl.pallas_call(functools.partial(finish_kernel, float(total_rows) ** 0.5,...  1.17 us
  transfers between devices with their start and end apart: 13, of which 6 were waited for; matrix products, arithmetic and copies ran while one was open for 0% of the time, Pallas kernels for 16%

profile of v12, /device:TPU:0, one launch (start us, length us, event | category | flops | bytes accessed | tf_op | source)
XLA Modules:
  0.0 37.0 jit_solution(9740961132314193986)
XLA Ops:
  0.6 5.0 %sketch_rows.1 = (bf16[576,4096]{1,0:T(8,128)(2,1)S(1)}, f32[576,128]{1,0:T(8,128)S(1)}, f32[72,128]{1,0:T(8,128)S(1)}, bf16[256,576]{1,0:T(8,128)(2,1)S(1)}, f32[8,128,128]{2,1,0:T(8,128)S(1)}) custom-call(s32[1]{0:T(128)} %bitcast.owner_ref, bf16[576,4096]{1,0:T(8,128)(2,1)} %slab_hbm.1, bf16[4096,128]{1,0:T(8,128)(2,1)} %sketch_hbm.1), custom_call_target="tpu_custom_call" | custom-call | flops 905969664 | bytes 4718592 | tf_op jit(solution)/shard_map/sketch_rows/pallas_call | solution.py:134
  5.6 0.5 %collective-permute-start = (f32[8,128,128]{2,1,0:T(8,128)S(1)}, f32[8,128,128]{2,1,0:T(8,128)S(1)}, u32[]{:S(2)}, u32[]{:S(2)}) collective-permute-start(f32[8,128,128]{2,1,0:T(8,128)S(1)} %get-tuple-element.23), channel_id=1, source_target_pairs={{0,1},{1,0},{2,3},{3,2},{4,5},{5,4},{6,7},{7,6},{8,9},{9,8},{10,11... | collective-permute-start | bytes 1572872 | tf_op jit(solution)/shard_map/ppermute | solution.py:283
  6.2 0.1 collective-permute-start.1
  6.2 0.7 %project_first.1 = f32[8,128,128]{2,1,0:T(8,128)S(1)} custom-call(s32[1]{0:T(128)} %bitcast.owner_ref, bf16[256,576]{1,0:T(8,128)(2,1)S(1)} %get-tuple-element.26.split_ref, bf16[576,4096]{1,0:T(8,128)(2,1)S(1)} %get-tuple-element.22.slab_ref), custom_call_target="tpu_custom_call" | custom-call | flops 301989888 | bytes 2359296 | tf_op jit(solution)/shard_map/project_first/pallas_call | solution.py:116
  6.9 0.8 %collective-permute-done.1 = f32[72,128]{1,0:T(8,128)S(1)} collective-permute-done((f32[72,128]{1,0:T(8,128)S(1)}, f32[72,128]{1,0:T(8,128)S(1)}, u32[]{:S(2)}, u32[]{:S(2)}) %collective-permute-start.1) | collective-permute-done | bytes 36896 | tf_op jit(solution)/shard_map/ppermute | solution.py:283
  7.8 0.1 add.35
  7.8 2.9 %collective-permute-start.3 = (f32[8,128,128]{2,1,0:T(8,128)S(1)}, f32[8,128,128]{2,1,0:T(8,128)S(1)}, u32[]{:S(2)}, u32[]{:S(2)}) collective-permute-start(f32[8,128,128]{2,1,0:T(8,128)S(1)} %add.35), channel_id=1, source_target_pairs={{0,2},{1,5},{2,0},{3,7},{4,6},{5,1},{6,4},{7,3},{8,10},{9,13},{10,... | collective-permute-start | bytes 1572872 | tf_op jit(solution)/shard_map/ppermute | solution.py:283
  10.8 1.1 %project_rest.1 = (f32[8,128,128]{2,1,0:T(8,128)S(1)}, f32[8,128,128]{2,1,0:T(8,128)S(1)}) custom-call(s32[1]{0:T(128)} %bitcast.owner_ref, bf16[256,576]{1,0:T(8,128)(2,1)S(1)} %get-tuple-element.26.split_ref, bf16[576,4096]{1,0:T(8,128)(2,1)S(1)} %get-tuple-element.22.slab_ref), custom_call_target="tpu_custom_call" | custom-call | flops 603979776 | bytes 2359296 | tf_op jit(solution)/shard_map/project_rest/pallas_call | solution.py:116
  11.9 0.1 collective-permute-start.2
  11.9 3.7 %collective-permute-start.4 = (f32[72,128]{1,0:T(8,128)S(1)}, f32[72,128]{1,0:T(8,128)S(1)}, u32[]{:S(2)}, u32[]{:S(2)}) collective-permute-start(f32[72,128]{1,0:T(8,128)S(1)} %add.34), channel_id=1, source_target_pairs={{0,24},{1,25},{2,26},{3,27},{4,28},{5,29},{6,30},{7,31},{8,16},{9,... | collective-permute-start | bytes 110600 | tf_op jit(solution)/shard_map/ppermute | solution.py:283
  15.6 0.8 %collective-permute-start.6 = (f32[72,128]{1,0:T(8,128)S(1)}, f32[72,128]{1,0:T(8,128)S(1)}, u32[]{:S(2)}, u32[]{:S(2)}) collective-permute-start(f32[72,128]{1,0:T(8,128)S(1)} %add.34), channel_id=1, source_target_pairs={{0,8},{1,9},{2,10},{3,11},{4,12},{5,13},{6,14},{7,15},{8,0},{9,1},... | collective-permute-start | bytes 110600 | tf_op jit(solution)/shard_map/ppermute | solution.py:283
  16.4 1.4 %collective-permute-done.4 = f32[72,128]{1,0:T(8,128)S(1)} collective-permute-done((f32[72,128]{1,0:T(8,128)S(1)}, f32[72,128]{1,0:T(8,128)S(1)}, u32[]{:S(2)}, u32[]{:S(2)}) %collective-permute-start.4) | collective-permute-done | bytes 36896 | tf_op jit(solution)/shard_map/ppermute | solution.py:283
  17.8 0.2 collective-permute-done.3
  17.9 0.1 add_add_fusion
  18.1 2.1 %collective-permute-start.5 = (f32[4,128,128]{2,1,0:T(8,128)S(1)}, f32[4,128,128]{2,1,0:T(8,128)S(1)}, u32[]{:S(2)}, u32[]{:S(2)}) collective-permute-start(f32[4,128,128]{2,1,0:T(8,128)S(1)} %slice.19), channel_id=1, source_target_pairs={{0,4},{1,3},{2,6},{3,1},{4,0},{5,7},{6,2},{7,5},{8,12},{9,11},{10,... | collective-permute-start | bytes 786440 | tf_op jit(solution)/shard_map/ppermute | solution.py:283
  20.2 0.3 collective-permute-done.7
  20.5 1.4 %collective-permute-start.8 = (f32[72,128]{1,0:T(8,128)S(1)}, f32[72,128]{1,0:T(8,128)S(1)}, u32[]{:S(2)}, u32[]{:S(2)}) collective-permute-start(f32[72,128]{1,0:T(8,128)S(1)} %add_add_fusion.1), channel_id=1, source_target_pairs={{0,2},{1,5},{2,0},{3,7},{4,6},{5,1},{6,4},{7,3},{8,10},{9,13},{10,... | collective-permute-start | bytes 110600 | tf_op jit(solution)/shard_map/ppermute | solution.py:283
  21.9 2.7 %collective-permute-done.8 = f32[72,128]{1,0:T(8,128)S(1)} collective-permute-done((f32[72,128]{1,0:T(8,128)S(1)}, f32[72,128]{1,0:T(8,128)S(1)}, u32[]{:S(2)}, u32[]{:S(2)}) %collective-permute-start.8) | collective-permute-done | bytes 36896 | tf_op jit(solution)/shard_map/ppermute | solution.py:283
  24.5 0.4 %collective-permute-done.5 = f32[4,128,128]{2,1,0:T(8,128)S(1)} collective-permute-done((f32[4,128,128]{2,1,0:T(8,128)S(1)}, f32[4,128,128]{2,1,0:T(8,128)S(1)}, u32[]{:S(2)}, u32[]{:S(2)}) %collective-permute-start.5) | collective-permute-done | bytes 262176 | tf_op jit(solution)/shard_map/ppermute | solution.py:283
  25.0 2.1 %collective-permute-start.9 = (f32[72,128]{1,0:T(8,128)S(1)}, f32[72,128]{1,0:T(8,128)S(1)}, u32[]{:S(2)}, u32[]{:S(2)}) collective-permute-start(f32[72,128]{1,0:T(8,128)S(1)} %add.41), channel_id=1, source_target_pairs={{0,4},{1,3},{2,6},{3,1},{4,0},{5,7},{6,2},{7,5},{8,12},{9,11},{10,... | collective-permute-start | bytes 110600 | tf_op jit(solution)/shard_map/ppermute | solution.py:283
  27.1 3.3 %collective-permute-start.12 = (f32[128,128]{1,0:T(8,128)S(1)}, f32[128,128]{1,0:T(8,128)S(1)}, u32[]{:S(2)}, u32[]{:S(2)}) collective-permute-start(f32[128,128]{1,0:T(8,128)S(1)} %get-tuple-element.40), channel_id=1, source_target_pairs={{0,24},{1,25},{2,26},{3,27},{4,28},{5,29},{6,30},{7,31},{8,16},{9,... | collective-permute-start | bytes 196616 | tf_op jit(solution)/shard_map/ppermute | solution.py:283
  30.3 1.2 %collective-permute-start.10 = (f32[128,128]{1,0:T(8,128)S(1)}, f32[128,128]{1,0:T(8,128)S(1)}, u32[]{:S(2)}, u32[]{:S(2)}) collective-permute-start(f32[128,128]{1,0:T(8,128)S(1)} %get-tuple-element.42), channel_id=1, source_target_pairs={{0,8},{1,9},{2,10},{3,11},{4,12},{5,13},{6,14},{7,15},{8,0},{9,1},... | collective-permute-start | bytes 196616 | tf_op jit(solution)/shard_map/ppermute | solution.py:283
  31.5 4.2 %factor.1.inverse_ref = f32[128,128]{1,0:T(8,128)S(1)} custom-call(f32[72,128]{1,0:T(8,128)S(1)} %add.43.gram_ref), custom_call_target="tpu_custom_call" | custom-call | flops 4000000000 | bytes 73728 | tf_op jit(solution)/shard_map/factor/pallas_call | solution.py:222
  35.8 1.2 %finish.1 = (f32[576,128]{1,0:T(8,128)}, bf16[128,128]{1,0:T(8,128)(2,1)}) custom-call(f32[128,128]{1,0:T(8,128)S(1)} %factor.1.inverse_ref, f32[576,128]{1,0:T(8,128)S(1)} %get-tuple-element.38.first_ref, f32[128,128]{1,0:T(8,128)S(1)} %slice_bitcast_fusion.3.sums_ref, f32[128,128]{1,0:T(8,128)S(1)} %collective-permute-done.10.refs_0_, ...), custom_call_target="tpu_custom_call" | custom-call | flops 113246208 | bytes 589824 | tf_op jit(solution)/shard_map/finish/pallas_call | solution.py:253
  (17 shorter events, 0.1 us)
Async XLA Ops:
  5.6 2.1 %collective-permute-start = (f32[8,128,128]{2,1,0:T(8,128)S(1)}, f32[8,128,128]{2,1,0:T(8,128)S(1)}, u32[]{:S(2)}, u32[]{:S(2)}) collective-permute-start(f32[8,128,128]{2,1,0:T(8,128)S(1)} %get-tuple-element.23), channel_id=1, source_target_pairs={{0,1},{1,0},{2,3},{3,2},{4,5},{5,4},{6,7},{7,6},{8,9},{9,8},{10,11... | collective-permute-start | bytes 1572872 | tf_op jit(solution)/shard_map/ppermute | solution.py:283
  6.2 1.6 %collective-permute-start.1 = (f32[72,128]{1,0:T(8,128)S(1)}, f32[72,128]{1,0:T(8,128)S(1)}, u32[]{:S(2)}, u32[]{:S(2)}) collective-permute-start(f32[72,128]{1,0:T(8,128)S(1)} %get-tuple-element.24), channel_id=1, source_target_pairs={{0,1},{1,0},{2,3},{3,2},{4,5},{5,4},{6,7},{7,6},{8,9},{9,8},{10,11... | collective-permute-start | bytes 110600 | tf_op jit(solution)/shard_map/ppermute | solution.py:283
  7.8 10.1 %collective-permute-start.3 = (f32[8,128,128]{2,1,0:T(8,128)S(1)}, f32[8,128,128]{2,1,0:T(8,128)S(1)}, u32[]{:S(2)}, u32[]{:S(2)}) collective-permute-start(f32[8,128,128]{2,1,0:T(8,128)S(1)} %add.35), channel_id=1, source_target_pairs={{0,2},{1,5},{2,0},{3,7},{4,6},{5,1},{6,4},{7,3},{8,10},{9,13},{10,... | collective-permute-start | bytes 1572872 | tf_op jit(solution)/shard_map/ppermute | solution.py:283
  11.9 6.1 %collective-permute-start.2 = (f32[8,128,128]{2,1,0:T(8,128)S(1)}, f32[8,128,128]{2,1,0:T(8,128)S(1)}, u32[]{:S(2)}, u32[]{:S(2)}) collective-permute-start(f32[8,128,128]{2,1,0:T(8,128)S(1)} %get-tuple-element.28), channel_id=1, source_target_pairs={{0,1},{1,0},{2,3},{3,2},{4,5},{5,4},{6,7},{7,6},{8,9},{9,8},{10,11... | collective-permute-start | bytes 1572872 | tf_op jit(solution)/shard_map/ppermute | solution.py:283
  11.9 5.8 %collective-permute-start.4 = (f32[72,128]{1,0:T(8,128)S(1)}, f32[72,128]{1,0:T(8,128)S(1)}, u32[]{:S(2)}, u32[]{:S(2)}) collective-permute-start(f32[72,128]{1,0:T(8,128)S(1)} %add.34), channel_id=1, source_target_pairs={{0,24},{1,25},{2,26},{3,27},{4,28},{5,29},{6,30},{7,31},{8,16},{9,... | collective-permute-start | bytes 110600 | tf_op jit(solution)/shard_map/ppermute | solution.py:283
  15.6 4.9 %collective-permute-start.7 = (f32[72,128]{1,0:T(8,128)S(1)}, f32[72,128]{1,0:T(8,128)S(1)}, u32[]{:S(2)}, u32[]{:S(2)}) collective-permute-start(f32[72,128]{1,0:T(8,128)S(1)} %add.34), channel_id=1, source_target_pairs={{0,16},{1,17},{2,18},{3,19},{4,20},{5,21},{6,22},{7,23},{8,24},{9,... | collective-permute-start | bytes 110600 | tf_op jit(solution)/shard_map/ppermute | solution.py:283
  15.6 4.9 %collective-permute-start.6 = (f32[72,128]{1,0:T(8,128)S(1)}, f32[72,128]{1,0:T(8,128)S(1)}, u32[]{:S(2)}, u32[]{:S(2)}) collective-permute-start(f32[72,128]{1,0:T(8,128)S(1)} %add.34), channel_id=1, source_target_pairs={{0,8},{1,9},{2,10},{3,11},{4,12},{5,13},{6,14},{7,15},{8,0},{9,1},... | collective-permute-start | bytes 110600 | tf_op jit(solution)/shard_map/ppermute | solution.py:283
  18.1 6.9 %collective-permute-start.5 = (f32[4,128,128]{2,1,0:T(8,128)S(1)}, f32[4,128,128]{2,1,0:T(8,128)S(1)}, u32[]{:S(2)}, u32[]{:S(2)}) collective-permute-start(f32[4,128,128]{2,1,0:T(8,128)S(1)} %slice.19), channel_id=1, source_target_pairs={{0,4},{1,3},{2,6},{3,1},{4,0},{5,7},{6,2},{7,5},{8,12},{9,11},{10,... | collective-permute-start | bytes 786440 | tf_op jit(solution)/shard_map/ppermute | solution.py:283
  20.5 4.0 %collective-permute-start.8 = (f32[72,128]{1,0:T(8,128)S(1)}, f32[72,128]{1,0:T(8,128)S(1)}, u32[]{:S(2)}, u32[]{:S(2)}) collective-permute-start(f32[72,128]{1,0:T(8,128)S(1)} %add_add_fusion.1), channel_id=1, source_target_pairs={{0,2},{1,5},{2,0},{3,7},{4,6},{5,1},{6,4},{7,3},{8,10},{9,13},{10,... | collective-permute-start | bytes 110600 | tf_op jit(solution)/shard_map/ppermute | solution.py:283
  25.0 6.6 %collective-permute-start.9 = (f32[72,128]{1,0:T(8,128)S(1)}, f32[72,128]{1,0:T(8,128)S(1)}, u32[]{:S(2)}, u32[]{:S(2)}) collective-permute-start(f32[72,128]{1,0:T(8,128)S(1)} %add.41), channel_id=1, source_target_pairs={{0,4},{1,3},{2,6},{3,1},{4,0},{5,7},{6,2},{7,5},{8,12},{9,11},{10,... | collective-permute-start | bytes 110600 | tf_op jit(solution)/shard_map/ppermute | solution.py:283
  27.1 8.7 %collective-permute-start.12 = (f32[128,128]{1,0:T(8,128)S(1)}, f32[128,128]{1,0:T(8,128)S(1)}, u32[]{:S(2)}, u32[]{:S(2)}) collective-permute-start(f32[128,128]{1,0:T(8,128)S(1)} %get-tuple-element.40), channel_id=1, source_target_pairs={{0,24},{1,25},{2,26},{3,27},{4,28},{5,29},{6,30},{7,31},{8,16},{9,... | collective-permute-start | bytes 196616 | tf_op jit(solution)/shard_map/ppermute | solution.py:283
  30.3 5.4 %collective-permute-start.11 = (f32[128,128]{1,0:T(8,128)S(1)}, f32[128,128]{1,0:T(8,128)S(1)}, u32[]{:S(2)}, u32[]{:S(2)}) collective-permute-start(f32[128,128]{1,0:T(8,128)S(1)} %get-tuple-element.41), channel_id=1, source_target_pairs={{0,16},{1,17},{2,18},{3,19},{4,20},{5,21},{6,22},{7,23},{8,24},{9,... | collective-permute-start | bytes 196616 | tf_op jit(solution)/shard_map/ppermute | solution.py:283
  30.3 5.4 %collective-permute-start.10 = (f32[128,128]{1,0:T(8,128)S(1)}, f32[128,128]{1,0:T(8,128)S(1)}, u32[]{:S(2)}, u32[]{:S(2)}) collective-permute-start(f32[128,128]{1,0:T(8,128)S(1)} %get-tuple-element.42), channel_id=1, source_target_pairs={{0,8},{1,9},{2,10},{3,11},{4,12},{5,13},{6,14},{7,15},{8,0},{9,1},... | collective-permute-start | bytes 196616 | tf_op jit(solution)/shard_map/ppermute | solution.py:283

commit v13 on v12

--- a/solution.py
+++ b/solution.py
@@ -174,44 +174,47 @@
 
 def inverse_factor(gram, inverse_ref):
     size = gram.shape[0]
-    blocks = size // 8
-    left = [gram[8 * i : 8 * i + 8, :] for i in range(blocks)]
+    blocks = [gram[i : i + 8, :] for i in range(0, size, 8)]
     row_at = lax.broadcasted_iota(jnp.int32, (8, size), 0)
     lane_at = lax.broadcasted_iota(jnp.int32, (8, size), 1)
-    right = [jnp.where(lane_at == row_at + 8 * i, 1.0, 0.0).astype(jnp.float32) for i in range(blocks)]
-    for p in range(blocks):
-        column = [lane(left[p], 8 * p + k) for k in range(8)]
+    for p in range(len(blocks)):
+        start = 8 * p
+        column = [lane(blocks[p], start + k) for k in range(8)]
         entry = {(r, c): sublane(column[c], r) for c in range(8) for r in range(c, 8)}
-        scale, lower = [], {}
+        root, inverse, lower = [], [], {}
         for k in range(8):
-            scale.append(lax.rsqrt(entry[k, k]))
+            root.append(lax.rsqrt(entry[k, k]))
+            inverse.append(root[k] * root[k])
             for r in range(k + 1, 8):
-                lower[r, k] = entry[r, k] * scale[k]
+                lower[r, k] = entry[r, k] * inverse[k]
             for c in range(k + 1, 8):
                 for r in range(c, 8):
-                    entry[r, c] = entry[r, c] - lower[r, k] * lower[c, k]
-        tops, sides = [], []
+                    entry[r, c] = entry[r, c] - lower[r, k] * entry[c, k]
+        in_panel = (lane_at >= start) & (lane_at < start + 8)
+        unit = jnp.where(lane_at - start == row_at, 1.0, 0.0)
+        panel = jnp.where(in_panel, unit, blocks[p])
+        tops = []
         for k in range(8):
-            top, side = sublane(left[p], k), sublane(right[p], k)
+            top = sublane(panel, k)
             for j in range(k):
                 top = top - lower[k, j] * tops[j]
-                side = side - lower[k, j] * sides[j]
-            tops.append(top * scale[k])
-            sides.append(side * scale[k])
-        result = sides[0]
+            tops.append(top)
+        result, scale = tops[0], root[0]
         for k in range(1, 8):
-            result = jnp.where(row_at == k, sides[k], result)
-        inverse_ref[8 * p : 8 * p + 8, :] = result
-        for i in range(p + 1, blocks):
+            result = jnp.where(row_at == k, tops[k], result)
+            scale = jnp.where(row_at == k, root[k], scale)
+        inverse_ref[start : start + 8, :] = jnp.where(lane_at < start + 8, result * scale, 0.0)
+        scaled = [tops[k] * inverse[k] for k in range(8)]
+        for i in range(p + 1, len(blocks)):
+            block = jnp.where(in_panel, 0.0, blocks[i])
             weights = []
             for k in range(8):
-                weight = lane(left[i], 8 * p + k)
+                weight = lane(blocks[i], start + k)
                 for j in range(k):
                     weight = weight - lower[k, j] * weights[j]
-                weights.append(weight * scale[k])
-            for k in range(8):
-                left[i] = left[i] - weights[k] * tops[k]
-                right[i] = right[i] - weights[k] * sides[k]
+                weights.append(weight)
+                block = block - weight * scaled[k]
+            blocks[i] = block
 
 
 def factor_kernel(gram_ref, inverse_ref):
@@ -232,14 +235,21 @@
     )(gram)
 
 
+def two_parts(array):
+    high = array.astype(jnp.bfloat16)
+    return high, (array - high.astype(jnp.float32)).astype(jnp.bfloat16)
+
+
 def finish_kernel(basis_factor, factor, inverse_ref, first_ref, sums_ref, *refs):
     basis_ref, out_ref = refs[-2:]
     inverse = inverse_ref[...]
-    one = lax.dot_general(
-        first_ref[...], inverse, (((1,), (1,)), ((), ())),
-        precision=HIGHEST, preferred_element_type=jnp.float32,
+    high, low = two_parts(first_ref[...])
+    inverse_high, inverse_low = two_parts(inverse.T * basis_factor)
+    basis_ref[...] = jnp.dot(
+        jnp.concatenate([high, high, low, low], axis=1),
+        jnp.concatenate([inverse_high, inverse_low, inverse_high, inverse_low], axis=0),
+        preferred_element_type=jnp.float32,
     )
-    basis_ref[...] = one * basis_factor
     sums = sums_ref[...]
     for got_ref in refs[:-2]:
         sums = sums + got_ref[...]

time: 37.1 us -> 37.2 us (level)
  no operation moved by 1% of the time
where the time goes in v13:
time: 37.2 us; the launch traced here: 37 us
  starting transfers between devices  18.1 us (49%)
  Pallas kernels  12.2 us (33%)
  waiting for transfers between devices  5.73 us (15%)
  between operations  0.74 us (2%)
    ppermute x13, starting transfers between devices, exchange(): return lax.ppermute(array, AXES, pairs)  18.1 us
    ppermute x13, waiting for transfers between devices, exchange(): return lax.ppermute(array, AXES, pairs)  5.73 us
    pallas_call x1, Pallas kernels, rows_call(): pl.pallas_call(rows_kernel, in_specs=[pl.BlockSpec(memory_space=pltpu.SME...  4.99 us
    pallas_call x1, Pallas kernels, factor_call(): pl.pallas_call(factor_kernel, in_specs=[pl.BlockSpec(memory_space=pltpu.V...  4.25 us
    pallas_call x2, Pallas kernels, project_call(): pl.pallas_call(functools.partial(project_kernel, parts), in_specs=[pl.Blo...  1.77 us
    pallas_call x1, Pallas kernels, finish_call(): pl.pallas_call(functools.partial(finish_kernel, float(total_rows) ** 0.5,...  1.18 us
  transfers between devices with their start and end apart: 13, of which 6 were waited for; matrix products, arithmetic and copies ran while one was open for 0% of the time, Pallas kernels for 16%

profile of v13, /device:TPU:0, one launch (start us, length us, event | category | flops | bytes accessed | tf_op | source)
XLA Modules:
  0.0 37.0 jit_solution(16276567181720702786)
XLA Ops:
  0.6 5.0 %sketch_rows.1 = (bf16[576,4096]{1,0:T(8,128)(2,1)S(1)}, f32[576,128]{1,0:T(8,128)S(1)}, f32[72,128]{1,0:T(8,128)S(1)}, bf16[256,576]{1,0:T(8,128)(2,1)S(1)}, f32[8,128,128]{2,1,0:T(8,128)S(1)}) custom-call(s32[1]{0:T(128)} %bitcast.owner_ref, bf16[576,4096]{1,0:T(8,128)(2,1)} %slab_hbm.1, bf16[4096,128]{1,0:T(8,128)(2,1)} %sketch_hbm.1), custom_call_target="tpu_custom_call" | custom-call | flops 905969664 | bytes 4718592 | tf_op jit(solution)/shard_map/sketch_rows/pallas_call | solution.py:134
  5.6 0.5 %collective-permute-start = (f32[8,128,128]{2,1,0:T(8,128)S(1)}, f32[8,128,128]{2,1,0:T(8,128)S(1)}, u32[]{:S(2)}, u32[]{:S(2)}) collective-permute-start(f32[8,128,128]{2,1,0:T(8,128)S(1)} %get-tuple-element.23), channel_id=1, source_target_pairs={{0,1},{1,0},{2,3},{3,2},{4,5},{5,4},{6,7},{7,6},{8,9},{9,8},{10,11... | collective-permute-start | bytes 1572872 | tf_op jit(solution)/shard_map/ppermute | solution.py:293
  6.2 0.1 collective-permute-start.1
  6.2 0.7 %project_first.1 = f32[8,128,128]{2,1,0:T(8,128)S(1)} custom-call(s32[1]{0:T(128)} %bitcast.owner_ref, bf16[256,576]{1,0:T(8,128)(2,1)S(1)} %get-tuple-element.26.split_ref, bf16[576,4096]{1,0:T(8,128)(2,1)S(1)} %get-tuple-element.22.slab_ref), custom_call_target="tpu_custom_call" | custom-call | flops 301989888 | bytes 2359296 | tf_op jit(solution)/shard_map/project_first/pallas_call | solution.py:116
  6.9 0.8 %collective-permute-done.1 = f32[72,128]{1,0:T(8,128)S(1)} collective-permute-done((f32[72,128]{1,0:T(8,128)S(1)}, f32[72,128]{1,0:T(8,128)S(1)}, u32[]{:S(2)}, u32[]{:S(2)}) %collective-permute-start.1) | collective-permute-done | bytes 36896 | tf_op jit(solution)/shard_map/ppermute | solution.py:293
  7.8 0.1 add.35
  7.8 2.9 %collective-permute-start.3 = (f32[8,128,128]{2,1,0:T(8,128)S(1)}, f32[8,128,128]{2,1,0:T(8,128)S(1)}, u32[]{:S(2)}, u32[]{:S(2)}) collective-permute-start(f32[8,128,128]{2,1,0:T(8,128)S(1)} %add.35), channel_id=1, source_target_pairs={{0,2},{1,5},{2,0},{3,7},{4,6},{5,1},{6,4},{7,3},{8,10},{9,13},{10,... | collective-permute-start | bytes 1572872 | tf_op jit(solution)/shard_map/ppermute | solution.py:293
  10.8 1.1 %project_rest.1 = (f32[8,128,128]{2,1,0:T(8,128)S(1)}, f32[8,128,128]{2,1,0:T(8,128)S(1)}) custom-call(s32[1]{0:T(128)} %bitcast.owner_ref, bf16[256,576]{1,0:T(8,128)(2,1)S(1)} %get-tuple-element.26.split_ref, bf16[576,4096]{1,0:T(8,128)(2,1)S(1)} %get-tuple-element.22.slab_ref), custom_call_target="tpu_custom_call" | custom-call | flops 603979776 | bytes 2359296 | tf_op jit(solution)/shard_map/project_rest/pallas_call | solution.py:116
  11.9 0.1 collective-permute-start.2
  11.9 3.7 %collective-permute-start.4 = (f32[72,128]{1,0:T(8,128)S(1)}, f32[72,128]{1,0:T(8,128)S(1)}, u32[]{:S(2)}, u32[]{:S(2)}) collective-permute-start(f32[72,128]{1,0:T(8,128)S(1)} %add.34), channel_id=1, source_target_pairs={{0,24},{1,25},{2,26},{3,27},{4,28},{5,29},{6,30},{7,31},{8,16},{9,... | collective-permute-start | bytes 110600 | tf_op jit(solution)/shard_map/ppermute | solution.py:293
  15.6 0.8 %collective-permute-start.6 = (f32[72,128]{1,0:T(8,128)S(1)}, f32[72,128]{1,0:T(8,128)S(1)}, u32[]{:S(2)}, u32[]{:S(2)}) collective-permute-start(f32[72,128]{1,0:T(8,128)S(1)} %add.34), channel_id=1, source_target_pairs={{0,8},{1,9},{2,10},{3,11},{4,12},{5,13},{6,14},{7,15},{8,0},{9,1},... | collective-permute-start | bytes 110600 | tf_op jit(solution)/shard_map/ppermute | solution.py:293
  16.4 1.4 %collective-permute-done.4 = f32[72,128]{1,0:T(8,128)S(1)} collective-permute-done((f32[72,128]{1,0:T(8,128)S(1)}, f32[72,128]{1,0:T(8,128)S(1)}, u32[]{:S(2)}, u32[]{:S(2)}) %collective-permute-start.4) | collective-permute-done | bytes 36896 | tf_op jit(solution)/shard_map/ppermute | solution.py:293
  17.8 0.2 collective-permute-done.3
  17.9 0.1 add_add_fusion
  18.1 2.1 %collective-permute-start.5 = (f32[4,128,128]{2,1,0:T(8,128)S(1)}, f32[4,128,128]{2,1,0:T(8,128)S(1)}, u32[]{:S(2)}, u32[]{:S(2)}) collective-permute-start(f32[4,128,128]{2,1,0:T(8,128)S(1)} %slice.19), channel_id=1, source_target_pairs={{0,4},{1,3},{2,6},{3,1},{4,0},{5,7},{6,2},{7,5},{8,12},{9,11},{10,... | collective-permute-start | bytes 786440 | tf_op jit(solution)/shard_map/ppermute | solution.py:293
  20.2 0.3 collective-permute-done.7
  20.5 1.4 %collective-permute-start.8 = (f32[72,128]{1,0:T(8,128)S(1)}, f32[72,128]{1,0:T(8,128)S(1)}, u32[]{:S(2)}, u32[]{:S(2)}) collective-permute-start(f32[72,128]{1,0:T(8,128)S(1)} %add_add_fusion.1), channel_id=1, source_target_pairs={{0,2},{1,5},{2,0},{3,7},{4,6},{5,1},{6,4},{7,3},{8,10},{9,13},{10,... | collective-permute-start | bytes 110600 | tf_op jit(solution)/shard_map/ppermute | solution.py:293
  21.9 2.7 %collective-permute-done.8 = f32[72,128]{1,0:T(8,128)S(1)} collective-permute-done((f32[72,128]{1,0:T(8,128)S(1)}, f32[72,128]{1,0:T(8,128)S(1)}, u32[]{:S(2)}, u32[]{:S(2)}) %collective-permute-start.8) | collective-permute-done | bytes 36896 | tf_op jit(solution)/shard_map/ppermute | solution.py:293
  24.5 0.4 %collective-permute-done.5 = f32[4,128,128]{2,1,0:T(8,128)S(1)} collective-permute-done((f32[4,128,128]{2,1,0:T(8,128)S(1)}, f32[4,128,128]{2,1,0:T(8,128)S(1)}, u32[]{:S(2)}, u32[]{:S(2)}) %collective-permute-start.5) | collective-permute-done | bytes 262176 | tf_op jit(solution)/shard_map/ppermute | solution.py:293
  25.0 2.1 %collective-permute-start.9 = (f32[72,128]{1,0:T(8,128)S(1)}, f32[72,128]{1,0:T(8,128)S(1)}, u32[]{:S(2)}, u32[]{:S(2)}) collective-permute-start(f32[72,128]{1,0:T(8,128)S(1)} %add.41), channel_id=1, source_target_pairs={{0,4},{1,3},{2,6},{3,1},{4,0},{5,7},{6,2},{7,5},{8,12},{9,11},{10,... | collective-permute-start | bytes 110600 | tf_op jit(solution)/shard_map/ppermute | solution.py:293
  27.1 3.3 %collective-permute-start.12 = (f32[128,128]{1,0:T(8,128)S(1)}, f32[128,128]{1,0:T(8,128)S(1)}, u32[]{:S(2)}, u32[]{:S(2)}) collective-permute-start(f32[128,128]{1,0:T(8,128)S(1)} %get-tuple-element.40), channel_id=1, source_target_pairs={{0,24},{1,25},{2,26},{3,27},{4,28},{5,29},{6,30},{7,31},{8,16},{9,... | collective-permute-start | bytes 196616 | tf_op jit(solution)/shard_map/ppermute | solution.py:293
  30.3 1.2 %collective-permute-start.10 = (f32[128,128]{1,0:T(8,128)S(1)}, f32[128,128]{1,0:T(8,128)S(1)}, u32[]{:S(2)}, u32[]{:S(2)}) collective-permute-start(f32[128,128]{1,0:T(8,128)S(1)} %get-tuple-element.42), channel_id=1, source_target_pairs={{0,8},{1,9},{2,10},{3,11},{4,12},{5,13},{6,14},{7,15},{8,0},{9,1},... | collective-permute-start | bytes 196616 | tf_op jit(solution)/shard_map/ppermute | solution.py:293
  31.5 4.3 %factor.1.inverse_ref = f32[128,128]{1,0:T(8,128)S(1)} custom-call(f32[72,128]{1,0:T(8,128)S(1)} %add.43.gram_ref), custom_call_target="tpu_custom_call" | custom-call | flops 4000000000 | bytes 73728 | tf_op jit(solution)/shard_map/factor/pallas_call | solution.py:225
  35.8 1.2 %finish.1 = (f32[576,128]{1,0:T(8,128)}, bf16[128,128]{1,0:T(8,128)(2,1)}) custom-call(f32[128,128]{1,0:T(8,128)S(1)} %factor.1.inverse_ref, f32[576,128]{1,0:T(8,128)S(1)} %get-tuple-element.38.first_ref, f32[128,128]{1,0:T(8,128)S(1)} %slice_bitcast_fusion.3.sums_ref, f32[128,128]{1,0:T(8,128)S(1)} %collective-permute-done.10.refs_0_, ...), custom_call_target="tpu_custom_call" | custom-call | flops 113246208 | bytes 589824 | tf_op jit(solution)/shard_map/finish/pallas_call | solution.py:263
  (17 shorter events, 0.1 us)
Async XLA Ops:
  5.6 2.1 %collective-permute-start = (f32[8,128,128]{2,1,0:T(8,128)S(1)}, f32[8,128,128]{2,1,0:T(8,128)S(1)}, u32[]{:S(2)}, u32[]{:S(2)}) collective-permute-start(f32[8,128,128]{2,1,0:T(8,128)S(1)} %get-tuple-element.23), channel_id=1, source_target_pairs={{0,1},{1,0},{2,3},{3,2},{4,5},{5,4},{6,7},{7,6},{8,9},{9,8},{10,11... | collective-permute-start | bytes 1572872 | tf_op jit(solution)/shard_map/ppermute | solution.py:293
  6.2 1.6 %collective-permute-start.1 = (f32[72,128]{1,0:T(8,128)S(1)}, f32[72,128]{1,0:T(8,128)S(1)}, u32[]{:S(2)}, u32[]{:S(2)}) collective-permute-start(f32[72,128]{1,0:T(8,128)S(1)} %get-tuple-element.24), channel_id=1, source_target_pairs={{0,1},{1,0},{2,3},{3,2},{4,5},{5,4},{6,7},{7,6},{8,9},{9,8},{10,11... | collective-permute-start | bytes 110600 | tf_op jit(solution)/shard_map/ppermute | solution.py:293
  7.8 10.1 %collective-permute-start.3 = (f32[8,128,128]{2,1,0:T(8,128)S(1)}, f32[8,128,128]{2,1,0:T(8,128)S(1)}, u32[]{:S(2)}, u32[]{:S(2)}) collective-permute-start(f32[8,128,128]{2,1,0:T(8,128)S(1)} %add.35), channel_id=1, source_target_pairs={{0,2},{1,5},{2,0},{3,7},{4,6},{5,1},{6,4},{7,3},{8,10},{9,13},{10,... | collective-permute-start | bytes 1572872 | tf_op jit(solution)/shard_map/ppermute | solution.py:293
  11.9 6.1 %collective-permute-start.2 = (f32[8,128,128]{2,1,0:T(8,128)S(1)}, f32[8,128,128]{2,1,0:T(8,128)S(1)}, u32[]{:S(2)}, u32[]{:S(2)}) collective-permute-start(f32[8,128,128]{2,1,0:T(8,128)S(1)} %get-tuple-element.28), channel_id=1, source_target_pairs={{0,1},{1,0},{2,3},{3,2},{4,5},{5,4},{6,7},{7,6},{8,9},{9,8},{10,11... | collective-permute-start | bytes 1572872 | tf_op jit(solution)/shard_map/ppermute | solution.py:293
  11.9 5.8 %collective-permute-start.4 = (f32[72,128]{1,0:T(8,128)S(1)}, f32[72,128]{1,0:T(8,128)S(1)}, u32[]{:S(2)}, u32[]{:S(2)}) collective-permute-start(f32[72,128]{1,0:T(8,128)S(1)} %add.34), channel_id=1, source_target_pairs={{0,24},{1,25},{2,26},{3,27},{4,28},{5,29},{6,30},{7,31},{8,16},{9,... | collective-permute-start | bytes 110600 | tf_op jit(solution)/shard_map/ppermute | solution.py:293
  15.6 4.9 %collective-permute-start.7 = (f32[72,128]{1,0:T(8,128)S(1)}, f32[72,128]{1,0:T(8,128)S(1)}, u32[]{:S(2)}, u32[]{:S(2)}) collective-permute-start(f32[72,128]{1,0:T(8,128)S(1)} %add.34), channel_id=1, source_target_pairs={{0,16},{1,17},{2,18},{3,19},{4,20},{5,21},{6,22},{7,23},{8,24},{9,... | collective-permute-start | bytes 110600 | tf_op jit(solution)/shard_map/ppermute | solution.py:293
  15.6 4.9 %collective-permute-start.6 = (f32[72,128]{1,0:T(8,128)S(1)}, f32[72,128]{1,0:T(8,128)S(1)}, u32[]{:S(2)}, u32[]{:S(2)}) collective-permute-start(f32[72,128]{1,0:T(8,128)S(1)} %add.34), channel_id=1, source_target_pairs={{0,8},{1,9},{2,10},{3,11},{4,12},{5,13},{6,14},{7,15},{8,0},{9,1},... | collective-permute-start | bytes 110600 | tf_op jit(solution)/shard_map/ppermute | solution.py:293
  18.1 6.9 %collective-permute-start.5 = (f32[4,128,128]{2,1,0:T(8,128)S(1)}, f32[4,128,128]{2,1,0:T(8,128)S(1)}, u32[]{:S(2)}, u32[]{:S(2)}) collective-permute-start(f32[4,128,128]{2,1,0:T(8,128)S(1)} %slice.19), channel_id=1, source_target_pairs={{0,4},{1,3},{2,6},{3,1},{4,0},{5,7},{6,2},{7,5},{8,12},{9,11},{10,... | collective-permute-start | bytes 786440 | tf_op jit(solution)/shard_map/ppermute | solution.py:293
  20.5 4.0 %collective-permute-start.8 = (f32[72,128]{1,0:T(8,128)S(1)}, f32[72,128]{1,0:T(8,128)S(1)}, u32[]{:S(2)}, u32[]{:S(2)}) collective-permute-start(f32[72,128]{1,0:T(8,128)S(1)} %add_add_fusion.1), channel_id=1, source_target_pairs={{0,2},{1,5},{2,0},{3,7},{4,6},{5,1},{6,4},{7,3},{8,10},{9,13},{10,... | collective-permute-start | bytes 110600 | tf_op jit(solution)/shard_map/ppermute | solution.py:293
  25.0 6.6 %collective-permute-start.9 = (f32[72,128]{1,0:T(8,128)S(1)}, f32[72,128]{1,0:T(8,128)S(1)}, u32[]{:S(2)}, u32[]{:S(2)}) collective-permute-start(f32[72,128]{1,0:T(8,128)S(1)} %add.41), channel_id=1, source_target_pairs={{0,4},{1,3},{2,6},{3,1},{4,0},{5,7},{6,2},{7,5},{8,12},{9,11},{10,... | collective-permute-start | bytes 110600 | tf_op jit(solution)/shard_map/ppermute | solution.py:293
  27.1 8.7 %collective-permute-start.12 = (f32[128,128]{1,0:T(8,128)S(1)}, f32[128,128]{1,0:T(8,128)S(1)}, u32[]{:S(2)}, u32[]{:S(2)}) collective-permute-start(f32[128,128]{1,0:T(8,128)S(1)} %get-tuple-element.40), channel_id=1, source_target_pairs={{0,24},{1,25},{2,26},{3,27},{4,28},{5,29},{6,30},{7,31},{8,16},{9,... | collective-permute-start | bytes 196616 | tf_op jit(solution)/shard_map/ppermute | solution.py:293
  30.3 5.5 %collective-permute-start.11 = (f32[128,128]{1,0:T(8,128)S(1)}, f32[128,128]{1,0:T(8,128)S(1)}, u32[]{:S(2)}, u32[]{:S(2)}) collective-permute-start(f32[128,128]{1,0:T(8,128)S(1)} %get-tuple-element.41), channel_id=1, source_target_pairs={{0,16},{1,17},{2,18},{3,19},{4,20},{5,21},{6,22},{7,23},{8,24},{9,... | collective-permute-start | bytes 196616 | tf_op jit(solution)/shard_map/ppermute | solution.py:293
  30.3 5.5 %collective-permute-start.10 = (f32[128,128]{1,0:T(8,128)S(1)}, f32[128,128]{1,0:T(8,128)S(1)}, u32[]{:S(2)}, u32[]{:S(2)}) collective-permute-start(f32[128,128]{1,0:T(8,128)S(1)} %get-tuple-element.42), channel_id=1, source_target_pairs={{0,8},{1,9},{2,10},{3,11},{4,12},{5,13},{6,14},{7,15},{8,0},{9,1},... | collective-permute-start | bytes 196616 | tf_op jit(solution)/shard_map/ppermute | solution.py:293

commit v14 on v13

--- a/solution.py
+++ b/solution.py
@@ -11,7 +11,7 @@
 HIGHEST = lax.Precision.HIGHEST
 LANES = 128
 VMEM_LIMIT = 24 * 1024 * 1024
-AHEAD = 2
+AHEAD = 1
 ROWS = 256
 
 
@@ -181,15 +181,20 @@
         start = 8 * p
         column = [lane(blocks[p], start + k) for k in range(8)]
         entry = {(r, c): sublane(column[c], r) for c in range(8) for r in range(c, 8)}
-        root, inverse, lower = [], [], {}
-        for k in range(8):
-            root.append(lax.rsqrt(entry[k, k]))
-            inverse.append(root[k] * root[k])
-            for r in range(k + 1, 8):
-                lower[r, k] = entry[r, k] * inverse[k]
-            for c in range(k + 1, 8):
+        root, lower = [], {}
+        for k in range(0, 8, 2):
+            first, side, second = entry[k, k], entry[k + 1, k], entry[k + 1, k + 1]
+            one = lax.rsqrt(first)
+            two = lax.rsqrt(first * second - side * side) * (first * one)
+            root += [one, two]
+            lower[k + 1, k] = side * one
+            for r in range(k + 2, 8):
+                lower[r, k] = entry[r, k] * one
+                lower[r, k + 1] = (entry[r, k + 1] - lower[r, k] * lower[k + 1, k]) * two
+            for c in range(k + 2, 8):
                 for r in range(c, 8):
-                    entry[r, c] = entry[r, c] - lower[r, k] * entry[c, k]
+                    pair = lower[r, k] * lower[c, k] + lower[r, k + 1] * lower[c, k + 1]
+                    entry[r, c] = entry[r, c] - pair
         in_panel = (lane_at >= start) & (lane_at < start + 8)
         unit = jnp.where(lane_at - start == row_at, 1.0, 0.0)
         panel = jnp.where(in_panel, unit, blocks[p])
@@ -198,13 +203,11 @@
             top = sublane(panel, k)
             for j in range(k):
                 top = top - lower[k, j] * tops[j]
-            tops.append(top)
-        result, scale = tops[0], root[0]
+            tops.append(top * root[k])
+        result = tops[0]
         for k in range(1, 8):
             result = jnp.where(row_at == k, tops[k], result)
-            scale = jnp.where(row_at == k, root[k], scale)
-        inverse_ref[start : start + 8, :] = jnp.where(lane_at < start + 8, result * scale, 0.0)
-        scaled = [tops[k] * inverse[k] for k in range(8)]
+        inverse_ref[start : start + 8, :] = jnp.where(lane_at < start + 8, result, 0.0)
         for i in range(p + 1, len(blocks)):
             block = jnp.where(in_panel, 0.0, blocks[i])
             weights = []
@@ -212,8 +215,8 @@
                 weight = lane(blocks[i], start + k)
                 for j in range(k):
                     weight = weight - lower[k, j] * weights[j]
-                weights.append(weight)
-                block = block - weight * scaled[k]
+                weights.append(weight * root[k])
+                block = block - weights[k] * tops[k]
             blocks[i] = block
 
 

time: 37.2 us -> 37.5 us (level)
    pallas_call x1, Pallas kernels: 4.99 us -> 5.64 us  [rows_call(): pl.pallas_call(rows_kernel, in_specs=[pl.BlockSpec(memory_space=pltpu.SME...]
    pallas_call x1, Pallas kernels: 4.25 us -> 3.78 us  [factor_call(): pl.pallas_call(factor_kernel, in_specs=[pl.BlockSpec(memory_space=pltpu.V...]
  transfers between devices with their start and end apart: 13 -> 13, of which waited for: 6 -> 7; matrix products, arithmetic and copies ran while one was open for 0% -> 0% of each run, Pallas kernels for 16% -> 15%
where the time goes in v14:
time: 37.5 us; the launch traced here: 37.3 us
  starting transfers between devices  18.1 us (48%)
  Pallas kernels  12.4 us (33%)
  waiting for transfers between devices  5.88 us (16%)
  between operations  0.73 us (2%)
    ppermute x13, starting transfers between devices, exchange(): return lax.ppermute(array, AXES, pairs)  18.1 us
    ppermute x13, waiting for transfers between devices, exchange(): return lax.ppermute(array, AXES, pairs)  5.88 us
    pallas_call x1, Pallas kernels, rows_call(): pl.pallas_call(rows_kernel, in_specs=[pl.BlockSpec(memory_space=pltpu.SME...  5.64 us
    pallas_call x1, Pallas kernels, factor_call(): pl.pallas_call(factor_kernel, in_specs=[pl.BlockSpec(memory_space=pltpu.V...  3.78 us
    pallas_call x2, Pallas kernels, project_call(): pl.pallas_call(functools.partial(project_kernel, parts), in_specs=[pl.Blo...  1.77 us
    pallas_call x1, Pallas kernels, finish_call(): pl.pallas_call(functools.partial(finish_kernel, float(total_rows) ** 0.5,...  1.18 us
  transfers between devices with their start and end apart: 13, of which 7 were waited for; matrix products, arithmetic and copies ran while one was open for 0% of the time, Pallas kernels for 15%

profile of v14, /device:TPU:0, one launch (start us, length us, event | category | flops | bytes accessed | tf_op | source)
XLA Modules:
  0.0 37.3 jit_solution(16404413635808185329)
XLA Ops:
  0.6 5.6 %sketch_rows.1 = (bf16[576,4096]{1,0:T(8,128)(2,1)S(1)}, f32[576,128]{1,0:T(8,128)S(1)}, f32[72,128]{1,0:T(8,128)S(1)}, bf16[256,576]{1,0:T(8,128)(2,1)S(1)}, f32[8,128,128]{2,1,0:T(8,128)S(1)}) custom-call(s32[1]{0:T(128)} %bitcast.owner_ref, bf16[576,4096]{1,0:T(8,128)(2,1)} %slab_hbm.1, bf16[4096,128]{1,0:T(8,128)(2,1)} %sketch_hbm.1), custom_call_target="tpu_custom_call" | custom-call | flops 905969664 | bytes 4718592 | tf_op jit(solution)/shard_map/sketch_rows/pallas_call | solution.py:134
  6.3 0.5 %collective-permute-start = (f32[8,128,128]{2,1,0:T(8,128)S(1)}, f32[8,128,128]{2,1,0:T(8,128)S(1)}, u32[]{:S(2)}, u32[]{:S(2)}) collective-permute-start(f32[8,128,128]{2,1,0:T(8,128)S(1)} %get-tuple-element.23), channel_id=1, source_target_pairs={{0,1},{1,0},{2,3},{3,2},{4,5},{5,4},{6,7},{7,6},{8,9},{9,8},{10,11... | collective-permute-start | bytes 1572872 | tf_op jit(solution)/shard_map/ppermute | solution.py:296
  6.8 0.1 collective-permute-start.1
  6.9 0.7 %project_first.1 = f32[8,128,128]{2,1,0:T(8,128)S(1)} custom-call(s32[1]{0:T(128)} %bitcast.owner_ref, bf16[256,576]{1,0:T(8,128)(2,1)S(1)} %get-tuple-element.26.split_ref, bf16[576,4096]{1,0:T(8,128)(2,1)S(1)} %get-tuple-element.22.slab_ref), custom_call_target="tpu_custom_call" | custom-call | flops 301989888 | bytes 2359296 | tf_op jit(solution)/shard_map/project_first/pallas_call | solution.py:116
  7.6 0.8 %collective-permute-done.1 = f32[72,128]{1,0:T(8,128)S(1)} collective-permute-done((f32[72,128]{1,0:T(8,128)S(1)}, f32[72,128]{1,0:T(8,128)S(1)}, u32[]{:S(2)}, u32[]{:S(2)}) %collective-permute-start.1) | collective-permute-done | bytes 36896 | tf_op jit(solution)/shard_map/ppermute | solution.py:296
  8.4 0.1 add.35
  8.5 2.9 %collective-permute-start.3 = (f32[8,128,128]{2,1,0:T(8,128)S(1)}, f32[8,128,128]{2,1,0:T(8,128)S(1)}, u32[]{:S(2)}, u32[]{:S(2)}) collective-permute-start(f32[8,128,128]{2,1,0:T(8,128)S(1)} %add.35), channel_id=1, source_target_pairs={{0,2},{1,5},{2,0},{3,7},{4,6},{5,1},{6,4},{7,3},{8,10},{9,13},{10,... | collective-permute-start | bytes 1572872 | tf_op jit(solution)/shard_map/ppermute | solution.py:296
  11.4 1.1 %project_rest.1 = (f32[8,128,128]{2,1,0:T(8,128)S(1)}, f32[8,128,128]{2,1,0:T(8,128)S(1)}) custom-call(s32[1]{0:T(128)} %bitcast.owner_ref, bf16[256,576]{1,0:T(8,128)(2,1)S(1)} %get-tuple-element.26.split_ref, bf16[576,4096]{1,0:T(8,128)(2,1)S(1)} %get-tuple-element.22.slab_ref), custom_call_target="tpu_custom_call" | custom-call | flops 603979776 | bytes 2359296 | tf_op jit(solution)/shard_map/project_rest/pallas_call | solution.py:116
  12.6 3.7 %collective-permute-start.4 = (f32[72,128]{1,0:T(8,128)S(1)}, f32[72,128]{1,0:T(8,128)S(1)}, u32[]{:S(2)}, u32[]{:S(2)}) collective-permute-start(f32[72,128]{1,0:T(8,128)S(1)} %add.34), channel_id=1, source_target_pairs={{0,24},{1,25},{2,26},{3,27},{4,28},{5,29},{6,30},{7,31},{8,16},{9,... | collective-permute-start | bytes 110600 | tf_op jit(solution)/shard_map/ppermute | solution.py:296
  16.3 0.8 %collective-permute-start.6 = (f32[72,128]{1,0:T(8,128)S(1)}, f32[72,128]{1,0:T(8,128)S(1)}, u32[]{:S(2)}, u32[]{:S(2)}) collective-permute-start(f32[72,128]{1,0:T(8,128)S(1)} %add.34), channel_id=1, source_target_pairs={{0,8},{1,9},{2,10},{3,11},{4,12},{5,13},{6,14},{7,15},{8,0},{9,1},... | collective-permute-start | bytes 110600 | tf_op jit(solution)/shard_map/ppermute | solution.py:296
  17.0 1.4 %collective-permute-done.4 = f32[72,128]{1,0:T(8,128)S(1)} collective-permute-done((f32[72,128]{1,0:T(8,128)S(1)}, f32[72,128]{1,0:T(8,128)S(1)}, u32[]{:S(2)}, u32[]{:S(2)}) %collective-permute-start.4) | collective-permute-done | bytes 36896 | tf_op jit(solution)/shard_map/ppermute | solution.py:296
  18.4 0.2 collective-permute-done.3
  18.6 0.1 add_add_fusion
  18.7 2.1 %collective-permute-start.5 = (f32[4,128,128]{2,1,0:T(8,128)S(1)}, f32[4,128,128]{2,1,0:T(8,128)S(1)}, u32[]{:S(2)}, u32[]{:S(2)}) collective-permute-start(f32[4,128,128]{2,1,0:T(8,128)S(1)} %slice.19), channel_id=1, source_target_pairs={{0,4},{1,3},{2,6},{3,1},{4,0},{5,7},{6,2},{7,5},{8,12},{9,11},{10,... | collective-permute-start | bytes 786440 | tf_op jit(solution)/shard_map/ppermute | solution.py:296
  20.8 0.3 collective-permute-done.7
  21.1 1.4 %collective-permute-start.8 = (f32[72,128]{1,0:T(8,128)S(1)}, f32[72,128]{1,0:T(8,128)S(1)}, u32[]{:S(2)}, u32[]{:S(2)}) collective-permute-start(f32[72,128]{1,0:T(8,128)S(1)} %add_add_fusion.1), channel_id=1, source_target_pairs={{0,2},{1,5},{2,0},{3,7},{4,6},{5,1},{6,4},{7,3},{8,10},{9,13},{10,... | collective-permute-start | bytes 110600 | tf_op jit(solution)/shard_map/ppermute | solution.py:296
  22.5 2.7 %collective-permute-done.8 = f32[72,128]{1,0:T(8,128)S(1)} collective-permute-done((f32[72,128]{1,0:T(8,128)S(1)}, f32[72,128]{1,0:T(8,128)S(1)}, u32[]{:S(2)}, u32[]{:S(2)}) %collective-permute-start.8) | collective-permute-done | bytes 36896 | tf_op jit(solution)/shard_map/ppermute | solution.py:296
  25.2 0.4 %collective-permute-done.5 = f32[4,128,128]{2,1,0:T(8,128)S(1)} collective-permute-done((f32[4,128,128]{2,1,0:T(8,128)S(1)}, f32[4,128,128]{2,1,0:T(8,128)S(1)}, u32[]{:S(2)}, u32[]{:S(2)}) %collective-permute-start.5) | collective-permute-done | bytes 262176 | tf_op jit(solution)/shard_map/ppermute | solution.py:296
  25.6 2.1 %collective-permute-start.9 = (f32[72,128]{1,0:T(8,128)S(1)}, f32[72,128]{1,0:T(8,128)S(1)}, u32[]{:S(2)}, u32[]{:S(2)}) collective-permute-start(f32[72,128]{1,0:T(8,128)S(1)} %add.41), channel_id=1, source_target_pairs={{0,4},{1,3},{2,6},{3,1},{4,0},{5,7},{6,2},{7,5},{8,12},{9,11},{10,... | collective-permute-start | bytes 110600 | tf_op jit(solution)/shard_map/ppermute | solution.py:296
  27.7 3.3 %collective-permute-start.12 = (f32[128,128]{1,0:T(8,128)S(1)}, f32[128,128]{1,0:T(8,128)S(1)}, u32[]{:S(2)}, u32[]{:S(2)}) collective-permute-start(f32[128,128]{1,0:T(8,128)S(1)} %get-tuple-element.40), channel_id=1, source_target_pairs={{0,24},{1,25},{2,26},{3,27},{4,28},{5,29},{6,30},{7,31},{8,16},{9,... | collective-permute-start | bytes 196616 | tf_op jit(solution)/shard_map/ppermute | solution.py:296
  31.0 1.2 %collective-permute-start.10 = (f32[128,128]{1,0:T(8,128)S(1)}, f32[128,128]{1,0:T(8,128)S(1)}, u32[]{:S(2)}, u32[]{:S(2)}) collective-permute-start(f32[128,128]{1,0:T(8,128)S(1)} %get-tuple-element.42), channel_id=1, source_target_pairs={{0,8},{1,9},{2,10},{3,11},{4,12},{5,13},{6,14},{7,15},{8,0},{9,1},... | collective-permute-start | bytes 196616 | tf_op jit(solution)/shard_map/ppermute | solution.py:296
  32.2 3.8 %factor.1.inverse_ref = f32[128,128]{1,0:T(8,128)S(1)} custom-call(f32[72,128]{1,0:T(8,128)S(1)} %add.43.gram_ref), custom_call_target="tpu_custom_call" | custom-call | flops 4000000000 | bytes 73728 | tf_op jit(solution)/shard_map/factor/pallas_call | solution.py:228
  36.0 0.2 collective-permute-done.11.refs_1_
  36.2 1.2 %finish.1 = (f32[576,128]{1,0:T(8,128)}, bf16[128,128]{1,0:T(8,128)(2,1)}) custom-call(f32[128,128]{1,0:T(8,128)S(1)} %factor.1.inverse_ref, f32[576,128]{1,0:T(8,128)S(1)} %get-tuple-element.38.first_ref, f32[128,128]{1,0:T(8,128)S(1)} %slice_bitcast_fusion.3.sums_ref, f32[128,128]{1,0:T(8,128)S(1)} %collective-permute-done.10.refs_0_, ...), custom_call_target="tpu_custom_call" | custom-call | flops 113246208 | bytes 589824 | tf_op jit(solution)/shard_map/finish/pallas_call | solution.py:266
  (17 shorter events, 0.2 us)
Async XLA Ops:
  6.3 2.1 %collective-permute-start = (f32[8,128,128]{2,1,0:T(8,128)S(1)}, f32[8,128,128]{2,1,0:T(8,128)S(1)}, u32[]{:S(2)}, u32[]{:S(2)}) collective-permute-start(f32[8,128,128]{2,1,0:T(8,128)S(1)} %get-tuple-element.23), channel_id=1, source_target_pairs={{0,1},{1,0},{2,3},{3,2},{4,5},{5,4},{6,7},{7,6},{8,9},{9,8},{10,11... | collective-permute-start | bytes 1572872 | tf_op jit(solution)/shard_map/ppermute | solution.py:296
  6.8 1.6 %collective-permute-start.1 = (f32[72,128]{1,0:T(8,128)S(1)}, f32[72,128]{1,0:T(8,128)S(1)}, u32[]{:S(2)}, u32[]{:S(2)}) collective-permute-start(f32[72,128]{1,0:T(8,128)S(1)} %get-tuple-element.24), channel_id=1, source_target_pairs={{0,1},{1,0},{2,3},{3,2},{4,5},{5,4},{6,7},{7,6},{8,9},{9,8},{10,11... | collective-permute-start | bytes 110600 | tf_op jit(solution)/shard_map/ppermute | solution.py:296
  8.5 10.1 %collective-permute-start.3 = (f32[8,128,128]{2,1,0:T(8,128)S(1)}, f32[8,128,128]{2,1,0:T(8,128)S(1)}, u32[]{:S(2)}, u32[]{:S(2)}) collective-permute-start(f32[8,128,128]{2,1,0:T(8,128)S(1)} %add.35), channel_id=1, source_target_pairs={{0,2},{1,5},{2,0},{3,7},{4,6},{5,1},{6,4},{7,3},{8,10},{9,13},{10,... | collective-permute-start | bytes 1572872 | tf_op jit(solution)/shard_map/ppermute | solution.py:296
  12.5 6.1 %collective-permute-start.2 = (f32[8,128,128]{2,1,0:T(8,128)S(1)}, f32[8,128,128]{2,1,0:T(8,128)S(1)}, u32[]{:S(2)}, u32[]{:S(2)}) collective-permute-start(f32[8,128,128]{2,1,0:T(8,128)S(1)} %get-tuple-element.28), channel_id=1, source_target_pairs={{0,1},{1,0},{2,3},{3,2},{4,5},{5,4},{6,7},{7,6},{8,9},{9,8},{10,11... | collective-permute-start | bytes 1572872 | tf_op jit(solution)/shard_map/ppermute | solution.py:296
  12.6 5.8 %collective-permute-start.4 = (f32[72,128]{1,0:T(8,128)S(1)}, f32[72,128]{1,0:T(8,128)S(1)}, u32[]{:S(2)}, u32[]{:S(2)}) collective-permute-start(f32[72,128]{1,0:T(8,128)S(1)} %add.34), channel_id=1, source_target_pairs={{0,24},{1,25},{2,26},{3,27},{4,28},{5,29},{6,30},{7,31},{8,16},{9,... | collective-permute-start | bytes 110600 | tf_op jit(solution)/shard_map/ppermute | solution.py:296
  16.3 4.9 %collective-permute-start.7 = (f32[72,128]{1,0:T(8,128)S(1)}, f32[72,128]{1,0:T(8,128)S(1)}, u32[]{:S(2)}, u32[]{:S(2)}) collective-permute-start(f32[72,128]{1,0:T(8,128)S(1)} %add.34), channel_id=1, source_target_pairs={{0,16},{1,17},{2,18},{3,19},{4,20},{5,21},{6,22},{7,23},{8,24},{9,... | collective-permute-start | bytes 110600 | tf_op jit(solution)/shard_map/ppermute | solution.py:296
  16.3 4.9 %collective-permute-start.6 = (f32[72,128]{1,0:T(8,128)S(1)}, f32[72,128]{1,0:T(8,128)S(1)}, u32[]{:S(2)}, u32[]{:S(2)}) collective-permute-start(f32[72,128]{1,0:T(8,128)S(1)} %add.34), channel_id=1, source_target_pairs={{0,8},{1,9},{2,10},{3,11},{4,12},{5,13},{6,14},{7,15},{8,0},{9,1},... | collective-permute-start | bytes 110600 | tf_op jit(solution)/shard_map/ppermute | solution.py:296
  18.7 6.9 %collective-permute-start.5 = (f32[4,128,128]{2,1,0:T(8,128)S(1)}, f32[4,128,128]{2,1,0:T(8,128)S(1)}, u32[]{:S(2)}, u32[]{:S(2)}) collective-permute-start(f32[4,128,128]{2,1,0:T(8,128)S(1)} %slice.19), channel_id=1, source_target_pairs={{0,4},{1,3},{2,6},{3,1},{4,0},{5,7},{6,2},{7,5},{8,12},{9,11},{10,... | collective-permute-start | bytes 786440 | tf_op jit(solution)/shard_map/ppermute | solution.py:296
  21.1 4.0 %collective-permute-start.8 = (f32[72,128]{1,0:T(8,128)S(1)}, f32[72,128]{1,0:T(8,128)S(1)}, u32[]{:S(2)}, u32[]{:S(2)}) collective-permute-start(f32[72,128]{1,0:T(8,128)S(1)} %add_add_fusion.1), channel_id=1, source_target_pairs={{0,2},{1,5},{2,0},{3,7},{4,6},{5,1},{6,4},{7,3},{8,10},{9,13},{10,... | collective-permute-start | bytes 110600 | tf_op jit(solution)/shard_map/ppermute | solution.py:296
  25.6 6.6 %collective-permute-start.9 = (f32[72,128]{1,0:T(8,128)S(1)}, f32[72,128]{1,0:T(8,128)S(1)}, u32[]{:S(2)}, u32[]{:S(2)}) collective-permute-start(f32[72,128]{1,0:T(8,128)S(1)} %add.41), channel_id=1, source_target_pairs={{0,4},{1,3},{2,6},{3,1},{4,0},{5,7},{6,2},{7,5},{8,12},{9,11},{10,... | collective-permute-start | bytes 110600 | tf_op jit(solution)/shard_map/ppermute | solution.py:296
  27.7 8.3 %collective-permute-start.12 = (f32[128,128]{1,0:T(8,128)S(1)}, f32[128,128]{1,0:T(8,128)S(1)}, u32[]{:S(2)}, u32[]{:S(2)}) collective-permute-start(f32[128,128]{1,0:T(8,128)S(1)} %get-tuple-element.40), channel_id=1, source_target_pairs={{0,24},{1,25},{2,26},{3,27},{4,28},{5,29},{6,30},{7,31},{8,16},{9,... | collective-permute-start | bytes 196616 | tf_op jit(solution)/shard_map/ppermute | solution.py:296
  31.0 5.2 %collective-permute-start.11 = (f32[128,128]{1,0:T(8,128)S(1)}, f32[128,128]{1,0:T(8,128)S(1)}, u32[]{:S(2)}, u32[]{:S(2)}) collective-permute-start(f32[128,128]{1,0:T(8,128)S(1)} %get-tuple-element.41), channel_id=1, source_target_pairs={{0,16},{1,17},{2,18},{3,19},{4,20},{5,21},{6,22},{7,23},{8,24},{9,... | collective-permute-start | bytes 196616 | tf_op jit(solution)/shard_map/ppermute | solution.py:296
  31.0 5.2 %collective-permute-start.10 = (f32[128,128]{1,0:T(8,128)S(1)}, f32[128,128]{1,0:T(8,128)S(1)}, u32[]{:S(2)}, u32[]{:S(2)}) collective-permute-start(f32[128,128]{1,0:T(8,128)S(1)} %get-tuple-element.42), channel_id=1, source_target_pairs={{0,8},{1,9},{2,10},{3,11},{4,12},{5,13},{6,14},{7,15},{8,0},{9,1},... | collective-permute-start | bytes 196616 | tf_op jit(solution)/shard_map/ppermute | solution.py:296

commit v15 on v14

--- a/solution.py
+++ b/solution.py
@@ -11,8 +11,7 @@
 HIGHEST = lax.Precision.HIGHEST
 LANES = 128
 VMEM_LIMIT = 24 * 1024 * 1024
-AHEAD = 1
-ROWS = 256
+AHEAD = 2
 
 
 def project(out_ref, split_ref, slab_ref, owner, sibling, first_place):
@@ -62,31 +61,38 @@
     return parts + jnp.where(row == column, 0.0, parts.T)
 
 
+def row_chunks(rows):
+    sizes, left = [], rows
+    while left > 0:
+        sizes.append(min(LANES if len(sizes) < 2 else 2 * LANES, left))
+        left -= sizes[-1]
+    return [(sum(sizes[:k]), size) for k, size in enumerate(sizes)]
+
+
 def rows_kernel(
     owner_ref, slab_hbm, sketch_hbm, slab_ref, first_ref, gram_ref, split_ref, send_ref,
     sketch_ref, sum_ref, slab_sem, sketch_sem,
 ):
     rows, width = slab_ref.shape
     rank = sketch_ref.shape[1]
-    starts = list(range(0, rows, ROWS))
+    chunks = [pl.ds(r, size) for r, size in row_chunks(rows)]
     copies = [
-        pltpu.make_async_copy(
-            slab_hbm.at[pl.ds(r, min(ROWS, rows - r)), :],
-            slab_ref.at[pl.ds(r, min(ROWS, rows - r)), :],
-            slab_sem.at[k],
-        )
-        for k, r in enumerate(starts)
+        pltpu.make_async_copy(slab_hbm.at[at, :], slab_ref.at[at, :], slab_sem.at[k])
+        for k, at in enumerate(chunks)
     ]
-    sketch_copy = pltpu.make_async_copy(sketch_hbm, sketch_ref, sketch_sem)
-    sketch_copy.start()
-    for copy in copies[:AHEAD]:
+    half = slab_ref.shape[1] // 2
+    sketch_copies = [
+        pltpu.make_async_copy(sketch_hbm.at[at, :], sketch_ref.at[at, :], sketch_sem.at[k])
+        for k, at in enumerate((pl.ds(0, half), pl.ds(half, half)))
+    ]
+    for copy in sketch_copies + copies[:AHEAD]:
         copy.start()
-    sketch_copy.wait()
-    for k, r in enumerate(starts):
+    for copy in sketch_copies:
+        copy.wait()
+    for k, at in enumerate(chunks):
         copies[k].wait()
-        if k + AHEAD < len(starts):
+        if k + AHEAD < len(chunks):
             copies[k + AHEAD].start()
-        at = pl.ds(r, min(ROWS, rows - r))
         first = jnp.dot(slab_ref[at, :], sketch_ref[...], preferred_element_type=jnp.float32)
         first_ref[at, :] = first
         turned = first.T
@@ -149,8 +155,8 @@
         scratch_shapes=[
             pltpu.VMEM((width, rank), jnp.bfloat16),
             pltpu.VMEM((rank, rank), jnp.float32),
-            pltpu.SemaphoreType.DMA((-(-rows // ROWS),)),
-            pltpu.SemaphoreType.DMA,
+            pltpu.SemaphoreType.DMA((len(row_chunks(rows)),)),
+            pltpu.SemaphoreType.DMA((2,)),
         ],
         compiler_params=pltpu.CompilerParams(vmem_limit_bytes=VMEM_LIMIT),
         cost_estimate=pl.CostEstimate(
@@ -243,21 +249,31 @@
     return high, (array - high.astype(jnp.float32)).astype(jnp.bfloat16)
 
 
-def finish_kernel(basis_factor, factor, inverse_ref, first_ref, sums_ref, *refs):
-    basis_ref, out_ref = refs[-2:]
+def finish_kernel(basis_factor, factor, inverse_ref, first_ref, *refs):
+    *sums_refs, basis_hbm, out_hbm, basis_ref, out_ref, sems = refs
     inverse = inverse_ref[...]
-    high, low = two_parts(first_ref[...])
     inverse_high, inverse_low = two_parts(inverse.T * basis_factor)
-    basis_ref[...] = jnp.dot(
-        jnp.concatenate([high, high, low, low], axis=1),
-        jnp.concatenate([inverse_high, inverse_low, inverse_high, inverse_low], axis=0),
-        preferred_element_type=jnp.float32,
-    )
-    sums = sums_ref[...]
-    for got_ref in refs[:-2]:
+    factors = jnp.concatenate([inverse_high, inverse_low, inverse_high, inverse_low], axis=0)
+    half = basis_ref.shape[0] // 2
+    copies = []
+    for k in range(2):
+        at = pl.ds(k * half, half)
+        high, low = two_parts(first_ref[at, :])
+        basis_ref[at, :] = jnp.dot(
+            jnp.concatenate([high, high, low, low], axis=1), factors,
+            preferred_element_type=jnp.float32,
+        )
+        copies.append(pltpu.make_async_copy(basis_ref.at[at, :], basis_hbm.at[at, :], sems.at[k]))
+        copies[k].start()
+    sums = sums_refs[0][...]
+    for got_ref in sums_refs[1:]:
         sums = sums + got_ref[...]
     result = jnp.dot(inverse, sums, precision=HIGHEST, preferred_element_type=jnp.float32)
     out_ref[...] = (result.T * factor).astype(out_ref.dtype)
+    copies.append(pltpu.make_async_copy(out_ref, out_hbm, sems.at[2]))
+    copies[2].start()
+    for copy in copies:
+        copy.wait()
 
 
 def finish_call(inverse, first, total_rows, factor, sums):
@@ -266,9 +282,15 @@
     return pl.pallas_call(
         functools.partial(finish_kernel, float(total_rows) ** 0.5, factor),
         in_specs=[pl.BlockSpec(memory_space=pltpu.VMEM)] * (2 + len(sums)),
+        out_specs=[pl.BlockSpec(memory_space=pltpu.HBM)] * 2,
         out_shape=[
             jax.ShapeDtypeStruct((rows, rank), jnp.float32),
             jax.ShapeDtypeStruct((own, rank), jnp.bfloat16),
+        ],
+        scratch_shapes=[
+            pltpu.VMEM((rows, rank), jnp.float32),
+            pltpu.VMEM((own, rank), jnp.bfloat16),
+            pltpu.SemaphoreType.DMA((3,)),
         ],
         compiler_params=pltpu.CompilerParams(vmem_limit_bytes=VMEM_LIMIT),
         cost_estimate=pl.CostEstimate(

time: 37.5 us -> 37.3 us (level)
  no operation moved by 1% of the time
where the time goes in v15:
time: 37.3 us; the launch traced here: 37.1 us
  starting transfers between devices  18.1 us (49%)
  Pallas kernels  12.1 us (32%)
  waiting for transfers between devices  5.89 us (16%)
  between operations  0.73 us (2%)
    ppermute x13, starting transfers between devices, exchange(): return lax.ppermute(array, AXES, pairs)  18.1 us
    ppermute x13, waiting for transfers between devices, exchange(): return lax.ppermute(array, AXES, pairs)  5.89 us
    pallas_call x1, Pallas kernels, rows_call(): pl.pallas_call(rows_kernel, in_specs=[pl.BlockSpec(memory_space=pltpu.SME...  5.41 us
    pallas_call x1, Pallas kernels, factor_call(): pl.pallas_call(factor_kernel, in_specs=[pl.BlockSpec(memory_space=pltpu.V...  3.78 us
    pallas_call x2, Pallas kernels, project_call(): pl.pallas_call(functools.partial(project_kernel, parts), in_specs=[pl.Blo...  1.77 us
    pallas_call x1, Pallas kernels, finish_call(): pl.pallas_call(functools.partial(finish_kernel, float(total_rows) ** 0.5,...  1.19 us
  transfers between devices with their start and end apart: 13, of which 7 were waited for; matrix products, arithmetic and copies ran while one was open for 0% of the time, Pallas kernels for 15%

profile of v15, /device:TPU:0, one launch (start us, length us, event | category | flops | bytes accessed | tf_op | source)
XLA Modules:
  0.0 37.1 jit_solution(12535616721135292089)
XLA Ops:
  0.6 5.4 %sketch_rows.1 = (bf16[576,4096]{1,0:T(8,128)(2,1)S(1)}, f32[576,128]{1,0:T(8,128)S(1)}, f32[72,128]{1,0:T(8,128)S(1)}, bf16[256,576]{1,0:T(8,128)(2,1)S(1)}, f32[8,128,128]{2,1,0:T(8,128)S(1)}) custom-call(s32[1]{0:T(128)} %bitcast.owner_ref, bf16[576,4096]{1,0:T(8,128)(2,1)} %slab_hbm.1, bf16[4096,128]{1,0:T(8,128)(2,1)} %sketch_hbm.1), custom_call_target="tpu_custom_call" | custom-call | flops 905969664 | bytes 4718592 | tf_op jit(solution)/shard_map/sketch_rows/pallas_call | solution.py:140
  6.1 0.5 %collective-permute-start = (f32[8,128,128]{2,1,0:T(8,128)S(1)}, f32[8,128,128]{2,1,0:T(8,128)S(1)}, u32[]{:S(2)}, u32[]{:S(2)}) collective-permute-start(f32[8,128,128]{2,1,0:T(8,128)S(1)} %get-tuple-element.23), channel_id=1, source_target_pairs={{0,1},{1,0},{2,3},{3,2},{4,5},{5,4},{6,7},{7,6},{8,9},{9,8},{10,11... | collective-permute-start | bytes 1572872 | tf_op jit(solution)/shard_map/ppermute | solution.py:318
  6.6 0.1 collective-permute-start.1
  6.7 0.7 %project_first.1 = f32[8,128,128]{2,1,0:T(8,128)S(1)} custom-call(s32[1]{0:T(128)} %bitcast.owner_ref, bf16[256,576]{1,0:T(8,128)(2,1)S(1)} %get-tuple-element.26.split_ref, bf16[576,4096]{1,0:T(8,128)(2,1)S(1)} %get-tuple-element.22.slab_ref), custom_call_target="tpu_custom_call" | custom-call | flops 301989888 | bytes 2359296 | tf_op jit(solution)/shard_map/project_first/pallas_call | solution.py:122
  7.3 0.8 %collective-permute-done.1 = f32[72,128]{1,0:T(8,128)S(1)} collective-permute-done((f32[72,128]{1,0:T(8,128)S(1)}, f32[72,128]{1,0:T(8,128)S(1)}, u32[]{:S(2)}, u32[]{:S(2)}) %collective-permute-start.1) | collective-permute-done | bytes 36896 | tf_op jit(solution)/shard_map/ppermute | solution.py:318
  8.2 0.1 add.35
  8.3 2.9 %collective-permute-start.3 = (f32[8,128,128]{2,1,0:T(8,128)S(1)}, f32[8,128,128]{2,1,0:T(8,128)S(1)}, u32[]{:S(2)}, u32[]{:S(2)}) collective-permute-start(f32[8,128,128]{2,1,0:T(8,128)S(1)} %add.35), channel_id=1, source_target_pairs={{0,2},{1,5},{2,0},{3,7},{4,6},{5,1},{6,4},{7,3},{8,10},{9,13},{10,... | collective-permute-start | bytes 1572872 | tf_op jit(solution)/shard_map/ppermute | solution.py:318
  11.2 1.1 %project_rest.1 = (f32[8,128,128]{2,1,0:T(8,128)S(1)}, f32[8,128,128]{2,1,0:T(8,128)S(1)}) custom-call(s32[1]{0:T(128)} %bitcast.owner_ref, bf16[256,576]{1,0:T(8,128)(2,1)S(1)} %get-tuple-element.26.split_ref, bf16[576,4096]{1,0:T(8,128)(2,1)S(1)} %get-tuple-element.22.slab_ref), custom_call_target="tpu_custom_call" | custom-call | flops 603979776 | bytes 2359296 | tf_op jit(solution)/shard_map/project_rest/pallas_call | solution.py:122
  12.4 3.7 %collective-permute-start.4 = (f32[72,128]{1,0:T(8,128)S(1)}, f32[72,128]{1,0:T(8,128)S(1)}, u32[]{:S(2)}, u32[]{:S(2)}) collective-permute-start(f32[72,128]{1,0:T(8,128)S(1)} %add.34), channel_id=1, source_target_pairs={{0,24},{1,25},{2,26},{3,27},{4,28},{5,29},{6,30},{7,31},{8,16},{9,... | collective-permute-start | bytes 110600 | tf_op jit(solution)/shard_map/ppermute | solution.py:318
  16.0 0.8 %collective-permute-start.6 = (f32[72,128]{1,0:T(8,128)S(1)}, f32[72,128]{1,0:T(8,128)S(1)}, u32[]{:S(2)}, u32[]{:S(2)}) collective-permute-start(f32[72,128]{1,0:T(8,128)S(1)} %add.34), channel_id=1, source_target_pairs={{0,8},{1,9},{2,10},{3,11},{4,12},{5,13},{6,14},{7,15},{8,0},{9,1},... | collective-permute-start | bytes 110600 | tf_op jit(solution)/shard_map/ppermute | solution.py:318
  16.8 1.4 %collective-permute-done.4 = f32[72,128]{1,0:T(8,128)S(1)} collective-permute-done((f32[72,128]{1,0:T(8,128)S(1)}, f32[72,128]{1,0:T(8,128)S(1)}, u32[]{:S(2)}, u32[]{:S(2)}) %collective-permute-start.4) | collective-permute-done | bytes 36896 | tf_op jit(solution)/shard_map/ppermute | solution.py:318
  18.2 0.2 collective-permute-done.3
  18.3 0.1 add_add_fusion
  18.5 2.1 %collective-permute-start.5 = (f32[4,128,128]{2,1,0:T(8,128)S(1)}, f32[4,128,128]{2,1,0:T(8,128)S(1)}, u32[]{:S(2)}, u32[]{:S(2)}) collective-permute-start(f32[4,128,128]{2,1,0:T(8,128)S(1)} %slice.19), channel_id=1, source_target_pairs={{0,4},{1,3},{2,6},{3,1},{4,0},{5,7},{6,2},{7,5},{8,12},{9,11},{10,... | collective-permute-start | bytes 786440 | tf_op jit(solution)/shard_map/ppermute | solution.py:318
  20.6 0.3 collective-permute-done.7
  20.9 1.4 %collective-permute-start.8 = (f32[72,128]{1,0:T(8,128)S(1)}, f32[72,128]{1,0:T(8,128)S(1)}, u32[]{:S(2)}, u32[]{:S(2)}) collective-permute-start(f32[72,128]{1,0:T(8,128)S(1)} %add_add_fusion.1), channel_id=1, source_target_pairs={{0,2},{1,5},{2,0},{3,7},{4,6},{5,1},{6,4},{7,3},{8,10},{9,13},{10,... | collective-permute-start | bytes 110600 | tf_op jit(solution)/shard_map/ppermute | solution.py:318
  22.3 2.7 %collective-permute-done.8 = f32[72,128]{1,0:T(8,128)S(1)} collective-permute-done((f32[72,128]{1,0:T(8,128)S(1)}, f32[72,128]{1,0:T(8,128)S(1)}, u32[]{:S(2)}, u32[]{:S(2)}) %collective-permute-start.8) | collective-permute-done | bytes 36896 | tf_op jit(solution)/shard_map/ppermute | solution.py:318
  24.9 0.4 %collective-permute-done.5 = f32[4,128,128]{2,1,0:T(8,128)S(1)} collective-permute-done((f32[4,128,128]{2,1,0:T(8,128)S(1)}, f32[4,128,128]{2,1,0:T(8,128)S(1)}, u32[]{:S(2)}, u32[]{:S(2)}) %collective-permute-start.5) | collective-permute-done | bytes 262176 | tf_op jit(solution)/shard_map/ppermute | solution.py:318
  25.4 2.1 %collective-permute-start.9 = (f32[72,128]{1,0:T(8,128)S(1)}, f32[72,128]{1,0:T(8,128)S(1)}, u32[]{:S(2)}, u32[]{:S(2)}) collective-permute-start(f32[72,128]{1,0:T(8,128)S(1)} %add.41), channel_id=1, source_target_pairs={{0,4},{1,3},{2,6},{3,1},{4,0},{5,7},{6,2},{7,5},{8,12},{9,11},{10,... | collective-permute-start | bytes 110600 | tf_op jit(solution)/shard_map/ppermute | solution.py:318
  27.5 3.3 %collective-permute-start.12 = (f32[128,128]{1,0:T(8,128)S(1)}, f32[128,128]{1,0:T(8,128)S(1)}, u32[]{:S(2)}, u32[]{:S(2)}) collective-permute-start(f32[128,128]{1,0:T(8,128)S(1)} %get-tuple-element.40), channel_id=1, source_target_pairs={{0,24},{1,25},{2,26},{3,27},{4,28},{5,29},{6,30},{7,31},{8,16},{9,... | collective-permute-start | bytes 196616 | tf_op jit(solution)/shard_map/ppermute | solution.py:318
  30.8 1.2 %collective-permute-start.10 = (f32[128,128]{1,0:T(8,128)S(1)}, f32[128,128]{1,0:T(8,128)S(1)}, u32[]{:S(2)}, u32[]{:S(2)}) collective-permute-start(f32[128,128]{1,0:T(8,128)S(1)} %get-tuple-element.42), channel_id=1, source_target_pairs={{0,8},{1,9},{2,10},{3,11},{4,12},{5,13},{6,14},{7,15},{8,0},{9,1},... | collective-permute-start | bytes 196616 | tf_op jit(solution)/shard_map/ppermute | solution.py:318
  31.9 3.8 %factor.1.inverse_ref = f32[128,128]{1,0:T(8,128)S(1)} custom-call(f32[72,128]{1,0:T(8,128)S(1)} %add.43.gram_ref), custom_call_target="tpu_custom_call" | custom-call | flops 4000000000 | bytes 73728 | tf_op jit(solution)/shard_map/factor/pallas_call | solution.py:234
  35.8 0.2 collective-permute-done.11.refs_2_
  35.9 1.2 %finish.1 = (f32[576,128]{1,0:T(8,128)}, bf16[128,128]{1,0:T(8,128)(2,1)}) custom-call(f32[128,128]{1,0:T(8,128)S(1)} %factor.1.inverse_ref, f32[576,128]{1,0:T(8,128)S(1)} %get-tuple-element.38.first_ref, f32[128,128]{1,0:T(8,128)S(1)} %slice_bitcast_fusion.3.refs_0_, f32[128,128]{1,0:T(8,128)S(1)} %collective-permute-done.10.refs_1_, ...), custom_call_target="tpu_custom_call" | custom-call | flops 113246208 | bytes 589824 | tf_op jit(solution)/shard_map/finish/pallas_call | solution.py:282
  (17 shorter events, 0.2 us)
Async XLA Ops:
  6.1 2.1 %collective-permute-start = (f32[8,128,128]{2,1,0:T(8,128)S(1)}, f32[8,128,128]{2,1,0:T(8,128)S(1)}, u32[]{:S(2)}, u32[]{:S(2)}) collective-permute-start(f32[8,128,128]{2,1,0:T(8,128)S(1)} %get-tuple-element.23), channel_id=1, source_target_pairs={{0,1},{1,0},{2,3},{3,2},{4,5},{5,4},{6,7},{7,6},{8,9},{9,8},{10,11... | collective-permute-start | bytes 1572872 | tf_op jit(solution)/shard_map/ppermute | solution.py:318
  6.6 1.6 %collective-permute-start.1 = (f32[72,128]{1,0:T(8,128)S(1)}, f32[72,128]{1,0:T(8,128)S(1)}, u32[]{:S(2)}, u32[]{:S(2)}) collective-permute-start(f32[72,128]{1,0:T(8,128)S(1)} %get-tuple-element.24), channel_id=1, source_target_pairs={{0,1},{1,0},{2,3},{3,2},{4,5},{5,4},{6,7},{7,6},{8,9},{9,8},{10,11... | collective-permute-start | bytes 110600 | tf_op jit(solution)/shard_map/ppermute | solution.py:318
  8.3 10.1 %collective-permute-start.3 = (f32[8,128,128]{2,1,0:T(8,128)S(1)}, f32[8,128,128]{2,1,0:T(8,128)S(1)}, u32[]{:S(2)}, u32[]{:S(2)}) collective-permute-start(f32[8,128,128]{2,1,0:T(8,128)S(1)} %add.35), channel_id=1, source_target_pairs={{0,2},{1,5},{2,0},{3,7},{4,6},{5,1},{6,4},{7,3},{8,10},{9,13},{10,... | collective-permute-start | bytes 1572872 | tf_op jit(solution)/shard_map/ppermute | solution.py:318
  12.3 6.1 %collective-permute-start.2 = (f32[8,128,128]{2,1,0:T(8,128)S(1)}, f32[8,128,128]{2,1,0:T(8,128)S(1)}, u32[]{:S(2)}, u32[]{:S(2)}) collective-permute-start(f32[8,128,128]{2,1,0:T(8,128)S(1)} %get-tuple-element.28), channel_id=1, source_target_pairs={{0,1},{1,0},{2,3},{3,2},{4,5},{5,4},{6,7},{7,6},{8,9},{9,8},{10,11... | collective-permute-start | bytes 1572872 | tf_op jit(solution)/shard_map/ppermute | solution.py:318
  12.4 5.8 %collective-permute-start.4 = (f32[72,128]{1,0:T(8,128)S(1)}, f32[72,128]{1,0:T(8,128)S(1)}, u32[]{:S(2)}, u32[]{:S(2)}) collective-permute-start(f32[72,128]{1,0:T(8,128)S(1)} %add.34), channel_id=1, source_target_pairs={{0,24},{1,25},{2,26},{3,27},{4,28},{5,29},{6,30},{7,31},{8,16},{9,... | collective-permute-start | bytes 110600 | tf_op jit(solution)/shard_map/ppermute | solution.py:318
  16.0 4.9 %collective-permute-start.7 = (f32[72,128]{1,0:T(8,128)S(1)}, f32[72,128]{1,0:T(8,128)S(1)}, u32[]{:S(2)}, u32[]{:S(2)}) collective-permute-start(f32[72,128]{1,0:T(8,128)S(1)} %add.34), channel_id=1, source_target_pairs={{0,16},{1,17},{2,18},{3,19},{4,20},{5,21},{6,22},{7,23},{8,24},{9,... | collective-permute-start | bytes 110600 | tf_op jit(solution)/shard_map/ppermute | solution.py:318
  16.0 4.9 %collective-permute-start.6 = (f32[72,128]{1,0:T(8,128)S(1)}, f32[72,128]{1,0:T(8,128)S(1)}, u32[]{:S(2)}, u32[]{:S(2)}) collective-permute-start(f32[72,128]{1,0:T(8,128)S(1)} %add.34), channel_id=1, source_target_pairs={{0,8},{1,9},{2,10},{3,11},{4,12},{5,13},{6,14},{7,15},{8,0},{9,1},... | collective-permute-start | bytes 110600 | tf_op jit(solution)/shard_map/ppermute | solution.py:318
  18.5 6.9 %collective-permute-start.5 = (f32[4,128,128]{2,1,0:T(8,128)S(1)}, f32[4,128,128]{2,1,0:T(8,128)S(1)}, u32[]{:S(2)}, u32[]{:S(2)}) collective-permute-start(f32[4,128,128]{2,1,0:T(8,128)S(1)} %slice.19), channel_id=1, source_target_pairs={{0,4},{1,3},{2,6},{3,1},{4,0},{5,7},{6,2},{7,5},{8,12},{9,11},{10,... | collective-permute-start | bytes 786440 | tf_op jit(solution)/shard_map/ppermute | solution.py:318
  20.9 4.0 %collective-permute-start.8 = (f32[72,128]{1,0:T(8,128)S(1)}, f32[72,128]{1,0:T(8,128)S(1)}, u32[]{:S(2)}, u32[]{:S(2)}) collective-permute-start(f32[72,128]{1,0:T(8,128)S(1)} %add_add_fusion.1), channel_id=1, source_target_pairs={{0,2},{1,5},{2,0},{3,7},{4,6},{5,1},{6,4},{7,3},{8,10},{9,13},{10,... | collective-permute-start | bytes 110600 | tf_op jit(solution)/shard_map/ppermute | solution.py:318
  25.4 6.6 %collective-permute-start.9 = (f32[72,128]{1,0:T(8,128)S(1)}, f32[72,128]{1,0:T(8,128)S(1)}, u32[]{:S(2)}, u32[]{:S(2)}) collective-permute-start(f32[72,128]{1,0:T(8,128)S(1)} %add.41), channel_id=1, source_target_pairs={{0,4},{1,3},{2,6},{3,1},{4,0},{5,7},{6,2},{7,5},{8,12},{9,11},{10,... | collective-permute-start | bytes 110600 | tf_op jit(solution)/shard_map/ppermute | solution.py:318
  27.5 8.3 %collective-permute-start.12 = (f32[128,128]{1,0:T(8,128)S(1)}, f32[128,128]{1,0:T(8,128)S(1)}, u32[]{:S(2)}, u32[]{:S(2)}) collective-permute-start(f32[128,128]{1,0:T(8,128)S(1)} %get-tuple-element.40), channel_id=1, source_target_pairs={{0,24},{1,25},{2,26},{3,27},{4,28},{5,29},{6,30},{7,31},{8,16},{9,... | collective-permute-start | bytes 196616 | tf_op jit(solution)/shard_map/ppermute | solution.py:318
  30.8 5.2 %collective-permute-start.11 = (f32[128,128]{1,0:T(8,128)S(1)}, f32[128,128]{1,0:T(8,128)S(1)}, u32[]{:S(2)}, u32[]{:S(2)}) collective-permute-start(f32[128,128]{1,0:T(8,128)S(1)} %get-tuple-element.41), channel_id=1, source_target_pairs={{0,16},{1,17},{2,18},{3,19},{4,20},{5,21},{6,22},{7,23},{8,24},{9,... | collective-permute-start | bytes 196616 | tf_op jit(solution)/shard_map/ppermute | solution.py:318
  30.8 5.2 %collective-permute-start.10 = (f32[128,128]{1,0:T(8,128)S(1)}, f32[128,128]{1,0:T(8,128)S(1)}, u32[]{:S(2)}, u32[]{:S(2)}) collective-permute-start(f32[128,128]{1,0:T(8,128)S(1)} %get-tuple-element.42), channel_id=1, source_target_pairs={{0,8},{1,9},{2,10},{3,11},{4,12},{5,13},{6,14},{7,15},{8,0},{9,1},... | collective-permute-start | bytes 196616 | tf_op jit(solution)/shard_map/ppermute | solution.py:318

commit v16 on v14

--- a/solution.py
+++ b/solution.py
@@ -11,8 +11,7 @@
 HIGHEST = lax.Precision.HIGHEST
 LANES = 128
 VMEM_LIMIT = 24 * 1024 * 1024
-AHEAD = 1
-ROWS = 256
+CUT = 256
 
 
 def project(out_ref, split_ref, slab_ref, owner, sibling, first_place):
@@ -68,25 +67,17 @@
 ):
     rows, width = slab_ref.shape
     rank = sketch_ref.shape[1]
-    starts = list(range(0, rows, ROWS))
+    chunks = [pl.ds(0, CUT), pl.ds(CUT, rows - CUT)]
     copies = [
-        pltpu.make_async_copy(
-            slab_hbm.at[pl.ds(r, min(ROWS, rows - r)), :],
-            slab_ref.at[pl.ds(r, min(ROWS, rows - r)), :],
-            slab_sem.at[k],
-        )
-        for k, r in enumerate(starts)
+        pltpu.make_async_copy(slab_hbm.at[at, :], slab_ref.at[at, :], slab_sem.at[k])
+        for k, at in enumerate(chunks)
     ]
     sketch_copy = pltpu.make_async_copy(sketch_hbm, sketch_ref, sketch_sem)
-    sketch_copy.start()
-    for copy in copies[:AHEAD]:
+    for copy in (sketch_copy, *copies):
         copy.start()
     sketch_copy.wait()
-    for k, r in enumerate(starts):
+    for k, at in enumerate(chunks):
         copies[k].wait()
-        if k + AHEAD < len(starts):
-            copies[k + AHEAD].start()
-        at = pl.ds(r, min(ROWS, rows - r))
         first = jnp.dot(slab_ref[at, :], sketch_ref[...], preferred_element_type=jnp.float32)
         first_ref[at, :] = first
         turned = first.T
@@ -149,7 +140,7 @@
         scratch_shapes=[
             pltpu.VMEM((width, rank), jnp.bfloat16),
             pltpu.VMEM((rank, rank), jnp.float32),
-            pltpu.SemaphoreType.DMA((-(-rows // ROWS),)),
+            pltpu.SemaphoreType.DMA((2,)),
             pltpu.SemaphoreType.DMA,
         ],
         compiler_params=pltpu.CompilerParams(vmem_limit_bytes=VMEM_LIMIT),

time: 37.5 us -> 37.5 us (level)
  no operation moved by 1% of the time
where the time goes in v16:
time: 37.5 us; the launch traced here: 37.3 us
  starting transfers between devices  18.1 us (48%)
  Pallas kernels  12.3 us (33%)
  waiting for transfers between devices  5.89 us (16%)
  between operations  0.73 us (2%)
    ppermute x13, starting transfers between devices, exchange(): return lax.ppermute(array, AXES, pairs)  18.1 us
    ppermute x13, waiting for transfers between devices, exchange(): return lax.ppermute(array, AXES, pairs)  5.89 us
    pallas_call x1, Pallas kernels, rows_call(): pl.pallas_call(rows_kernel, in_specs=[pl.BlockSpec(memory_space=pltpu.SME...  5.61 us
    pallas_call x1, Pallas kernels, factor_call(): pl.pallas_call(factor_kernel, in_specs=[pl.BlockSpec(memory_space=pltpu.V...  3.78 us
    pallas_call x2, Pallas kernels, project_call(): pl.pallas_call(functools.partial(project_kernel, parts), in_specs=[pl.Blo...  1.77 us
    pallas_call x1, Pallas kernels, finish_call(): pl.pallas_call(functools.partial(finish_kernel, float(total_rows) ** 0.5,...  1.18 us
  transfers between devices with their start and end apart: 13, of which 7 were waited for; matrix products, arithmetic and copies ran while one was open for 0% of the time, Pallas kernels for 15%

profile of v16, /device:TPU:0, one launch (start us, length us, event | category | flops | bytes accessed | tf_op | source)
XLA Modules:
  0.0 37.3 jit_solution(9416617796762122591)
XLA Ops:
  0.6 5.6 %sketch_rows.1 = (bf16[576,4096]{1,0:T(8,128)(2,1)S(1)}, f32[576,128]{1,0:T(8,128)S(1)}, f32[72,128]{1,0:T(8,128)S(1)}, bf16[256,576]{1,0:T(8,128)(2,1)S(1)}, f32[8,128,128]{2,1,0:T(8,128)S(1)}) custom-call(s32[1]{0:T(128)} %bitcast.owner_ref, bf16[576,4096]{1,0:T(8,128)(2,1)} %slab_hbm.1, bf16[4096,128]{1,0:T(8,128)(2,1)} %sketch_hbm.1), custom_call_target="tpu_custom_call" | custom-call | flops 905969664 | bytes 4718592 | tf_op jit(solution)/shard_map/sketch_rows/pallas_call | solution.py:125
  6.3 0.5 %collective-permute-start = (f32[8,128,128]{2,1,0:T(8,128)S(1)}, f32[8,128,128]{2,1,0:T(8,128)S(1)}, u32[]{:S(2)}, u32[]{:S(2)}) collective-permute-start(f32[8,128,128]{2,1,0:T(8,128)S(1)} %get-tuple-element.23), channel_id=1, source_target_pairs={{0,1},{1,0},{2,3},{3,2},{4,5},{5,4},{6,7},{7,6},{8,9},{9,8},{10,11... | collective-permute-start | bytes 1572872 | tf_op jit(solution)/shard_map/ppermute | solution.py:287
  6.8 0.1 collective-permute-start.1
  6.9 0.7 %project_first.1 = f32[8,128,128]{2,1,0:T(8,128)S(1)} custom-call(s32[1]{0:T(128)} %bitcast.owner_ref, bf16[256,576]{1,0:T(8,128)(2,1)S(1)} %get-tuple-element.26.split_ref, bf16[576,4096]{1,0:T(8,128)(2,1)S(1)} %get-tuple-element.22.slab_ref), custom_call_target="tpu_custom_call" | custom-call | flops 301989888 | bytes 2359296 | tf_op jit(solution)/shard_map/project_first/pallas_call | solution.py:107
  7.5 0.8 %collective-permute-done.1 = f32[72,128]{1,0:T(8,128)S(1)} collective-permute-done((f32[72,128]{1,0:T(8,128)S(1)}, f32[72,128]{1,0:T(8,128)S(1)}, u32[]{:S(2)}, u32[]{:S(2)}) %collective-permute-start.1) | collective-permute-done | bytes 36896 | tf_op jit(solution)/shard_map/ppermute | solution.py:287
  8.4 0.1 add.35
  8.5 2.9 %collective-permute-start.3 = (f32[8,128,128]{2,1,0:T(8,128)S(1)}, f32[8,128,128]{2,1,0:T(8,128)S(1)}, u32[]{:S(2)}, u32[]{:S(2)}) collective-permute-start(f32[8,128,128]{2,1,0:T(8,128)S(1)} %add.35), channel_id=1, source_target_pairs={{0,2},{1,5},{2,0},{3,7},{4,6},{5,1},{6,4},{7,3},{8,10},{9,13},{10,... | collective-permute-start | bytes 1572872 | tf_op jit(solution)/shard_map/ppermute | solution.py:287
  11.4 1.1 %project_rest.1 = (f32[8,128,128]{2,1,0:T(8,128)S(1)}, f32[8,128,128]{2,1,0:T(8,128)S(1)}) custom-call(s32[1]{0:T(128)} %bitcast.owner_ref, bf16[256,576]{1,0:T(8,128)(2,1)S(1)} %get-tuple-element.26.split_ref, bf16[576,4096]{1,0:T(8,128)(2,1)S(1)} %get-tuple-element.22.slab_ref), custom_call_target="tpu_custom_call" | custom-call | flops 603979776 | bytes 2359296 | tf_op jit(solution)/shard_map/project_rest/pallas_call | solution.py:107
  12.6 3.7 %collective-permute-start.4 = (f32[72,128]{1,0:T(8,128)S(1)}, f32[72,128]{1,0:T(8,128)S(1)}, u32[]{:S(2)}, u32[]{:S(2)}) collective-permute-start(f32[72,128]{1,0:T(8,128)S(1)} %add.34), channel_id=1, source_target_pairs={{0,24},{1,25},{2,26},{3,27},{4,28},{5,29},{6,30},{7,31},{8,16},{9,... | collective-permute-start | bytes 110600 | tf_op jit(solution)/shard_map/ppermute | solution.py:287
  16.2 0.8 %collective-permute-start.6 = (f32[72,128]{1,0:T(8,128)S(1)}, f32[72,128]{1,0:T(8,128)S(1)}, u32[]{:S(2)}, u32[]{:S(2)}) collective-permute-start(f32[72,128]{1,0:T(8,128)S(1)} %add.34), channel_id=1, source_target_pairs={{0,8},{1,9},{2,10},{3,11},{4,12},{5,13},{6,14},{7,15},{8,0},{9,1},... | collective-permute-start | bytes 110600 | tf_op jit(solution)/shard_map/ppermute | solution.py:287
  17.0 1.4 %collective-permute-done.4 = f32[72,128]{1,0:T(8,128)S(1)} collective-permute-done((f32[72,128]{1,0:T(8,128)S(1)}, f32[72,128]{1,0:T(8,128)S(1)}, u32[]{:S(2)}, u32[]{:S(2)}) %collective-permute-start.4) | collective-permute-done | bytes 36896 | tf_op jit(solution)/shard_map/ppermute | solution.py:287
  18.4 0.2 collective-permute-done.3
  18.5 0.1 add_add_fusion
  18.7 2.1 %collective-permute-start.5 = (f32[4,128,128]{2,1,0:T(8,128)S(1)}, f32[4,128,128]{2,1,0:T(8,128)S(1)}, u32[]{:S(2)}, u32[]{:S(2)}) collective-permute-start(f32[4,128,128]{2,1,0:T(8,128)S(1)} %slice.19), channel_id=1, source_target_pairs={{0,4},{1,3},{2,6},{3,1},{4,0},{5,7},{6,2},{7,5},{8,12},{9,11},{10,... | collective-permute-start | bytes 786440 | tf_op jit(solution)/shard_map/ppermute | solution.py:287
  20.8 0.3 collective-permute-done.7
  21.1 1.4 %collective-permute-start.8 = (f32[72,128]{1,0:T(8,128)S(1)}, f32[72,128]{1,0:T(8,128)S(1)}, u32[]{:S(2)}, u32[]{:S(2)}) collective-permute-start(f32[72,128]{1,0:T(8,128)S(1)} %add_add_fusion.1), channel_id=1, source_target_pairs={{0,2},{1,5},{2,0},{3,7},{4,6},{5,1},{6,4},{7,3},{8,10},{9,13},{10,... | collective-permute-start | bytes 110600 | tf_op jit(solution)/shard_map/ppermute | solution.py:287
  22.5 2.7 %collective-permute-done.8 = f32[72,128]{1,0:T(8,128)S(1)} collective-permute-done((f32[72,128]{1,0:T(8,128)S(1)}, f32[72,128]{1,0:T(8,128)S(1)}, u32[]{:S(2)}, u32[]{:S(2)}) %collective-permute-start.8) | collective-permute-done | bytes 36896 | tf_op jit(solution)/shard_map/ppermute | solution.py:287
  25.1 0.4 %collective-permute-done.5 = f32[4,128,128]{2,1,0:T(8,128)S(1)} collective-permute-done((f32[4,128,128]{2,1,0:T(8,128)S(1)}, f32[4,128,128]{2,1,0:T(8,128)S(1)}, u32[]{:S(2)}, u32[]{:S(2)}) %collective-permute-start.5) | collective-permute-done | bytes 262176 | tf_op jit(solution)/shard_map/ppermute | solution.py:287
  25.6 2.1 %collective-permute-start.9 = (f32[72,128]{1,0:T(8,128)S(1)}, f32[72,128]{1,0:T(8,128)S(1)}, u32[]{:S(2)}, u32[]{:S(2)}) collective-permute-start(f32[72,128]{1,0:T(8,128)S(1)} %add.41), channel_id=1, source_target_pairs={{0,4},{1,3},{2,6},{3,1},{4,0},{5,7},{6,2},{7,5},{8,12},{9,11},{10,... | collective-permute-start | bytes 110600 | tf_op jit(solution)/shard_map/ppermute | solution.py:287
  27.7 3.3 %collective-permute-start.12 = (f32[128,128]{1,0:T(8,128)S(1)}, f32[128,128]{1,0:T(8,128)S(1)}, u32[]{:S(2)}, u32[]{:S(2)}) collective-permute-start(f32[128,128]{1,0:T(8,128)S(1)} %get-tuple-element.40), channel_id=1, source_target_pairs={{0,24},{1,25},{2,26},{3,27},{4,28},{5,29},{6,30},{7,31},{8,16},{9,... | collective-permute-start | bytes 196616 | tf_op jit(solution)/shard_map/ppermute | solution.py:287
  31.0 1.2 %collective-permute-start.10 = (f32[128,128]{1,0:T(8,128)S(1)}, f32[128,128]{1,0:T(8,128)S(1)}, u32[]{:S(2)}, u32[]{:S(2)}) collective-permute-start(f32[128,128]{1,0:T(8,128)S(1)} %get-tuple-element.42), channel_id=1, source_target_pairs={{0,8},{1,9},{2,10},{3,11},{4,12},{5,13},{6,14},{7,15},{8,0},{9,1},... | collective-permute-start | bytes 196616 | tf_op jit(solution)/shard_map/ppermute | solution.py:287
  32.2 3.8 %factor.1.inverse_ref = f32[128,128]{1,0:T(8,128)S(1)} custom-call(f32[72,128]{1,0:T(8,128)S(1)} %add.43.gram_ref), custom_call_target="tpu_custom_call" | custom-call | flops 4000000000 | bytes 73728 | tf_op jit(solution)/shard_map/factor/pallas_call | solution.py:219
  36.0 0.2 collective-permute-done.11.refs_1_
  36.1 1.2 %finish.1 = (f32[576,128]{1,0:T(8,128)}, bf16[128,128]{1,0:T(8,128)(2,1)}) custom-call(f32[128,128]{1,0:T(8,128)S(1)} %factor.1.inverse_ref, f32[576,128]{1,0:T(8,128)S(1)} %get-tuple-element.38.first_ref, f32[128,128]{1,0:T(8,128)S(1)} %slice_bitcast_fusion.3.sums_ref, f32[128,128]{1,0:T(8,128)S(1)} %collective-permute-done.10.refs_0_, ...), custom_call_target="tpu_custom_call" | custom-call | flops 113246208 | bytes 589824 | tf_op jit(solution)/shard_map/finish/pallas_call | solution.py:257
  (17 shorter events, 0.2 us)
Async XLA Ops:
  6.3 2.1 %collective-permute-start = (f32[8,128,128]{2,1,0:T(8,128)S(1)}, f32[8,128,128]{2,1,0:T(8,128)S(1)}, u32[]{:S(2)}, u32[]{:S(2)}) collective-permute-start(f32[8,128,128]{2,1,0:T(8,128)S(1)} %get-tuple-element.23), channel_id=1, source_target_pairs={{0,1},{1,0},{2,3},{3,2},{4,5},{5,4},{6,7},{7,6},{8,9},{9,8},{10,11... | collective-permute-start | bytes 1572872 | tf_op jit(solution)/shard_map/ppermute | solution.py:287
  6.8 1.6 %collective-permute-start.1 = (f32[72,128]{1,0:T(8,128)S(1)}, f32[72,128]{1,0:T(8,128)S(1)}, u32[]{:S(2)}, u32[]{:S(2)}) collective-permute-start(f32[72,128]{1,0:T(8,128)S(1)} %get-tuple-element.24), channel_id=1, source_target_pairs={{0,1},{1,0},{2,3},{3,2},{4,5},{5,4},{6,7},{7,6},{8,9},{9,8},{10,11... | collective-permute-start | bytes 110600 | tf_op jit(solution)/shard_map/ppermute | solution.py:287
  8.5 10.1 %collective-permute-start.3 = (f32[8,128,128]{2,1,0:T(8,128)S(1)}, f32[8,128,128]{2,1,0:T(8,128)S(1)}, u32[]{:S(2)}, u32[]{:S(2)}) collective-permute-start(f32[8,128,128]{2,1,0:T(8,128)S(1)} %add.35), channel_id=1, source_target_pairs={{0,2},{1,5},{2,0},{3,7},{4,6},{5,1},{6,4},{7,3},{8,10},{9,13},{10,... | collective-permute-start | bytes 1572872 | tf_op jit(solution)/shard_map/ppermute | solution.py:287
  12.5 6.1 %collective-permute-start.2 = (f32[8,128,128]{2,1,0:T(8,128)S(1)}, f32[8,128,128]{2,1,0:T(8,128)S(1)}, u32[]{:S(2)}, u32[]{:S(2)}) collective-permute-start(f32[8,128,128]{2,1,0:T(8,128)S(1)} %get-tuple-element.28), channel_id=1, source_target_pairs={{0,1},{1,0},{2,3},{3,2},{4,5},{5,4},{6,7},{7,6},{8,9},{9,8},{10,11... | collective-permute-start | bytes 1572872 | tf_op jit(solution)/shard_map/ppermute | solution.py:287
  12.6 5.8 %collective-permute-start.4 = (f32[72,128]{1,0:T(8,128)S(1)}, f32[72,128]{1,0:T(8,128)S(1)}, u32[]{:S(2)}, u32[]{:S(2)}) collective-permute-start(f32[72,128]{1,0:T(8,128)S(1)} %add.34), channel_id=1, source_target_pairs={{0,24},{1,25},{2,26},{3,27},{4,28},{5,29},{6,30},{7,31},{8,16},{9,... | collective-permute-start | bytes 110600 | tf_op jit(solution)/shard_map/ppermute | solution.py:287
  16.2 4.9 %collective-permute-start.7 = (f32[72,128]{1,0:T(8,128)S(1)}, f32[72,128]{1,0:T(8,128)S(1)}, u32[]{:S(2)}, u32[]{:S(2)}) collective-permute-start(f32[72,128]{1,0:T(8,128)S(1)} %add.34), channel_id=1, source_target_pairs={{0,16},{1,17},{2,18},{3,19},{4,20},{5,21},{6,22},{7,23},{8,24},{9,... | collective-permute-start | bytes 110600 | tf_op jit(solution)/shard_map/ppermute | solution.py:287
  16.2 4.9 %collective-permute-start.6 = (f32[72,128]{1,0:T(8,128)S(1)}, f32[72,128]{1,0:T(8,128)S(1)}, u32[]{:S(2)}, u32[]{:S(2)}) collective-permute-start(f32[72,128]{1,0:T(8,128)S(1)} %add.34), channel_id=1, source_target_pairs={{0,8},{1,9},{2,10},{3,11},{4,12},{5,13},{6,14},{7,15},{8,0},{9,1},... | collective-permute-start | bytes 110600 | tf_op jit(solution)/shard_map/ppermute | solution.py:287
  18.7 6.9 %collective-permute-start.5 = (f32[4,128,128]{2,1,0:T(8,128)S(1)}, f32[4,128,128]{2,1,0:T(8,128)S(1)}, u32[]{:S(2)}, u32[]{:S(2)}) collective-permute-start(f32[4,128,128]{2,1,0:T(8,128)S(1)} %slice.19), channel_id=1, source_target_pairs={{0,4},{1,3},{2,6},{3,1},{4,0},{5,7},{6,2},{7,5},{8,12},{9,11},{10,... | collective-permute-start | bytes 786440 | tf_op jit(solution)/shard_map/ppermute | solution.py:287
  21.1 4.0 %collective-permute-start.8 = (f32[72,128]{1,0:T(8,128)S(1)}, f32[72,128]{1,0:T(8,128)S(1)}, u32[]{:S(2)}, u32[]{:S(2)}) collective-permute-start(f32[72,128]{1,0:T(8,128)S(1)} %add_add_fusion.1), channel_id=1, source_target_pairs={{0,2},{1,5},{2,0},{3,7},{4,6},{5,1},{6,4},{7,3},{8,10},{9,13},{10,... | collective-permute-start | bytes 110600 | tf_op jit(solution)/shard_map/ppermute | solution.py:287
  25.6 6.6 %collective-permute-start.9 = (f32[72,128]{1,0:T(8,128)S(1)}, f32[72,128]{1,0:T(8,128)S(1)}, u32[]{:S(2)}, u32[]{:S(2)}) collective-permute-start(f32[72,128]{1,0:T(8,128)S(1)} %add.41), channel_id=1, source_target_pairs={{0,4},{1,3},{2,6},{3,1},{4,0},{5,7},{6,2},{7,5},{8,12},{9,11},{10,... | collective-permute-start | bytes 110600 | tf_op jit(solution)/shard_map/ppermute | solution.py:287
  27.7 8.3 %collective-permute-start.12 = (f32[128,128]{1,0:T(8,128)S(1)}, f32[128,128]{1,0:T(8,128)S(1)}, u32[]{:S(2)}, u32[]{:S(2)}) collective-permute-start(f32[128,128]{1,0:T(8,128)S(1)} %get-tuple-element.40), channel_id=1, source_target_pairs={{0,24},{1,25},{2,26},{3,27},{4,28},{5,29},{6,30},{7,31},{8,16},{9,... | collective-permute-start | bytes 196616 | tf_op jit(solution)/shard_map/ppermute | solution.py:287
  31.0 5.2 %collective-permute-start.11 = (f32[128,128]{1,0:T(8,128)S(1)}, f32[128,128]{1,0:T(8,128)S(1)}, u32[]{:S(2)}, u32[]{:S(2)}) collective-permute-start(f32[128,128]{1,0:T(8,128)S(1)} %get-tuple-element.41), channel_id=1, source_target_pairs={{0,16},{1,17},{2,18},{3,19},{4,20},{5,21},{6,22},{7,23},{8,24},{9,... | collective-permute-start | bytes 196616 | tf_op jit(solution)/shard_map/ppermute | solution.py:287
  31.0 5.2 %collective-permute-start.10 = (f32[128,128]{1,0:T(8,128)S(1)}, f32[128,128]{1,0:T(8,128)S(1)}, u32[]{:S(2)}, u32[]{:S(2)}) collective-permute-start(f32[128,128]{1,0:T(8,128)S(1)} %get-tuple-element.42), channel_id=1, source_target_pairs={{0,8},{1,9},{2,10},{3,11},{4,12},{5,13},{6,14},{7,15},{8,0},{9,1},... | collective-permute-start | bytes 196616 | tf_op jit(solution)/shard_map/ppermute | solution.py:287

commit v17 on v16

--- a/solution.py
+++ b/solution.py
@@ -11,7 +11,8 @@
 HIGHEST = lax.Precision.HIGHEST
 LANES = 128
 VMEM_LIMIT = 24 * 1024 * 1024
-CUT = 256
+AHEAD = 2
+CHUNKS = 4
 
 
 def project(out_ref, split_ref, slab_ref, owner, sibling, first_place):
@@ -63,34 +64,40 @@
 
 def rows_kernel(
     owner_ref, slab_hbm, sketch_hbm, slab_ref, first_ref, gram_ref, split_ref, send_ref,
-    sketch_ref, sum_ref, slab_sem, sketch_sem,
+    sketch_ref, slab_sem, sketch_sem,
 ):
     rows, width = slab_ref.shape
     rank = sketch_ref.shape[1]
-    chunks = [pl.ds(0, CUT), pl.ds(CUT, rows - CUT)]
+    step = width // CHUNKS
+    chunks = [pl.ds(k * step, step) for k in range(CHUNKS)]
     copies = [
-        pltpu.make_async_copy(slab_hbm.at[at, :], slab_ref.at[at, :], slab_sem.at[k])
+        (
+            pltpu.make_async_copy(sketch_hbm.at[at, :], sketch_ref.at[at, :], sketch_sem.at[k]),
+            pltpu.make_async_copy(slab_hbm.at[:, at], slab_ref.at[:, at], slab_sem.at[k]),
+        )
         for k, at in enumerate(chunks)
     ]
-    sketch_copy = pltpu.make_async_copy(sketch_hbm, sketch_ref, sketch_sem)
-    for copy in (sketch_copy, *copies):
-        copy.start()
-    sketch_copy.wait()
+    for pair in copies[:AHEAD]:
+        for copy in pair:
+            copy.start()
     for k, at in enumerate(chunks):
-        copies[k].wait()
-        first = jnp.dot(slab_ref[at, :], sketch_ref[...], preferred_element_type=jnp.float32)
-        first_ref[at, :] = first
-        turned = first.T
-        high = turned.astype(jnp.bfloat16)
-        split_ref[:rank, at] = high
-        split_ref[rank:, at] = (turned - high.astype(jnp.float32)).astype(jnp.bfloat16)
-        gram = jnp.dot(turned, first, precision=HIGHEST, preferred_element_type=jnp.float32)
+        for copy in copies[k]:
+            copy.wait()
+        if k + AHEAD < CHUNKS:
+            for copy in copies[k + AHEAD]:
+                copy.start()
+        part = jnp.dot(slab_ref[:, at], sketch_ref[at, :], preferred_element_type=jnp.float32)
         if k == 0:
-            sum_ref[...] = gram
+            first_ref[...] = part
         else:
-            sum_ref[...] += gram
-    gram_ref[...] = pack(sum_ref[...])
-
+            first_ref[...] += part
+    first = first_ref[...]
+    turned = first.T
+    high = turned.astype(jnp.bfloat16)
+    split_ref[:rank] = high
+    split_ref[rank:] = (turned - high.astype(jnp.float32)).astype(jnp.bfloat16)
+    gram = jnp.dot(turned, first, precision=HIGHEST, preferred_element_type=jnp.float32)
+    gram_ref[...] = pack(gram)
     project(send_ref, split_ref, slab_ref, owner_ref[0], 1, 8)
 
 
@@ -139,9 +146,8 @@
         ],
         scratch_shapes=[
             pltpu.VMEM((width, rank), jnp.bfloat16),
-            pltpu.VMEM((rank, rank), jnp.float32),
-            pltpu.SemaphoreType.DMA((2,)),
-            pltpu.SemaphoreType.DMA,
+            pltpu.SemaphoreType.DMA((CHUNKS,)),
+            pltpu.SemaphoreType.DMA((CHUNKS,)),
         ],
         compiler_params=pltpu.CompilerParams(vmem_limit_bytes=VMEM_LIMIT),
         cost_estimate=pl.CostEstimate(

time: 37.5 us -> 37.7 us (level)
  no operation moved by 1% of the time
where the time goes in v17:
time: 37.7 us; the launch traced here: 37.5 us
  starting transfers between devices  18.1 us (48%)
  Pallas kernels  12.5 us (33%)
  waiting for transfers between devices  5.88 us (16%)
  between operations  0.73 us (2%)
    ppermute x13, starting transfers between devices, exchange(): return lax.ppermute(array, AXES, pairs)  18.1 us
    ppermute x13, waiting for transfers between devices, exchange(): return lax.ppermute(array, AXES, pairs)  5.88 us
    pallas_call x1, Pallas kernels, rows_call(): pl.pallas_call(rows_kernel, in_specs=[pl.BlockSpec(memory_space=pltpu.SME...  5.77 us
    pallas_call x1, Pallas kernels, factor_call(): pl.pallas_call(factor_kernel, in_specs=[pl.BlockSpec(memory_space=pltpu.V...  3.78 us
    pallas_call x2, Pallas kernels, project_call(): pl.pallas_call(functools.partial(project_kernel, parts), in_specs=[pl.Blo...  1.78 us
    pallas_call x1, Pallas kernels, finish_call(): pl.pallas_call(functools.partial(finish_kernel, float(total_rows) ** 0.5,...  1.18 us
  transfers between devices with their start and end apart: 13, of which 7 were waited for; matrix products, arithmetic and copies ran while one was open for 0% of the time, Pallas kernels for 15%

profile of v17, /device:TPU:0, one launch (start us, length us, event | category | flops | bytes accessed | tf_op | source)
XLA Modules:
  0.0 37.5 jit_solution(2534286567758728353)
XLA Ops:
  0.6 5.8 %sketch_rows.1 = (bf16[576,4096]{1,0:T(8,128)(2,1)S(1)}, f32[576,128]{1,0:T(8,128)S(1)}, f32[72,128]{1,0:T(8,128)S(1)}, bf16[256,576]{1,0:T(8,128)(2,1)S(1)}, f32[8,128,128]{2,1,0:T(8,128)S(1)}) custom-call(s32[1]{0:T(128)} %bitcast.owner_ref, bf16[576,4096]{1,0:T(8,128)(2,1)} %slab_hbm.1, bf16[4096,128]{1,0:T(8,128)(2,1)} %sketch_hbm.1), custom_call_target="tpu_custom_call" | custom-call | flops 905969664 | bytes 4718592 | tf_op jit(solution)/shard_map/sketch_rows/pallas_call | solution.py:132
  6.4 0.5 %collective-permute-start = (f32[8,128,128]{2,1,0:T(8,128)S(1)}, f32[8,128,128]{2,1,0:T(8,128)S(1)}, u32[]{:S(2)}, u32[]{:S(2)}) collective-permute-start(f32[8,128,128]{2,1,0:T(8,128)S(1)} %get-tuple-element.23), channel_id=1, source_target_pairs={{0,1},{1,0},{2,3},{3,2},{4,5},{5,4},{6,7},{7,6},{8,9},{9,8},{10,11... | collective-permute-start | bytes 1572872 | tf_op jit(solution)/shard_map/ppermute | solution.py:293
  6.9 0.1 collective-permute-start.1
  7.0 0.7 %project_first.1 = f32[8,128,128]{2,1,0:T(8,128)S(1)} custom-call(s32[1]{0:T(128)} %bitcast.owner_ref, bf16[256,576]{1,0:T(8,128)(2,1)S(1)} %get-tuple-element.26.split_ref, bf16[576,4096]{1,0:T(8,128)(2,1)S(1)} %get-tuple-element.22.slab_ref), custom_call_target="tpu_custom_call" | custom-call | flops 301989888 | bytes 2359296 | tf_op jit(solution)/shard_map/project_first/pallas_call | solution.py:114
  7.7 0.8 %collective-permute-done.1 = f32[72,128]{1,0:T(8,128)S(1)} collective-permute-done((f32[72,128]{1,0:T(8,128)S(1)}, f32[72,128]{1,0:T(8,128)S(1)}, u32[]{:S(2)}, u32[]{:S(2)}) %collective-permute-start.1) | collective-permute-done | bytes 36896 | tf_op jit(solution)/shard_map/ppermute | solution.py:293
  8.5 0.1 add.35
  8.6 2.9 %collective-permute-start.3 = (f32[8,128,128]{2,1,0:T(8,128)S(1)}, f32[8,128,128]{2,1,0:T(8,128)S(1)}, u32[]{:S(2)}, u32[]{:S(2)}) collective-permute-start(f32[8,128,128]{2,1,0:T(8,128)S(1)} %add.35), channel_id=1, source_target_pairs={{0,2},{1,5},{2,0},{3,7},{4,6},{5,1},{6,4},{7,3},{8,10},{9,13},{10,... | collective-permute-start | bytes 1572872 | tf_op jit(solution)/shard_map/ppermute | solution.py:293
  11.5 1.1 %project_rest.1 = (f32[8,128,128]{2,1,0:T(8,128)S(1)}, f32[8,128,128]{2,1,0:T(8,128)S(1)}) custom-call(s32[1]{0:T(128)} %bitcast.owner_ref, bf16[256,576]{1,0:T(8,128)(2,1)S(1)} %get-tuple-element.26.split_ref, bf16[576,4096]{1,0:T(8,128)(2,1)S(1)} %get-tuple-element.22.slab_ref), custom_call_target="tpu_custom_call" | custom-call | flops 603979776 | bytes 2359296 | tf_op jit(solution)/shard_map/project_rest/pallas_call | solution.py:114
  12.7 3.7 %collective-permute-start.4 = (f32[72,128]{1,0:T(8,128)S(1)}, f32[72,128]{1,0:T(8,128)S(1)}, u32[]{:S(2)}, u32[]{:S(2)}) collective-permute-start(f32[72,128]{1,0:T(8,128)S(1)} %add.34), channel_id=1, source_target_pairs={{0,24},{1,25},{2,26},{3,27},{4,28},{5,29},{6,30},{7,31},{8,16},{9,... | collective-permute-start | bytes 110600 | tf_op jit(solution)/shard_map/ppermute | solution.py:293
  16.4 0.8 %collective-permute-start.6 = (f32[72,128]{1,0:T(8,128)S(1)}, f32[72,128]{1,0:T(8,128)S(1)}, u32[]{:S(2)}, u32[]{:S(2)}) collective-permute-start(f32[72,128]{1,0:T(8,128)S(1)} %add.34), channel_id=1, source_target_pairs={{0,8},{1,9},{2,10},{3,11},{4,12},{5,13},{6,14},{7,15},{8,0},{9,1},... | collective-permute-start | bytes 110600 | tf_op jit(solution)/shard_map/ppermute | solution.py:293
  17.2 1.4 %collective-permute-done.4 = f32[72,128]{1,0:T(8,128)S(1)} collective-permute-done((f32[72,128]{1,0:T(8,128)S(1)}, f32[72,128]{1,0:T(8,128)S(1)}, u32[]{:S(2)}, u32[]{:S(2)}) %collective-permute-start.4) | collective-permute-done | bytes 36896 | tf_op jit(solution)/shard_map/ppermute | solution.py:293
  18.5 0.2 collective-permute-done.3
  18.7 0.1 add_add_fusion
  18.8 2.1 %collective-permute-start.5 = (f32[4,128,128]{2,1,0:T(8,128)S(1)}, f32[4,128,128]{2,1,0:T(8,128)S(1)}, u32[]{:S(2)}, u32[]{:S(2)}) collective-permute-start(f32[4,128,128]{2,1,0:T(8,128)S(1)} %slice.19), channel_id=1, source_target_pairs={{0,4},{1,3},{2,6},{3,1},{4,0},{5,7},{6,2},{7,5},{8,12},{9,11},{10,... | collective-permute-start | bytes 786440 | tf_op jit(solution)/shard_map/ppermute | solution.py:293
  20.9 0.3 collective-permute-done.7
  21.3 1.4 %collective-permute-start.8 = (f32[72,128]{1,0:T(8,128)S(1)}, f32[72,128]{1,0:T(8,128)S(1)}, u32[]{:S(2)}, u32[]{:S(2)}) collective-permute-start(f32[72,128]{1,0:T(8,128)S(1)} %add_add_fusion.1), channel_id=1, source_target_pairs={{0,2},{1,5},{2,0},{3,7},{4,6},{5,1},{6,4},{7,3},{8,10},{9,13},{10,... | collective-permute-start | bytes 110600 | tf_op jit(solution)/shard_map/ppermute | solution.py:293
  22.6 2.7 %collective-permute-done.8 = f32[72,128]{1,0:T(8,128)S(1)} collective-permute-done((f32[72,128]{1,0:T(8,128)S(1)}, f32[72,128]{1,0:T(8,128)S(1)}, u32[]{:S(2)}, u32[]{:S(2)}) %collective-permute-start.8) | collective-permute-done | bytes 36896 | tf_op jit(solution)/shard_map/ppermute | solution.py:293
  25.3 0.4 %collective-permute-done.5 = f32[4,128,128]{2,1,0:T(8,128)S(1)} collective-permute-done((f32[4,128,128]{2,1,0:T(8,128)S(1)}, f32[4,128,128]{2,1,0:T(8,128)S(1)}, u32[]{:S(2)}, u32[]{:S(2)}) %collective-permute-start.5) | collective-permute-done | bytes 262176 | tf_op jit(solution)/shard_map/ppermute | solution.py:293
  25.7 2.1 %collective-permute-start.9 = (f32[72,128]{1,0:T(8,128)S(1)}, f32[72,128]{1,0:T(8,128)S(1)}, u32[]{:S(2)}, u32[]{:S(2)}) collective-permute-start(f32[72,128]{1,0:T(8,128)S(1)} %add.41), channel_id=1, source_target_pairs={{0,4},{1,3},{2,6},{3,1},{4,0},{5,7},{6,2},{7,5},{8,12},{9,11},{10,... | collective-permute-start | bytes 110600 | tf_op jit(solution)/shard_map/ppermute | solution.py:293
  27.8 3.3 %collective-permute-start.12 = (f32[128,128]{1,0:T(8,128)S(1)}, f32[128,128]{1,0:T(8,128)S(1)}, u32[]{:S(2)}, u32[]{:S(2)}) collective-permute-start(f32[128,128]{1,0:T(8,128)S(1)} %get-tuple-element.40), channel_id=1, source_target_pairs={{0,24},{1,25},{2,26},{3,27},{4,28},{5,29},{6,30},{7,31},{8,16},{9,... | collective-permute-start | bytes 196616 | tf_op jit(solution)/shard_map/ppermute | solution.py:293
  31.1 1.2 %collective-permute-start.10 = (f32[128,128]{1,0:T(8,128)S(1)}, f32[128,128]{1,0:T(8,128)S(1)}, u32[]{:S(2)}, u32[]{:S(2)}) collective-permute-start(f32[128,128]{1,0:T(8,128)S(1)} %get-tuple-element.42), channel_id=1, source_target_pairs={{0,8},{1,9},{2,10},{3,11},{4,12},{5,13},{6,14},{7,15},{8,0},{9,1},... | collective-permute-start | bytes 196616 | tf_op jit(solution)/shard_map/ppermute | solution.py:293
  32.3 3.8 %factor.1.inverse_ref = f32[128,128]{1,0:T(8,128)S(1)} custom-call(f32[72,128]{1,0:T(8,128)S(1)} %add.43.gram_ref), custom_call_target="tpu_custom_call" | custom-call | flops 4000000000 | bytes 73728 | tf_op jit(solution)/shard_map/factor/pallas_call | solution.py:225
  36.1 0.2 collective-permute-done.11.refs_1_
  36.3 1.2 %finish.1 = (f32[576,128]{1,0:T(8,128)}, bf16[128,128]{1,0:T(8,128)(2,1)}) custom-call(f32[128,128]{1,0:T(8,128)S(1)} %factor.1.inverse_ref, f32[576,128]{1,0:T(8,128)S(1)} %get-tuple-element.38.first_ref, f32[128,128]{1,0:T(8,128)S(1)} %slice_bitcast_fusion.3.sums_ref, f32[128,128]{1,0:T(8,128)S(1)} %collective-permute-done.10.refs_0_, ...), custom_call_target="tpu_custom_call" | custom-call | flops 113246208 | bytes 589824 | tf_op jit(solution)/shard_map/finish/pallas_call | solution.py:263
  (17 shorter events, 0.2 us)
Async XLA Ops:
  6.4 2.1 %collective-permute-start = (f32[8,128,128]{2,1,0:T(8,128)S(1)}, f32[8,128,128]{2,1,0:T(8,128)S(1)}, u32[]{:S(2)}, u32[]{:S(2)}) collective-permute-start(f32[8,128,128]{2,1,0:T(8,128)S(1)} %get-tuple-element.23), channel_id=1, source_target_pairs={{0,1},{1,0},{2,3},{3,2},{4,5},{5,4},{6,7},{7,6},{8,9},{9,8},{10,11... | collective-permute-start | bytes 1572872 | tf_op jit(solution)/shard_map/ppermute | solution.py:293
  6.9 1.6 %collective-permute-start.1 = (f32[72,128]{1,0:T(8,128)S(1)}, f32[72,128]{1,0:T(8,128)S(1)}, u32[]{:S(2)}, u32[]{:S(2)}) collective-permute-start(f32[72,128]{1,0:T(8,128)S(1)} %get-tuple-element.24), channel_id=1, source_target_pairs={{0,1},{1,0},{2,3},{3,2},{4,5},{5,4},{6,7},{7,6},{8,9},{9,8},{10,11... | collective-permute-start | bytes 110600 | tf_op jit(solution)/shard_map/ppermute | solution.py:293
  8.6 10.1 %collective-permute-start.3 = (f32[8,128,128]{2,1,0:T(8,128)S(1)}, f32[8,128,128]{2,1,0:T(8,128)S(1)}, u32[]{:S(2)}, u32[]{:S(2)}) collective-permute-start(f32[8,128,128]{2,1,0:T(8,128)S(1)} %add.35), channel_id=1, source_target_pairs={{0,2},{1,5},{2,0},{3,7},{4,6},{5,1},{6,4},{7,3},{8,10},{9,13},{10,... | collective-permute-start | bytes 1572872 | tf_op jit(solution)/shard_map/ppermute | solution.py:293
  12.6 6.1 %collective-permute-start.2 = (f32[8,128,128]{2,1,0:T(8,128)S(1)}, f32[8,128,128]{2,1,0:T(8,128)S(1)}, u32[]{:S(2)}, u32[]{:S(2)}) collective-permute-start(f32[8,128,128]{2,1,0:T(8,128)S(1)} %get-tuple-element.28), channel_id=1, source_target_pairs={{0,1},{1,0},{2,3},{3,2},{4,5},{5,4},{6,7},{7,6},{8,9},{9,8},{10,11... | collective-permute-start | bytes 1572872 | tf_op jit(solution)/shard_map/ppermute | solution.py:293
  12.7 5.8 %collective-permute-start.4 = (f32[72,128]{1,0:T(8,128)S(1)}, f32[72,128]{1,0:T(8,128)S(1)}, u32[]{:S(2)}, u32[]{:S(2)}) collective-permute-start(f32[72,128]{1,0:T(8,128)S(1)} %add.34), channel_id=1, source_target_pairs={{0,24},{1,25},{2,26},{3,27},{4,28},{5,29},{6,30},{7,31},{8,16},{9,... | collective-permute-start | bytes 110600 | tf_op jit(solution)/shard_map/ppermute | solution.py:293
  16.4 4.9 %collective-permute-start.7 = (f32[72,128]{1,0:T(8,128)S(1)}, f32[72,128]{1,0:T(8,128)S(1)}, u32[]{:S(2)}, u32[]{:S(2)}) collective-permute-start(f32[72,128]{1,0:T(8,128)S(1)} %add.34), channel_id=1, source_target_pairs={{0,16},{1,17},{2,18},{3,19},{4,20},{5,21},{6,22},{7,23},{8,24},{9,... | collective-permute-start | bytes 110600 | tf_op jit(solution)/shard_map/ppermute | solution.py:293
  16.4 4.9 %collective-permute-start.6 = (f32[72,128]{1,0:T(8,128)S(1)}, f32[72,128]{1,0:T(8,128)S(1)}, u32[]{:S(2)}, u32[]{:S(2)}) collective-permute-start(f32[72,128]{1,0:T(8,128)S(1)} %add.34), channel_id=1, source_target_pairs={{0,8},{1,9},{2,10},{3,11},{4,12},{5,13},{6,14},{7,15},{8,0},{9,1},... | collective-permute-start | bytes 110600 | tf_op jit(solution)/shard_map/ppermute | solution.py:293
  18.8 6.9 %collective-permute-start.5 = (f32[4,128,128]{2,1,0:T(8,128)S(1)}, f32[4,128,128]{2,1,0:T(8,128)S(1)}, u32[]{:S(2)}, u32[]{:S(2)}) collective-permute-start(f32[4,128,128]{2,1,0:T(8,128)S(1)} %slice.19), channel_id=1, source_target_pairs={{0,4},{1,3},{2,6},{3,1},{4,0},{5,7},{6,2},{7,5},{8,12},{9,11},{10,... | collective-permute-start | bytes 786440 | tf_op jit(solution)/shard_map/ppermute | solution.py:293
  21.3 4.0 %collective-permute-start.8 = (f32[72,128]{1,0:T(8,128)S(1)}, f32[72,128]{1,0:T(8,128)S(1)}, u32[]{:S(2)}, u32[]{:S(2)}) collective-permute-start(f32[72,128]{1,0:T(8,128)S(1)} %add_add_fusion.1), channel_id=1, source_target_pairs={{0,2},{1,5},{2,0},{3,7},{4,6},{5,1},{6,4},{7,3},{8,10},{9,13},{10,... | collective-permute-start | bytes 110600 | tf_op jit(solution)/shard_map/ppermute | solution.py:293
  25.7 6.6 %collective-permute-start.9 = (f32[72,128]{1,0:T(8,128)S(1)}, f32[72,128]{1,0:T(8,128)S(1)}, u32[]{:S(2)}, u32[]{:S(2)}) collective-permute-start(f32[72,128]{1,0:T(8,128)S(1)} %add.41), channel_id=1, source_target_pairs={{0,4},{1,3},{2,6},{3,1},{4,0},{5,7},{6,2},{7,5},{8,12},{9,11},{10,... | collective-permute-start | bytes 110600 | tf_op jit(solution)/shard_map/ppermute | solution.py:293
  27.8 8.3 %collective-permute-start.12 = (f32[128,128]{1,0:T(8,128)S(1)}, f32[128,128]{1,0:T(8,128)S(1)}, u32[]{:S(2)}, u32[]{:S(2)}) collective-permute-start(f32[128,128]{1,0:T(8,128)S(1)} %get-tuple-element.40), channel_id=1, source_target_pairs={{0,24},{1,25},{2,26},{3,27},{4,28},{5,29},{6,30},{7,31},{8,16},{9,... | collective-permute-start | bytes 196616 | tf_op jit(solution)/shard_map/ppermute | solution.py:293
  31.1 5.2 %collective-permute-start.11 = (f32[128,128]{1,0:T(8,128)S(1)}, f32[128,128]{1,0:T(8,128)S(1)}, u32[]{:S(2)}, u32[]{:S(2)}) collective-permute-start(f32[128,128]{1,0:T(8,128)S(1)} %get-tuple-element.41), channel_id=1, source_target_pairs={{0,16},{1,17},{2,18},{3,19},{4,20},{5,21},{6,22},{7,23},{8,24},{9,... | collective-permute-start | bytes 196616 | tf_op jit(solution)/shard_map/ppermute | solution.py:293
  31.1 5.2 %collective-permute-start.10 = (f32[128,128]{1,0:T(8,128)S(1)}, f32[128,128]{1,0:T(8,128)S(1)}, u32[]{:S(2)}, u32[]{:S(2)}) collective-permute-start(f32[128,128]{1,0:T(8,128)S(1)} %get-tuple-element.42), channel_id=1, source_target_pairs={{0,8},{1,9},{2,10},{3,11},{4,12},{5,13},{6,14},{7,15},{8,0},{9,1},... | collective-permute-start | bytes 196616 | tf_op jit(solution)/shard_map/ppermute | solution.py:293

commit v18 on v14

--- a/solution.py
+++ b/solution.py
@@ -11,7 +11,7 @@
 HIGHEST = lax.Precision.HIGHEST
 LANES = 128
 VMEM_LIMIT = 24 * 1024 * 1024
-AHEAD = 1
+AHEAD = 2
 ROWS = 256
 
 

time: 37.5 us -> 36.8 us (0.981)
  Pallas kernels: 12.4 us -> 11.7 us
    pallas_call x1, Pallas kernels: 5.64 us -> 4.99 us  [rows_call(): pl.pallas_call(rows_kernel, in_specs=[pl.BlockSpec(memory_space=pltpu.SME...]
where the time goes in v18:
time: 36.8 us; the launch traced here: 36.7 us
  starting transfers between devices  18.1 us (49%)
  Pallas kernels  11.7 us (32%)
  waiting for transfers between devices  5.9 us (16%)
  between operations  0.73 us (2%)
    ppermute x13, starting transfers between devices, exchange(): return lax.ppermute(array, AXES, pairs)  18.1 us
    ppermute x13, waiting for transfers between devices, exchange(): return lax.ppermute(array, AXES, pairs)  5.9 us
    pallas_call x1, Pallas kernels, rows_call(): pl.pallas_call(rows_kernel, in_specs=[pl.BlockSpec(memory_space=pltpu.SME...  4.99 us
    pallas_call x1, Pallas kernels, factor_call(): pl.pallas_call(factor_kernel, in_specs=[pl.BlockSpec(memory_space=pltpu.V...  3.78 us
    pallas_call x2, Pallas kernels, project_call(): pl.pallas_call(functools.partial(project_kernel, parts), in_specs=[pl.Blo...  1.77 us
    pallas_call x1, Pallas kernels, finish_call(): pl.pallas_call(functools.partial(finish_kernel, float(total_rows) ** 0.5,...  1.18 us
  transfers between devices with their start and end apart: 13, of which 7 were waited for; matrix products, arithmetic and copies ran while one was open for 0% of the time, Pallas kernels for 15%

profile of v18, /device:TPU:0, one launch (start us, length us, event | category | flops | bytes accessed | tf_op | source)
XLA Modules:
  0.0 36.7 jit_solution(17447746071462532498)
XLA Ops:
  0.6 5.0 %sketch_rows.1 = (bf16[576,4096]{1,0:T(8,128)(2,1)S(1)}, f32[576,128]{1,0:T(8,128)S(1)}, f32[72,128]{1,0:T(8,128)S(1)}, bf16[256,576]{1,0:T(8,128)(2,1)S(1)}, f32[8,128,128]{2,1,0:T(8,128)S(1)}) custom-call(s32[1]{0:T(128)} %bitcast.owner_ref, bf16[576,4096]{1,0:T(8,128)(2,1)} %slab_hbm.1, bf16[4096,128]{1,0:T(8,128)(2,1)} %sketch_hbm.1), custom_call_target="tpu_custom_call" | custom-call | flops 905969664 | bytes 4718592 | tf_op jit(solution)/shard_map/sketch_rows/pallas_call | solution.py:134
  5.6 0.5 %collective-permute-start = (f32[8,128,128]{2,1,0:T(8,128)S(1)}, f32[8,128,128]{2,1,0:T(8,128)S(1)}, u32[]{:S(2)}, u32[]{:S(2)}) collective-permute-start(f32[8,128,128]{2,1,0:T(8,128)S(1)} %get-tuple-element.23), channel_id=1, source_target_pairs={{0,1},{1,0},{2,3},{3,2},{4,5},{5,4},{6,7},{7,6},{8,9},{9,8},{10,11... | collective-permute-start | bytes 1572872 | tf_op jit(solution)/shard_map/ppermute | solution.py:296
  6.2 0.1 collective-permute-start.1
  6.2 0.7 %project_first.1 = f32[8,128,128]{2,1,0:T(8,128)S(1)} custom-call(s32[1]{0:T(128)} %bitcast.owner_ref, bf16[256,576]{1,0:T(8,128)(2,1)S(1)} %get-tuple-element.26.split_ref, bf16[576,4096]{1,0:T(8,128)(2,1)S(1)} %get-tuple-element.22.slab_ref), custom_call_target="tpu_custom_call" | custom-call | flops 301989888 | bytes 2359296 | tf_op jit(solution)/shard_map/project_first/pallas_call | solution.py:116
  6.9 0.8 %collective-permute-done.1 = f32[72,128]{1,0:T(8,128)S(1)} collective-permute-done((f32[72,128]{1,0:T(8,128)S(1)}, f32[72,128]{1,0:T(8,128)S(1)}, u32[]{:S(2)}, u32[]{:S(2)}) %collective-permute-start.1) | collective-permute-done | bytes 36896 | tf_op jit(solution)/shard_map/ppermute | solution.py:296
  7.8 0.1 add.35
  7.8 2.9 %collective-permute-start.3 = (f32[8,128,128]{2,1,0:T(8,128)S(1)}, f32[8,128,128]{2,1,0:T(8,128)S(1)}, u32[]{:S(2)}, u32[]{:S(2)}) collective-permute-start(f32[8,128,128]{2,1,0:T(8,128)S(1)} %add.35), channel_id=1, source_target_pairs={{0,2},{1,5},{2,0},{3,7},{4,6},{5,1},{6,4},{7,3},{8,10},{9,13},{10,... | collective-permute-start | bytes 1572872 | tf_op jit(solution)/shard_map/ppermute | solution.py:296
  10.8 1.1 %project_rest.1 = (f32[8,128,128]{2,1,0:T(8,128)S(1)}, f32[8,128,128]{2,1,0:T(8,128)S(1)}) custom-call(s32[1]{0:T(128)} %bitcast.owner_ref, bf16[256,576]{1,0:T(8,128)(2,1)S(1)} %get-tuple-element.26.split_ref, bf16[576,4096]{1,0:T(8,128)(2,1)S(1)} %get-tuple-element.22.slab_ref), custom_call_target="tpu_custom_call" | custom-call | flops 603979776 | bytes 2359296 | tf_op jit(solution)/shard_map/project_rest/pallas_call | solution.py:116
  11.9 3.7 %collective-permute-start.4 = (f32[72,128]{1,0:T(8,128)S(1)}, f32[72,128]{1,0:T(8,128)S(1)}, u32[]{:S(2)}, u32[]{:S(2)}) collective-permute-start(f32[72,128]{1,0:T(8,128)S(1)} %add.34), channel_id=1, source_target_pairs={{0,24},{1,25},{2,26},{3,27},{4,28},{5,29},{6,30},{7,31},{8,16},{9,... | collective-permute-start | bytes 110600 | tf_op jit(solution)/shard_map/ppermute | solution.py:296
  15.6 0.8 %collective-permute-start.6 = (f32[72,128]{1,0:T(8,128)S(1)}, f32[72,128]{1,0:T(8,128)S(1)}, u32[]{:S(2)}, u32[]{:S(2)}) collective-permute-start(f32[72,128]{1,0:T(8,128)S(1)} %add.34), channel_id=1, source_target_pairs={{0,8},{1,9},{2,10},{3,11},{4,12},{5,13},{6,14},{7,15},{8,0},{9,1},... | collective-permute-start | bytes 110600 | tf_op jit(solution)/shard_map/ppermute | solution.py:296
  16.4 1.4 %collective-permute-done.4 = f32[72,128]{1,0:T(8,128)S(1)} collective-permute-done((f32[72,128]{1,0:T(8,128)S(1)}, f32[72,128]{1,0:T(8,128)S(1)}, u32[]{:S(2)}, u32[]{:S(2)}) %collective-permute-start.4) | collective-permute-done | bytes 36896 | tf_op jit(solution)/shard_map/ppermute | solution.py:296
  17.8 0.2 collective-permute-done.3
  17.9 0.1 add_add_fusion
  18.1 2.1 %collective-permute-start.5 = (f32[4,128,128]{2,1,0:T(8,128)S(1)}, f32[4,128,128]{2,1,0:T(8,128)S(1)}, u32[]{:S(2)}, u32[]{:S(2)}) collective-permute-start(f32[4,128,128]{2,1,0:T(8,128)S(1)} %slice.19), channel_id=1, source_target_pairs={{0,4},{1,3},{2,6},{3,1},{4,0},{5,7},{6,2},{7,5},{8,12},{9,11},{10,... | collective-permute-start | bytes 786440 | tf_op jit(solution)/shard_map/ppermute | solution.py:296
  20.2 0.3 collective-permute-done.7
  20.5 1.4 %collective-permute-start.8 = (f32[72,128]{1,0:T(8,128)S(1)}, f32[72,128]{1,0:T(8,128)S(1)}, u32[]{:S(2)}, u32[]{:S(2)}) collective-permute-start(f32[72,128]{1,0:T(8,128)S(1)} %add_add_fusion.1), channel_id=1, source_target_pairs={{0,2},{1,5},{2,0},{3,7},{4,6},{5,1},{6,4},{7,3},{8,10},{9,13},{10,... | collective-permute-start | bytes 110600 | tf_op jit(solution)/shard_map/ppermute | solution.py:296
  21.9 2.7 %collective-permute-done.8 = f32[72,128]{1,0:T(8,128)S(1)} collective-permute-done((f32[72,128]{1,0:T(8,128)S(1)}, f32[72,128]{1,0:T(8,128)S(1)}, u32[]{:S(2)}, u32[]{:S(2)}) %collective-permute-start.8) | collective-permute-done | bytes 36896 | tf_op jit(solution)/shard_map/ppermute | solution.py:296
  24.5 0.4 %collective-permute-done.5 = f32[4,128,128]{2,1,0:T(8,128)S(1)} collective-permute-done((f32[4,128,128]{2,1,0:T(8,128)S(1)}, f32[4,128,128]{2,1,0:T(8,128)S(1)}, u32[]{:S(2)}, u32[]{:S(2)}) %collective-permute-start.5) | collective-permute-done | bytes 262176 | tf_op jit(solution)/shard_map/ppermute | solution.py:296
  25.0 2.1 %collective-permute-start.9 = (f32[72,128]{1,0:T(8,128)S(1)}, f32[72,128]{1,0:T(8,128)S(1)}, u32[]{:S(2)}, u32[]{:S(2)}) collective-permute-start(f32[72,128]{1,0:T(8,128)S(1)} %add.41), channel_id=1, source_target_pairs={{0,4},{1,3},{2,6},{3,1},{4,0},{5,7},{6,2},{7,5},{8,12},{9,11},{10,... | collective-permute-start | bytes 110600 | tf_op jit(solution)/shard_map/ppermute | solution.py:296
  27.1 3.3 %collective-permute-start.12 = (f32[128,128]{1,0:T(8,128)S(1)}, f32[128,128]{1,0:T(8,128)S(1)}, u32[]{:S(2)}, u32[]{:S(2)}) collective-permute-start(f32[128,128]{1,0:T(8,128)S(1)} %get-tuple-element.40), channel_id=1, source_target_pairs={{0,24},{1,25},{2,26},{3,27},{4,28},{5,29},{6,30},{7,31},{8,16},{9,... | collective-permute-start | bytes 196616 | tf_op jit(solution)/shard_map/ppermute | solution.py:296
  30.3 1.2 %collective-permute-start.10 = (f32[128,128]{1,0:T(8,128)S(1)}, f32[128,128]{1,0:T(8,128)S(1)}, u32[]{:S(2)}, u32[]{:S(2)}) collective-permute-start(f32[128,128]{1,0:T(8,128)S(1)} %get-tuple-element.42), channel_id=1, source_target_pairs={{0,8},{1,9},{2,10},{3,11},{4,12},{5,13},{6,14},{7,15},{8,0},{9,1},... | collective-permute-start | bytes 196616 | tf_op jit(solution)/shard_map/ppermute | solution.py:296
  31.5 3.8 %factor.1.inverse_ref = f32[128,128]{1,0:T(8,128)S(1)} custom-call(f32[72,128]{1,0:T(8,128)S(1)} %add.43.gram_ref), custom_call_target="tpu_custom_call" | custom-call | flops 4000000000 | bytes 73728 | tf_op jit(solution)/shard_map/factor/pallas_call | solution.py:228
  35.3 0.2 collective-permute-done.11.refs_1_
  35.5 1.2 %finish.1 = (f32[576,128]{1,0:T(8,128)}, bf16[128,128]{1,0:T(8,128)(2,1)}) custom-call(f32[128,128]{1,0:T(8,128)S(1)} %factor.1.inverse_ref, f32[576,128]{1,0:T(8,128)S(1)} %get-tuple-element.38.first_ref, f32[128,128]{1,0:T(8,128)S(1)} %slice_bitcast_fusion.3.sums_ref, f32[128,128]{1,0:T(8,128)S(1)} %collective-permute-done.10.refs_0_, ...), custom_call_target="tpu_custom_call" | custom-call | flops 113246208 | bytes 589824 | tf_op jit(solution)/shard_map/finish/pallas_call | solution.py:266
  (17 shorter events, 0.2 us)
Async XLA Ops:
  5.6 2.1 %collective-permute-start = (f32[8,128,128]{2,1,0:T(8,128)S(1)}, f32[8,128,128]{2,1,0:T(8,128)S(1)}, u32[]{:S(2)}, u32[]{:S(2)}) collective-permute-start(f32[8,128,128]{2,1,0:T(8,128)S(1)} %get-tuple-element.23), channel_id=1, source_target_pairs={{0,1},{1,0},{2,3},{3,2},{4,5},{5,4},{6,7},{7,6},{8,9},{9,8},{10,11... | collective-permute-start | bytes 1572872 | tf_op jit(solution)/shard_map/ppermute | solution.py:296
  6.2 1.6 %collective-permute-start.1 = (f32[72,128]{1,0:T(8,128)S(1)}, f32[72,128]{1,0:T(8,128)S(1)}, u32[]{:S(2)}, u32[]{:S(2)}) collective-permute-start(f32[72,128]{1,0:T(8,128)S(1)} %get-tuple-element.24), channel_id=1, source_target_pairs={{0,1},{1,0},{2,3},{3,2},{4,5},{5,4},{6,7},{7,6},{8,9},{9,8},{10,11... | collective-permute-start | bytes 110600 | tf_op jit(solution)/shard_map/ppermute | solution.py:296
  7.8 10.1 %collective-permute-start.3 = (f32[8,128,128]{2,1,0:T(8,128)S(1)}, f32[8,128,128]{2,1,0:T(8,128)S(1)}, u32[]{:S(2)}, u32[]{:S(2)}) collective-permute-start(f32[8,128,128]{2,1,0:T(8,128)S(1)} %add.35), channel_id=1, source_target_pairs={{0,2},{1,5},{2,0},{3,7},{4,6},{5,1},{6,4},{7,3},{8,10},{9,13},{10,... | collective-permute-start | bytes 1572872 | tf_op jit(solution)/shard_map/ppermute | solution.py:296
  11.9 6.1 %collective-permute-start.2 = (f32[8,128,128]{2,1,0:T(8,128)S(1)}, f32[8,128,128]{2,1,0:T(8,128)S(1)}, u32[]{:S(2)}, u32[]{:S(2)}) collective-permute-start(f32[8,128,128]{2,1,0:T(8,128)S(1)} %get-tuple-element.28), channel_id=1, source_target_pairs={{0,1},{1,0},{2,3},{3,2},{4,5},{5,4},{6,7},{7,6},{8,9},{9,8},{10,11... | collective-permute-start | bytes 1572872 | tf_op jit(solution)/shard_map/ppermute | solution.py:296
  11.9 5.8 %collective-permute-start.4 = (f32[72,128]{1,0:T(8,128)S(1)}, f32[72,128]{1,0:T(8,128)S(1)}, u32[]{:S(2)}, u32[]{:S(2)}) collective-permute-start(f32[72,128]{1,0:T(8,128)S(1)} %add.34), channel_id=1, source_target_pairs={{0,24},{1,25},{2,26},{3,27},{4,28},{5,29},{6,30},{7,31},{8,16},{9,... | collective-permute-start | bytes 110600 | tf_op jit(solution)/shard_map/ppermute | solution.py:296
  15.6 4.9 %collective-permute-start.7 = (f32[72,128]{1,0:T(8,128)S(1)}, f32[72,128]{1,0:T(8,128)S(1)}, u32[]{:S(2)}, u32[]{:S(2)}) collective-permute-start(f32[72,128]{1,0:T(8,128)S(1)} %add.34), channel_id=1, source_target_pairs={{0,16},{1,17},{2,18},{3,19},{4,20},{5,21},{6,22},{7,23},{8,24},{9,... | collective-permute-start | bytes 110600 | tf_op jit(solution)/shard_map/ppermute | solution.py:296
  15.6 4.9 %collective-permute-start.6 = (f32[72,128]{1,0:T(8,128)S(1)}, f32[72,128]{1,0:T(8,128)S(1)}, u32[]{:S(2)}, u32[]{:S(2)}) collective-permute-start(f32[72,128]{1,0:T(8,128)S(1)} %add.34), channel_id=1, source_target_pairs={{0,8},{1,9},{2,10},{3,11},{4,12},{5,13},{6,14},{7,15},{8,0},{9,1},... | collective-permute-start | bytes 110600 | tf_op jit(solution)/shard_map/ppermute | solution.py:296
  18.1 6.9 %collective-permute-start.5 = (f32[4,128,128]{2,1,0:T(8,128)S(1)}, f32[4,128,128]{2,1,0:T(8,128)S(1)}, u32[]{:S(2)}, u32[]{:S(2)}) collective-permute-start(f32[4,128,128]{2,1,0:T(8,128)S(1)} %slice.19), channel_id=1, source_target_pairs={{0,4},{1,3},{2,6},{3,1},{4,0},{5,7},{6,2},{7,5},{8,12},{9,11},{10,... | collective-permute-start | bytes 786440 | tf_op jit(solution)/shard_map/ppermute | solution.py:296
  20.5 4.0 %collective-permute-start.8 = (f32[72,128]{1,0:T(8,128)S(1)}, f32[72,128]{1,0:T(8,128)S(1)}, u32[]{:S(2)}, u32[]{:S(2)}) collective-permute-start(f32[72,128]{1,0:T(8,128)S(1)} %add_add_fusion.1), channel_id=1, source_target_pairs={{0,2},{1,5},{2,0},{3,7},{4,6},{5,1},{6,4},{7,3},{8,10},{9,13},{10,... | collective-permute-start | bytes 110600 | tf_op jit(solution)/shard_map/ppermute | solution.py:296
  25.0 6.6 %collective-permute-start.9 = (f32[72,128]{1,0:T(8,128)S(1)}, f32[72,128]{1,0:T(8,128)S(1)}, u32[]{:S(2)}, u32[]{:S(2)}) collective-permute-start(f32[72,128]{1,0:T(8,128)S(1)} %add.41), channel_id=1, source_target_pairs={{0,4},{1,3},{2,6},{3,1},{4,0},{5,7},{6,2},{7,5},{8,12},{9,11},{10,... | collective-permute-start | bytes 110600 | tf_op jit(solution)/shard_map/ppermute | solution.py:296
  27.1 8.3 %collective-permute-start.12 = (f32[128,128]{1,0:T(8,128)S(1)}, f32[128,128]{1,0:T(8,128)S(1)}, u32[]{:S(2)}, u32[]{:S(2)}) collective-permute-start(f32[128,128]{1,0:T(8,128)S(1)} %get-tuple-element.40), channel_id=1, source_target_pairs={{0,24},{1,25},{2,26},{3,27},{4,28},{5,29},{6,30},{7,31},{8,16},{9,... | collective-permute-start | bytes 196616 | tf_op jit(solution)/shard_map/ppermute | solution.py:296
  30.3 5.2 %collective-permute-start.11 = (f32[128,128]{1,0:T(8,128)S(1)}, f32[128,128]{1,0:T(8,128)S(1)}, u32[]{:S(2)}, u32[]{:S(2)}) collective-permute-start(f32[128,128]{1,0:T(8,128)S(1)} %get-tuple-element.41), channel_id=1, source_target_pairs={{0,16},{1,17},{2,18},{3,19},{4,20},{5,21},{6,22},{7,23},{8,24},{9,... | collective-permute-start | bytes 196616 | tf_op jit(solution)/shard_map/ppermute | solution.py:296
  30.3 5.2 %collective-permute-start.10 = (f32[128,128]{1,0:T(8,128)S(1)}, f32[128,128]{1,0:T(8,128)S(1)}, u32[]{:S(2)}, u32[]{:S(2)}) collective-permute-start(f32[128,128]{1,0:T(8,128)S(1)} %get-tuple-element.42), channel_id=1, source_target_pairs={{0,8},{1,9},{2,10},{3,11},{4,12},{5,13},{6,14},{7,15},{8,0},{9,1},... | collective-permute-start | bytes 196616 | tf_op jit(solution)/shard_map/ppermute | solution.py:296

commit v19 on v18

--- a/solution.py
+++ b/solution.py
@@ -220,14 +220,14 @@
             blocks[i] = block
 
 
-def factor_kernel(gram_ref, inverse_ref):
-    inverse_factor(unpack(gram_ref[...]), inverse_ref)
-
-
-def factor_call(gram):
+def factor_kernel(gram_ref, got_ref, inverse_ref):
+    inverse_factor(unpack(gram_ref[...] + got_ref[...]), inverse_ref)
+
+
+def factor_call(gram, got):
     return pl.pallas_call(
         factor_kernel,
-        in_specs=[pl.BlockSpec(memory_space=pltpu.VMEM)],
+        in_specs=[pl.BlockSpec(memory_space=pltpu.VMEM)] * 2,
         out_specs=pl.BlockSpec(memory_space=pltpu.VMEM),
         out_shape=jax.ShapeDtypeStruct((gram.shape[1], gram.shape[1]), jnp.float32),
         compiler_params=pltpu.CompilerParams(vmem_limit_bytes=VMEM_LIMIT),
@@ -235,7 +235,7 @@
             flops=4000000000, bytes_accessed=gram.size * 8, transcendentals=gram.shape[0]
         ),
         name="factor",
-    )(gram)
+    )(gram, got)
 
 
 def two_parts(array):
@@ -310,14 +310,15 @@
     got = exchange(sums[4:], y, x)
     gram = (gram + over_z[2]) + (over_z[1] + over_z[0])
     gram = gram + exchange(gram, x, y)
-    got, gram = tie((got, gram))
-    sums = sums[:4] + got
-    gram = gram + exchange(gram, y, x)
+    got, _ = tie((got, gram))
+    got_gram = exchange(gram, y, x)
+    sums, gram = tie((sums[:4] + got, gram))
     over_z = [exchange(sums[i], away) for i, away in ((1, z), (2, zz), (3, z | zz))]
     for bit in range(low_bits):
-        gram = gram + exchange(gram, 1 << bit)
+        gram = gram + got_gram
+        got_gram = exchange(gram, 1 << bit)
     sums, gram = tie((sums, gram))
-    inverse = factor_call(gram)
+    inverse = factor_call(gram, got_gram)
     sums = [sums[0], *over_z]
     if low_bits > 0:
         sums = sum(sums)

time: 36.8 us -> 35.7 us (0.970)
  starting transfers between devices: 18.1 us -> 17.5 us
  waiting for transfers between devices: 5.9 us -> 5.34 us
    ppermute x13, starting transfers between devices: 18.1 us -> 17.5 us  [exchange(): return lax.ppermute(array, AXES, pairs)]
    ppermute x13, waiting for transfers between devices: 5.9 us -> 5.34 us  [exchange(): return lax.ppermute(array, AXES, pairs)]
  transfers between devices with their start and end apart: 13 -> 13, of which waited for: 7 -> 5; matrix products, arithmetic and copies ran while one was open for 0% -> 1% of each run, Pallas kernels for 15% -> 16%
where the time goes in v19:
time: 35.7 us; the launch traced here: 35.6 us
  starting transfers between devices  17.5 us (49%)
  Pallas kernels  11.7 us (33%)
  waiting for transfers between devices  5.34 us (15%)
  between operations  0.74 us (2%)
    ppermute x13, starting transfers between devices, exchange(): return lax.ppermute(array, AXES, pairs)  17.5 us
    ppermute x13, waiting for transfers between devices, exchange(): return lax.ppermute(array, AXES, pairs)  5.34 us
    pallas_call x1, Pallas kernels, rows_call(): pl.pallas_call(rows_kernel, in_specs=[pl.BlockSpec(memory_space=pltpu.SME...  4.99 us
    pallas_call x1, Pallas kernels, factor_call(): pl.pallas_call(factor_kernel, in_specs=[pl.BlockSpec(memory_space=pltpu.V...  3.78 us
    pallas_call x2, Pallas kernels, project_call(): pl.pallas_call(functools.partial(project_kernel, parts), in_specs=[pl.Blo...  1.77 us
    pallas_call x1, Pallas kernels, finish_call(): pl.pallas_call(functools.partial(finish_kernel, float(total_rows) ** 0.5,...  1.18 us
  transfers between devices with their start and end apart: 13, of which 5 were waited for; matrix products, arithmetic and copies ran while one was open for 1% of the time, Pallas kernels for 16%

profile of v19, /device:TPU:0, one launch (start us, length us, event | category | flops | bytes accessed | tf_op | source)
XLA Modules:
  0.0 35.6 jit_solution(3379689607779137017)
XLA Ops:
  0.6 5.0 %sketch_rows.1 = (bf16[576,4096]{1,0:T(8,128)(2,1)S(1)}, f32[576,128]{1,0:T(8,128)S(1)}, f32[72,128]{1,0:T(8,128)S(1)}, bf16[256,576]{1,0:T(8,128)(2,1)S(1)}, f32[8,128,128]{2,1,0:T(8,128)S(1)}) custom-call(s32[1]{0:T(128)} %bitcast.owner_ref, bf16[576,4096]{1,0:T(8,128)(2,1)} %slab_hbm.1, bf16[4096,128]{1,0:T(8,128)(2,1)} %sketch_hbm.1), custom_call_target="tpu_custom_call" | custom-call | flops 905969664 | bytes 4718592 | tf_op jit(solution)/shard_map/sketch_rows/pallas_call | solution.py:134
  5.6 0.5 %collective-permute-start = (f32[8,128,128]{2,1,0:T(8,128)S(1)}, f32[8,128,128]{2,1,0:T(8,128)S(1)}, u32[]{:S(2)}, u32[]{:S(2)}) collective-permute-start(f32[8,128,128]{2,1,0:T(8,128)S(1)} %get-tuple-element.23), channel_id=1, source_target_pairs={{0,1},{1,0},{2,3},{3,2},{4,5},{5,4},{6,7},{7,6},{8,9},{9,8},{10,11... | collective-permute-start | bytes 1572872 | tf_op jit(solution)/shard_map/ppermute | solution.py:296
  6.2 0.1 collective-permute-start.1
  6.2 0.7 %project_first.1 = f32[8,128,128]{2,1,0:T(8,128)S(1)} custom-call(s32[1]{0:T(128)} %bitcast.owner_ref, bf16[256,576]{1,0:T(8,128)(2,1)S(1)} %get-tuple-element.26.split_ref, bf16[576,4096]{1,0:T(8,128)(2,1)S(1)} %get-tuple-element.22.slab_ref), custom_call_target="tpu_custom_call" | custom-call | flops 301989888 | bytes 2359296 | tf_op jit(solution)/shard_map/project_first/pallas_call | solution.py:116
  6.9 0.8 %collective-permute-done.1 = f32[72,128]{1,0:T(8,128)S(1)} collective-permute-done((f32[72,128]{1,0:T(8,128)S(1)}, f32[72,128]{1,0:T(8,128)S(1)}, u32[]{:S(2)}, u32[]{:S(2)}) %collective-permute-start.1) | collective-permute-done | bytes 36896 | tf_op jit(solution)/shard_map/ppermute | solution.py:296
  7.8 0.0 collective-permute-done
  7.8 0.1 add.32
  7.8 2.9 %collective-permute-start.3 = (f32[8,128,128]{2,1,0:T(8,128)S(1)}, f32[8,128,128]{2,1,0:T(8,128)S(1)}, u32[]{:S(2)}, u32[]{:S(2)}) collective-permute-start(f32[8,128,128]{2,1,0:T(8,128)S(1)} %add.32), channel_id=1, source_target_pairs={{0,2},{1,5},{2,0},{3,7},{4,6},{5,1},{6,4},{7,3},{8,10},{9,13},{10,... | collective-permute-start | bytes 1572872 | tf_op jit(solution)/shard_map/ppermute | solution.py:296
  10.8 1.1 %project_rest.1 = (f32[8,128,128]{2,1,0:T(8,128)S(1)}, f32[8,128,128]{2,1,0:T(8,128)S(1)}) custom-call(s32[1]{0:T(128)} %bitcast.owner_ref, bf16[256,576]{1,0:T(8,128)(2,1)S(1)} %get-tuple-element.26.split_ref, bf16[576,4096]{1,0:T(8,128)(2,1)S(1)} %get-tuple-element.22.slab_ref), custom_call_target="tpu_custom_call" | custom-call | flops 603979776 | bytes 2359296 | tf_op jit(solution)/shard_map/project_rest/pallas_call | solution.py:116
  11.9 0.1 collective-permute-start.2
  11.9 3.7 %collective-permute-start.4 = (f32[72,128]{1,0:T(8,128)S(1)}, f32[72,128]{1,0:T(8,128)S(1)}, u32[]{:S(2)}, u32[]{:S(2)}) collective-permute-start(f32[72,128]{1,0:T(8,128)S(1)} %add.31), channel_id=1, source_target_pairs={{0,24},{1,25},{2,26},{3,27},{4,28},{5,29},{6,30},{7,31},{8,16},{9,... | collective-permute-start | bytes 110600 | tf_op jit(solution)/shard_map/ppermute | solution.py:296
  15.6 0.8 %collective-permute-start.6 = (f32[72,128]{1,0:T(8,128)S(1)}, f32[72,128]{1,0:T(8,128)S(1)}, u32[]{:S(2)}, u32[]{:S(2)}) collective-permute-start(f32[72,128]{1,0:T(8,128)S(1)} %add.31), channel_id=1, source_target_pairs={{0,8},{1,9},{2,10},{3,11},{4,12},{5,13},{6,14},{7,15},{8,0},{9,1},... | collective-permute-start | bytes 110600 | tf_op jit(solution)/shard_map/ppermute | solution.py:296
  16.4 1.4 %collective-permute-done.4 = f32[72,128]{1,0:T(8,128)S(1)} collective-permute-done((f32[72,128]{1,0:T(8,128)S(1)}, f32[72,128]{1,0:T(8,128)S(1)}, u32[]{:S(2)}, u32[]{:S(2)}) %collective-permute-start.4) | collective-permute-done | bytes 36896 | tf_op jit(solution)/shard_map/ppermute | solution.py:296
  17.8 0.2 collective-permute-done.3
  17.9 0.1 add_add_fusion
  18.1 2.1 %collective-permute-start.5 = (f32[4,128,128]{2,1,0:T(8,128)S(1)}, f32[4,128,128]{2,1,0:T(8,128)S(1)}, u32[]{:S(2)}, u32[]{:S(2)}) collective-permute-start(f32[4,128,128]{2,1,0:T(8,128)S(1)} %slice.19), channel_id=1, source_target_pairs={{0,4},{1,3},{2,6},{3,1},{4,0},{5,7},{6,2},{7,5},{8,12},{9,11},{10,... | collective-permute-start | bytes 786440 | tf_op jit(solution)/shard_map/ppermute | solution.py:296
  20.2 0.3 collective-permute-done.7
  20.5 1.4 %collective-permute-start.8 = (f32[72,128]{1,0:T(8,128)S(1)}, f32[72,128]{1,0:T(8,128)S(1)}, u32[]{:S(2)}, u32[]{:S(2)}) collective-permute-start(f32[72,128]{1,0:T(8,128)S(1)} %add_add_fusion.1), channel_id=1, source_target_pairs={{0,2},{1,5},{2,0},{3,7},{4,6},{5,1},{6,4},{7,3},{8,10},{9,13},{10,... | collective-permute-start | bytes 110600 | tf_op jit(solution)/shard_map/ppermute | solution.py:296
  21.9 2.7 %collective-permute-done.8 = f32[72,128]{1,0:T(8,128)S(1)} collective-permute-done((f32[72,128]{1,0:T(8,128)S(1)}, f32[72,128]{1,0:T(8,128)S(1)}, u32[]{:S(2)}, u32[]{:S(2)}) %collective-permute-start.8) | collective-permute-done | bytes 36896 | tf_op jit(solution)/shard_map/ppermute | solution.py:296
  24.5 1.5 %collective-permute-start.9 = (f32[72,128]{1,0:T(8,128)S(1)}, f32[72,128]{1,0:T(8,128)S(1)}, u32[]{:S(2)}, u32[]{:S(2)}) collective-permute-start(f32[72,128]{1,0:T(8,128)S(1)} %add.38.gram_ref), channel_id=1, source_target_pairs={{0,4},{1,3},{2,6},{3,1},{4,0},{5,7},{6,2},{7,5},{8,12},{9,11},{10,... | collective-permute-start | bytes 110600 | tf_op jit(solution)/shard_map/ppermute | solution.py:296
  26.1 2.8 %collective-permute-start.12 = (f32[128,128]{1,0:T(8,128)S(1)}, f32[128,128]{1,0:T(8,128)S(1)}, u32[]{:S(2)}, u32[]{:S(2)}) collective-permute-start(f32[128,128]{1,0:T(8,128)S(1)} %get-tuple-element.40), channel_id=1, source_target_pairs={{0,24},{1,25},{2,26},{3,27},{4,28},{5,29},{6,30},{7,31},{8,16},{9,... | collective-permute-start | bytes 196616 | tf_op jit(solution)/shard_map/ppermute | solution.py:296
  28.9 1.6 %collective-permute-start.10 = (f32[128,128]{1,0:T(8,128)S(1)}, f32[128,128]{1,0:T(8,128)S(1)}, u32[]{:S(2)}, u32[]{:S(2)}) collective-permute-start(f32[128,128]{1,0:T(8,128)S(1)} %get-tuple-element.42), channel_id=1, source_target_pairs={{0,8},{1,9},{2,10},{3,11},{4,12},{5,13},{6,14},{7,15},{8,0},{9,1},... | collective-permute-start | bytes 196616 | tf_op jit(solution)/shard_map/ppermute | solution.py:296
  30.6 3.8 %factor.1.inverse_ref = f32[128,128]{1,0:T(8,128)S(1)} custom-call(f32[72,128]{1,0:T(8,128)S(1)} %add.38.gram_ref, f32[72,128]{1,0:T(8,128)S(1)} %collective-permute-done.9.got_ref), custom_call_target="tpu_custom_call" | custom-call | flops 4000000000 | bytes 73728 | tf_op jit(solution)/shard_map/factor/pallas_call | solution.py:228
  34.4 1.2 %finish.1 = (f32[576,128]{1,0:T(8,128)}, bf16[128,128]{1,0:T(8,128)(2,1)}) custom-call(f32[128,128]{1,0:T(8,128)S(1)} %factor.1.inverse_ref, f32[576,128]{1,0:T(8,128)S(1)} %get-tuple-element.37.first_ref, f32[128,128]{1,0:T(8,128)S(1)} %slice_bitcast_fusion.3.sums_ref, f32[128,128]{1,0:T(8,128)S(1)} %collective-permute-done.10.refs_0_, ...), custom_call_target="tpu_custom_call" | custom-call | flops 113246208 | bytes 589824 | tf_op jit(solution)/shard_map/finish/pallas_call | solution.py:266
  (16 shorter events, 0.1 us)
Async XLA Ops:
  5.6 2.1 %collective-permute-start = (f32[8,128,128]{2,1,0:T(8,128)S(1)}, f32[8,128,128]{2,1,0:T(8,128)S(1)}, u32[]{:S(2)}, u32[]{:S(2)}) collective-permute-start(f32[8,128,128]{2,1,0:T(8,128)S(1)} %get-tuple-element.23), channel_id=1, source_target_pairs={{0,1},{1,0},{2,3},{3,2},{4,5},{5,4},{6,7},{7,6},{8,9},{9,8},{10,11... | collective-permute-start | bytes 1572872 | tf_op jit(solution)/shard_map/ppermute | solution.py:296
  6.2 1.6 %collective-permute-start.1 = (f32[72,128]{1,0:T(8,128)S(1)}, f32[72,128]{1,0:T(8,128)S(1)}, u32[]{:S(2)}, u32[]{:S(2)}) collective-permute-start(f32[72,128]{1,0:T(8,128)S(1)} %get-tuple-element.24), channel_id=1, source_target_pairs={{0,1},{1,0},{2,3},{3,2},{4,5},{5,4},{6,7},{7,6},{8,9},{9,8},{10,11... | collective-permute-start | bytes 110600 | tf_op jit(solution)/shard_map/ppermute | solution.py:296
  7.8 10.1 %collective-permute-start.3 = (f32[8,128,128]{2,1,0:T(8,128)S(1)}, f32[8,128,128]{2,1,0:T(8,128)S(1)}, u32[]{:S(2)}, u32[]{:S(2)}) collective-permute-start(f32[8,128,128]{2,1,0:T(8,128)S(1)} %add.32), channel_id=1, source_target_pairs={{0,2},{1,5},{2,0},{3,7},{4,6},{5,1},{6,4},{7,3},{8,10},{9,13},{10,... | collective-permute-start | bytes 1572872 | tf_op jit(solution)/shard_map/ppermute | solution.py:296
  11.9 6.1 %collective-permute-start.2 = (f32[8,128,128]{2,1,0:T(8,128)S(1)}, f32[8,128,128]{2,1,0:T(8,128)S(1)}, u32[]{:S(2)}, u32[]{:S(2)}) collective-permute-start(f32[8,128,128]{2,1,0:T(8,128)S(1)} %get-tuple-element.28), channel_id=1, source_target_pairs={{0,1},{1,0},{2,3},{3,2},{4,5},{5,4},{6,7},{7,6},{8,9},{9,8},{10,11... | collective-permute-start | bytes 1572872 | tf_op jit(solution)/shard_map/ppermute | solution.py:296
  11.9 5.8 %collective-permute-start.4 = (f32[72,128]{1,0:T(8,128)S(1)}, f32[72,128]{1,0:T(8,128)S(1)}, u32[]{:S(2)}, u32[]{:S(2)}) collective-permute-start(f32[72,128]{1,0:T(8,128)S(1)} %add.31), channel_id=1, source_target_pairs={{0,24},{1,25},{2,26},{3,27},{4,28},{5,29},{6,30},{7,31},{8,16},{9,... | collective-permute-start | bytes 110600 | tf_op jit(solution)/shard_map/ppermute | solution.py:296
  15.6 4.9 %collective-permute-start.7 = (f32[72,128]{1,0:T(8,128)S(1)}, f32[72,128]{1,0:T(8,128)S(1)}, u32[]{:S(2)}, u32[]{:S(2)}) collective-permute-start(f32[72,128]{1,0:T(8,128)S(1)} %add.31), channel_id=1, source_target_pairs={{0,16},{1,17},{2,18},{3,19},{4,20},{5,21},{6,22},{7,23},{8,24},{9,... | collective-permute-start | bytes 110600 | tf_op jit(solution)/shard_map/ppermute | solution.py:296
  15.6 4.9 %collective-permute-start.6 = (f32[72,128]{1,0:T(8,128)S(1)}, f32[72,128]{1,0:T(8,128)S(1)}, u32[]{:S(2)}, u32[]{:S(2)}) collective-permute-start(f32[72,128]{1,0:T(8,128)S(1)} %add.31), channel_id=1, source_target_pairs={{0,8},{1,9},{2,10},{3,11},{4,12},{5,13},{6,14},{7,15},{8,0},{9,1},... | collective-permute-start | bytes 110600 | tf_op jit(solution)/shard_map/ppermute | solution.py:296
  18.1 8.0 %collective-permute-start.5 = (f32[4,128,128]{2,1,0:T(8,128)S(1)}, f32[4,128,128]{2,1,0:T(8,128)S(1)}, u32[]{:S(2)}, u32[]{:S(2)}) collective-permute-start(f32[4,128,128]{2,1,0:T(8,128)S(1)} %slice.19), channel_id=1, source_target_pairs={{0,4},{1,3},{2,6},{3,1},{4,0},{5,7},{6,2},{7,5},{8,12},{9,11},{10,... | collective-permute-start | bytes 786440 | tf_op jit(solution)/shard_map/ppermute | solution.py:296
  20.5 4.0 %collective-permute-start.8 = (f32[72,128]{1,0:T(8,128)S(1)}, f32[72,128]{1,0:T(8,128)S(1)}, u32[]{:S(2)}, u32[]{:S(2)}) collective-permute-start(f32[72,128]{1,0:T(8,128)S(1)} %add_add_fusion.1), channel_id=1, source_target_pairs={{0,2},{1,5},{2,0},{3,7},{4,6},{5,1},{6,4},{7,3},{8,10},{9,13},{10,... | collective-permute-start | bytes 110600 | tf_op jit(solution)/shard_map/ppermute | solution.py:296
  24.5 6.0 %collective-permute-start.9 = (f32[72,128]{1,0:T(8,128)S(1)}, f32[72,128]{1,0:T(8,128)S(1)}, u32[]{:S(2)}, u32[]{:S(2)}) collective-permute-start(f32[72,128]{1,0:T(8,128)S(1)} %add.38.gram_ref), channel_id=1, source_target_pairs={{0,4},{1,3},{2,6},{3,1},{4,0},{5,7},{6,2},{7,5},{8,12},{9,11},{10,... | collective-permute-start | bytes 110600 | tf_op jit(solution)/shard_map/ppermute | solution.py:296
  26.1 8.3 %collective-permute-start.12 = (f32[128,128]{1,0:T(8,128)S(1)}, f32[128,128]{1,0:T(8,128)S(1)}, u32[]{:S(2)}, u32[]{:S(2)}) collective-permute-start(f32[128,128]{1,0:T(8,128)S(1)} %get-tuple-element.40), channel_id=1, source_target_pairs={{0,24},{1,25},{2,26},{3,27},{4,28},{5,29},{6,30},{7,31},{8,16},{9,... | collective-permute-start | bytes 196616 | tf_op jit(solution)/shard_map/ppermute | solution.py:296
  28.9 5.4 %collective-permute-start.11 = (f32[128,128]{1,0:T(8,128)S(1)}, f32[128,128]{1,0:T(8,128)S(1)}, u32[]{:S(2)}, u32[]{:S(2)}) collective-permute-start(f32[128,128]{1,0:T(8,128)S(1)} %get-tuple-element.41), channel_id=1, source_target_pairs={{0,16},{1,17},{2,18},{3,19},{4,20},{5,21},{6,22},{7,23},{8,24},{9,... | collective-permute-start | bytes 196616 | tf_op jit(solution)/shard_map/ppermute | solution.py:296
  28.9 5.5 %collective-permute-start.10 = (f32[128,128]{1,0:T(8,128)S(1)}, f32[128,128]{1,0:T(8,128)S(1)}, u32[]{:S(2)}, u32[]{:S(2)}) collective-permute-start(f32[128,128]{1,0:T(8,128)S(1)} %get-tuple-element.42), channel_id=1, source_target_pairs={{0,8},{1,9},{2,10},{3,11},{4,12},{5,13},{6,14},{7,15},{8,0},{9,1},... | collective-permute-start | bytes 196616 | tf_op jit(solution)/shard_map/ppermute | solution.py:296

commit v20 on v19

--- a/solution.py
+++ b/solution.py
@@ -313,7 +313,7 @@
     got, _ = tie((got, gram))
     got_gram = exchange(gram, y, x)
     sums, gram = tie((sums[:4] + got, gram))
-    over_z = [exchange(sums[i], away) for i, away in ((1, z), (2, zz), (3, z | zz))]
+    over_z = [exchange(sums[i], away) for i, away in ((2, zz), (1, z), (3, z | zz))]
     for bit in range(low_bits):
         gram = gram + got_gram
         got_gram = exchange(gram, 1 << bit)

time: 35.7 us -> 35.7 us (level)
  no operation moved by 1% of the time
where the time goes in v20:
time: 35.7 us; the launch traced here: 35.6 us
  starting transfers between devices  17.5 us (49%)
  Pallas kernels  11.7 us (33%)
  waiting for transfers between devices  5.34 us (15%)
  between operations  0.74 us (2%)
    ppermute x13, starting transfers between devices, exchange(): return lax.ppermute(array, AXES, pairs)  17.5 us
    ppermute x13, waiting for transfers between devices, exchange(): return lax.ppermute(array, AXES, pairs)  5.34 us
    pallas_call x1, Pallas kernels, rows_call(): pl.pallas_call(rows_kernel, in_specs=[pl.BlockSpec(memory_space=pltpu.SME...  4.99 us
    pallas_call x1, Pallas kernels, factor_call(): pl.pallas_call(factor_kernel, in_specs=[pl.BlockSpec(memory_space=pltpu.V...  3.78 us
    pallas_call x2, Pallas kernels, project_call(): pl.pallas_call(functools.partial(project_kernel, parts), in_specs=[pl.Blo...  1.77 us
    pallas_call x1, Pallas kernels, finish_call(): pl.pallas_call(functools.partial(finish_kernel, float(total_rows) ** 0.5,...  1.18 us
  transfers between devices with their start and end apart: 13, of which 5 were waited for; matrix products, arithmetic and copies ran while one was open for 1% of the time, Pallas kernels for 16%

profile of v20, /device:TPU:0, one launch (start us, length us, event | category | flops | bytes accessed | tf_op | source)
XLA Modules:
  0.0 35.6 jit_solution(17918535916901878546)
XLA Ops:
  0.6 5.0 %sketch_rows.1 = (bf16[576,4096]{1,0:T(8,128)(2,1)S(1)}, f32[576,128]{1,0:T(8,128)S(1)}, f32[72,128]{1,0:T(8,128)S(1)}, bf16[256,576]{1,0:T(8,128)(2,1)S(1)}, f32[8,128,128]{2,1,0:T(8,128)S(1)}) custom-call(s32[1]{0:T(128)} %bitcast.owner_ref, bf16[576,4096]{1,0:T(8,128)(2,1)} %slab_hbm.1, bf16[4096,128]{1,0:T(8,128)(2,1)} %sketch_hbm.1), custom_call_target="tpu_custom_call" | custom-call | flops 905969664 | bytes 4718592 | tf_op jit(solution)/shard_map/sketch_rows/pallas_call | solution.py:134
  5.6 0.5 %collective-permute-start = (f32[8,128,128]{2,1,0:T(8,128)S(1)}, f32[8,128,128]{2,1,0:T(8,128)S(1)}, u32[]{:S(2)}, u32[]{:S(2)}) collective-permute-start(f32[8,128,128]{2,1,0:T(8,128)S(1)} %get-tuple-element.23), channel_id=1, source_target_pairs={{0,1},{1,0},{2,3},{3,2},{4,5},{5,4},{6,7},{7,6},{8,9},{9,8},{10,11... | collective-permute-start | bytes 1572872 | tf_op jit(solution)/shard_map/ppermute | solution.py:296
  6.2 0.1 collective-permute-start.1
  6.2 0.7 %project_first.1 = f32[8,128,128]{2,1,0:T(8,128)S(1)} custom-call(s32[1]{0:T(128)} %bitcast.owner_ref, bf16[256,576]{1,0:T(8,128)(2,1)S(1)} %get-tuple-element.26.split_ref, bf16[576,4096]{1,0:T(8,128)(2,1)S(1)} %get-tuple-element.22.slab_ref), custom_call_target="tpu_custom_call" | custom-call | flops 301989888 | bytes 2359296 | tf_op jit(solution)/shard_map/project_first/pallas_call | solution.py:116
  6.9 0.8 %collective-permute-done.1 = f32[72,128]{1,0:T(8,128)S(1)} collective-permute-done((f32[72,128]{1,0:T(8,128)S(1)}, f32[72,128]{1,0:T(8,128)S(1)}, u32[]{:S(2)}, u32[]{:S(2)}) %collective-permute-start.1) | collective-permute-done | bytes 36896 | tf_op jit(solution)/shard_map/ppermute | solution.py:296
  7.8 0.0 collective-permute-done
  7.8 0.1 add.32
  7.8 2.9 %collective-permute-start.3 = (f32[8,128,128]{2,1,0:T(8,128)S(1)}, f32[8,128,128]{2,1,0:T(8,128)S(1)}, u32[]{:S(2)}, u32[]{:S(2)}) collective-permute-start(f32[8,128,128]{2,1,0:T(8,128)S(1)} %add.32), channel_id=1, source_target_pairs={{0,2},{1,5},{2,0},{3,7},{4,6},{5,1},{6,4},{7,3},{8,10},{9,13},{10,... | collective-permute-start | bytes 1572872 | tf_op jit(solution)/shard_map/ppermute | solution.py:296
  10.8 1.1 %project_rest.1 = (f32[8,128,128]{2,1,0:T(8,128)S(1)}, f32[8,128,128]{2,1,0:T(8,128)S(1)}) custom-call(s32[1]{0:T(128)} %bitcast.owner_ref, bf16[256,576]{1,0:T(8,128)(2,1)S(1)} %get-tuple-element.26.split_ref, bf16[576,4096]{1,0:T(8,128)(2,1)S(1)} %get-tuple-element.22.slab_ref), custom_call_target="tpu_custom_call" | custom-call | flops 603979776 | bytes 2359296 | tf_op jit(solution)/shard_map/project_rest/pallas_call | solution.py:116
  11.9 0.1 collective-permute-start.2
  11.9 3.7 %collective-permute-start.4 = (f32[72,128]{1,0:T(8,128)S(1)}, f32[72,128]{1,0:T(8,128)S(1)}, u32[]{:S(2)}, u32[]{:S(2)}) collective-permute-start(f32[72,128]{1,0:T(8,128)S(1)} %add.31), channel_id=1, source_target_pairs={{0,24},{1,25},{2,26},{3,27},{4,28},{5,29},{6,30},{7,31},{8,16},{9,... | collective-permute-start | bytes 110600 | tf_op jit(solution)/shard_map/ppermute | solution.py:296
  15.6 0.8 %collective-permute-start.6 = (f32[72,128]{1,0:T(8,128)S(1)}, f32[72,128]{1,0:T(8,128)S(1)}, u32[]{:S(2)}, u32[]{:S(2)}) collective-permute-start(f32[72,128]{1,0:T(8,128)S(1)} %add.31), channel_id=1, source_target_pairs={{0,8},{1,9},{2,10},{3,11},{4,12},{5,13},{6,14},{7,15},{8,0},{9,1},... | collective-permute-start | bytes 110600 | tf_op jit(solution)/shard_map/ppermute | solution.py:296
  16.4 1.4 %collective-permute-done.4 = f32[72,128]{1,0:T(8,128)S(1)} collective-permute-done((f32[72,128]{1,0:T(8,128)S(1)}, f32[72,128]{1,0:T(8,128)S(1)}, u32[]{:S(2)}, u32[]{:S(2)}) %collective-permute-start.4) | collective-permute-done | bytes 36896 | tf_op jit(solution)/shard_map/ppermute | solution.py:296
  17.8 0.2 collective-permute-done.3
  17.9 0.1 add_add_fusion
  18.1 2.1 %collective-permute-start.5 = (f32[4,128,128]{2,1,0:T(8,128)S(1)}, f32[4,128,128]{2,1,0:T(8,128)S(1)}, u32[]{:S(2)}, u32[]{:S(2)}) collective-permute-start(f32[4,128,128]{2,1,0:T(8,128)S(1)} %slice.19), channel_id=1, source_target_pairs={{0,4},{1,3},{2,6},{3,1},{4,0},{5,7},{6,2},{7,5},{8,12},{9,11},{10,... | collective-permute-start | bytes 786440 | tf_op jit(solution)/shard_map/ppermute | solution.py:296
  20.2 0.3 collective-permute-done.7
  20.5 1.4 %collective-permute-start.8 = (f32[72,128]{1,0:T(8,128)S(1)}, f32[72,128]{1,0:T(8,128)S(1)}, u32[]{:S(2)}, u32[]{:S(2)}) collective-permute-start(f32[72,128]{1,0:T(8,128)S(1)} %add_add_fusion.1), channel_id=1, source_target_pairs={{0,2},{1,5},{2,0},{3,7},{4,6},{5,1},{6,4},{7,3},{8,10},{9,13},{10,... | collective-permute-start | bytes 110600 | tf_op jit(solution)/shard_map/ppermute | solution.py:296
  21.9 2.7 %collective-permute-done.8 = f32[72,128]{1,0:T(8,128)S(1)} collective-permute-done((f32[72,128]{1,0:T(8,128)S(1)}, f32[72,128]{1,0:T(8,128)S(1)}, u32[]{:S(2)}, u32[]{:S(2)}) %collective-permute-start.8) | collective-permute-done | bytes 36896 | tf_op jit(solution)/shard_map/ppermute | solution.py:296
  24.5 1.5 %collective-permute-start.9 = (f32[72,128]{1,0:T(8,128)S(1)}, f32[72,128]{1,0:T(8,128)S(1)}, u32[]{:S(2)}, u32[]{:S(2)}) collective-permute-start(f32[72,128]{1,0:T(8,128)S(1)} %add.38.gram_ref), channel_id=1, source_target_pairs={{0,4},{1,3},{2,6},{3,1},{4,0},{5,7},{6,2},{7,5},{8,12},{9,11},{10,... | collective-permute-start | bytes 110600 | tf_op jit(solution)/shard_map/ppermute | solution.py:296
  26.1 2.8 %collective-permute-start.12 = (f32[128,128]{1,0:T(8,128)S(1)}, f32[128,128]{1,0:T(8,128)S(1)}, u32[]{:S(2)}, u32[]{:S(2)}) collective-permute-start(f32[128,128]{1,0:T(8,128)S(1)} %get-tuple-element.40), channel_id=1, source_target_pairs={{0,24},{1,25},{2,26},{3,27},{4,28},{5,29},{6,30},{7,31},{8,16},{9,... | collective-permute-start | bytes 196616 | tf_op jit(solution)/shard_map/ppermute | solution.py:296
  28.9 1.6 %collective-permute-start.10 = (f32[128,128]{1,0:T(8,128)S(1)}, f32[128,128]{1,0:T(8,128)S(1)}, u32[]{:S(2)}, u32[]{:S(2)}) collective-permute-start(f32[128,128]{1,0:T(8,128)S(1)} %get-tuple-element.42), channel_id=1, source_target_pairs={{0,16},{1,17},{2,18},{3,19},{4,20},{5,21},{6,22},{7,23},{8,24},{9,... | collective-permute-start | bytes 196616 | tf_op jit(solution)/shard_map/ppermute | solution.py:296
  30.6 3.8 %factor.1.inverse_ref = f32[128,128]{1,0:T(8,128)S(1)} custom-call(f32[72,128]{1,0:T(8,128)S(1)} %add.38.gram_ref, f32[72,128]{1,0:T(8,128)S(1)} %collective-permute-done.9.got_ref), custom_call_target="tpu_custom_call" | custom-call | flops 4000000000 | bytes 73728 | tf_op jit(solution)/shard_map/factor/pallas_call | solution.py:228
  34.4 1.2 %finish.1 = (f32[576,128]{1,0:T(8,128)}, bf16[128,128]{1,0:T(8,128)(2,1)}) custom-call(f32[128,128]{1,0:T(8,128)S(1)} %factor.1.inverse_ref, f32[576,128]{1,0:T(8,128)S(1)} %get-tuple-element.37.first_ref, f32[128,128]{1,0:T(8,128)S(1)} %slice_bitcast_fusion.3.sums_ref, f32[128,128]{1,0:T(8,128)S(1)} %collective-permute-done.10.refs_0_, ...), custom_call_target="tpu_custom_call" | custom-call | flops 113246208 | bytes 589824 | tf_op jit(solution)/shard_map/finish/pallas_call | solution.py:266
  (16 shorter events, 0.1 us)
Async XLA Ops:
  5.6 2.1 %collective-permute-start = (f32[8,128,128]{2,1,0:T(8,128)S(1)}, f32[8,128,128]{2,1,0:T(8,128)S(1)}, u32[]{:S(2)}, u32[]{:S(2)}) collective-permute-start(f32[8,128,128]{2,1,0:T(8,128)S(1)} %get-tuple-element.23), channel_id=1, source_target_pairs={{0,1},{1,0},{2,3},{3,2},{4,5},{5,4},{6,7},{7,6},{8,9},{9,8},{10,11... | collective-permute-start | bytes 1572872 | tf_op jit(solution)/shard_map/ppermute | solution.py:296
  6.2 1.6 %collective-permute-start.1 = (f32[72,128]{1,0:T(8,128)S(1)}, f32[72,128]{1,0:T(8,128)S(1)}, u32[]{:S(2)}, u32[]{:S(2)}) collective-permute-start(f32[72,128]{1,0:T(8,128)S(1)} %get-tuple-element.24), channel_id=1, source_target_pairs={{0,1},{1,0},{2,3},{3,2},{4,5},{5,4},{6,7},{7,6},{8,9},{9,8},{10,11... | collective-permute-start | bytes 110600 | tf_op jit(solution)/shard_map/ppermute | solution.py:296
  7.8 10.1 %collective-permute-start.3 = (f32[8,128,128]{2,1,0:T(8,128)S(1)}, f32[8,128,128]{2,1,0:T(8,128)S(1)}, u32[]{:S(2)}, u32[]{:S(2)}) collective-permute-start(f32[8,128,128]{2,1,0:T(8,128)S(1)} %add.32), channel_id=1, source_target_pairs={{0,2},{1,5},{2,0},{3,7},{4,6},{5,1},{6,4},{7,3},{8,10},{9,13},{10,... | collective-permute-start | bytes 1572872 | tf_op jit(solution)/shard_map/ppermute | solution.py:296
  11.9 6.1 %collective-permute-start.2 = (f32[8,128,128]{2,1,0:T(8,128)S(1)}, f32[8,128,128]{2,1,0:T(8,128)S(1)}, u32[]{:S(2)}, u32[]{:S(2)}) collective-permute-start(f32[8,128,128]{2,1,0:T(8,128)S(1)} %get-tuple-element.28), channel_id=1, source_target_pairs={{0,1},{1,0},{2,3},{3,2},{4,5},{5,4},{6,7},{7,6},{8,9},{9,8},{10,11... | collective-permute-start | bytes 1572872 | tf_op jit(solution)/shard_map/ppermute | solution.py:296
  11.9 5.8 %collective-permute-start.4 = (f32[72,128]{1,0:T(8,128)S(1)}, f32[72,128]{1,0:T(8,128)S(1)}, u32[]{:S(2)}, u32[]{:S(2)}) collective-permute-start(f32[72,128]{1,0:T(8,128)S(1)} %add.31), channel_id=1, source_target_pairs={{0,24},{1,25},{2,26},{3,27},{4,28},{5,29},{6,30},{7,31},{8,16},{9,... | collective-permute-start | bytes 110600 | tf_op jit(solution)/shard_map/ppermute | solution.py:296
  15.6 4.9 %collective-permute-start.7 = (f32[72,128]{1,0:T(8,128)S(1)}, f32[72,128]{1,0:T(8,128)S(1)}, u32[]{:S(2)}, u32[]{:S(2)}) collective-permute-start(f32[72,128]{1,0:T(8,128)S(1)} %add.31), channel_id=1, source_target_pairs={{0,16},{1,17},{2,18},{3,19},{4,20},{5,21},{6,22},{7,23},{8,24},{9,... | collective-permute-start | bytes 110600 | tf_op jit(solution)/shard_map/ppermute | solution.py:296
  15.6 4.9 %collective-permute-start.6 = (f32[72,128]{1,0:T(8,128)S(1)}, f32[72,128]{1,0:T(8,128)S(1)}, u32[]{:S(2)}, u32[]{:S(2)}) collective-permute-start(f32[72,128]{1,0:T(8,128)S(1)} %add.31), channel_id=1, source_target_pairs={{0,8},{1,9},{2,10},{3,11},{4,12},{5,13},{6,14},{7,15},{8,0},{9,1},... | collective-permute-start | bytes 110600 | tf_op jit(solution)/shard_map/ppermute | solution.py:296
  18.1 8.0 %collective-permute-start.5 = (f32[4,128,128]{2,1,0:T(8,128)S(1)}, f32[4,128,128]{2,1,0:T(8,128)S(1)}, u32[]{:S(2)}, u32[]{:S(2)}) collective-permute-start(f32[4,128,128]{2,1,0:T(8,128)S(1)} %slice.19), channel_id=1, source_target_pairs={{0,4},{1,3},{2,6},{3,1},{4,0},{5,7},{6,2},{7,5},{8,12},{9,11},{10,... | collective-permute-start | bytes 786440 | tf_op jit(solution)/shard_map/ppermute | solution.py:296
  20.5 4.0 %collective-permute-start.8 = (f32[72,128]{1,0:T(8,128)S(1)}, f32[72,128]{1,0:T(8,128)S(1)}, u32[]{:S(2)}, u32[]{:S(2)}) collective-permute-start(f32[72,128]{1,0:T(8,128)S(1)} %add_add_fusion.1), channel_id=1, source_target_pairs={{0,2},{1,5},{2,0},{3,7},{4,6},{5,1},{6,4},{7,3},{8,10},{9,13},{10,... | collective-permute-start | bytes 110600 | tf_op jit(solution)/shard_map/ppermute | solution.py:296
  24.5 6.0 %collective-permute-start.9 = (f32[72,128]{1,0:T(8,128)S(1)}, f32[72,128]{1,0:T(8,128)S(1)}, u32[]{:S(2)}, u32[]{:S(2)}) collective-permute-start(f32[72,128]{1,0:T(8,128)S(1)} %add.38.gram_ref), channel_id=1, source_target_pairs={{0,4},{1,3},{2,6},{3,1},{4,0},{5,7},{6,2},{7,5},{8,12},{9,11},{10,... | collective-permute-start | bytes 110600 | tf_op jit(solution)/shard_map/ppermute | solution.py:296
  26.1 8.3 %collective-permute-start.12 = (f32[128,128]{1,0:T(8,128)S(1)}, f32[128,128]{1,0:T(8,128)S(1)}, u32[]{:S(2)}, u32[]{:S(2)}) collective-permute-start(f32[128,128]{1,0:T(8,128)S(1)} %get-tuple-element.40), channel_id=1, source_target_pairs={{0,24},{1,25},{2,26},{3,27},{4,28},{5,29},{6,30},{7,31},{8,16},{9,... | collective-permute-start | bytes 196616 | tf_op jit(solution)/shard_map/ppermute | solution.py:296
  28.9 5.4 %collective-permute-start.11 = (f32[128,128]{1,0:T(8,128)S(1)}, f32[128,128]{1,0:T(8,128)S(1)}, u32[]{:S(2)}, u32[]{:S(2)}) collective-permute-start(f32[128,128]{1,0:T(8,128)S(1)} %get-tuple-element.41), channel_id=1, source_target_pairs={{0,8},{1,9},{2,10},{3,11},{4,12},{5,13},{6,14},{7,15},{8,0},{9,1},... | collective-permute-start | bytes 196616 | tf_op jit(solution)/shard_map/ppermute | solution.py:296
  28.9 5.5 %collective-permute-start.10 = (f32[128,128]{1,0:T(8,128)S(1)}, f32[128,128]{1,0:T(8,128)S(1)}, u32[]{:S(2)}, u32[]{:S(2)}) collective-permute-start(f32[128,128]{1,0:T(8,128)S(1)} %get-tuple-element.42), channel_id=1, source_target_pairs={{0,16},{1,17},{2,18},{3,19},{4,20},{5,21},{6,22},{7,23},{8,24},{9,... | collective-permute-start | bytes 196616 | tf_op jit(solution)/shard_map/ppermute | solution.py:296

commit v21 on v19

--- a/solution.py
+++ b/solution.py
@@ -245,19 +245,21 @@
 
 def finish_kernel(basis_factor, factor, inverse_ref, first_ref, sums_ref, *refs):
     basis_ref, out_ref = refs[-2:]
-    inverse = inverse_ref[...]
-    high, low = two_parts(first_ref[...])
-    inverse_high, inverse_low = two_parts(inverse.T * basis_factor)
-    basis_ref[...] = jnp.dot(
-        jnp.concatenate([high, high, low, low], axis=1),
-        jnp.concatenate([inverse_high, inverse_low, inverse_high, inverse_low], axis=0),
-        preferred_element_type=jnp.float32,
-    )
     sums = sums_ref[...]
     for got_ref in refs[:-2]:
         sums = sums + got_ref[...]
-    result = jnp.dot(inverse, sums, precision=HIGHEST, preferred_element_type=jnp.float32)
-    out_ref[...] = (result.T * factor).astype(out_ref.dtype)
+    inverse_high, inverse_low = two_parts(inverse_ref[...].T * basis_factor)
+    factors = jnp.concatenate([inverse_high, inverse_low, inverse_high, inverse_low], axis=0)
+
+    def product(rows):
+        high, low = two_parts(rows)
+        return jnp.dot(
+            jnp.concatenate([high, high, low, low], axis=1), factors,
+            preferred_element_type=jnp.float32,
+        )
+
+    out_ref[...] = (product(sums.T) * (factor / basis_factor)).astype(out_ref.dtype)
+    basis_ref[...] = product(first_ref[...])
 
 
 def finish_call(inverse, first, total_rows, factor, sums):

time: 35.7 us -> 35.7 us (level)
  no operation moved by 1% of the time
where the time goes in v21:
time: 35.7 us; the launch traced here: 35.6 us
  starting transfers between devices  17.5 us (49%)
  Pallas kernels  11.7 us (33%)
  waiting for transfers between devices  5.34 us (15%)
  between operations  0.74 us (2%)
    ppermute x13, starting transfers between devices, exchange(): return lax.ppermute(array, AXES, pairs)  17.5 us
    ppermute x13, waiting for transfers between devices, exchange(): return lax.ppermute(array, AXES, pairs)  5.34 us
    pallas_call x1, Pallas kernels, rows_call(): pl.pallas_call(rows_kernel, in_specs=[pl.BlockSpec(memory_space=pltpu.SME...  4.99 us
    pallas_call x1, Pallas kernels, factor_call(): pl.pallas_call(factor_kernel, in_specs=[pl.BlockSpec(memory_space=pltpu.V...  3.78 us
    pallas_call x2, Pallas kernels, project_call(): pl.pallas_call(functools.partial(project_kernel, parts), in_specs=[pl.Blo...  1.77 us
    pallas_call x1, Pallas kernels, finish_call(): pl.pallas_call(functools.partial(finish_kernel, float(total_rows) ** 0.5,...  1.16 us
  transfers between devices with their start and end apart: 13, of which 5 were waited for; matrix products, arithmetic and copies ran while one was open for 1% of the time, Pallas kernels for 16%

profile of v21, /device:TPU:0, one launch (start us, length us, event | category | flops | bytes accessed | tf_op | source)
XLA Modules:
  0.0 35.6 jit_solution(17303435496404781803)
XLA Ops:
  0.6 5.0 %sketch_rows.1 = (bf16[576,4096]{1,0:T(8,128)(2,1)S(1)}, f32[576,128]{1,0:T(8,128)S(1)}, f32[72,128]{1,0:T(8,128)S(1)}, bf16[256,576]{1,0:T(8,128)(2,1)S(1)}, f32[8,128,128]{2,1,0:T(8,128)S(1)}) custom-call(s32[1]{0:T(128)} %bitcast.owner_ref, bf16[576,4096]{1,0:T(8,128)(2,1)} %slab_hbm.1, bf16[4096,128]{1,0:T(8,128)(2,1)} %sketch_hbm.1), custom_call_target="tpu_custom_call" | custom-call | flops 905969664 | bytes 4718592 | tf_op jit(solution)/shard_map/sketch_rows/pallas_call | solution.py:134
  5.6 0.5 %collective-permute-start = (f32[8,128,128]{2,1,0:T(8,128)S(1)}, f32[8,128,128]{2,1,0:T(8,128)S(1)}, u32[]{:S(2)}, u32[]{:S(2)}) collective-permute-start(f32[8,128,128]{2,1,0:T(8,128)S(1)} %get-tuple-element.23), channel_id=1, source_target_pairs={{0,1},{1,0},{2,3},{3,2},{4,5},{5,4},{6,7},{7,6},{8,9},{9,8},{10,11... | collective-permute-start | bytes 1572872 | tf_op jit(solution)/shard_map/ppermute | solution.py:298
  6.2 0.1 collective-permute-start.1
  6.2 0.7 %project_first.1 = f32[8,128,128]{2,1,0:T(8,128)S(1)} custom-call(s32[1]{0:T(128)} %bitcast.owner_ref, bf16[256,576]{1,0:T(8,128)(2,1)S(1)} %get-tuple-element.26.split_ref, bf16[576,4096]{1,0:T(8,128)(2,1)S(1)} %get-tuple-element.22.slab_ref), custom_call_target="tpu_custom_call" | custom-call | flops 301989888 | bytes 2359296 | tf_op jit(solution)/shard_map/project_first/pallas_call | solution.py:116
  6.9 0.8 %collective-permute-done.1 = f32[72,128]{1,0:T(8,128)S(1)} collective-permute-done((f32[72,128]{1,0:T(8,128)S(1)}, f32[72,128]{1,0:T(8,128)S(1)}, u32[]{:S(2)}, u32[]{:S(2)}) %collective-permute-start.1) | collective-permute-done | bytes 36896 | tf_op jit(solution)/shard_map/ppermute | solution.py:298
  7.8 0.0 collective-permute-done
  7.8 0.1 add.32
  7.8 2.9 %collective-permute-start.3 = (f32[8,128,128]{2,1,0:T(8,128)S(1)}, f32[8,128,128]{2,1,0:T(8,128)S(1)}, u32[]{:S(2)}, u32[]{:S(2)}) collective-permute-start(f32[8,128,128]{2,1,0:T(8,128)S(1)} %add.32), channel_id=1, source_target_pairs={{0,2},{1,5},{2,0},{3,7},{4,6},{5,1},{6,4},{7,3},{8,10},{9,13},{10,... | collective-permute-start | bytes 1572872 | tf_op jit(solution)/shard_map/ppermute | solution.py:298
  10.8 1.1 %project_rest.1 = (f32[8,128,128]{2,1,0:T(8,128)S(1)}, f32[8,128,128]{2,1,0:T(8,128)S(1)}) custom-call(s32[1]{0:T(128)} %bitcast.owner_ref, bf16[256,576]{1,0:T(8,128)(2,1)S(1)} %get-tuple-element.26.split_ref, bf16[576,4096]{1,0:T(8,128)(2,1)S(1)} %get-tuple-element.22.slab_ref), custom_call_target="tpu_custom_call" | custom-call | flops 603979776 | bytes 2359296 | tf_op jit(solution)/shard_map/project_rest/pallas_call | solution.py:116
  11.9 0.1 collective-permute-start.2
  11.9 3.7 %collective-permute-start.4 = (f32[72,128]{1,0:T(8,128)S(1)}, f32[72,128]{1,0:T(8,128)S(1)}, u32[]{:S(2)}, u32[]{:S(2)}) collective-permute-start(f32[72,128]{1,0:T(8,128)S(1)} %add.31), channel_id=1, source_target_pairs={{0,24},{1,25},{2,26},{3,27},{4,28},{5,29},{6,30},{7,31},{8,16},{9,... | collective-permute-start | bytes 110600 | tf_op jit(solution)/shard_map/ppermute | solution.py:298
  15.6 0.8 %collective-permute-start.6 = (f32[72,128]{1,0:T(8,128)S(1)}, f32[72,128]{1,0:T(8,128)S(1)}, u32[]{:S(2)}, u32[]{:S(2)}) collective-permute-start(f32[72,128]{1,0:T(8,128)S(1)} %add.31), channel_id=1, source_target_pairs={{0,8},{1,9},{2,10},{3,11},{4,12},{5,13},{6,14},{7,15},{8,0},{9,1},... | collective-permute-start | bytes 110600 | tf_op jit(solution)/shard_map/ppermute | solution.py:298
  16.4 1.4 %collective-permute-done.4 = f32[72,128]{1,0:T(8,128)S(1)} collective-permute-done((f32[72,128]{1,0:T(8,128)S(1)}, f32[72,128]{1,0:T(8,128)S(1)}, u32[]{:S(2)}, u32[]{:S(2)}) %collective-permute-start.4) | collective-permute-done | bytes 36896 | tf_op jit(solution)/shard_map/ppermute | solution.py:298
  17.8 0.2 collective-permute-done.3
  17.9 0.1 add_add_fusion
  18.1 2.1 %collective-permute-start.5 = (f32[4,128,128]{2,1,0:T(8,128)S(1)}, f32[4,128,128]{2,1,0:T(8,128)S(1)}, u32[]{:S(2)}, u32[]{:S(2)}) collective-permute-start(f32[4,128,128]{2,1,0:T(8,128)S(1)} %slice.19), channel_id=1, source_target_pairs={{0,4},{1,3},{2,6},{3,1},{4,0},{5,7},{6,2},{7,5},{8,12},{9,11},{10,... | collective-permute-start | bytes 786440 | tf_op jit(solution)/shard_map/ppermute | solution.py:298
  20.2 0.3 collective-permute-done.7
  20.5 1.4 %collective-permute-start.8 = (f32[72,128]{1,0:T(8,128)S(1)}, f32[72,128]{1,0:T(8,128)S(1)}, u32[]{:S(2)}, u32[]{:S(2)}) collective-permute-start(f32[72,128]{1,0:T(8,128)S(1)} %add_add_fusion.1), channel_id=1, source_target_pairs={{0,2},{1,5},{2,0},{3,7},{4,6},{5,1},{6,4},{7,3},{8,10},{9,13},{10,... | collective-permute-start | bytes 110600 | tf_op jit(solution)/shard_map/ppermute | solution.py:298
  21.9 2.7 %collective-permute-done.8 = f32[72,128]{1,0:T(8,128)S(1)} collective-permute-done((f32[72,128]{1,0:T(8,128)S(1)}, f32[72,128]{1,0:T(8,128)S(1)}, u32[]{:S(2)}, u32[]{:S(2)}) %collective-permute-start.8) | collective-permute-done | bytes 36896 | tf_op jit(solution)/shard_map/ppermute | solution.py:298
  24.5 1.5 %collective-permute-start.9 = (f32[72,128]{1,0:T(8,128)S(1)}, f32[72,128]{1,0:T(8,128)S(1)}, u32[]{:S(2)}, u32[]{:S(2)}) collective-permute-start(f32[72,128]{1,0:T(8,128)S(1)} %add.38.gram_ref), channel_id=1, source_target_pairs={{0,4},{1,3},{2,6},{3,1},{4,0},{5,7},{6,2},{7,5},{8,12},{9,11},{10,... | collective-permute-start | bytes 110600 | tf_op jit(solution)/shard_map/ppermute | solution.py:298
  26.1 2.8 %collective-permute-start.12 = (f32[128,128]{1,0:T(8,128)S(1)}, f32[128,128]{1,0:T(8,128)S(1)}, u32[]{:S(2)}, u32[]{:S(2)}) collective-permute-start(f32[128,128]{1,0:T(8,128)S(1)} %get-tuple-element.40), channel_id=1, source_target_pairs={{0,24},{1,25},{2,26},{3,27},{4,28},{5,29},{6,30},{7,31},{8,16},{9,... | collective-permute-start | bytes 196616 | tf_op jit(solution)/shard_map/ppermute | solution.py:298
  28.9 1.6 %collective-permute-start.10 = (f32[128,128]{1,0:T(8,128)S(1)}, f32[128,128]{1,0:T(8,128)S(1)}, u32[]{:S(2)}, u32[]{:S(2)}) collective-permute-start(f32[128,128]{1,0:T(8,128)S(1)} %get-tuple-element.42), channel_id=1, source_target_pairs={{0,8},{1,9},{2,10},{3,11},{4,12},{5,13},{6,14},{7,15},{8,0},{9,1},... | collective-permute-start | bytes 196616 | tf_op jit(solution)/shard_map/ppermute | solution.py:298
  30.6 3.8 %factor.1.inverse_ref = f32[128,128]{1,0:T(8,128)S(1)} custom-call(f32[72,128]{1,0:T(8,128)S(1)} %add.38.gram_ref, f32[72,128]{1,0:T(8,128)S(1)} %collective-permute-done.9.got_ref), custom_call_target="tpu_custom_call" | custom-call | flops 4000000000 | bytes 73728 | tf_op jit(solution)/shard_map/factor/pallas_call | solution.py:228
  34.4 1.2 %finish.1 = (f32[576,128]{1,0:T(8,128)}, bf16[128,128]{1,0:T(8,128)(2,1)}) custom-call(f32[128,128]{1,0:T(8,128)S(1)} %factor.1.inverse_ref, f32[576,128]{1,0:T(8,128)S(1)} %get-tuple-element.37.first_ref, f32[128,128]{1,0:T(8,128)S(1)} %slice_bitcast_fusion.3.sums_ref, f32[128,128]{1,0:T(8,128)S(1)} %collective-permute-done.10.refs_0_, ...), custom_call_target="tpu_custom_call" | custom-call | flops 113246208 | bytes 589824 | tf_op jit(solution)/shard_map/finish/pallas_call | solution.py:268
  (16 shorter events, 0.1 us)
Async XLA Ops:
  5.6 2.1 %collective-permute-start = (f32[8,128,128]{2,1,0:T(8,128)S(1)}, f32[8,128,128]{2,1,0:T(8,128)S(1)}, u32[]{:S(2)}, u32[]{:S(2)}) collective-permute-start(f32[8,128,128]{2,1,0:T(8,128)S(1)} %get-tuple-element.23), channel_id=1, source_target_pairs={{0,1},{1,0},{2,3},{3,2},{4,5},{5,4},{6,7},{7,6},{8,9},{9,8},{10,11... | collective-permute-start | bytes 1572872 | tf_op jit(solution)/shard_map/ppermute | solution.py:298
  6.2 1.6 %collective-permute-start.1 = (f32[72,128]{1,0:T(8,128)S(1)}, f32[72,128]{1,0:T(8,128)S(1)}, u32[]{:S(2)}, u32[]{:S(2)}) collective-permute-start(f32[72,128]{1,0:T(8,128)S(1)} %get-tuple-element.24), channel_id=1, source_target_pairs={{0,1},{1,0},{2,3},{3,2},{4,5},{5,4},{6,7},{7,6},{8,9},{9,8},{10,11... | collective-permute-start | bytes 110600 | tf_op jit(solution)/shard_map/ppermute | solution.py:298
  7.8 10.1 %collective-permute-start.3 = (f32[8,128,128]{2,1,0:T(8,128)S(1)}, f32[8,128,128]{2,1,0:T(8,128)S(1)}, u32[]{:S(2)}, u32[]{:S(2)}) collective-permute-start(f32[8,128,128]{2,1,0:T(8,128)S(1)} %add.32), channel_id=1, source_target_pairs={{0,2},{1,5},{2,0},{3,7},{4,6},{5,1},{6,4},{7,3},{8,10},{9,13},{10,... | collective-permute-start | bytes 1572872 | tf_op jit(solution)/shard_map/ppermute | solution.py:298
  11.9 6.1 %collective-permute-start.2 = (f32[8,128,128]{2,1,0:T(8,128)S(1)}, f32[8,128,128]{2,1,0:T(8,128)S(1)}, u32[]{:S(2)}, u32[]{:S(2)}) collective-permute-start(f32[8,128,128]{2,1,0:T(8,128)S(1)} %get-tuple-element.28), channel_id=1, source_target_pairs={{0,1},{1,0},{2,3},{3,2},{4,5},{5,4},{6,7},{7,6},{8,9},{9,8},{10,11... | collective-permute-start | bytes 1572872 | tf_op jit(solution)/shard_map/ppermute | solution.py:298
  11.9 5.8 %collective-permute-start.4 = (f32[72,128]{1,0:T(8,128)S(1)}, f32[72,128]{1,0:T(8,128)S(1)}, u32[]{:S(2)}, u32[]{:S(2)}) collective-permute-start(f32[72,128]{1,0:T(8,128)S(1)} %add.31), channel_id=1, source_target_pairs={{0,24},{1,25},{2,26},{3,27},{4,28},{5,29},{6,30},{7,31},{8,16},{9,... | collective-permute-start | bytes 110600 | tf_op jit(solution)/shard_map/ppermute | solution.py:298
  15.6 4.9 %collective-permute-start.7 = (f32[72,128]{1,0:T(8,128)S(1)}, f32[72,128]{1,0:T(8,128)S(1)}, u32[]{:S(2)}, u32[]{:S(2)}) collective-permute-start(f32[72,128]{1,0:T(8,128)S(1)} %add.31), channel_id=1, source_target_pairs={{0,16},{1,17},{2,18},{3,19},{4,20},{5,21},{6,22},{7,23},{8,24},{9,... | collective-permute-start | bytes 110600 | tf_op jit(solution)/shard_map/ppermute | solution.py:298
  15.6 4.9 %collective-permute-start.6 = (f32[72,128]{1,0:T(8,128)S(1)}, f32[72,128]{1,0:T(8,128)S(1)}, u32[]{:S(2)}, u32[]{:S(2)}) collective-permute-start(f32[72,128]{1,0:T(8,128)S(1)} %add.31), channel_id=1, source_target_pairs={{0,8},{1,9},{2,10},{3,11},{4,12},{5,13},{6,14},{7,15},{8,0},{9,1},... | collective-permute-start | bytes 110600 | tf_op jit(solution)/shard_map/ppermute | solution.py:298
  18.1 8.0 %collective-permute-start.5 = (f32[4,128,128]{2,1,0:T(8,128)S(1)}, f32[4,128,128]{2,1,0:T(8,128)S(1)}, u32[]{:S(2)}, u32[]{:S(2)}) collective-permute-start(f32[4,128,128]{2,1,0:T(8,128)S(1)} %slice.19), channel_id=1, source_target_pairs={{0,4},{1,3},{2,6},{3,1},{4,0},{5,7},{6,2},{7,5},{8,12},{9,11},{10,... | collective-permute-start | bytes 786440 | tf_op jit(solution)/shard_map/ppermute | solution.py:298
  20.5 4.0 %collective-permute-start.8 = (f32[72,128]{1,0:T(8,128)S(1)}, f32[72,128]{1,0:T(8,128)S(1)}, u32[]{:S(2)}, u32[]{:S(2)}) collective-permute-start(f32[72,128]{1,0:T(8,128)S(1)} %add_add_fusion.1), channel_id=1, source_target_pairs={{0,2},{1,5},{2,0},{3,7},{4,6},{5,1},{6,4},{7,3},{8,10},{9,13},{10,... | collective-permute-start | bytes 110600 | tf_op jit(solution)/shard_map/ppermute | solution.py:298
  24.5 6.0 %collective-permute-start.9 = (f32[72,128]{1,0:T(8,128)S(1)}, f32[72,128]{1,0:T(8,128)S(1)}, u32[]{:S(2)}, u32[]{:S(2)}) collective-permute-start(f32[72,128]{1,0:T(8,128)S(1)} %add.38.gram_ref), channel_id=1, source_target_pairs={{0,4},{1,3},{2,6},{3,1},{4,0},{5,7},{6,2},{7,5},{8,12},{9,11},{10,... | collective-permute-start | bytes 110600 | tf_op jit(solution)/shard_map/ppermute | solution.py:298
  26.1 8.3 %collective-permute-start.12 = (f32[128,128]{1,0:T(8,128)S(1)}, f32[128,128]{1,0:T(8,128)S(1)}, u32[]{:S(2)}, u32[]{:S(2)}) collective-permute-start(f32[128,128]{1,0:T(8,128)S(1)} %get-tuple-element.40), channel_id=1, source_target_pairs={{0,24},{1,25},{2,26},{3,27},{4,28},{5,29},{6,30},{7,31},{8,16},{9,... | collective-permute-start | bytes 196616 | tf_op jit(solution)/shard_map/ppermute | solution.py:298
  28.9 5.4 %collective-permute-start.11 = (f32[128,128]{1,0:T(8,128)S(1)}, f32[128,128]{1,0:T(8,128)S(1)}, u32[]{:S(2)}, u32[]{:S(2)}) collective-permute-start(f32[128,128]{1,0:T(8,128)S(1)} %get-tuple-element.41), channel_id=1, source_target_pairs={{0,16},{1,17},{2,18},{3,19},{4,20},{5,21},{6,22},{7,23},{8,24},{9,... | collective-permute-start | bytes 196616 | tf_op jit(solution)/shard_map/ppermute | solution.py:298
  28.9 5.5 %collective-permute-start.10 = (f32[128,128]{1,0:T(8,128)S(1)}, f32[128,128]{1,0:T(8,128)S(1)}, u32[]{:S(2)}, u32[]{:S(2)}) collective-permute-start(f32[128,128]{1,0:T(8,128)S(1)} %get-tuple-element.42), channel_id=1, source_target_pairs={{0,8},{1,9},{2,10},{3,11},{4,12},{5,13},{6,14},{7,15},{8,0},{9,1},... | collective-permute-start | bytes 196616 | tf_op jit(solution)/shard_map/ppermute | solution.py:298

commit v22 on v21

--- a/solution.py
+++ b/solution.py
@@ -11,7 +11,7 @@
 HIGHEST = lax.Precision.HIGHEST
 LANES = 128
 VMEM_LIMIT = 24 * 1024 * 1024
-AHEAD = 2
+AHEAD = 3
 ROWS = 256
 
 

time: 35.7 us -> 36.3 us (1.017)
  Pallas kernels: 11.7 us -> 12.3 us
    pallas_call x1, Pallas kernels: 4.99 us -> 5.63 us  [rows_call(): pl.pallas_call(rows_kernel, in_specs=[pl.BlockSpec(memory_space=pltpu.SME...]
  transfers between devices with their start and end apart: 13 -> 13, of which waited for: 5 -> 5; matrix products, arithmetic and copies ran while one was open for 1% -> 1% of each run, Pallas kernels for 16% -> 15%
where the time goes in v22:
time: 36.3 us; the launch traced here: 36.2 us
  starting transfers between devices  17.5 us (48%)
  Pallas kernels  12.3 us (34%)
  waiting for transfers between devices  5.33 us (15%)
  between operations  0.74 us (2%)
    ppermute x13, starting transfers between devices, exchange(): return lax.ppermute(array, AXES, pairs)  17.5 us
    pallas_call x1, Pallas kernels, rows_call(): pl.pallas_call(rows_kernel, in_specs=[pl.BlockSpec(memory_space=pltpu.SME...  5.63 us
    ppermute x13, waiting for transfers between devices, exchange(): return lax.ppermute(array, AXES, pairs)  5.33 us
    pallas_call x1, Pallas kernels, factor_call(): pl.pallas_call(factor_kernel, in_specs=[pl.BlockSpec(memory_space=pltpu.V...  3.78 us
    pallas_call x2, Pallas kernels, project_call(): pl.pallas_call(functools.partial(project_kernel, parts), in_specs=[pl.Blo...  1.77 us
    pallas_call x1, Pallas kernels, finish_call(): pl.pallas_call(functools.partial(finish_kernel, float(total_rows) ** 0.5,...  1.16 us
  transfers between devices with their start and end apart: 13, of which 5 were waited for; matrix products, arithmetic and copies ran while one was open for 1% of the time, Pallas kernels for 15%

profile of v22, /device:TPU:0, one launch (start us, length us, event | category | flops | bytes accessed | tf_op | source)
XLA Modules:
  0.0 36.2 jit_solution(14843467705314388895)
XLA Ops:
  0.6 5.6 %sketch_rows.1 = (bf16[576,4096]{1,0:T(8,128)(2,1)S(1)}, f32[576,128]{1,0:T(8,128)S(1)}, f32[72,128]{1,0:T(8,128)S(1)}, bf16[256,576]{1,0:T(8,128)(2,1)S(1)}, f32[8,128,128]{2,1,0:T(8,128)S(1)}) custom-call(s32[1]{0:T(128)} %bitcast.owner_ref, bf16[576,4096]{1,0:T(8,128)(2,1)} %slab_hbm.1, bf16[4096,128]{1,0:T(8,128)(2,1)} %sketch_hbm.1), custom_call_target="tpu_custom_call" | custom-call | flops 905969664 | bytes 4718592 | tf_op jit(solution)/shard_map/sketch_rows/pallas_call | solution.py:134
  6.3 0.5 %collective-permute-start = (f32[8,128,128]{2,1,0:T(8,128)S(1)}, f32[8,128,128]{2,1,0:T(8,128)S(1)}, u32[]{:S(2)}, u32[]{:S(2)}) collective-permute-start(f32[8,128,128]{2,1,0:T(8,128)S(1)} %get-tuple-element.23), channel_id=1, source_target_pairs={{0,1},{1,0},{2,3},{3,2},{4,5},{5,4},{6,7},{7,6},{8,9},{9,8},{10,11... | collective-permute-start | bytes 1572872 | tf_op jit(solution)/shard_map/ppermute | solution.py:298
  6.8 0.1 collective-permute-start.1
  6.9 0.7 %project_first.1 = f32[8,128,128]{2,1,0:T(8,128)S(1)} custom-call(s32[1]{0:T(128)} %bitcast.owner_ref, bf16[256,576]{1,0:T(8,128)(2,1)S(1)} %get-tuple-element.26.split_ref, bf16[576,4096]{1,0:T(8,128)(2,1)S(1)} %get-tuple-element.22.slab_ref), custom_call_target="tpu_custom_call" | custom-call | flops 301989888 | bytes 2359296 | tf_op jit(solution)/shard_map/project_first/pallas_call | solution.py:116
  7.6 0.8 %collective-permute-done.1 = f32[72,128]{1,0:T(8,128)S(1)} collective-permute-done((f32[72,128]{1,0:T(8,128)S(1)}, f32[72,128]{1,0:T(8,128)S(1)}, u32[]{:S(2)}, u32[]{:S(2)}) %collective-permute-start.1) | collective-permute-done | bytes 36896 | tf_op jit(solution)/shard_map/ppermute | solution.py:298
  8.4 0.0 collective-permute-done
  8.4 0.1 add.32
  8.5 2.9 %collective-permute-start.3 = (f32[8,128,128]{2,1,0:T(8,128)S(1)}, f32[8,128,128]{2,1,0:T(8,128)S(1)}, u32[]{:S(2)}, u32[]{:S(2)}) collective-permute-start(f32[8,128,128]{2,1,0:T(8,128)S(1)} %add.32), channel_id=1, source_target_pairs={{0,2},{1,5},{2,0},{3,7},{4,6},{5,1},{6,4},{7,3},{8,10},{9,13},{10,... | collective-permute-start | bytes 1572872 | tf_op jit(solution)/shard_map/ppermute | solution.py:298
  11.4 1.1 %project_rest.1 = (f32[8,128,128]{2,1,0:T(8,128)S(1)}, f32[8,128,128]{2,1,0:T(8,128)S(1)}) custom-call(s32[1]{0:T(128)} %bitcast.owner_ref, bf16[256,576]{1,0:T(8,128)(2,1)S(1)} %get-tuple-element.26.split_ref, bf16[576,4096]{1,0:T(8,128)(2,1)S(1)} %get-tuple-element.22.slab_ref), custom_call_target="tpu_custom_call" | custom-call | flops 603979776 | bytes 2359296 | tf_op jit(solution)/shard_map/project_rest/pallas_call | solution.py:116
  12.5 0.1 collective-permute-start.2
  12.6 3.7 %collective-permute-start.4 = (f32[72,128]{1,0:T(8,128)S(1)}, f32[72,128]{1,0:T(8,128)S(1)}, u32[]{:S(2)}, u32[]{:S(2)}) collective-permute-start(f32[72,128]{1,0:T(8,128)S(1)} %add.31), channel_id=1, source_target_pairs={{0,24},{1,25},{2,26},{3,27},{4,28},{5,29},{6,30},{7,31},{8,16},{9,... | collective-permute-start | bytes 110600 | tf_op jit(solution)/shard_map/ppermute | solution.py:298
  16.2 0.8 %collective-permute-start.6 = (f32[72,128]{1,0:T(8,128)S(1)}, f32[72,128]{1,0:T(8,128)S(1)}, u32[]{:S(2)}, u32[]{:S(2)}) collective-permute-start(f32[72,128]{1,0:T(8,128)S(1)} %add.31), channel_id=1, source_target_pairs={{0,8},{1,9},{2,10},{3,11},{4,12},{5,13},{6,14},{7,15},{8,0},{9,1},... | collective-permute-start | bytes 110600 | tf_op jit(solution)/shard_map/ppermute | solution.py:298
  17.0 1.4 %collective-permute-done.4 = f32[72,128]{1,0:T(8,128)S(1)} collective-permute-done((f32[72,128]{1,0:T(8,128)S(1)}, f32[72,128]{1,0:T(8,128)S(1)}, u32[]{:S(2)}, u32[]{:S(2)}) %collective-permute-start.4) | collective-permute-done | bytes 36896 | tf_op jit(solution)/shard_map/ppermute | solution.py:298
  18.4 0.1 collective-permute-done.3
  18.6 0.1 add_add_fusion
  18.7 2.1 %collective-permute-start.5 = (f32[4,128,128]{2,1,0:T(8,128)S(1)}, f32[4,128,128]{2,1,0:T(8,128)S(1)}, u32[]{:S(2)}, u32[]{:S(2)}) collective-permute-start(f32[4,128,128]{2,1,0:T(8,128)S(1)} %slice.19), channel_id=1, source_target_pairs={{0,4},{1,3},{2,6},{3,1},{4,0},{5,7},{6,2},{7,5},{8,12},{9,11},{10,... | collective-permute-start | bytes 786440 | tf_op jit(solution)/shard_map/ppermute | solution.py:298
  20.8 0.3 collective-permute-done.7
  21.1 1.4 %collective-permute-start.8 = (f32[72,128]{1,0:T(8,128)S(1)}, f32[72,128]{1,0:T(8,128)S(1)}, u32[]{:S(2)}, u32[]{:S(2)}) collective-permute-start(f32[72,128]{1,0:T(8,128)S(1)} %add_add_fusion.1), channel_id=1, source_target_pairs={{0,2},{1,5},{2,0},{3,7},{4,6},{5,1},{6,4},{7,3},{8,10},{9,13},{10,... | collective-permute-start | bytes 110600 | tf_op jit(solution)/shard_map/ppermute | solution.py:298
  22.5 2.7 %collective-permute-done.8 = f32[72,128]{1,0:T(8,128)S(1)} collective-permute-done((f32[72,128]{1,0:T(8,128)S(1)}, f32[72,128]{1,0:T(8,128)S(1)}, u32[]{:S(2)}, u32[]{:S(2)}) %collective-permute-start.8) | collective-permute-done | bytes 36896 | tf_op jit(solution)/shard_map/ppermute | solution.py:298
  25.1 1.5 %collective-permute-start.9 = (f32[72,128]{1,0:T(8,128)S(1)}, f32[72,128]{1,0:T(8,128)S(1)}, u32[]{:S(2)}, u32[]{:S(2)}) collective-permute-start(f32[72,128]{1,0:T(8,128)S(1)} %add.38.gram_ref), channel_id=1, source_target_pairs={{0,4},{1,3},{2,6},{3,1},{4,0},{5,7},{6,2},{7,5},{8,12},{9,11},{10,... | collective-permute-start | bytes 110600 | tf_op jit(solution)/shard_map/ppermute | solution.py:298
  26.7 2.8 %collective-permute-start.12 = (f32[128,128]{1,0:T(8,128)S(1)}, f32[128,128]{1,0:T(8,128)S(1)}, u32[]{:S(2)}, u32[]{:S(2)}) collective-permute-start(f32[128,128]{1,0:T(8,128)S(1)} %get-tuple-element.40), channel_id=1, source_target_pairs={{0,24},{1,25},{2,26},{3,27},{4,28},{5,29},{6,30},{7,31},{8,16},{9,... | collective-permute-start | bytes 196616 | tf_op jit(solution)/shard_map/ppermute | solution.py:298
  29.6 1.6 %collective-permute-start.10 = (f32[128,128]{1,0:T(8,128)S(1)}, f32[128,128]{1,0:T(8,128)S(1)}, u32[]{:S(2)}, u32[]{:S(2)}) collective-permute-start(f32[128,128]{1,0:T(8,128)S(1)} %get-tuple-element.42), channel_id=1, source_target_pairs={{0,8},{1,9},{2,10},{3,11},{4,12},{5,13},{6,14},{7,15},{8,0},{9,1},... | collective-permute-start | bytes 196616 | tf_op jit(solution)/shard_map/ppermute | solution.py:298
  31.2 3.8 %factor.1.inverse_ref = f32[128,128]{1,0:T(8,128)S(1)} custom-call(f32[72,128]{1,0:T(8,128)S(1)} %add.38.gram_ref, f32[72,128]{1,0:T(8,128)S(1)} %collective-permute-done.9.got_ref), custom_call_target="tpu_custom_call" | custom-call | flops 4000000000 | bytes 73728 | tf_op jit(solution)/shard_map/factor/pallas_call | solution.py:228
  35.0 1.2 %finish.1 = (f32[576,128]{1,0:T(8,128)}, bf16[128,128]{1,0:T(8,128)(2,1)}) custom-call(f32[128,128]{1,0:T(8,128)S(1)} %factor.1.inverse_ref, f32[576,128]{1,0:T(8,128)S(1)} %get-tuple-element.37.first_ref, f32[128,128]{1,0:T(8,128)S(1)} %slice_bitcast_fusion.3.sums_ref, f32[128,128]{1,0:T(8,128)S(1)} %collective-permute-done.10.refs_0_, ...), custom_call_target="tpu_custom_call" | custom-call | flops 113246208 | bytes 589824 | tf_op jit(solution)/shard_map/finish/pallas_call | solution.py:268
  (16 shorter events, 0.1 us)
Async XLA Ops:
  6.3 2.1 %collective-permute-start = (f32[8,128,128]{2,1,0:T(8,128)S(1)}, f32[8,128,128]{2,1,0:T(8,128)S(1)}, u32[]{:S(2)}, u32[]{:S(2)}) collective-permute-start(f32[8,128,128]{2,1,0:T(8,128)S(1)} %get-tuple-element.23), channel_id=1, source_target_pairs={{0,1},{1,0},{2,3},{3,2},{4,5},{5,4},{6,7},{7,6},{8,9},{9,8},{10,11... | collective-permute-start | bytes 1572872 | tf_op jit(solution)/shard_map/ppermute | solution.py:298
  6.8 1.6 %collective-permute-start.1 = (f32[72,128]{1,0:T(8,128)S(1)}, f32[72,128]{1,0:T(8,128)S(1)}, u32[]{:S(2)}, u32[]{:S(2)}) collective-permute-start(f32[72,128]{1,0:T(8,128)S(1)} %get-tuple-element.24), channel_id=1, source_target_pairs={{0,1},{1,0},{2,3},{3,2},{4,5},{5,4},{6,7},{7,6},{8,9},{9,8},{10,11... | collective-permute-start | bytes 110600 | tf_op jit(solution)/shard_map/ppermute | solution.py:298
  8.5 10.1 %collective-permute-start.3 = (f32[8,128,128]{2,1,0:T(8,128)S(1)}, f32[8,128,128]{2,1,0:T(8,128)S(1)}, u32[]{:S(2)}, u32[]{:S(2)}) collective-permute-start(f32[8,128,128]{2,1,0:T(8,128)S(1)} %add.32), channel_id=1, source_target_pairs={{0,2},{1,5},{2,0},{3,7},{4,6},{5,1},{6,4},{7,3},{8,10},{9,13},{10,... | collective-permute-start | bytes 1572872 | tf_op jit(solution)/shard_map/ppermute | solution.py:298
  12.5 6.1 %collective-permute-start.2 = (f32[8,128,128]{2,1,0:T(8,128)S(1)}, f32[8,128,128]{2,1,0:T(8,128)S(1)}, u32[]{:S(2)}, u32[]{:S(2)}) collective-permute-start(f32[8,128,128]{2,1,0:T(8,128)S(1)} %get-tuple-element.28), channel_id=1, source_target_pairs={{0,1},{1,0},{2,3},{3,2},{4,5},{5,4},{6,7},{7,6},{8,9},{9,8},{10,11... | collective-permute-start | bytes 1572872 | tf_op jit(solution)/shard_map/ppermute | solution.py:298
  12.6 5.8 %collective-permute-start.4 = (f32[72,128]{1,0:T(8,128)S(1)}, f32[72,128]{1,0:T(8,128)S(1)}, u32[]{:S(2)}, u32[]{:S(2)}) collective-permute-start(f32[72,128]{1,0:T(8,128)S(1)} %add.31), channel_id=1, source_target_pairs={{0,24},{1,25},{2,26},{3,27},{4,28},{5,29},{6,30},{7,31},{8,16},{9,... | collective-permute-start | bytes 110600 | tf_op jit(solution)/shard_map/ppermute | solution.py:298
  16.2 4.9 %collective-permute-start.7 = (f32[72,128]{1,0:T(8,128)S(1)}, f32[72,128]{1,0:T(8,128)S(1)}, u32[]{:S(2)}, u32[]{:S(2)}) collective-permute-start(f32[72,128]{1,0:T(8,128)S(1)} %add.31), channel_id=1, source_target_pairs={{0,16},{1,17},{2,18},{3,19},{4,20},{5,21},{6,22},{7,23},{8,24},{9,... | collective-permute-start | bytes 110600 | tf_op jit(solution)/shard_map/ppermute | solution.py:298
  16.2 4.9 %collective-permute-start.6 = (f32[72,128]{1,0:T(8,128)S(1)}, f32[72,128]{1,0:T(8,128)S(1)}, u32[]{:S(2)}, u32[]{:S(2)}) collective-permute-start(f32[72,128]{1,0:T(8,128)S(1)} %add.31), channel_id=1, source_target_pairs={{0,8},{1,9},{2,10},{3,11},{4,12},{5,13},{6,14},{7,15},{8,0},{9,1},... | collective-permute-start | bytes 110600 | tf_op jit(solution)/shard_map/ppermute | solution.py:298
  18.7 8.0 %collective-permute-start.5 = (f32[4,128,128]{2,1,0:T(8,128)S(1)}, f32[4,128,128]{2,1,0:T(8,128)S(1)}, u32[]{:S(2)}, u32[]{:S(2)}) collective-permute-start(f32[4,128,128]{2,1,0:T(8,128)S(1)} %slice.19), channel_id=1, source_target_pairs={{0,4},{1,3},{2,6},{3,1},{4,0},{5,7},{6,2},{7,5},{8,12},{9,11},{10,... | collective-permute-start | bytes 786440 | tf_op jit(solution)/shard_map/ppermute | solution.py:298
  21.1 4.0 %collective-permute-start.8 = (f32[72,128]{1,0:T(8,128)S(1)}, f32[72,128]{1,0:T(8,128)S(1)}, u32[]{:S(2)}, u32[]{:S(2)}) collective-permute-start(f32[72,128]{1,0:T(8,128)S(1)} %add_add_fusion.1), channel_id=1, source_target_pairs={{0,2},{1,5},{2,0},{3,7},{4,6},{5,1},{6,4},{7,3},{8,10},{9,13},{10,... | collective-permute-start | bytes 110600 | tf_op jit(solution)/shard_map/ppermute | solution.py:298
  25.1 6.0 %collective-permute-start.9 = (f32[72,128]{1,0:T(8,128)S(1)}, f32[72,128]{1,0:T(8,128)S(1)}, u32[]{:S(2)}, u32[]{:S(2)}) collective-permute-start(f32[72,128]{1,0:T(8,128)S(1)} %add.38.gram_ref), channel_id=1, source_target_pairs={{0,4},{1,3},{2,6},{3,1},{4,0},{5,7},{6,2},{7,5},{8,12},{9,11},{10,... | collective-permute-start | bytes 110600 | tf_op jit(solution)/shard_map/ppermute | solution.py:298
  26.7 8.3 %collective-permute-start.12 = (f32[128,128]{1,0:T(8,128)S(1)}, f32[128,128]{1,0:T(8,128)S(1)}, u32[]{:S(2)}, u32[]{:S(2)}) collective-permute-start(f32[128,128]{1,0:T(8,128)S(1)} %get-tuple-element.40), channel_id=1, source_target_pairs={{0,24},{1,25},{2,26},{3,27},{4,28},{5,29},{6,30},{7,31},{8,16},{9,... | collective-permute-start | bytes 196616 | tf_op jit(solution)/shard_map/ppermute | solution.py:298
  29.5 5.5 %collective-permute-start.11 = (f32[128,128]{1,0:T(8,128)S(1)}, f32[128,128]{1,0:T(8,128)S(1)}, u32[]{:S(2)}, u32[]{:S(2)}) collective-permute-start(f32[128,128]{1,0:T(8,128)S(1)} %get-tuple-element.41), channel_id=1, source_target_pairs={{0,16},{1,17},{2,18},{3,19},{4,20},{5,21},{6,22},{7,23},{8,24},{9,... | collective-permute-start | bytes 196616 | tf_op jit(solution)/shard_map/ppermute | solution.py:298
  29.6 5.5 %collective-permute-start.10 = (f32[128,128]{1,0:T(8,128)S(1)}, f32[128,128]{1,0:T(8,128)S(1)}, u32[]{:S(2)}, u32[]{:S(2)}) collective-permute-start(f32[128,128]{1,0:T(8,128)S(1)} %get-tuple-element.42), channel_id=1, source_target_pairs={{0,8},{1,9},{2,10},{3,11},{4,12},{5,13},{6,14},{7,15},{8,0},{9,1},... | collective-permute-start | bytes 196616 | tf_op jit(solution)/shard_map/ppermute | solution.py:298

commit v23 on v21

--- a/solution.py
+++ b/solution.py
@@ -79,9 +79,10 @@
     ]
     sketch_copy = pltpu.make_async_copy(sketch_hbm, sketch_ref, sketch_sem)
     sketch_copy.start()
-    for copy in copies[:AHEAD]:
+    copies[0].start()
+    sketch_copy.wait()
+    for copy in copies[1:AHEAD]:
         copy.start()
-    sketch_copy.wait()
     for k, r in enumerate(starts):
         copies[k].wait()
         if k + AHEAD < len(starts):

time: 35.7 us -> 35.8 us (level)
  no operation moved by 1% of the time
where the time goes in v23:
time: 35.8 us; the launch traced here: 35.6 us
  starting transfers between devices  17.5 us (49%)
  Pallas kernels  11.8 us (33%)
  waiting for transfers between devices  5.32 us (15%)
  between operations  0.74 us (2%)
    ppermute x13, starting transfers between devices, exchange(): return lax.ppermute(array, AXES, pairs)  17.5 us
    ppermute x13, waiting for transfers between devices, exchange(): return lax.ppermute(array, AXES, pairs)  5.32 us
    pallas_call x1, Pallas kernels, rows_call(): pl.pallas_call(rows_kernel, in_specs=[pl.BlockSpec(memory_space=pltpu.SME...  5.06 us
    pallas_call x1, Pallas kernels, factor_call(): pl.pallas_call(factor_kernel, in_specs=[pl.BlockSpec(memory_space=pltpu.V...  3.78 us
    pallas_call x2, Pallas kernels, project_call(): pl.pallas_call(functools.partial(project_kernel, parts), in_specs=[pl.Blo...  1.77 us
    pallas_call x1, Pallas kernels, finish_call(): pl.pallas_call(functools.partial(finish_kernel, float(total_rows) ** 0.5,...  1.16 us
  transfers between devices with their start and end apart: 13, of which 5 were waited for; matrix products, arithmetic and copies ran while one was open for 1% of the time, Pallas kernels for 16%

profile of v23, /device:TPU:0, one launch (start us, length us, event | category | flops | bytes accessed | tf_op | source)
XLA Modules:
  0.0 35.6 jit_solution(14096755191803909037)
XLA Ops:
  0.6 5.1 %sketch_rows.1 = (bf16[576,4096]{1,0:T(8,128)(2,1)S(1)}, f32[576,128]{1,0:T(8,128)S(1)}, f32[72,128]{1,0:T(8,128)S(1)}, bf16[256,576]{1,0:T(8,128)(2,1)S(1)}, f32[8,128,128]{2,1,0:T(8,128)S(1)}) custom-call(s32[1]{0:T(128)} %bitcast.owner_ref, bf16[576,4096]{1,0:T(8,128)(2,1)} %slab_hbm.1, bf16[4096,128]{1,0:T(8,128)(2,1)} %sketch_hbm.1), custom_call_target="tpu_custom_call" | custom-call | flops 905969664 | bytes 4718592 | tf_op jit(solution)/shard_map/sketch_rows/pallas_call | solution.py:135
  5.7 0.5 %collective-permute-start = (f32[8,128,128]{2,1,0:T(8,128)S(1)}, f32[8,128,128]{2,1,0:T(8,128)S(1)}, u32[]{:S(2)}, u32[]{:S(2)}) collective-permute-start(f32[8,128,128]{2,1,0:T(8,128)S(1)} %get-tuple-element.23), channel_id=1, source_target_pairs={{0,1},{1,0},{2,3},{3,2},{4,5},{5,4},{6,7},{7,6},{8,9},{9,8},{10,11... | collective-permute-start | bytes 1572872 | tf_op jit(solution)/shard_map/ppermute | solution.py:299
  6.2 0.1 collective-permute-start.1
  6.3 0.7 %project_first.1 = f32[8,128,128]{2,1,0:T(8,128)S(1)} custom-call(s32[1]{0:T(128)} %bitcast.owner_ref, bf16[256,576]{1,0:T(8,128)(2,1)S(1)} %get-tuple-element.26.split_ref, bf16[576,4096]{1,0:T(8,128)(2,1)S(1)} %get-tuple-element.22.slab_ref), custom_call_target="tpu_custom_call" | custom-call | flops 301989888 | bytes 2359296 | tf_op jit(solution)/shard_map/project_first/pallas_call | solution.py:117
  7.0 0.8 %collective-permute-done.1 = f32[72,128]{1,0:T(8,128)S(1)} collective-permute-done((f32[72,128]{1,0:T(8,128)S(1)}, f32[72,128]{1,0:T(8,128)S(1)}, u32[]{:S(2)}, u32[]{:S(2)}) %collective-permute-start.1) | collective-permute-done | bytes 36896 | tf_op jit(solution)/shard_map/ppermute | solution.py:299
  7.8 0.0 collective-permute-done
  7.8 0.1 add.32
  7.9 2.9 %collective-permute-start.3 = (f32[8,128,128]{2,1,0:T(8,128)S(1)}, f32[8,128,128]{2,1,0:T(8,128)S(1)}, u32[]{:S(2)}, u32[]{:S(2)}) collective-permute-start(f32[8,128,128]{2,1,0:T(8,128)S(1)} %add.32), channel_id=1, source_target_pairs={{0,2},{1,5},{2,0},{3,7},{4,6},{5,1},{6,4},{7,3},{8,10},{9,13},{10,... | collective-permute-start | bytes 1572872 | tf_op jit(solution)/shard_map/ppermute | solution.py:299
  10.8 1.1 %project_rest.1 = (f32[8,128,128]{2,1,0:T(8,128)S(1)}, f32[8,128,128]{2,1,0:T(8,128)S(1)}) custom-call(s32[1]{0:T(128)} %bitcast.owner_ref, bf16[256,576]{1,0:T(8,128)(2,1)S(1)} %get-tuple-element.26.split_ref, bf16[576,4096]{1,0:T(8,128)(2,1)S(1)} %get-tuple-element.22.slab_ref), custom_call_target="tpu_custom_call" | custom-call | flops 603979776 | bytes 2359296 | tf_op jit(solution)/shard_map/project_rest/pallas_call | solution.py:117
  11.9 0.1 collective-permute-start.2
  12.0 3.7 %collective-permute-start.4 = (f32[72,128]{1,0:T(8,128)S(1)}, f32[72,128]{1,0:T(8,128)S(1)}, u32[]{:S(2)}, u32[]{:S(2)}) collective-permute-start(f32[72,128]{1,0:T(8,128)S(1)} %add.31), channel_id=1, source_target_pairs={{0,24},{1,25},{2,26},{3,27},{4,28},{5,29},{6,30},{7,31},{8,16},{9,... | collective-permute-start | bytes 110600 | tf_op jit(solution)/shard_map/ppermute | solution.py:299
  15.7 0.8 %collective-permute-start.6 = (f32[72,128]{1,0:T(8,128)S(1)}, f32[72,128]{1,0:T(8,128)S(1)}, u32[]{:S(2)}, u32[]{:S(2)}) collective-permute-start(f32[72,128]{1,0:T(8,128)S(1)} %add.31), channel_id=1, source_target_pairs={{0,8},{1,9},{2,10},{3,11},{4,12},{5,13},{6,14},{7,15},{8,0},{9,1},... | collective-permute-start | bytes 110600 | tf_op jit(solution)/shard_map/ppermute | solution.py:299
  16.5 1.4 %collective-permute-done.4 = f32[72,128]{1,0:T(8,128)S(1)} collective-permute-done((f32[72,128]{1,0:T(8,128)S(1)}, f32[72,128]{1,0:T(8,128)S(1)}, u32[]{:S(2)}, u32[]{:S(2)}) %collective-permute-start.4) | collective-permute-done | bytes 36896 | tf_op jit(solution)/shard_map/ppermute | solution.py:299
  17.8 0.2 collective-permute-done.3
  18.0 0.1 add_add_fusion
  18.1 2.1 %collective-permute-start.5 = (f32[4,128,128]{2,1,0:T(8,128)S(1)}, f32[4,128,128]{2,1,0:T(8,128)S(1)}, u32[]{:S(2)}, u32[]{:S(2)}) collective-permute-start(f32[4,128,128]{2,1,0:T(8,128)S(1)} %slice.19), channel_id=1, source_target_pairs={{0,4},{1,3},{2,6},{3,1},{4,0},{5,7},{6,2},{7,5},{8,12},{9,11},{10,... | collective-permute-start | bytes 786440 | tf_op jit(solution)/shard_map/ppermute | solution.py:299
  20.2 0.3 collective-permute-done.7
  20.5 1.4 %collective-permute-start.8 = (f32[72,128]{1,0:T(8,128)S(1)}, f32[72,128]{1,0:T(8,128)S(1)}, u32[]{:S(2)}, u32[]{:S(2)}) collective-permute-start(f32[72,128]{1,0:T(8,128)S(1)} %add_add_fusion.1), channel_id=1, source_target_pairs={{0,2},{1,5},{2,0},{3,7},{4,6},{5,1},{6,4},{7,3},{8,10},{9,13},{10,... | collective-permute-start | bytes 110600 | tf_op jit(solution)/shard_map/ppermute | solution.py:299
  21.9 2.7 %collective-permute-done.8 = f32[72,128]{1,0:T(8,128)S(1)} collective-permute-done((f32[72,128]{1,0:T(8,128)S(1)}, f32[72,128]{1,0:T(8,128)S(1)}, u32[]{:S(2)}, u32[]{:S(2)}) %collective-permute-start.8) | collective-permute-done | bytes 36896 | tf_op jit(solution)/shard_map/ppermute | solution.py:299
  24.6 1.5 %collective-permute-start.9 = (f32[72,128]{1,0:T(8,128)S(1)}, f32[72,128]{1,0:T(8,128)S(1)}, u32[]{:S(2)}, u32[]{:S(2)}) collective-permute-start(f32[72,128]{1,0:T(8,128)S(1)} %add.38.gram_ref), channel_id=1, source_target_pairs={{0,4},{1,3},{2,6},{3,1},{4,0},{5,7},{6,2},{7,5},{8,12},{9,11},{10,... | collective-permute-start | bytes 110600 | tf_op jit(solution)/shard_map/ppermute | solution.py:299
  26.2 2.8 %collective-permute-start.12 = (f32[128,128]{1,0:T(8,128)S(1)}, f32[128,128]{1,0:T(8,128)S(1)}, u32[]{:S(2)}, u32[]{:S(2)}) collective-permute-start(f32[128,128]{1,0:T(8,128)S(1)} %get-tuple-element.40), channel_id=1, source_target_pairs={{0,24},{1,25},{2,26},{3,27},{4,28},{5,29},{6,30},{7,31},{8,16},{9,... | collective-permute-start | bytes 196616 | tf_op jit(solution)/shard_map/ppermute | solution.py:299
  29.0 1.6 %collective-permute-start.10 = (f32[128,128]{1,0:T(8,128)S(1)}, f32[128,128]{1,0:T(8,128)S(1)}, u32[]{:S(2)}, u32[]{:S(2)}) collective-permute-start(f32[128,128]{1,0:T(8,128)S(1)} %get-tuple-element.42), channel_id=1, source_target_pairs={{0,8},{1,9},{2,10},{3,11},{4,12},{5,13},{6,14},{7,15},{8,0},{9,1},... | collective-permute-start | bytes 196616 | tf_op jit(solution)/shard_map/ppermute | solution.py:299
  30.6 3.8 %factor.1.inverse_ref = f32[128,128]{1,0:T(8,128)S(1)} custom-call(f32[72,128]{1,0:T(8,128)S(1)} %add.38.gram_ref, f32[72,128]{1,0:T(8,128)S(1)} %collective-permute-done.9.got_ref), custom_call_target="tpu_custom_call" | custom-call | flops 4000000000 | bytes 73728 | tf_op jit(solution)/shard_map/factor/pallas_call | solution.py:229
  34.5 1.2 %finish.1 = (f32[576,128]{1,0:T(8,128)}, bf16[128,128]{1,0:T(8,128)(2,1)}) custom-call(f32[128,128]{1,0:T(8,128)S(1)} %factor.1.inverse_ref, f32[576,128]{1,0:T(8,128)S(1)} %get-tuple-element.37.first_ref, f32[128,128]{1,0:T(8,128)S(1)} %slice_bitcast_fusion.3.sums_ref, f32[128,128]{1,0:T(8,128)S(1)} %collective-permute-done.10.refs_0_, ...), custom_call_target="tpu_custom_call" | custom-call | flops 113246208 | bytes 589824 | tf_op jit(solution)/shard_map/finish/pallas_call | solution.py:269
  (16 shorter events, 0.1 us)
Async XLA Ops:
  5.7 2.1 %collective-permute-start = (f32[8,128,128]{2,1,0:T(8,128)S(1)}, f32[8,128,128]{2,1,0:T(8,128)S(1)}, u32[]{:S(2)}, u32[]{:S(2)}) collective-permute-start(f32[8,128,128]{2,1,0:T(8,128)S(1)} %get-tuple-element.23), channel_id=1, source_target_pairs={{0,1},{1,0},{2,3},{3,2},{4,5},{5,4},{6,7},{7,6},{8,9},{9,8},{10,11... | collective-permute-start | bytes 1572872 | tf_op jit(solution)/shard_map/ppermute | solution.py:299
  6.2 1.6 %collective-permute-start.1 = (f32[72,128]{1,0:T(8,128)S(1)}, f32[72,128]{1,0:T(8,128)S(1)}, u32[]{:S(2)}, u32[]{:S(2)}) collective-permute-start(f32[72,128]{1,0:T(8,128)S(1)} %get-tuple-element.24), channel_id=1, source_target_pairs={{0,1},{1,0},{2,3},{3,2},{4,5},{5,4},{6,7},{7,6},{8,9},{9,8},{10,11... | collective-permute-start | bytes 110600 | tf_op jit(solution)/shard_map/ppermute | solution.py:299
  7.9 10.1 %collective-permute-start.3 = (f32[8,128,128]{2,1,0:T(8,128)S(1)}, f32[8,128,128]{2,1,0:T(8,128)S(1)}, u32[]{:S(2)}, u32[]{:S(2)}) collective-permute-start(f32[8,128,128]{2,1,0:T(8,128)S(1)} %add.32), channel_id=1, source_target_pairs={{0,2},{1,5},{2,0},{3,7},{4,6},{5,1},{6,4},{7,3},{8,10},{9,13},{10,... | collective-permute-start | bytes 1572872 | tf_op jit(solution)/shard_map/ppermute | solution.py:299
  11.9 6.1 %collective-permute-start.2 = (f32[8,128,128]{2,1,0:T(8,128)S(1)}, f32[8,128,128]{2,1,0:T(8,128)S(1)}, u32[]{:S(2)}, u32[]{:S(2)}) collective-permute-start(f32[8,128,128]{2,1,0:T(8,128)S(1)} %get-tuple-element.28), channel_id=1, source_target_pairs={{0,1},{1,0},{2,3},{3,2},{4,5},{5,4},{6,7},{7,6},{8,9},{9,8},{10,11... | collective-permute-start | bytes 1572872 | tf_op jit(solution)/shard_map/ppermute | solution.py:299
  12.0 5.8 %collective-permute-start.4 = (f32[72,128]{1,0:T(8,128)S(1)}, f32[72,128]{1,0:T(8,128)S(1)}, u32[]{:S(2)}, u32[]{:S(2)}) collective-permute-start(f32[72,128]{1,0:T(8,128)S(1)} %add.31), channel_id=1, source_target_pairs={{0,24},{1,25},{2,26},{3,27},{4,28},{5,29},{6,30},{7,31},{8,16},{9,... | collective-permute-start | bytes 110600 | tf_op jit(solution)/shard_map/ppermute | solution.py:299
  15.7 4.9 %collective-permute-start.7 = (f32[72,128]{1,0:T(8,128)S(1)}, f32[72,128]{1,0:T(8,128)S(1)}, u32[]{:S(2)}, u32[]{:S(2)}) collective-permute-start(f32[72,128]{1,0:T(8,128)S(1)} %add.31), channel_id=1, source_target_pairs={{0,16},{1,17},{2,18},{3,19},{4,20},{5,21},{6,22},{7,23},{8,24},{9,... | collective-permute-start | bytes 110600 | tf_op jit(solution)/shard_map/ppermute | solution.py:299
  15.7 4.9 %collective-permute-start.6 = (f32[72,128]{1,0:T(8,128)S(1)}, f32[72,128]{1,0:T(8,128)S(1)}, u32[]{:S(2)}, u32[]{:S(2)}) collective-permute-start(f32[72,128]{1,0:T(8,128)S(1)} %add.31), channel_id=1, source_target_pairs={{0,8},{1,9},{2,10},{3,11},{4,12},{5,13},{6,14},{7,15},{8,0},{9,1},... | collective-permute-start | bytes 110600 | tf_op jit(solution)/shard_map/ppermute | solution.py:299
  18.1 8.0 %collective-permute-start.5 = (f32[4,128,128]{2,1,0:T(8,128)S(1)}, f32[4,128,128]{2,1,0:T(8,128)S(1)}, u32[]{:S(2)}, u32[]{:S(2)}) collective-permute-start(f32[4,128,128]{2,1,0:T(8,128)S(1)} %slice.19), channel_id=1, source_target_pairs={{0,4},{1,3},{2,6},{3,1},{4,0},{5,7},{6,2},{7,5},{8,12},{9,11},{10,... | collective-permute-start | bytes 786440 | tf_op jit(solution)/shard_map/ppermute | solution.py:299
  20.5 4.0 %collective-permute-start.8 = (f32[72,128]{1,0:T(8,128)S(1)}, f32[72,128]{1,0:T(8,128)S(1)}, u32[]{:S(2)}, u32[]{:S(2)}) collective-permute-start(f32[72,128]{1,0:T(8,128)S(1)} %add_add_fusion.1), channel_id=1, source_target_pairs={{0,2},{1,5},{2,0},{3,7},{4,6},{5,1},{6,4},{7,3},{8,10},{9,13},{10,... | collective-permute-start | bytes 110600 | tf_op jit(solution)/shard_map/ppermute | solution.py:299
  24.6 6.0 %collective-permute-start.9 = (f32[72,128]{1,0:T(8,128)S(1)}, f32[72,128]{1,0:T(8,128)S(1)}, u32[]{:S(2)}, u32[]{:S(2)}) collective-permute-start(f32[72,128]{1,0:T(8,128)S(1)} %add.38.gram_ref), channel_id=1, source_target_pairs={{0,4},{1,3},{2,6},{3,1},{4,0},{5,7},{6,2},{7,5},{8,12},{9,11},{10,... | collective-permute-start | bytes 110600 | tf_op jit(solution)/shard_map/ppermute | solution.py:299
  26.2 8.3 %collective-permute-start.12 = (f32[128,128]{1,0:T(8,128)S(1)}, f32[128,128]{1,0:T(8,128)S(1)}, u32[]{:S(2)}, u32[]{:S(2)}) collective-permute-start(f32[128,128]{1,0:T(8,128)S(1)} %get-tuple-element.40), channel_id=1, source_target_pairs={{0,24},{1,25},{2,26},{3,27},{4,28},{5,29},{6,30},{7,31},{8,16},{9,... | collective-permute-start | bytes 196616 | tf_op jit(solution)/shard_map/ppermute | solution.py:299
  29.0 5.4 %collective-permute-start.11 = (f32[128,128]{1,0:T(8,128)S(1)}, f32[128,128]{1,0:T(8,128)S(1)}, u32[]{:S(2)}, u32[]{:S(2)}) collective-permute-start(f32[128,128]{1,0:T(8,128)S(1)} %get-tuple-element.41), channel_id=1, source_target_pairs={{0,16},{1,17},{2,18},{3,19},{4,20},{5,21},{6,22},{7,23},{8,24},{9,... | collective-permute-start | bytes 196616 | tf_op jit(solution)/shard_map/ppermute | solution.py:299
  29.0 5.5 %collective-permute-start.10 = (f32[128,128]{1,0:T(8,128)S(1)}, f32[128,128]{1,0:T(8,128)S(1)}, u32[]{:S(2)}, u32[]{:S(2)}) collective-permute-start(f32[128,128]{1,0:T(8,128)S(1)} %get-tuple-element.42), channel_id=1, source_target_pairs={{0,8},{1,9},{2,10},{3,11},{4,12},{5,13},{6,14},{7,15},{8,0},{9,1},... | collective-permute-start | bytes 196616 | tf_op jit(solution)/shard_map/ppermute | solution.py:299
